TPU v7x, 32 devices: a whole 2x2x4 slice. The times are simulated.
32 devices in a mesh: section: 8 (over z, core), expert: 4 (over y, x).
Axes of the slice: x: 2, y: 2, z: 4, core: 2. Of those that a mesh axis runs over, the one named last changes fastest.
Arguments:
- section_layer_input: bfloat16 [8, 512, 4096], P('section', 'expert'), may hold values from -6 to 6
- token_expert_choice: int32 [8, 512, 8], P('section', 'expert'), may hold values from 0 to 31, as said below
- route_gate_steps: int32 [8, 512, 8], P('section', 'expert'), may hold values from 1 to 4096
- gate_weight: bfloat16 [8, 1024, 4096], P('section', 'expert'), may hold values from -0.09375 to 0.09375
- up_weight: bfloat16 [8, 1024, 4096], P('section', 'expert'), may hold values from -0.09375 to 0.09375
- down_weight: bfloat16 [8, 1024, 4096], P('section', 'expert'), may hold values from -0.1875 to 0.1875
- adapter_down_maps: bfloat16 [8, 1024, 16], P('section', 'expert'), may hold values from -0.1875 to 0.1875
- adapter_up_maps: bfloat16 [8, 1, 16, 4096], P('section'), may hold values from -1.5 to 1.5
- cotangent: bfloat16 [8, 512, 4096], P('section', 'expert'), may hold values from -6 to 6
Outputs:
- next_input: bfloat16 [8, 512, 4096], P('section', 'expert')
- prev_grad: bfloat16 [8, 512, 4096], P('section', 'expert')
- adapter_a_grad: float32 [8, 1024, 16], P('section', 'expert')
- adapter_b_grad: float32 [8, 1, 16, 4096], P('section', None, None, 'expert')
Inputs may be any that keep to these rules, and one draw needn't show every extreme that they name: `token_expert_choice`: every token names 8 different experts. The experts below 1 are those in flight; the tokens of one device (aligned blocks of 128 tokens of a section) name any one of them at most 16 times, and in every section one of them is named exactly 16 times by the tokens of every device.
All inputs are finite; a program needn't handle non-finite values.
Results may differ from a plain program's by a relative error of at most 0.0069.
Values may be sent and summed in bfloat16 or wider, within the bound.
No kernel may reach another device: no remote copies, remote signals or barrier semaphores. Data moves between devices by JAX's collectives and lax.ppermute only.
A program may use at most 64 MiB of HBM per device.

v0:
```python
import jax
import jax.numpy as jnp
from jax import lax
from jax.sharding import PartitionSpec as P

SPLIT = 4
MOST = 16


LOWRANK_SCALE = 2.0
LEVEL_STEP = 1.0 / 4096.0


def from_behind(block, axis, distance):
    devices = range(lax.axis_size(axis))
    route = [((i - distance) % len(devices), i) for i in devices]
    return lax.ppermute(block, axis, route)


def expert_forward(in_rows, gate_proj, up_proj, down_proj, down_adapter_factor, up_adapter_factor):
    contract_last = (((1,), (1,)), ((), ()))
    pre_gate = lax.dot_general(
        in_rows, gate_proj, contract_last, preferred_element_type=jnp.float32
    )
    pre_up = lax.dot_general(in_rows, up_proj, contract_last, preferred_element_type=jnp.float32)
    hidden = (jax.nn.silu(pre_gate) * pre_up).astype(jnp.bfloat16)
    projected_hidden = jnp.dot(
        hidden, down_adapter_factor, preferred_element_type=jnp.float32
    ).astype(jnp.bfloat16)
    layer_result_rows = jnp.dot(hidden, down_proj, preferred_element_type=jnp.float32)
    layer_result_rows = (
        layer_result_rows
        + LOWRANK_SCALE
        * jnp.dot(projected_hidden, up_adapter_factor, preferred_element_type=jnp.float32)
    ).astype(jnp.bfloat16)
    return (pre_gate, pre_up, hidden, projected_hidden, layer_result_rows)


def expert_backward(
    grad_in_rows,
    pre_gate,
    pre_up,
    gate_proj,
    up_proj,
    down_proj,
    down_adapter_factor,
    up_adapter_factor,
):
    contract_last = (((1,), (1,)), ((), ()))
    adapter_product = lax.dot_general(
        grad_in_rows, up_adapter_factor, contract_last, preferred_element_type=jnp.float32
    )
    adapter_product = (LOWRANK_SCALE * adapter_product).astype(jnp.bfloat16)
    grad_hidden = lax.dot_general(
        grad_in_rows, down_proj, contract_last, preferred_element_type=jnp.float32
    )
    grad_hidden = grad_hidden + lax.dot_general(
        adapter_product, down_adapter_factor, contract_last, preferred_element_type=jnp.float32
    )
    sigmoid_gate = jax.nn.sigmoid(pre_gate)
    grad_gate = (
        grad_hidden * pre_up * sigmoid_gate * (1.0 + pre_gate * (1.0 - sigmoid_gate))
    ).astype(jnp.bfloat16)
    grad_up = (grad_hidden * pre_gate * sigmoid_gate).astype(jnp.bfloat16)
    grad_input = jnp.dot(grad_gate, gate_proj, preferred_element_type=jnp.float32)
    grad_input = (
        grad_input + jnp.dot(grad_up, up_proj, preferred_element_type=jnp.float32)
    ).astype(jnp.bfloat16)
    return (adapter_product, grad_input)


def on_device(
    section_layer_input,
    token_expert_choice,
    route_gate_steps,
    gate_weight,
    up_weight,
    down_weight,
    adapter_down_maps,
    adapter_up_maps,
    cotangent,
):
    model_width = section_layer_input.shape[2]
    sources = lax.axis_size("expert")
    flight = sources // SPLIT
    local_expert_group = lax.axis_index("expert") // SPLIT
    gate_proj = gate_weight[0]
    up_proj = up_weight[0]
    down_proj = down_weight[0]
    down_adapter_factor = adapter_down_maps[0]
    up_adapter_factor = lax.dynamic_index_in_dim(
        adapter_up_maps[0], local_expert_group, 0, keepdims=False
    )
    unit_count = gate_proj.shape[0]
    rank_width = down_adapter_factor.shape[1]
    reduce_over_rows = (((0,), (0,)), ((), ()))
    route_ids = token_expert_choice[0]
    onehot = (route_ids[:, :, None] == jnp.arange(flight, dtype=jnp.int32)).astype(jnp.int32)
    routed = onehot.sum(1)
    weight = (onehot * route_gate_steps[0][:, :, None]).sum(1).astype(jnp.float32) * LEVEL_STEP
    slot_index = jnp.cumsum(routed, axis=0) - routed
    placement = (slot_index[:, :, None] == jnp.arange(MOST, dtype=jnp.int32)) & (
        routed[:, :, None] > 0
    )
    place_half = placement.astype(jnp.bfloat16)
    place_full = placement.astype(jnp.float32)
    slot_gate = jnp.einsum("tfs,tf->fs", place_full, weight, precision=lax.Precision.HIGHEST)
    token_rows = jnp.einsum(
        "tfs,td->fsd", place_half, section_layer_input[0], preferred_element_type=jnp.float32
    ).astype(jnp.bfloat16)
    gradient_rows_local = jnp.einsum(
        "tfs,td->fsd", place_half, cotangent[0], preferred_element_type=jnp.float32
    )
    gradient_rows_local = (gradient_rows_local * slot_gate[:, :, None]).astype(jnp.bfloat16)
    send_tokens = jnp.repeat(token_rows, SPLIT, axis=0)
    send_grads = jnp.repeat(gradient_rows_local, SPLIT, axis=0)
    received = lax.all_to_all(send_tokens, "expert", split_axis=0, concat_axis=0, tiled=True)
    item_count = received.shape[1]
    pre_gate, pre_up, hidden, projected_hidden, layer_result_rows = expert_forward(
        received.reshape(-1, model_width),
        gate_proj,
        up_proj,
        down_proj,
        down_adapter_factor,
        up_adapter_factor,
    )
    returned = lax.all_to_all(
        layer_result_rows.reshape(sources, item_count, model_width),
        "expert",
        split_axis=0,
        concat_axis=0,
        tiled=True,
    )
    back_out, pre_gate, pre_up, hidden, projected_hidden = (
        returned,
        pre_gate.reshape(sources, item_count, unit_count),
        pre_up.reshape(sources, item_count, unit_count),
        hidden.reshape(sources, item_count, unit_count),
        projected_hidden.reshape(sources, item_count, rank_width),
    )
    recv_grads = lax.all_to_all(send_grads, "expert", split_axis=0, concat_axis=0, tiled=True)
    adapter_product, grad_input = expert_backward(
        recv_grads.reshape(-1, model_width),
        pre_gate.reshape(-1, unit_count),
        pre_up.reshape(-1, unit_count),
        gate_proj,
        up_proj,
        down_proj,
        down_adapter_factor,
        up_adapter_factor,
    )
    back_grad = lax.all_to_all(
        grad_input.reshape(sources, MOST, model_width),
        "expert",
        split_axis=0,
        concat_axis=0,
        tiled=True,
    )
    adapter_a_grad = lax.dot_general(
        hidden.reshape(-1, unit_count),
        adapter_product,
        reduce_over_rows,
        preferred_element_type=jnp.float32,
    )
    up_factor_partial = LOWRANK_SCALE * lax.dot_general(
        projected_hidden.reshape(-1, rank_width),
        recv_grads.reshape(-1, model_width),
        reduce_over_rows,
        preferred_element_type=jnp.float32,
    )
    b_spread = jnp.where(
        (jnp.arange(flight, dtype=jnp.int32) == local_expert_group)[:, None, None],
        up_factor_partial[None],
        jnp.zeros((), jnp.float32),
    )
    adapter_b_grad = lax.psum_scatter(b_spread, "expert", scatter_dimension=2, tiled=True)
    out_total = back_out.astype(jnp.float32).reshape(flight, SPLIT, MOST, model_width).sum(1)
    moe_out = jnp.einsum(
        "tfs,fsd->td", place_full * weight[:, :, None], out_total, precision=lax.Precision.HIGHEST
    ).astype(jnp.bfloat16)
    grad_total = back_grad.astype(jnp.float32).reshape(flight, SPLIT, MOST, model_width).sum(1)
    layer_grad = jnp.einsum(
        "tfs,fsd->td", place_full, grad_total, precision=lax.Precision.HIGHEST
    ).astype(jnp.bfloat16)
    next_input = from_behind(moe_out[None], "section", 1)
    prev_grad = from_behind(layer_grad[None], "section", -1)
    return (next_input, prev_grad, adapter_a_grad[None], adapter_b_grad[None])


def solution(mesh):
    placed = (
        P("section", "expert", None),
        P("section", "expert", None),
        P("section", "expert", None),
        P("section", "expert", None),
        P("section", "expert", None),
        P("section", "expert", None),
        P("section", "expert", None),
        P("section", None, None, None),
        P("section", "expert", None),
    )
    return jax.shard_map(
        on_device,
        mesh=mesh,
        in_specs=placed,
        out_specs=(
            P("section", "expert", None),
            P("section", "expert", None),
            P("section", "expert", None),
            P("section", None, None, "expert"),
        ),
        check_vma=False,
    )
```

profile of v0, /device:TPU:0, one launch (start us, length us, event | category | flops | bytes accessed | tf_op | source)
XLA Modules:
  0.0 100.3 jit_solution(3873182613181734883)
XLA Ops:
  7.2 0.9 select_reduce_fusion
  8.5 1.5 %convolution_convert_fusion.2 = bf16[16,4096]{1,0:T(8,128)(2,1)S(1)} fusion(bf16[1,128,4096]{2,1,0:T(8,128)(2,1)} %param.9, s32[128]{0:T(128)S(1)} %sub.16, pred[128]{0:T(512)(128)(4,1)S(1)} %broadcast_compare_fusion.1), kind=kOutput, calls=%fused_computation.14 | convolution fusion | flops 16846848 | bytes 1180288 | tf_op jit(solution)/shard_map/tfs,td->fsd/dot_general | solution.py:108
  9.9 0.8 reshape.292
  10.8 5.2 %all-to-all-start = ((bf16[4,16,4096]{2,1,0:T(8,128)(2,1)}), bf16[4,16,4096]{2,1,0:T(8,128)(2,1)S(1)}, u32[]{:S(2)}, u32[]{:S(2)}) async-start(bf16[4,16,4096]{2,1,0:T(8,128)(2,1)} %reshape.292), calls=%async_computation | async-start | bytes 1048576 | tf_op jit(solution)/shard_map/all_to_all | solution.py:117
  15.9 0.2 convolution_bitcast_fusion.1
  16.1 1.5 %fusion.7 = bf16[16,4096]{1,0:T(8,128)(2,1)S(1)} fusion(bf16[1,128,4096]{2,1,0:T(8,128)(2,1)} %param.17, f32[16]{0:T(128)S(1)} %convolution_bitcast_fusion.1, s32[128]{0:T(128)S(1)} %sub.16, pred[128]{0:T(512)(128)(4,1)S(1)} %broadcast_compare_fusion.1), kind=kOutput, calls=%fused_computation.13 | convolution fusion | flops 16912384 | bytes 1180352 | tf_op jit(solution)/shard_map/tfs,td->fsd/dot_general | solution.py:111
  17.7 6.3 %all-to-all-done = bf16[4,16,4096]{2,1,0:T(8,128)(2,1)S(1)} async-done(((bf16[4,16,4096]{2,1,0:T(8,128)(2,1)}), bf16[4,16,4096]{2,1,0:T(8,128)(2,1)S(1)}, u32[]{:S(2)}, u32[]{:S(2)}) %all-to-all-start) | async-done | bytes 524320 | tf_op jit(solution)/shard_map/all_to_all | solution.py:117
  24.0 0.8 reshape.295
  24.8 3.5 %all-to-all-start.2 = ((bf16[4,16,4096]{2,1,0:T(8,128)(2,1)}), bf16[4,16,4096]{2,1,0:T(8,128)(2,1)S(1)}, u32[]{:S(2)}, u32[]{:S(2)}) async-start(bf16[4,16,4096]{2,1,0:T(8,128)(2,1)} %reshape.295), calls=%async_computation.2 | async-start | bytes 1048576 | tf_op jit(solution)/shard_map/all_to_all | solution.py:141
  28.3 2.5 %fusion.17 = f32[64,256]{1,0:T(8,128)S(1)} fusion(bf16[64,4096]{1,0:T(8,128)(2,1)S(1)} %bitcast.73, bf16[1,256,4096]{2,1,0:T(8,128)(2,1)} %param.12), kind=kOutput, calls=%fused_computation.24 | convolution fusion | flops 134217728 | bytes 2686976 | tf_op jit(solution)/shard_map/dot_general | solution.py:22
  30.8 0.8 multiply_convert_fusion.2
  31.7 1.5 %fusion.10 = f32[64,4096]{1,0:T(8,128)} fusion(bf16[64,256]{1,0:T(8,128)(2,1)S(1)} %get-tuple-element.6, bf16[1,256,4096]{2,1,0:T(8,128)(2,1)S(1)} %copy-done.1), kind=kOutput, calls=%fused_computation.17 | convolution fusion | flops 134217728 | bytes 3178496 | tf_op jit(solution)/shard_map/dot_general | solution.py:30
  33.2 2.2 %all-to-all-done.2 = bf16[4,16,4096]{2,1,0:T(8,128)(2,1)S(1)} async-done(((bf16[4,16,4096]{2,1,0:T(8,128)(2,1)}), bf16[4,16,4096]{2,1,0:T(8,128)(2,1)S(1)}, u32[]{:S(2)}, u32[]{:S(2)}) %all-to-all-start.2) | async-done | bytes 524320 | tf_op jit(solution)/shard_map/all_to_all | solution.py:141
  35.4 2.4 %fusion.8 = f32[64,256]{1,0:T(8,128)S(1)} fusion(bf16[64,4096]{1,0:T(8,128)(2,1)S(1)} %bitcast.70, bf16[1,256,4096]{2,1,0:T(8,128)(2,1)} %param.14), kind=kOutput, calls=%fused_computation.15 | convolution fusion | flops 134217728 | bytes 2686976 | tf_op jit(solution)/shard_map/dot_general | solution.py:54
  37.8 0.2 fusion.19
  38.1 1.1 %fusion.3 = bf16[64,4096]{1,0:T(8,128)(2,1)} fusion(f32[64,4096]{1,0:T(8,128)S(1)} %copy-done.2, bf16[64,16]{0,1:T(8,128)(2,1)S(1)} %convolution_convert_fusion.3, bf16[1,1,16,4096]{3,2,1,0:T(8,128)(2,1)S(1)} %copy-done.3), kind=kOutput, calls=%fused_computation.7 | convolution fusion | flops 9175040 | bytes 1705984 | tf_op jit(solution)/shard_map/dot_general | solution.py:34
  39.2 3.5 %all-to-all-start.1 = ((bf16[4,16,4096]{2,1,0:T(8,128)(2,1)}), bf16[4,16,4096]{2,1,0:T(8,128)(2,1)S(1)}, u32[]{:S(2)}, u32[]{:S(2)}) async-start(bf16[4,16,4096]{2,1,0:T(8,128)(2,1)} %bitcast.75), calls=%async_computation.1 | async-start | bytes 1048576 | tf_op jit(solution)/shard_map/all_to_all | solution.py:127
  42.9 2.1 %fusion.15 = f32[64,4096]{1,0:T(8,128)S(1)} fusion(bf16[1,256,4096]{2,1,0:T(8,128)(2,1)} %param.12, f32[64,256]{1,0:T(8,128)S(1)} %fusion.17, f32[64,256]{1,0:T(8,128)S(1)} %convolution_add_fusion.1, f32[64,256]{1,0:T(8,128)S(1)} %get-tuple-element.7), kind=kOutput, calls=%fused_computation.22 | convolution fusion | flops 134381568 | bytes 3342336 | tf_op jit(solution)/shard_map/dot_general | solution.py:65
  44.9 1.3 %fusion.4 = bf16[64,4096]{1,0:T(8,128)(2,1)} fusion(f32[64,4096]{1,0:T(8,128)S(1)} %fusion.15, bf16[1,256,4096]{2,1,0:T(8,128)(2,1)S(1)} %copy-done, f32[64,256]{1,0:T(8,128)S(1)} %convolution_add_fusion.1, f32[64,256]{1,0:T(8,128)S(1)} %fusion.17), kind=kOutput, calls=%fused_computation.8 | convolution fusion | flops 134840320 | bytes 3801088 | tf_op jit(solution)/shard_map/dot_general | solution.py:67
  46.2 3.0 %all-to-all-done.1 = bf16[4,16,4096]{2,1,0:T(8,128)(2,1)S(1)} async-done(((bf16[4,16,4096]{2,1,0:T(8,128)(2,1)}), bf16[4,16,4096]{2,1,0:T(8,128)(2,1)S(1)}, u32[]{:S(2)}, u32[]{:S(2)}) %all-to-all-start.1) | async-done | bytes 524320 | tf_op jit(solution)/shard_map/all_to_all | solution.py:127
  49.2 4.1 %all-to-all-start.3 = ((bf16[4,16,4096]{2,1,0:T(8,128)(2,1)}), bf16[4,16,4096]{2,1,0:T(8,128)(2,1)}, u32[]{:S(2)}, u32[]{:S(2)}) async-start(bf16[4,16,4096]{2,1,0:T(8,128)(2,1)} %bitcast.76), calls=%async_computation.3 | async-start | bytes 1048576 | tf_op jit(solution)/shard_map/all_to_all | solution.py:152
  53.5 2.8 %fusion = bf16[1,128,4096]{2,1,0:T(8,128)(2,1)} fusion(f32[16,4096]{1,0:T(8,128)S(1)} %convert_reduce_fusion.1, f32[128]{0:T(128)S(1)} %convert_multiply_fusion, s32[128]{0:T(128)S(1)} %sub.16, pred[128]{0:T(512)(128)(4,1)S(1)} %broadcast_compare_fusion.1), kind=kOutput, calls=%fused_computation.2 | convolution fusion | flops 101193728 | bytes 1311872 | tf_op jit(solution)/shard_map/tfs,fsd->td/dot_general | solution.py:178
  56.3 3.7 %all-to-all-done.3 = bf16[4,16,4096]{2,1,0:T(8,128)(2,1)} async-done(((bf16[4,16,4096]{2,1,0:T(8,128)(2,1)}), bf16[4,16,4096]{2,1,0:T(8,128)(2,1)}, u32[]{:S(2)}, u32[]{:S(2)}) %all-to-all-start.3) | async-done | bytes 524320 | tf_op jit(solution)/shard_map/all_to_all | solution.py:152
  60.0 1.1 %convert_reduce_fusion = f32[16,4096]{1,0:T(8,128)S(1)} fusion(bf16[4,16,4096]{2,1,0:T(8,128)(2,1)} %all-to-all-done.3), kind=kLoop, calls=%fused_computation.34 | loop fusion | flops 458752 | bytes 786432 | tf_op jit(solution)/shard_map/reduce_sum | solution.py:181
  61.2 2.0 %fusion.1 = bf16[1,128,4096]{2,1,0:T(8,128)(2,1)} fusion(f32[16,4096]{1,0:T(8,128)S(1)} %convert_reduce_fusion, s32[128]{0:T(128)S(1)} %sub.16, pred[128]{0:T(512)(128)(4,1)S(1)} %broadcast_compare_fusion.1), kind=kOutput, calls=%fused_computation.3 | convolution fusion | flops 101191680 | bytes 1311360 | tf_op jit(solution)/shard_map/tfs,fsd->td/dot_general | solution.py:182
  63.2 0.9 fusion.6
  64.1 0.7 convolution_bitcast_fusion
  64.8 11.8 %collective-permute-done = bf16[1,128,4096]{2,1,0:T(8,128)(2,1)} collective-permute-done((bf16[1,128,4096]{2,1,0:T(8,128)(2,1)}, bf16[1,128,4096]{2,1,0:T(8,128)(2,1)}, u32[]{:S(2)}, u32[]{:S(2)}) %collective-permute-start) | collective-permute-done | bytes 1048608 | tf_op jit(solution)/shard_map/ppermute | solution.py:17
  76.6 4.6 %collective-permute-done.1 = bf16[1,128,4096]{2,1,0:T(8,128)(2,1)} collective-permute-done((bf16[1,128,4096]{2,1,0:T(8,128)(2,1)}, bf16[1,128,4096]{2,1,0:T(8,128)(2,1)}, u32[]{:S(2)}, u32[]{:S(2)}) %collective-permute-start.1) | collective-permute-done | bytes 1048608 | tf_op jit(solution)/shard_map/ppermute | solution.py:17
  81.2 7.6 %reduce-scatter.2.cloned.1.call-done = f32[1,16,1024]{2,1,0:T(8,128)} async-done(((f32[1,16,4096]{2,1,0:T(8,128)}), f32[1,16,1024]{2,1,0:T(8,128)}) %reduce-scatter.2.cloned.1.call-update) | async-done | bytes 65552 | tf_op jit(solution)/shard_map/reduce_scatter | solution.py:176
  88.9 2.3 %copy.17 = bf16[1,128,4096]{2,1,0:T(8,128)(2,1)} copy(bf16[1,128,4096]{2,1,0:T(8,128)(2,1)} %collective-permute-done) | data formatting | bytes 2097152
  91.1 2.3 %copy.18 = bf16[1,128,4096]{2,1,0:T(8,128)(2,1)} copy(bf16[1,128,4096]{2,1,0:T(8,128)(2,1)} %collective-permute-done.1) | data formatting | bytes 2097152
  (23 shorter events, 0.9 us)
Async XLA Ops:
  7.2 23.6 %copy-start = (bf16[1,256,4096]{2,1,0:T(8,128)(2,1)S(1)}, bf16[1,256,4096]{2,1,0:T(8,128)(2,1)}, u32[]{:S(2)}) copy-start(bf16[1,256,4096]{2,1,0:T(8,128)(2,1)} %param.13) | copy-start | bytes 6291460
  10.8 13.2 %all-to-all-start = ((bf16[4,16,4096]{2,1,0:T(8,128)(2,1)}), bf16[4,16,4096]{2,1,0:T(8,128)(2,1)S(1)}, u32[]{:S(2)}, u32[]{:S(2)}) async-start(bf16[4,16,4096]{2,1,0:T(8,128)(2,1)} %reshape.292), calls=%async_computation | async-start | bytes 1048576 | tf_op jit(solution)/shard_map/all_to_all | solution.py:117
  24.8 10.6 %all-to-all-start.2 = ((bf16[4,16,4096]{2,1,0:T(8,128)(2,1)}), bf16[4,16,4096]{2,1,0:T(8,128)(2,1)S(1)}, u32[]{:S(2)}, u32[]{:S(2)}) async-start(bf16[4,16,4096]{2,1,0:T(8,128)(2,1)} %reshape.295), calls=%async_computation.2 | async-start | bytes 1048576 | tf_op jit(solution)/shard_map/all_to_all | solution.py:141
  28.3 3.3 %copy-start.4 = (bf16[1,256,16]{1,2,0:T(8,128)(2,1)S(1)}, bf16[1,256,16]{1,2,0:T(8,128)(2,1)}, u32[]{:S(2)}) copy-start(bf16[1,256,16]{1,2,0:T(8,128)(2,1)} %param.15) | copy-start | bytes 24580
  28.3 3.4 %copy-start.1 = (bf16[1,256,4096]{2,1,0:T(8,128)(2,1)S(1)}, bf16[1,256,4096]{2,1,0:T(8,128)(2,1)}, u32[]{:S(2)}) copy-start(bf16[1,256,4096]{2,1,0:T(8,128)(2,1)} %param.14) | copy-start | bytes 6291460
  33.2 4.7 %copy-start.3 = (bf16[1,1,16,4096]{3,2,1,0:T(8,128)(2,1)S(1)}, bf16[1,1,16,4096]{3,2,1,0:T(8,128)(2,1)}, u32[]{:S(2)}) copy-start(bf16[1,1,16,4096]{3,2,1,0:T(8,128)(2,1)} %param.16) | copy-start | bytes 393220
  35.4 2.7 %copy-start.2 = (f32[64,4096]{1,0:T(8,128)S(1)}, f32[64,4096]{1,0:T(8,128)}, u32[]{:S(2)}) copy-start(f32[64,4096]{1,0:T(8,128)} %fusion.10) | copy-start | bytes 3145732
  39.2 10.0 %all-to-all-start.1 = ((bf16[4,16,4096]{2,1,0:T(8,128)(2,1)}), bf16[4,16,4096]{2,1,0:T(8,128)(2,1)S(1)}, u32[]{:S(2)}, u32[]{:S(2)}) async-start(bf16[4,16,4096]{2,1,0:T(8,128)(2,1)} %bitcast.75), calls=%async_computation.1 | async-start | bytes 1048576 | tf_op jit(solution)/shard_map/all_to_all | solution.py:127
  49.2 10.8 %all-to-all-start.3 = ((bf16[4,16,4096]{2,1,0:T(8,128)(2,1)}), bf16[4,16,4096]{2,1,0:T(8,128)(2,1)}, u32[]{:S(2)}, u32[]{:S(2)}) async-start(bf16[4,16,4096]{2,1,0:T(8,128)(2,1)} %bitcast.76), calls=%async_computation.3 | async-start | bytes 1048576 | tf_op jit(solution)/shard_map/all_to_all | solution.py:152
  53.4 35.5 %reduce-scatter.2.cloned.1.call-start = ((), (), s32[]{:S(2)}) async-start(), calls=%async_computation.5 | async-start | bytes 327680 | tf_op jit(solution)/shard_map/reduce_scatter | solution.py:176
  56.3 20.3 %collective-permute-start = (bf16[1,128,4096]{2,1,0:T(8,128)(2,1)}, bf16[1,128,4096]{2,1,0:T(8,128)(2,1)}, u32[]{:S(2)}, u32[]{:S(2)}) collective-permute-start(bf16[1,128,4096]{2,1,0:T(8,128)(2,1)} %fusion), channel_id=1, source_target_pairs={{28,0},{0,4},{4,8},{8,12},{12,16},{16,20},{20,24},{24,28},{29,1},{... | collective-permute-start | bytes 3145736 | tf_op jit(solution)/shard_map/ppermute | solution.py:17
  63.2 18.1 %collective-permute-start.1 = (bf16[1,128,4096]{2,1,0:T(8,128)(2,1)}, bf16[1,128,4096]{2,1,0:T(8,128)(2,1)}, u32[]{:S(2)}, u32[]{:S(2)}) collective-permute-start(bf16[1,128,4096]{2,1,0:T(8,128)(2,1)} %fusion.1), channel_id=1, source_target_pairs={{4,0},{8,4},{12,8},{16,12},{20,16},{24,20},{28,24},{0,28},{5,1},{9... | collective-permute-start | bytes 3145736 | tf_op jit(solution)/shard_map/ppermute | solution.py:17
Sparse Core Ops, SparseCore 0:
  64.2 24.5 reduce-scatter.1
where the time goes:
time: 101 us; the launch traced here: 100 us
  waiting for transfers between devices  39.2 us (39%)
  matrix products  21.8 us (22%)
  starting transfers between devices  16.3 us (16%)
  between operations  14.1 us (14%)
  local copies, waits for them, and re-layouts  6.38 us (6%)
  other arithmetic  2.37 us (2%)
    ppermute x2, waiting for transfers between devices, from_behind(): return lax.ppermute(block, axis, route)  16.4 us
    reduce_scatter x1, waiting for transfers between devices, on_device(): lax.psum_scatter(b_spread, 'expert', scatter_dimension=2, tiled=True)  7.62 us
    all_to_all x1, waiting for transfers between devices, on_device(): lax.all_to_all(send_tokens, 'expert', split_axis=0, concat_axis=0, tiled=...  6.3 us
    all_to_all x1, starting transfers between devices, on_device(): lax.all_to_all(send_tokens, 'expert', split_axis=0, concat_axis=0, tiled=...  5.16 us
    unnamed x12, local copies, waits for them, and re-layouts  4.6 us
    all_to_all x1, starting transfers between devices, on_device(): lax.all_to_all(grad_input.reshape(sources, MOST, model_width), 'expert',...  4.14 us
    all_to_all x1, waiting for transfers between devices, on_device(): lax.all_to_all(grad_input.reshape(sources, MOST, model_width), 'expert',...  3.69 us
    all_to_all x1, starting transfers between devices, on_device(): lax.all_to_all(send_grads, 'expert', split_axis=0, concat_axis=0, tiled=T...  3.47 us
  transfers between devices with their start and end apart: 7, of which 7 were waited for; matrix products, arithmetic and copies ran while one was open for 18% of the time, Pallas kernels for 0%

commit v1 on v0

v1 whole, which is shorter than its diff:
```python
import functools

import jax
import jax.numpy as jnp
from jax import lax
from jax.experimental import pallas as pl
from jax.experimental.pallas import tpu as pltpu
from jax.sharding import PartitionSpec as P

SPLIT = 4
MOST = 16
LOWRANK_SCALE = 2.0
LEVEL_STEP = 1.0 / 4096.0
MIB = 1 << 20
LAST = (((1,), (1,)), ((), ()))
FIRST = (((0,), (0,)), ((), ()))
WHOLE = pl.BlockSpec(memory_space=pltpu.VMEM)


def f32dot(a, b, dims=(((1,), (0,)), ((), ()))):
    return lax.dot_general(a, b, dims, preferred_element_type=jnp.float32)


def call(body, outs, *args, flops=0, grant=24 * MIB):
    moved = sum(a.size * a.dtype.itemsize for a in (*args, *outs))
    return pl.pallas_call(
        body,
        out_shape=outs,
        in_specs=[WHOLE] * len(args),
        out_specs=[WHOLE] * len(outs),
        compiler_params=pltpu.CompilerParams(vmem_limit_bytes=grant),
        cost_estimate=pl.CostEstimate(flops=flops, bytes_accessed=moved, transcendentals=0),
    )(*args)


def sds(*shape, dtype=jnp.bfloat16):
    return jax.ShapeDtypeStruct(shape, dtype)


def gather_tokens(flight, choice_ref, steps_ref, x_ref, rows_ref, place_ref):
    choice = choice_ref[0]
    steps = steps_ref[0].astype(jnp.float32)
    tokens = choice.shape[0]
    across = lax.broadcasted_iota(jnp.int32, (tokens, tokens), 0)
    along = lax.broadcasted_iota(jnp.int32, (tokens, tokens), 1)
    slot = lax.broadcasted_iota(jnp.int32, (MOST, tokens), 0).astype(jnp.float32)
    for f in range(flight):
        level = jnp.sum(jnp.where(choice == f, steps, 0.0), axis=1, keepdims=True)
        routed = jnp.where(level > 0, 1.0, 0.0)
        before = jnp.sum(jnp.where(across < along, routed, 0.0), axis=0, keepdims=True)
        gate = jnp.sum(jnp.where(across == along, level, 0.0), axis=0, keepdims=True)
        place_ref[f * MOST:(f + 1) * MOST, :] = jnp.where(
            slot == before, gate * LEVEL_STEP, 0.0
        )
    pick = jnp.where(place_ref[...] > 0, 1.0, 0.0).astype(jnp.bfloat16)
    rows_ref[...] = f32dot(pick, x_ref[0]).astype(jnp.bfloat16)


def gather_grads(place_ref, cotangent_ref, rows_ref):
    place = place_ref[...]
    pick = jnp.where(place > 0, 1.0, 0.0).astype(jnp.bfloat16)
    gate = jnp.sum(place, axis=1, keepdims=True)
    rows_ref[...] = (f32dot(pick, cotangent_ref[0]) * gate).astype(jnp.bfloat16)


def forward(n, x_refs, gate_ref, up_ref, down_ref, a_ref, b_ref, outs):
    *out_refs, pre_gate_ref, pre_up_ref, hidden_ref, latent_ref = outs
    rows = jnp.concatenate([r[...] for r in x_refs], axis=0)
    height = rows.shape[0] // n
    pre_gate = f32dot(rows, gate_ref[0], LAST)
    pre_up = f32dot(rows, up_ref[0], LAST)
    pre_gate_ref[...] = pre_gate
    pre_up_ref[...] = pre_up
    hidden = (pre_gate * jax.nn.sigmoid(pre_gate) * pre_up).astype(jnp.bfloat16)
    hidden_ref[...] = hidden
    latent = f32dot(hidden, a_ref[0]).astype(jnp.bfloat16)
    latent_ref[...] = latent
    result = f32dot(hidden, down_ref[0]) + LOWRANK_SCALE * f32dot(latent, b_ref[...])
    result = result.astype(jnp.bfloat16)
    for k, ref in enumerate(out_refs):
        ref[...] = result[k * height:(k + 1) * height]


def backward(
    n, g_refs, pre_gate_ref, pre_up_ref, hidden_ref, gate_ref, up_ref, down_ref, a_ref, b_ref, outs
):
    *out_refs, a_grad_ref, lowrank_ref = outs
    rows = jnp.concatenate([r[...] for r in g_refs], axis=0)
    height = rows.shape[0] // n
    lowrank = (LOWRANK_SCALE * f32dot(rows, b_ref[...], LAST)).astype(jnp.bfloat16)
    lowrank_ref[...] = lowrank
    grad_hidden = f32dot(rows, down_ref[0], LAST) + f32dot(lowrank, a_ref[0], LAST)
    pre_gate = pre_gate_ref[...]
    pre_up = pre_up_ref[...]
    g = jax.nn.sigmoid(pre_gate)
    grad_gate = (grad_hidden * pre_up * g * (1.0 + pre_gate * (1.0 - g))).astype(jnp.bfloat16)
    grad_up = (grad_hidden * pre_gate * g).astype(jnp.bfloat16)
    result = (f32dot(grad_gate, gate_ref[0]) + f32dot(grad_up, up_ref[0])).astype(jnp.bfloat16)
    for k, ref in enumerate(out_refs):
        ref[...] = result[k * height:(k + 1) * height]
    a_grad_ref[0] = f32dot(hidden_ref[...], lowrank, FIRST)


def up_map_grad(n, lat_refs, g_refs, out_ref):
    width = out_ref.shape[-1]
    column = pl.multiple_of(lax.axis_index("expert") * width, 128)
    height = g_refs[0].shape[0]
    total = jnp.zeros(out_ref.shape[2:], jnp.float32)
    for i in range(n):
        block = sum(
            lat_refs[k][(i ^ k) * height:((i ^ k) + 1) * height, :].astype(jnp.float32)
            for k in range(n)
        )
        rows = g_refs[i][:, pl.ds(column, width)].astype(jnp.float32)
        total = total + lax.dot_general(
            block, rows, FIRST, precision=lax.Precision.HIGHEST, preferred_element_type=jnp.float32
        )
    out_ref[0, 0] = LOWRANK_SCALE * total


def expand(gated, place_ref, part_refs, out_ref):
    place = place_ref[...]
    pick = jnp.where(place > 0, 1.0, 0.0).astype(jnp.bfloat16)
    rows = sum(r[...].astype(jnp.float32) for r in part_refs)
    if gated:
        rows = rows * jnp.sum(place, axis=1, keepdims=True)
    high = rows.astype(jnp.bfloat16)
    spread = f32dot(pick, high, FIRST)
    if place.shape[0] > MOST:
        low = (rows - high.astype(jnp.float32)).astype(jnp.bfloat16)
        spread = spread + f32dot(pick, low, FIRST)
    out_ref[0] = spread.astype(jnp.bfloat16)


def split_refs(body, n, total_in, *extra):
    def packed(*refs):
        return body(*extra, n, refs[:n], *refs[n:total_in], refs[total_in:])

    return packed


def shifted(block, step, flip):
    sections, experts = lax.axis_size("section"), lax.axis_size("expert")
    route = [
        (s * experts + e, (s + step) % sections * experts + (e ^ flip))
        for s in range(sections)
        for e in range(experts)
    ]
    return lax.ppermute(block, ("section", "expert"), route)


def between_groups(rows, flight):
    if flight == 1:
        return rows
    groups = [[g * SPLIT + q for g in range(flight)] for q in range(SPLIT)]
    return lax.all_to_all(
        rows, "expert", split_axis=0, concat_axis=0, axis_index_groups=groups, tiled=True
    )


def on_device(
    section_layer_input,
    token_expert_choice,
    route_gate_steps,
    gate_weight,
    up_weight,
    down_weight,
    adapter_down_maps,
    adapter_up_maps,
    cotangent,
):
    tokens, width = section_layer_input.shape[1:]
    units, rank = adapter_down_maps.shape[1:]
    flight = lax.axis_size("expert") // SPLIT
    slots = flight * MOST
    rows = SPLIT * slots
    flips = range(SPLIT)
    if flight == 1:
        up_map = adapter_up_maps[0, 0]
    else:
        group = lax.axis_index("expert") // SPLIT
        up_map = lax.dynamic_index_in_dim(adapter_up_maps[0], group, 0, keepdims=False)

    x_rows, place = call(
        functools.partial(gather_tokens, flight),
        [sds(slots, width), sds(slots, tokens, dtype=jnp.float32)],
        token_expert_choice,
        route_gate_steps,
        section_layer_input,
        flops=2 * slots * tokens * width,
    )
    x_rows = between_groups(x_rows, flight)
    x_blocks = [x_rows] + [shifted(x_rows, 0, k) for k in flips[1:]]
    (g_rows,) = call(
        gather_grads,
        [sds(slots, width)],
        place,
        cotangent,
        flops=2 * slots * tokens * width,
    )
    g_rows = between_groups(g_rows, flight)
    g_blocks = [g_rows] + [shifted(g_rows, 0, k) for k in flips[1:]]
    place_before = shifted(place, 1, 0)
    place_after = shifted(place, -1, 0)

    weights = (gate_weight, up_weight, down_weight, adapter_down_maps, up_map)
    block_outs = [sds(slots, width)] * SPLIT
    *out_blocks, pre_gate, pre_up, hidden, latent = call(
        split_refs(forward, SPLIT, SPLIT + 5),
        block_outs
        + [sds(rows, units, dtype=jnp.float32)] * 2
        + [sds(rows, units), sds(rows, rank)],
        *x_blocks,
        *weights,
        flops=6 * rows * units * width,
    )
    out_parts = [shifted(out_blocks[k], 1, k) for k in flips]
    *grad_blocks, a_grad, lowrank = call(
        split_refs(backward, SPLIT, SPLIT + 8),
        block_outs + [sds(1, units, rank, dtype=jnp.float32), sds(rows, rank)],
        *g_blocks,
        pre_gate,
        pre_up,
        hidden,
        *weights,
        flops=6 * rows * units * width,
    )
    grad_parts = [shifted(grad_blocks[k], -1, k) for k in flips]

    if flight == 1:
        latents = [latent] + [shifted(latent, 0, k) for k in flips[1:]]

        def b_body(*refs):
            up_map_grad(SPLIT, refs[:SPLIT], refs[SPLIT:2 * SPLIT], refs[2 * SPLIT])

        (b_grad,) = call(
            b_body,
            [sds(1, 1, rank, width // SPLIT, dtype=jnp.float32)],
            *latents,
            *g_blocks,
            flops=2 * rows * rank * width // SPLIT,
        )
    else:
        part = LOWRANK_SCALE * f32dot(latent, jnp.concatenate(g_blocks, axis=0), FIRST)
        mine = jnp.arange(flight, dtype=jnp.int32) == group
        spread = jnp.where(mine[:, None, None], part[None], 0.0)
        b_grad = lax.psum_scatter(spread, "expert", scatter_dimension=2, tiled=True)[None]

    def finish(parts, place, gated):
        if flight > 1:
            total = sum(p.astype(jnp.float32) for p in parts).astype(jnp.bfloat16)
            parts = [between_groups(total, flight)]

        def body(place_ref, *refs):
            expand(gated, place_ref, refs[:-1], refs[-1])

        return call(
            body, [sds(1, tokens, width)], place, *parts, flops=2 * slots * tokens * width
        )[0]

    next_input = finish(out_parts, place_before, True)
    prev_grad = finish(grad_parts, place_after, False)
    return next_input, prev_grad, a_grad, b_grad


def solution(mesh):
    rows = P("section", "expert", None)
    return jax.shard_map(
        on_device,
        mesh=mesh,
        in_specs=(rows,) * 7 + (P("section", None, None, None), rows),
        out_specs=(rows, rows, rows, P("section", None, None, "expert")),
        check_vma=False,
    )
```

time: 101 us -> 53.4 us (0.53)
  waiting for transfers between devices: 39.2 us -> 7.82 us
  matrix products: 21.8 us -> 0 us
  between operations: 14.1 us -> 0.69 us
  Pallas kernels: 0 us -> 10.2 us
  starting transfers between devices: 16.3 us -> 24.6 us
  local copies, waits for them, and re-layouts: 6.38 us -> 9.74 us
  other arithmetic: 2.37 us -> 0 us
    ppermute x2 -> x19, starting transfers between devices: 0.01 us -> 24.6 us  [shifted(): return lax.ppermute(block, ('section', 'expert'), route)]
    dot_general x17 -> x0, matrix products: 21.8 us -> none  [the longest x1 2.81 us: on_device(): jnp.einsum('tfs,fsd->td', place_full * weight[:, :, None], out_total, pre...]
    all_to_all x4 -> x0, starting transfers between devices: 16.2 us -> none  [the longest x1 5.16 us: on_device(): lax.all_to_all(send_tokens, 'expert', split_axis=0, concat_axis=0, tiled=...]
    all_to_all x4 -> x0, waiting for transfers between devices: 15.2 us -> none  [the longest x1 6.3 us: on_device(): lax.all_to_all(send_tokens, 'expert', split_axis=0, concat_axis=0, tiled=...]
    pallas_call x0 -> x7, Pallas kernels: none -> 10.2 us  [call(): pl.pallas_call(body, out_shape=outs, in_specs=[WHOLE] * len(args), out_sp...]
    ppermute x2 -> x19, waiting for transfers between devices: 16.4 us -> 7.82 us  [shifted(): return lax.ppermute(block, ('section', 'expert'), route)]
    reduce_scatter x1 -> x0, waiting for transfers between devices: 7.62 us -> none  [on_device(): lax.psum_scatter(b_spread, 'expert', scatter_dimension=2, tiled=True)]
    unnamed x12 -> x16, local copies, waits for them, and re-layouts: 4.6 us -> 9.74 us
  transfers between devices with their start and end apart: 7 -> 19, of which waited for: 7 -> 4; matrix products, arithmetic and copies ran while one was open for 18% -> 3% of each run, Pallas kernels for 0% -> 16%
where the time goes in v1:
time: 53.4 us; the launch traced here: 53.1 us
  starting transfers between devices  24.6 us (46%)
  Pallas kernels  10.2 us (19%)
  local copies, waits for them, and re-layouts  9.74 us (18%)
  waiting for transfers between devices  7.82 us (15%)
  between operations  0.69 us (1%)
    ppermute x19, starting transfers between devices, shifted(): return lax.ppermute(block, ('section', 'expert'), route)  24.6 us
    pallas_call x7, Pallas kernels, call(): pl.pallas_call(body, out_shape=outs, in_specs=[WHOLE] * len(args), out_sp...  10.2 us
    unnamed x16, local copies, waits for them, and re-layouts  9.74 us
    ppermute x19, waiting for transfers between devices, shifted(): return lax.ppermute(block, ('section', 'expert'), route)  7.82 us
  transfers between devices with their start and end apart: 19, of which 4 were waited for; matrix products, arithmetic and copies ran while one was open for 3% of the time, Pallas kernels for 16%

profile of v1, /device:TPU:0, one launch (start us, length us, event | category | flops | bytes accessed | tf_op | source)
XLA Modules:
  0.0 53.1 jit_solution(10423717112133662630)
XLA Ops:
  0.6 0.9 %copy.13.choice_ref = s32[1,128,8]{2,1,0:T(8,128)S(1)} copy(s32[1,128,8]{1,2,0:T(8,128)} %param.10) | data formatting | bytes 8192 | tf_op args[1]
  1.6 0.8 %copy.14.steps_ref = s32[1,128,8]{2,1,0:T(8,128)S(1)} copy(s32[1,128,8]{1,2,0:T(8,128)} %param.11) | data formatting | bytes 8192 | tf_op args[2]
  2.4 1.2 %copy-done.3 = bf16[1,128,4096]{2,1,0:T(8,128)(2,1)S(1)} copy-done((bf16[1,128,4096]{2,1,0:T(8,128)(2,1)S(1)}, bf16[1,128,4096]{2,1,0:T(8,128)(2,1)}, u32[]{:S(2)}) %copy-start.3) | copy-done | bytes 1048600
  3.6 0.3 shard_map.120
  3.9 3.9 %collective-permute-start.3 = (bf16[16,4096]{1,0:T(8,128)(2,1)S(1)}, bf16[16,4096]{1,0:T(8,128)(2,1)S(1)}, u32[]{:S(2)}, u32[]{:S(2)}) collective-permute-start(bf16[16,4096]{1,0:T(8,128)(2,1)S(1)} %get-tuple-element.20.refs_0_), channel_id=1, source_target_pairs={{0,3},{1,2},{2,1},{3,0},{4,7},{5,6},{6,5},{7,4},{8,11},{9,10},{10,... | collective-permute-start | bytes 393224 | tf_op jit(solution)/shard_map/ppermute | solution.py:149
  7.9 0.5 collective-permute-start.2
  8.5 1.2 %copy-done.4 = bf16[1,128,4096]{2,1,0:T(8,128)(2,1)S(1)} copy-done((bf16[1,128,4096]{2,1,0:T(8,128)(2,1)S(1)}, bf16[1,128,4096]{2,1,0:T(8,128)(2,1)}, u32[]{:S(2)}) %copy-start.4) | copy-done | bytes 1048600
  10.0 2.9 %collective-permute-start.11 = (bf16[16,4096]{1,0:T(8,128)(2,1)S(1)}, bf16[16,4096]{1,0:T(8,128)(2,1)S(1)}, u32[]{:S(2)}, u32[]{:S(2)}) collective-permute-start(bf16[16,4096]{1,0:T(8,128)(2,1)S(1)} %shard_map.123.refs_0_.refs_4_), channel_id=1, source_target_pairs={{0,3},{1,2},{2,1},{3,0},{4,7},{5,6},{6,5},{7,4},{8,11},{9,10},{10,... | collective-permute-start | bytes 393224 | tf_op jit(solution)/shard_map/ppermute | solution.py:149
  12.9 0.5 collective-permute-start.10
  13.4 0.8 %collective-permute-start.9 = (bf16[16,4096]{1,0:T(8,128)(2,1)S(1)}, bf16[16,4096]{1,0:T(8,128)(2,1)S(1)}, u32[]{:S(2)}, u32[]{:S(2)}) collective-permute-start(bf16[16,4096]{1,0:T(8,128)(2,1)S(1)} %shard_map.123.refs_0_.refs_4_), channel_id=1, source_target_pairs={{0,1},{1,0},{2,3},{3,2},{4,5},{5,4},{6,7},{7,6},{8,9},{9,8},{10,11... | collective-permute-start | bytes 393224 | tf_op jit(solution)/shard_map/ppermute | solution.py:149
  14.2 0.8 %copy.15.refs_7_.refs_10_ = bf16[1,256,16]{2,1,0:T(8,128)(2,1)S(1)} copy(bf16[1,256,16]{1,2,0:T(8,128)(2,1)} %param.15) | data formatting | bytes 16384 | tf_op args[6]
  15.0 0.7 %collective-permute-done.2.refs_2_ = bf16[16,4096]{1,0:T(8,128)(2,1)S(1)} collective-permute-done((bf16[16,4096]{1,0:T(8,128)(2,1)S(1)}, bf16[16,4096]{1,0:T(8,128)(2,1)S(1)}, u32[]{:S(2)}, u32[]{:S(2)}) %collective-permute-start.2) | collective-permute-done | bytes 131104 | tf_op jit(solution)/shard_map/ppermute | solution.py:149
  15.7 1.6 %copy-done.1 = bf16[1,256,4096]{2,1,0:T(8,128)(2,1)S(1)} copy-done((bf16[1,256,4096]{2,1,0:T(8,128)(2,1)S(1)}, bf16[1,256,4096]{2,1,0:T(8,128)(2,1)}, u32[]{:S(2)}) %copy-start.1) | copy-done | bytes 2097176
  17.3 1.6 %copy-done.2 = bf16[1,256,4096]{2,1,0:T(8,128)(2,1)S(1)} copy-done((bf16[1,256,4096]{2,1,0:T(8,128)(2,1)S(1)}, bf16[1,256,4096]{2,1,0:T(8,128)(2,1)}, u32[]{:S(2)}) %copy-start.2) | copy-done | bytes 2097176
  18.9 0.9 %copy-done.5 = bf16[1,1,16,4096]{3,2,1,0:T(8,128)(2,1)S(1)} copy-done((bf16[1,1,16,4096]{3,2,1,0:T(8,128)(2,1)S(1)}, bf16[1,1,16,4096]{3,2,1,0:T(8,128)(2,1)}, u32[]{:S(2)}) %copy-start.5) | copy-done | bytes 131096
  19.8 2.1 %shard_map.121 = (bf16[16,4096]{1,0:T(8,128)(2,1)S(1)}, bf16[16,4096]{1,0:T(8,128)(2,1)S(1)}, bf16[16,4096]{1,0:T(8,128)(2,1)S(1)}, bf16[16,4096]{1,0:T(8,128)(2...) custom-call(bf16[16,4096]{1,0:T(8,128)(2,1)S(1)} %get-tuple-element., ...), custom_call_target="tpu_custom_call" | custom-call | flops 402653184 | bytes 7645184 | tf_op jit(solution)/shard_map/pallas_call | solution.py:26
  21.9 1.9 %collective-permute-start.4 = (bf16[16,4096]{1,0:T(8,128)(2,1)S(1)}, bf16[16,4096]{1,0:T(8,128)(2,1)S(1)}, u32[]{:S(2)}, u32[]{:S(2)}) collective-permute-start(bf16[16,4096]{1,0:T(8,128)(2,1)S(1)} %get-tuple-element.21), channel_id=1, source_target_pairs={{0,4},{1,5},{2,6},{3,7},{4,8},{5,9},{6,10},{7,11},{8,12},{9,13},{1... | collective-permute-start | bytes 393224 | tf_op jit(solution)/shard_map/ppermute | solution.py:149
  23.8 0.9 %collective-permute-start.5 = (bf16[16,4096]{1,0:T(8,128)(2,1)S(1)}, bf16[16,4096]{1,0:T(8,128)(2,1)S(1)}, u32[]{:S(2)}, u32[]{:S(2)}) collective-permute-start(bf16[16,4096]{1,0:T(8,128)(2,1)S(1)} %get-tuple-element.22), channel_id=1, source_target_pairs={{0,5},{1,4},{2,7},{3,6},{4,9},{5,8},{6,11},{7,10},{8,13},{9,12},{1... | collective-permute-start | bytes 393224 | tf_op jit(solution)/shard_map/ppermute | solution.py:149
  24.7 3.2 %collective-permute-start.6 = (bf16[16,4096]{1,0:T(8,128)(2,1)S(1)}, bf16[16,4096]{1,0:T(8,128)(2,1)S(1)}, u32[]{:S(2)}, u32[]{:S(2)}) collective-permute-start(bf16[16,4096]{1,0:T(8,128)(2,1)S(1)} %get-tuple-element.23), channel_id=1, source_target_pairs={{0,6},{1,7},{2,4},{3,5},{4,10},{5,11},{6,8},{7,9},{8,14},{9,15},{1... | collective-permute-start | bytes 393224 | tf_op jit(solution)/shard_map/ppermute | solution.py:149
  28.1 1.3 %collective-permute-start.17 = (bf16[64,16]{1,0:T(8,128)(2,1)S(1)}, bf16[64,16]{1,0:T(8,128)(2,1)S(1)}, u32[]{:S(2)}, u32[]{:S(2)}) collective-permute-start(bf16[64,16]{1,0:T(8,128)(2,1)S(1)} %get-tuple-element.33.refs_0_), channel_id=1, source_target_pairs={{0,2},{1,3},{2,0},{3,1},{4,6},{5,7},{6,4},{7,5},{8,10},{9,11},{10,... | collective-permute-start | bytes 6152 | tf_op jit(solution)/shard_map/ppermute | solution.py:149
  29.3 3.5 %collective-permute-done.18.refs_3_ = bf16[64,16]{1,0:T(8,128)(2,1)S(1)} collective-permute-done((bf16[64,16]{1,0:T(8,128)(2,1)S(1)}, bf16[64,16]{1,0:T(8,128)(2,1)S(1)}, u32[]{:S(2)}, u32[]{:S(2)}) %collective-permute-start.18) | collective-permute-done | bytes 2080 | tf_op jit(solution)/shard_map/ppermute | solution.py:149
  32.8 1.1 %collective-permute-start.16 = (bf16[64,16]{1,0:T(8,128)(2,1)S(1)}, bf16[64,16]{1,0:T(8,128)(2,1)S(1)}, u32[]{:S(2)}, u32[]{:S(2)}) collective-permute-start(bf16[64,16]{1,0:T(8,128)(2,1)S(1)} %get-tuple-element.33.refs_0_), channel_id=1, source_target_pairs={{0,1},{1,0},{2,3},{3,2},{4,5},{5,4},{6,7},{7,6},{8,9},{9,8},{10,11... | collective-permute-start | bytes 6152 | tf_op jit(solution)/shard_map/ppermute | solution.py:149
  33.9 3.5 %shard_map.124 = (bf16[16,4096]{1,0:T(8,128)(2,1)}, bf16[16,4096]{1,0:T(8,128)(2,1)}, bf16[16,4096]{1,0:T(8,128)(2,1)}, bf16[16,4096]{1,0:T(8,128)(2,1)S(1)}, f3...) custom-call(bf16[16,4096]{1,0:T(8,128)(2,1)S(1)} %shard_map.123.refs_0_.refs_4_, ...), custom_call_target="tpu_custom_call" | custom-call | flops 402653184 | bytes 7661568 | tf_op jit(solution)/shard_map/pallas_call | solution.py:26
  37.4 3.7 %collective-permute-start.12 = (bf16[16,4096]{1,0:T(8,128)(2,1)}, bf16[16,4096]{1,0:T(8,128)(2,1)S(1)}, u32[]{:S(2)}, u32[]{:S(2)}) collective-permute-start(bf16[16,4096]{1,0:T(8,128)(2,1)} %get-tuple-element.28), channel_id=1, source_target_pairs={{0,28},{1,29},{2,30},{3,31},{4,0},{5,1},{6,2},{7,3},{8,4},{9,5},{1... | collective-permute-start | bytes 393224 | tf_op jit(solution)/shard_map/ppermute | solution.py:149
  41.1 1.4 %collective-permute-start.13 = (bf16[16,4096]{1,0:T(8,128)(2,1)}, bf16[16,4096]{1,0:T(8,128)(2,1)S(1)}, u32[]{:S(2)}, u32[]{:S(2)}) collective-permute-start(bf16[16,4096]{1,0:T(8,128)(2,1)} %get-tuple-element.29), channel_id=1, source_target_pairs={{0,29},{1,28},{2,31},{3,30},{4,1},{5,0},{6,3},{7,2},{8,5},{9,4},{1... | collective-permute-start | bytes 393224 | tf_op jit(solution)/shard_map/ppermute | solution.py:149
  42.5 1.3 %collective-permute-start.15 = (bf16[16,4096]{1,0:T(8,128)(2,1)S(1)}, bf16[16,4096]{1,0:T(8,128)(2,1)S(1)}, u32[]{:S(2)}, u32[]{:S(2)}) collective-permute-start(bf16[16,4096]{1,0:T(8,128)(2,1)S(1)} %get-tuple-element.31), channel_id=1, source_target_pairs={{0,31},{1,30},{2,29},{3,28},{4,3},{5,2},{6,1},{7,0},{8,7},{9,6},{1... | collective-permute-start | bytes 393224 | tf_op jit(solution)/shard_map/ppermute | solution.py:149
  43.9 0.9 %collective-permute-start.8 = (f32[16,128]{1,0:T(8,128)S(1)}, f32[16,128]{1,0:T(8,128)S(1)}, u32[]{:S(2)}, u32[]{:S(2)}) collective-permute-start(f32[16,128]{1,0:T(8,128)S(1)} %get-tuple-element.19.place_ref), channel_id=1, source_target_pairs={{0,28},{1,29},{2,30},{3,31},{4,0},{5,1},{6,2},{7,3},{8,4},{9,5},{1... | collective-permute-start | bytes 24584 | tf_op jit(solution)/shard_map/ppermute | solution.py:149
  44.7 0.7 %copy.17 = f32[1,256,16]{1,2,0:T(8,128)} copy(f32[1,256,16]{2,1,0:T(8,128)S(1)} %get-tuple-element.36) | data formatting | bytes 32768
  45.4 1.1 %shard_map.126 = f32[1,1,16,1024]{3,2,1,0:T(8,128)} custom-call(bf16[64,16]{1,0:T(8,128)(2,1)S(1)} %get-tuple-element.33.refs_0_, bf16[64,16]{1,0:T(8,128)(2,1)S(1)} %collective-permute-done.16.refs_1_, bf16[64,16]{1,0:T(8,128)(2,1)S(1)} %collective-permute-done.17.refs_2_, bf16[64,16]{1,0:T(8,128)(2,1)S(1)} %collective-permute-done.18.refs_3_, ...), custom_call_target="tpu_custom_call" | custom-call | flops 2097152 | bytes 598016 | tf_op jit(solution)/shard_map/pallas_call | solution.py:26
  46.5 1.5 %shard_map.122 = bf16[1,128,4096]{2,1,0:T(8,128)(2,1)} custom-call(f32[16,128]{1,0:T(8,128)S(1)} %collective-permute-done.place_ref, bf16[16,4096]{1,0:T(8,128)(2,1)S(1)} %collective-permute-done.4.refs_0_, bf16[16,4096]{1,0:T(8,128)(2,1)S(1)} %collective-permute-done.5.refs_1_, bf16[16,4096]{1,0:T(8,128)(2,1)S(1)} %collective-permute-done.6.refs_2_, ...), custom_call_target="tpu_custom_call" | custom-call | flops 16777216 | bytes 1581056 | tf_op jit(solution)/shard_map/pallas_call | solution.py:26
  48.2 3.5 %collective-permute-done.15.refs_3_ = bf16[16,4096]{1,0:T(8,128)(2,1)S(1)} collective-permute-done((bf16[16,4096]{1,0:T(8,128)(2,1)S(1)}, bf16[16,4096]{1,0:T(8,128)(2,1)S(1)}, u32[]{:S(2)}, u32[]{:S(2)}) %collective-permute-start.15) | collective-permute-done | bytes 131104 | tf_op jit(solution)/shard_map/ppermute | solution.py:149
  51.6 1.4 %shard_map.125 = bf16[1,128,4096]{2,1,0:T(8,128)(2,1)} custom-call(f32[16,128]{1,0:T(8,128)S(1)} %collective-permute-done.8.place_ref, bf16[16,4096]{1,0:T(8,128)(2,1)S(1)} %collective-permute-done.12.refs_0_, bf16[16,4096]{1,0:T(8,128)(2,1)S(1)} %collective-permute-done.13.refs_1_, bf16[16,4096]{1,0:T(8,128)(2,1)S(1)} %collective-permute-done.14.refs_2_, ...), custom_call_target="tpu_custom_call" | custom-call | flops 16777216 | bytes 1581056 | tf_op jit(solution)/shard_map/pallas_call | solution.py:26
  (29 shorter events, 0.7 us)
Async XLA Ops:
  0.6 15.0 %copy-start = (bf16[1,256,4096]{2,1,0:T(8,128)(2,1)S(1)}, bf16[1,256,4096]{2,1,0:T(8,128)(2,1)}, u32[]{:S(2)}) copy-start(bf16[1,256,4096]{2,1,0:T(8,128)(2,1)} %refs_7_.2) | copy-start | bytes 6291460
  2.4 1.2 %copy-start.3 = (bf16[1,128,4096]{2,1,0:T(8,128)(2,1)S(1)}, bf16[1,128,4096]{2,1,0:T(8,128)(2,1)}, u32[]{:S(2)}) copy-start(bf16[1,128,4096]{2,1,0:T(8,128)(2,1)} %x_ref.1) | copy-start | bytes 3145732
  3.9 9.5 %collective-permute-start.3 = (bf16[16,4096]{1,0:T(8,128)(2,1)S(1)}, bf16[16,4096]{1,0:T(8,128)(2,1)S(1)}, u32[]{:S(2)}, u32[]{:S(2)}) collective-permute-start(bf16[16,4096]{1,0:T(8,128)(2,1)S(1)} %get-tuple-element.20.refs_0_), channel_id=1, source_target_pairs={{0,3},{1,2},{2,1},{3,0},{4,7},{5,6},{6,5},{7,4},{8,11},{9,10},{10,... | collective-permute-start | bytes 393224 | tf_op jit(solution)/shard_map/ppermute | solution.py:149
  7.9 7.8 %collective-permute-start.2 = (bf16[16,4096]{1,0:T(8,128)(2,1)S(1)}, bf16[16,4096]{1,0:T(8,128)(2,1)S(1)}, u32[]{:S(2)}, u32[]{:S(2)}) collective-permute-start(bf16[16,4096]{1,0:T(8,128)(2,1)S(1)} %get-tuple-element.20.refs_0_), channel_id=1, source_target_pairs={{0,2},{1,3},{2,0},{3,1},{4,6},{5,7},{6,4},{7,5},{8,10},{9,11},{10,... | collective-permute-start | bytes 393224 | tf_op jit(solution)/shard_map/ppermute | solution.py:149
  8.4 7.3 %collective-permute-start.1 = (bf16[16,4096]{1,0:T(8,128)(2,1)S(1)}, bf16[16,4096]{1,0:T(8,128)(2,1)S(1)}, u32[]{:S(2)}, u32[]{:S(2)}) collective-permute-start(bf16[16,4096]{1,0:T(8,128)(2,1)S(1)} %get-tuple-element.20.refs_0_), channel_id=1, source_target_pairs={{0,1},{1,0},{2,3},{3,2},{4,5},{5,4},{6,7},{7,6},{8,9},{9,8},{10,11... | collective-permute-start | bytes 393224 | tf_op jit(solution)/shard_map/ppermute | solution.py:149
  8.5 1.2 %copy-start.4 = (bf16[1,128,4096]{2,1,0:T(8,128)(2,1)S(1)}, bf16[1,128,4096]{2,1,0:T(8,128)(2,1)}, u32[]{:S(2)}) copy-start(bf16[1,128,4096]{2,1,0:T(8,128)(2,1)} %cotangent_ref.1) | copy-start | bytes 3145732
  10.0 14.8 %collective-permute-start.11 = (bf16[16,4096]{1,0:T(8,128)(2,1)S(1)}, bf16[16,4096]{1,0:T(8,128)(2,1)S(1)}, u32[]{:S(2)}, u32[]{:S(2)}) collective-permute-start(bf16[16,4096]{1,0:T(8,128)(2,1)S(1)} %shard_map.123.refs_0_.refs_4_), channel_id=1, source_target_pairs={{0,3},{1,2},{2,1},{3,0},{4,7},{5,6},{6,5},{7,4},{8,11},{9,10},{10,... | collective-permute-start | bytes 393224 | tf_op jit(solution)/shard_map/ppermute | solution.py:149
  12.9 15.1 %collective-permute-start.10 = (bf16[16,4096]{1,0:T(8,128)(2,1)S(1)}, bf16[16,4096]{1,0:T(8,128)(2,1)S(1)}, u32[]{:S(2)}, u32[]{:S(2)}) collective-permute-start(bf16[16,4096]{1,0:T(8,128)(2,1)S(1)} %shard_map.123.refs_0_.refs_4_), channel_id=1, source_target_pairs={{0,2},{1,3},{2,0},{3,1},{4,6},{5,7},{6,4},{7,5},{8,10},{9,11},{10,... | collective-permute-start | bytes 393224 | tf_op jit(solution)/shard_map/ppermute | solution.py:149
  13.4 14.7 %collective-permute-start.9 = (bf16[16,4096]{1,0:T(8,128)(2,1)S(1)}, bf16[16,4096]{1,0:T(8,128)(2,1)S(1)}, u32[]{:S(2)}, u32[]{:S(2)}) collective-permute-start(bf16[16,4096]{1,0:T(8,128)(2,1)S(1)} %shard_map.123.refs_0_.refs_4_), channel_id=1, source_target_pairs={{0,1},{1,0},{2,3},{3,2},{4,5},{5,4},{6,7},{7,6},{8,9},{9,8},{10,11... | collective-permute-start | bytes 393224 | tf_op jit(solution)/shard_map/ppermute | solution.py:149
  15.7 8.2 %collective-permute-start = (f32[16,128]{1,0:T(8,128)S(1)}, f32[16,128]{1,0:T(8,128)S(1)}, u32[]{:S(2)}, u32[]{:S(2)}) collective-permute-start(f32[16,128]{1,0:T(8,128)S(1)} %get-tuple-element.19.place_ref), channel_id=1, source_target_pairs={{0,4},{1,5},{2,6},{3,7},{4,8},{5,9},{6,10},{7,11},{8,12},{9,13},{1... | collective-permute-start | bytes 24584 | tf_op jit(solution)/shard_map/ppermute | solution.py:149
  15.7 1.6 %copy-start.1 = (bf16[1,256,4096]{2,1,0:T(8,128)(2,1)S(1)}, bf16[1,256,4096]{2,1,0:T(8,128)(2,1)}, u32[]{:S(2)}) copy-start(bf16[1,256,4096]{2,1,0:T(8,128)(2,1)} %refs_8_.1) | copy-start | bytes 6291460
  17.3 1.6 %copy-start.2 = (bf16[1,256,4096]{2,1,0:T(8,128)(2,1)S(1)}, bf16[1,256,4096]{2,1,0:T(8,128)(2,1)}, u32[]{:S(2)}) copy-start(bf16[1,256,4096]{2,1,0:T(8,128)(2,1)} %refs_9_.1) | copy-start | bytes 6291460
  18.9 0.9 %copy-start.5 = (bf16[1,1,16,4096]{3,2,1,0:T(8,128)(2,1)S(1)}, bf16[1,1,16,4096]{3,2,1,0:T(8,128)(2,1)}, u32[]{:S(2)}) copy-start(bf16[1,1,16,4096]{3,2,1,0:T(8,128)(2,1)} %param.16) | copy-start | bytes 393220
  21.9 19.2 %collective-permute-start.4 = (bf16[16,4096]{1,0:T(8,128)(2,1)S(1)}, bf16[16,4096]{1,0:T(8,128)(2,1)S(1)}, u32[]{:S(2)}, u32[]{:S(2)}) collective-permute-start(bf16[16,4096]{1,0:T(8,128)(2,1)S(1)} %get-tuple-element.21), channel_id=1, source_target_pairs={{0,4},{1,5},{2,6},{3,7},{4,8},{5,9},{6,10},{7,11},{8,12},{9,13},{1... | collective-permute-start | bytes 393224 | tf_op jit(solution)/shard_map/ppermute | solution.py:149
  23.8 18.7 %collective-permute-start.5 = (bf16[16,4096]{1,0:T(8,128)(2,1)S(1)}, bf16[16,4096]{1,0:T(8,128)(2,1)S(1)}, u32[]{:S(2)}, u32[]{:S(2)}) collective-permute-start(bf16[16,4096]{1,0:T(8,128)(2,1)S(1)} %get-tuple-element.22), channel_id=1, source_target_pairs={{0,5},{1,4},{2,7},{3,6},{4,9},{5,8},{6,11},{7,10},{8,13},{9,12},{1... | collective-permute-start | bytes 393224 | tf_op jit(solution)/shard_map/ppermute | solution.py:149
  24.7 17.8 %collective-permute-start.6 = (bf16[16,4096]{1,0:T(8,128)(2,1)S(1)}, bf16[16,4096]{1,0:T(8,128)(2,1)S(1)}, u32[]{:S(2)}, u32[]{:S(2)}) collective-permute-start(bf16[16,4096]{1,0:T(8,128)(2,1)S(1)} %get-tuple-element.23), channel_id=1, source_target_pairs={{0,6},{1,7},{2,4},{3,5},{4,10},{5,11},{6,8},{7,9},{8,14},{9,15},{1... | collective-permute-start | bytes 393224 | tf_op jit(solution)/shard_map/ppermute | solution.py:149
  28.0 4.8 %collective-permute-start.18 = (bf16[64,16]{1,0:T(8,128)(2,1)S(1)}, bf16[64,16]{1,0:T(8,128)(2,1)S(1)}, u32[]{:S(2)}, u32[]{:S(2)}) collective-permute-start(bf16[64,16]{1,0:T(8,128)(2,1)S(1)} %get-tuple-element.33.refs_0_), channel_id=1, source_target_pairs={{0,3},{1,2},{2,1},{3,0},{4,7},{5,6},{6,5},{7,4},{8,11},{9,10},{10,... | collective-permute-start | bytes 6152 | tf_op jit(solution)/shard_map/ppermute | solution.py:149
  28.1 5.8 %collective-permute-start.17 = (bf16[64,16]{1,0:T(8,128)(2,1)S(1)}, bf16[64,16]{1,0:T(8,128)(2,1)S(1)}, u32[]{:S(2)}, u32[]{:S(2)}) collective-permute-start(bf16[64,16]{1,0:T(8,128)(2,1)S(1)} %get-tuple-element.33.refs_0_), channel_id=1, source_target_pairs={{0,2},{1,3},{2,0},{3,1},{4,6},{5,7},{6,4},{7,5},{8,10},{9,11},{10,... | collective-permute-start | bytes 6152 | tf_op jit(solution)/shard_map/ppermute | solution.py:149
  32.8 4.6 %collective-permute-start.16 = (bf16[64,16]{1,0:T(8,128)(2,1)S(1)}, bf16[64,16]{1,0:T(8,128)(2,1)S(1)}, u32[]{:S(2)}, u32[]{:S(2)}) collective-permute-start(bf16[64,16]{1,0:T(8,128)(2,1)S(1)} %get-tuple-element.33.refs_0_), channel_id=1, source_target_pairs={{0,1},{1,0},{2,3},{3,2},{4,5},{5,4},{6,7},{7,6},{8,9},{9,8},{10,11... | collective-permute-start | bytes 6152 | tf_op jit(solution)/shard_map/ppermute | solution.py:149
  33.9 9.9 %collective-permute-start.7 = (bf16[16,4096]{1,0:T(8,128)(2,1)S(1)}, bf16[16,4096]{1,0:T(8,128)(2,1)S(1)}, u32[]{:S(2)}, u32[]{:S(2)}) collective-permute-start(bf16[16,4096]{1,0:T(8,128)(2,1)S(1)} %get-tuple-element.24), channel_id=1, source_target_pairs={{0,7},{1,6},{2,5},{3,4},{4,11},{5,10},{6,9},{7,8},{8,15},{9,14},{1... | collective-permute-start | bytes 393224 | tf_op jit(solution)/shard_map/ppermute | solution.py:149
  37.4 10.7 %collective-permute-start.12 = (bf16[16,4096]{1,0:T(8,128)(2,1)}, bf16[16,4096]{1,0:T(8,128)(2,1)S(1)}, u32[]{:S(2)}, u32[]{:S(2)}) collective-permute-start(bf16[16,4096]{1,0:T(8,128)(2,1)} %get-tuple-element.28), channel_id=1, source_target_pairs={{0,28},{1,29},{2,30},{3,31},{4,0},{5,1},{6,2},{7,3},{8,4},{9,5},{1... | collective-permute-start | bytes 393224 | tf_op jit(solution)/shard_map/ppermute | solution.py:149
  41.1 7.0 %collective-permute-start.13 = (bf16[16,4096]{1,0:T(8,128)(2,1)}, bf16[16,4096]{1,0:T(8,128)(2,1)S(1)}, u32[]{:S(2)}, u32[]{:S(2)}) collective-permute-start(bf16[16,4096]{1,0:T(8,128)(2,1)} %get-tuple-element.29), channel_id=1, source_target_pairs={{0,29},{1,28},{2,31},{3,30},{4,1},{5,0},{6,3},{7,2},{8,5},{9,4},{1... | collective-permute-start | bytes 393224 | tf_op jit(solution)/shard_map/ppermute | solution.py:149
  42.5 5.6 %collective-permute-start.14 = (bf16[16,4096]{1,0:T(8,128)(2,1)}, bf16[16,4096]{1,0:T(8,128)(2,1)S(1)}, u32[]{:S(2)}, u32[]{:S(2)}) collective-permute-start(bf16[16,4096]{1,0:T(8,128)(2,1)} %get-tuple-element.30), channel_id=1, source_target_pairs={{0,30},{1,31},{2,28},{3,29},{4,2},{5,3},{6,0},{7,1},{8,6},{9,7},{1... | collective-permute-start | bytes 393224 | tf_op jit(solution)/shard_map/ppermute | solution.py:149
  42.5 9.1 %collective-permute-start.15 = (bf16[16,4096]{1,0:T(8,128)(2,1)S(1)}, bf16[16,4096]{1,0:T(8,128)(2,1)S(1)}, u32[]{:S(2)}, u32[]{:S(2)}) collective-permute-start(bf16[16,4096]{1,0:T(8,128)(2,1)S(1)} %get-tuple-element.31), channel_id=1, source_target_pairs={{0,31},{1,30},{2,29},{3,28},{4,3},{5,2},{6,1},{7,0},{8,7},{9,6},{1... | collective-permute-start | bytes 393224 | tf_op jit(solution)/shard_map/ppermute | solution.py:149
  43.9 4.3 %collective-permute-start.8 = (f32[16,128]{1,0:T(8,128)S(1)}, f32[16,128]{1,0:T(8,128)S(1)}, u32[]{:S(2)}, u32[]{:S(2)}) collective-permute-start(f32[16,128]{1,0:T(8,128)S(1)} %get-tuple-element.19.place_ref), channel_id=1, source_target_pairs={{0,28},{1,29},{2,30},{3,31},{4,0},{5,1},{6,2},{7,3},{8,4},{9,5},{1... | collective-permute-start | bytes 24584 | tf_op jit(solution)/shard_map/ppermute | solution.py:149

commit v2 on v1

v2 whole, which is shorter than its diff:
```python
import functools

import jax
import jax.numpy as jnp
from jax import lax
from jax.experimental import pallas as pl
from jax.experimental.pallas import tpu as pltpu
from jax.sharding import PartitionSpec as P

SPLIT = 4
MOST = 16
LOWRANK_SCALE = 2.0
LEVEL_STEP = 1.0 / 4096.0
CHUNKS = 4
MIB = 1 << 20
LAST = (((1,), (1,)), ((), ()))
FIRST = (((0,), (0,)), ((), ()))
NEAR = pl.BlockSpec(memory_space=pltpu.VMEM)
FAR = pl.BlockSpec(memory_space=pltpu.HBM)


def f32dot(a, b, dims=(((1,), (0,)), ((), ()))):
    return lax.dot_general(a, b, dims, preferred_element_type=jnp.float32)


def sds(*shape, dtype=jnp.bfloat16):
    return jax.ShapeDtypeStruct(shape, dtype)


def call(body, outs, args, far_args=(), far_outs=False, scratch=(), flops=0, grant=24 * MIB):
    moved = sum(a.size * a.dtype.itemsize for a in (*args, *far_args, *outs))
    return pl.pallas_call(
        body,
        out_shape=outs,
        in_specs=[NEAR] * len(args) + [FAR] * len(far_args),
        out_specs=[FAR if far_outs else NEAR] * len(outs),
        scratch_shapes=scratch,
        compiler_params=pltpu.CompilerParams(vmem_limit_bytes=grant),
        cost_estimate=pl.CostEstimate(flops=flops, bytes_accessed=moved, transcendentals=0),
    )(*args, *(pltpu.with_memory_space_constraint(a, pltpu.HBM) for a in far_args))


def gather(
    flight,
    choice_hbm,
    steps_hbm,
    x_hbm,
    cot_hbm,
    x_rows_ref,
    g_rows_ref,
    place_ref,
    choice_ref,
    steps_ref,
    x_ref,
    cot_ref,
    small_sems,
    x_sems,
    cot_sems,
):
    tokens, width = x_ref.shape
    span = width // CHUNKS
    small = [
        pltpu.make_async_copy(choice_hbm, choice_ref, small_sems.at[0]),
        pltpu.make_async_copy(steps_hbm, steps_ref, small_sems.at[1]),
    ]
    for copy in small:
        copy.start()

    def fetch(hbm, ref, sems):
        copies = [
            pltpu.make_async_copy(
                hbm.at[0, :, pl.ds(c * span, span)], ref.at[:, pl.ds(c * span, span)], sems.at[c]
            )
            for c in range(CHUNKS)
        ]
        for copy in copies:
            copy.start()
        return copies

    x_copies = fetch(x_hbm, x_ref, x_sems)
    cot_copies = fetch(cot_hbm, cot_ref, cot_sems)
    for copy in small:
        copy.wait()
    choice = choice_ref[...]
    steps = steps_ref[...].astype(jnp.float32)
    before = lax.broadcasted_iota(jnp.int32, (tokens, tokens), 0) < lax.broadcasted_iota(
        jnp.int32, (tokens, tokens), 1
    )
    before = jnp.where(before, 1.0, 0.0).astype(jnp.bfloat16)
    slot = lax.broadcasted_iota(jnp.int32, (MOST, tokens), 0).astype(jnp.float32)
    for f in range(flight):
        level = jnp.sum(jnp.where(choice == f, steps, 0.0), axis=0, keepdims=True)
        routed = jnp.broadcast_to(jnp.where(level > 0, 1.0, 0.0), (MOST, tokens))
        index = f32dot(routed.astype(jnp.bfloat16), before)
        place_ref[f * MOST:(f + 1) * MOST, :] = jnp.where(slot == index, level * LEVEL_STEP, 0.0)
    place = place_ref[...]
    pick = jnp.where(place > 0, 1.0, 0.0).astype(jnp.bfloat16)
    gate = jnp.sum(place, axis=1, keepdims=True)
    for c in range(CHUNKS):
        x_copies[c].wait()
        part = slice(c * span, (c + 1) * span)
        x_rows_ref[:, part] = f32dot(pick, x_ref[:, part]).astype(jnp.bfloat16)
    for c in range(CHUNKS):
        cot_copies[c].wait()
        part = slice(c * span, (c + 1) * span)
        g_rows_ref[:, part] = (f32dot(pick, cot_ref[:, part]) * gate).astype(jnp.bfloat16)


def load(
    _,
    gate_hbm,
    up_hbm,
    down_hbm,
    a_hbm,
    b_hbm,
    gate_ref,
    up_ref,
    down_ref,
    a_ref,
    b_ref,
    raw_ref,
    weight_sems,
    small_sems,
):
    units, width = raw_ref.shape
    band = units // CHUNKS
    small = [
        pltpu.make_async_copy(a_hbm, a_ref, small_sems.at[0]),
        pltpu.make_async_copy(b_hbm, b_ref, small_sems.at[1]),
    ]
    for copy in small:
        copy.start()
    copies = []
    for i, (hbm, ref) in enumerate(((down_hbm, raw_ref), (gate_hbm, gate_ref), (up_hbm, up_ref))):
        for c in range(CHUNKS):
            bands = pl.ds(c * band, band)
            copy = pltpu.make_async_copy(
                hbm.at[0, bands, :], ref.at[bands, :], weight_sems.at[i * CHUNKS + c]
            )
            copy.start()
            copies.append(copy)
    for copy in small + copies[:CHUNKS]:
        copy.wait()
    span = 512
    for c in range(width // span):
        part = slice(c * span, (c + 1) * span)
        adapter = LOWRANK_SCALE * f32dot(a_ref[...], b_ref[:, part], FIRST)
        down_ref[:, part] = (raw_ref[:, part].astype(jnp.float32) + adapter).astype(jnp.bfloat16)
    for copy in copies[CHUNKS:]:
        copy.wait()


def forward(*refs):
    x_refs, (gate_ref, up_ref, down_ref, a_ref) = refs[:SPLIT], refs[SPLIT:SPLIT + 4]
    out_refs = refs[SPLIT + 4:2 * SPLIT + 4]
    pre_gate_ref, pre_up_ref, hidden_ref, latent_ref = refs[2 * SPLIT + 4:]
    rows = jnp.concatenate([r[...] for r in x_refs], axis=0)
    height = x_refs[0].shape[0]
    pre_gate = f32dot(rows, gate_ref[...], LAST)
    pre_up = f32dot(rows, up_ref[...], LAST)
    pre_gate_ref[...] = pre_gate
    pre_up_ref[...] = pre_up
    hidden = (pre_gate * jax.nn.sigmoid(pre_gate) * pre_up).astype(jnp.bfloat16)
    hidden_ref[...] = hidden
    latent_ref[...] = f32dot(hidden, a_ref[...], LAST).astype(jnp.bfloat16)
    result = f32dot(hidden, down_ref[...]).astype(jnp.bfloat16)
    for k, ref in enumerate(out_refs):
        ref[...] = result[k * height:(k + 1) * height]


def backward(*refs):
    g_refs = refs[:SPLIT]
    pre_gate_ref, pre_up_ref, gate_ref, up_ref, down_ref = refs[SPLIT:SPLIT + 5]
    out_refs = refs[SPLIT + 5:]
    rows = jnp.concatenate([r[...] for r in g_refs], axis=0)
    height = g_refs[0].shape[0]
    grad_hidden = f32dot(rows, down_ref[...], LAST)
    pre_gate = pre_gate_ref[...]
    g = jax.nn.sigmoid(pre_gate)
    grad_gate = grad_hidden * pre_up_ref[...] * g * (1.0 + pre_gate * (1.0 - g))
    grad_up = grad_hidden * pre_gate * g
    result = f32dot(grad_gate.astype(jnp.bfloat16), gate_ref[...])
    result = result + f32dot(grad_up.astype(jnp.bfloat16), up_ref[...])
    result = result.astype(jnp.bfloat16)
    for k, ref in enumerate(out_refs):
        ref[...] = result[k * height:(k + 1) * height]


def down_map_grad(*refs):
    g_refs, (hidden_ref, b_ref, out_ref) = refs[:SPLIT], refs[SPLIT:]
    rows = jnp.concatenate([r[...] for r in g_refs], axis=0)
    lowrank = (LOWRANK_SCALE * f32dot(rows, b_ref[...], LAST)).astype(jnp.bfloat16)
    out_ref[...] = f32dot(lowrank, hidden_ref[...], FIRST)


def up_map_grad(*refs):
    lat_refs, g_refs, out_ref = refs[:SPLIT], refs[SPLIT:2 * SPLIT], refs[2 * SPLIT]
    width = out_ref.shape[-1]
    column = pl.multiple_of(lax.axis_index("expert") * width, 128)
    height = g_refs[0].shape[0]
    total = jnp.zeros(out_ref.shape[2:], jnp.float32)
    for i in range(SPLIT):
        block = sum(
            lat_refs[k][(i ^ k) * height:((i ^ k) + 1) * height, :].astype(jnp.float32)
            for k in range(SPLIT)
        )
        high = block.astype(jnp.bfloat16)
        low = (block - high.astype(jnp.float32)).astype(jnp.bfloat16)
        rows = g_refs[i][:, pl.ds(column, width)]
        total = total + f32dot(high, rows, FIRST) + f32dot(low, rows, FIRST)
    out_ref[0, 0] = LOWRANK_SCALE * total


def expand(gated, place_ref, *refs):
    *part_refs, out_hbm, out_ref, sems = refs
    place = place_ref[...]
    pick = jnp.where(place > 0, 1.0, 0.0).astype(jnp.bfloat16)
    gate = jnp.sum(place, axis=1, keepdims=True)
    span = out_ref.shape[1] // CHUNKS
    copies = []
    for c in range(CHUNKS):
        part = slice(c * span, (c + 1) * span)
        rows = sum(r[:, part].astype(jnp.float32) for r in part_refs)
        if gated:
            rows = rows * gate
        high = rows.astype(jnp.bfloat16)
        spread = f32dot(pick, high, FIRST)
        if place.shape[0] > MOST:
            low = (rows - high.astype(jnp.float32)).astype(jnp.bfloat16)
            spread = spread + f32dot(pick, low, FIRST)
        out_ref[:, part] = spread.astype(jnp.bfloat16)
        columns = pl.ds(c * span, span)
        copy = pltpu.make_async_copy(
            out_ref.at[:, columns], out_hbm.at[0, :, columns], sems.at[c]
        )
        copy.start()
        copies.append(copy)
    for copy in copies:
        copy.wait()


def shifted(block, step, flip):
    sections, experts = lax.axis_size("section"), lax.axis_size("expert")
    route = [
        (s * experts + e, (s + step) % sections * experts + (e ^ flip))
        for s in range(sections)
        for e in range(experts)
    ]
    return lax.ppermute(block, ("section", "expert"), route)


def between_groups(rows, flight):
    if flight == 1:
        return rows
    groups = [[g * SPLIT + q for g in range(flight)] for q in range(SPLIT)]
    return lax.all_to_all(
        rows, "expert", split_axis=0, concat_axis=0, axis_index_groups=groups, tiled=True
    )


def on_device(
    section_layer_input,
    token_expert_choice,
    route_gate_steps,
    gate_weight,
    up_weight,
    down_weight,
    adapter_down_maps,
    adapter_up_maps,
    cotangent,
):
    tokens, width = section_layer_input.shape[1:]
    top = token_expert_choice.shape[2]
    units, rank = adapter_down_maps.shape[1:]
    flight = lax.axis_size("expert") // SPLIT
    slots = flight * MOST
    rows = SPLIT * slots
    flips = range(SPLIT)
    dma = pltpu.SemaphoreType.DMA
    if flight == 1:
        up_map = adapter_up_maps[0, 0]
    else:
        group = lax.axis_index("expert") // SPLIT
        up_map = lax.dynamic_index_in_dim(adapter_up_maps[0], group, 0, keepdims=False)
    down_map = jnp.swapaxes(adapter_down_maps[0], 0, 1)

    x_rows, g_rows, place = call(
        functools.partial(gather, flight),
        [sds(slots, width), sds(slots, width), sds(slots, tokens, dtype=jnp.float32)],
        (),
        (
            jnp.swapaxes(token_expert_choice[0], 0, 1),
            jnp.swapaxes(route_gate_steps[0], 0, 1),
            section_layer_input,
            cotangent,
        ),
        scratch=[
            pltpu.VMEM((top, tokens), jnp.int32),
            pltpu.VMEM((top, tokens), jnp.int32),
            pltpu.VMEM((tokens, width), jnp.bfloat16),
            pltpu.VMEM((tokens, width), jnp.bfloat16),
            dma((2,)),
            dma((CHUNKS,)),
            dma((CHUNKS,)),
        ],
        flops=4 * slots * tokens * width,
    )
    x_rows = between_groups(x_rows, flight)
    g_rows = between_groups(g_rows, flight)
    x_blocks = [x_rows] + [shifted(x_rows, 0, k) for k in flips[1:]]
    g_blocks = [g_rows] + [shifted(g_rows, 0, k) for k in flips[1:]]
    place_before = shifted(place, 1, 0)
    place_after = shifted(place, -1, 0)

    gate_near, up_near, down_near, a_near, b_near = call(
        load,
        [sds(units, width)] * 3 + [sds(rank, units), sds(rank, width)],
        (place,),
        (gate_weight, up_weight, down_weight, down_map, up_map),
        scratch=[
            pltpu.VMEM((units, width), jnp.bfloat16),
            dma((3 * CHUNKS,)),
            dma((2,)),
        ],
        flops=2 * units * rank * width,
    )

    x_blocks, place_before, place_after = lax.optimization_barrier(
        (x_blocks, place_before, place_after)
    )
    block_outs = [sds(slots, width)] * SPLIT
    *out_blocks, pre_gate, pre_up, hidden, latent = call(
        forward,
        block_outs
        + [sds(rows, units, dtype=jnp.float32)] * 2
        + [sds(rows, units), sds(rows, rank)],
        (*x_blocks, gate_near, up_near, down_near, a_near),
        flops=6 * rows * units * width,
    )
    latents = [latent] + [shifted(latent, 0, k) for k in flips[1:]]
    out_parts = [shifted(out_blocks[k], 1, k) for k in flips]
    grad_blocks = call(
        backward,
        block_outs,
        (*g_blocks, pre_gate, pre_up, gate_near, up_near, down_near),
        flops=6 * rows * units * width,
    )
    grad_parts = [shifted(grad_blocks[k], -1, k) for k in flips]

    hidden, _ = lax.optimization_barrier((hidden, grad_blocks[0]))
    (a_grad,) = call(
        down_map_grad,
        [sds(rank, units, dtype=jnp.float32)],
        (*g_blocks, hidden, b_near),
        flops=2 * rows * rank * width,
    )
    if flight == 1:
        (b_grad,) = call(
            up_map_grad,
            [sds(1, 1, rank, width // SPLIT, dtype=jnp.float32)],
            (*latents, *g_blocks),
            flops=4 * rows * rank * width // SPLIT,
        )
    else:
        part = LOWRANK_SCALE * f32dot(latent, jnp.concatenate(g_blocks, axis=0), FIRST)
        mine = jnp.arange(flight, dtype=jnp.int32) == group
        spread = jnp.where(mine[:, None, None], part[None], 0.0)
        b_grad = lax.psum_scatter(spread, "expert", scatter_dimension=2, tiled=True)[None]

    def finish(parts, place, gated):
        if flight > 1:
            total = sum(p.astype(jnp.float32) for p in parts).astype(jnp.bfloat16)
            parts = [between_groups(total, flight)]
        return call(
            functools.partial(expand, gated),
            [sds(1, tokens, width)],
            (place, *parts),
            far_outs=True,
            scratch=[pltpu.VMEM((tokens, width), jnp.bfloat16), dma((CHUNKS,))],
            flops=2 * slots * tokens * width,
        )[0]

    next_input = finish(out_parts, place_before, True)
    prev_grad = finish(grad_parts, place_after, False)
    return next_input, prev_grad, jnp.swapaxes(a_grad, 0, 1)[None], b_grad


def solution(mesh):
    rows = P("section", "expert", None)
    return jax.shard_map(
        on_device,
        mesh=mesh,
        in_specs=(rows,) * 7 + (P("section", None, None, None), rows),
        out_specs=(rows, rows, rows, P("section", None, None, "expert")),
        check_vma=False,
    )
```

time: 53.4 us -> 52.5 us (0.983)
  local copies, waits for them, and re-layouts: 9.74 us -> 0 us
  waiting for transfers between devices: 7.82 us -> 13.5 us
  Pallas kernels: 10.2 us -> 15.1 us
  starting transfers between devices: 24.6 us -> 23.1 us
    unnamed x16 -> x0, local copies, waits for them, and re-layouts: 9.74 us -> none
    ppermute x19, waiting for transfers between devices: 7.82 us -> 13.5 us  [shifted(): return lax.ppermute(block, ('section', 'expert'), route)]
    pallas_call x7 -> x8, Pallas kernels: 10.2 us -> 15.1 us  [call(): pl.pallas_call(body, out_shape=outs, in_specs=[NEAR] * len(args) + [FAR]...]
    ppermute x19, starting transfers between devices: 24.6 us -> 23.1 us  [shifted(): return lax.ppermute(block, ('section', 'expert'), route)]
  transfers between devices with their start and end apart: 19 -> 19, of which waited for: 4 -> 8; matrix products, arithmetic and copies ran while one was open for 3% -> 0% of each run, Pallas kernels for 16% -> 16%
where the time goes in v2:
time: 52.5 us; the launch traced here: 52.3 us
  starting transfers between devices  23.1 us (44%)
  Pallas kernels  15.1 us (29%)
  waiting for transfers between devices  13.5 us (26%)
  between operations  0.73 us (1%)
    ppermute x19, starting transfers between devices, shifted(): return lax.ppermute(block, ('section', 'expert'), route)  23.1 us
    pallas_call x8, Pallas kernels, call(): pl.pallas_call(body, out_shape=outs, in_specs=[NEAR] * len(args) + [FAR]...  15.1 us
    ppermute x19, waiting for transfers between devices, shifted(): return lax.ppermute(block, ('section', 'expert'), route)  13.5 us
  transfers between devices with their start and end apart: 19, of which 8 were waited for; matrix products, arithmetic and copies ran while one was open for 0% of the time, Pallas kernels for 16%

profile of v2, /device:TPU:0, one launch (start us, length us, event | category | flops | bytes accessed | tf_op | source)
XLA Modules:
  0.0 52.3 jit_solution(11300448817463624997)
XLA Ops:
  0.6 2.7 %shard_map.120 = (bf16[16,4096]{1,0:T(8,128)(2,1)S(1)}, bf16[16,4096]{1,0:T(8,128)(2,1)S(1)}, f32[16,128]{1,0:T(8,128)S(1)}) custom-call(s32[8,128]{1,0:T(8,128)} %bitcast.16, s32[8,128]{1,0:T(8,128)} %bitcast.17, bf16[1,128,4096]{2,1,0:T(8,128)(2,1)} %x_hbm.1, bf16[1,128,4096]{2,1,0:T(8,128)(2,1)} %cot_hbm.1), custom_call_target="tpu_custom_call" | custom-call | flops 33554432 | bytes 2375680 | tf_op jit(solution)/shard_map/pallas_call | solution.py:32
  3.3 4.0 %collective-permute-start.2 = (bf16[16,4096]{1,0:T(8,128)(2,1)S(1)}, bf16[16,4096]{1,0:T(8,128)(2,1)S(1)}, u32[]{:S(2)}, u32[]{:S(2)}) collective-permute-start(bf16[16,4096]{1,0:T(8,128)(2,1)S(1)} %get-tuple-element.34.refs_0_), channel_id=1, source_target_pairs={{0,3},{1,2},{2,1},{3,0},{4,7},{5,6},{6,5},{7,4},{8,11},{9,10},{10,... | collective-permute-start | bytes 393224 | tf_op jit(solution)/shard_map/ppermute | solution.py:249
  7.3 0.5 collective-permute-start.1
  7.8 0.1 collective-permute-start
  8.0 2.6 %collective-permute-start.4 = (f32[16,128]{1,0:T(8,128)S(1)}, f32[16,128]{1,0:T(8,128)S(1)}, u32[]{:S(2)}, u32[]{:S(2)}) collective-permute-start(f32[16,128]{1,0:T(8,128)S(1)} %get-tuple-element.32._), channel_id=1, source_target_pairs={{0,28},{1,29},{2,30},{3,31},{4,0},{5,1},{6,2},{7,3},{8,4},{9,5},{1... | collective-permute-start | bytes 24584 | tf_op jit(solution)/shard_map/ppermute | solution.py:249
  10.6 1.4 %collective-permute-done.4.place_ref = f32[16,128]{1,0:T(8,128)S(1)} collective-permute-done((f32[16,128]{1,0:T(8,128)S(1)}, f32[16,128]{1,0:T(8,128)S(1)}, u32[]{:S(2)}, u32[]{:S(2)}) %collective-permute-start.4) | collective-permute-done | bytes 8224 | tf_op jit(solution)/shard_map/ppermute | solution.py:249
  11.9 2.4 %collective-permute-start.11 = (bf16[16,4096]{1,0:T(8,128)(2,1)S(1)}, bf16[16,4096]{1,0:T(8,128)(2,1)S(1)}, u32[]{:S(2)}, u32[]{:S(2)}) collective-permute-start(bf16[16,4096]{1,0:T(8,128)(2,1)S(1)} %get-tuple-element.47.refs_0_.refs_4_), channel_id=1, source_target_pairs={{0,3},{1,2},{2,1},{3,0},{4,7},{5,6},{6,5},{7,4},{8,11},{9,10},{10,... | collective-permute-start | bytes 393224 | tf_op jit(solution)/shard_map/ppermute | solution.py:249
  14.4 1.1 %collective-permute-done.3.place_ref = f32[16,128]{1,0:T(8,128)S(1)} collective-permute-done((f32[16,128]{1,0:T(8,128)S(1)}, f32[16,128]{1,0:T(8,128)S(1)}, u32[]{:S(2)}, u32[]{:S(2)}) %collective-permute-start.3) | collective-permute-done | bytes 8224 | tf_op jit(solution)/shard_map/ppermute | solution.py:249
  15.4 1.5 %collective-permute-start.10 = (bf16[16,4096]{1,0:T(8,128)(2,1)S(1)}, bf16[16,4096]{1,0:T(8,128)(2,1)S(1)}, u32[]{:S(2)}, u32[]{:S(2)}) collective-permute-start(bf16[16,4096]{1,0:T(8,128)(2,1)S(1)} %get-tuple-element.47.refs_0_.refs_4_), channel_id=1, source_target_pairs={{0,2},{1,3},{2,0},{3,1},{4,6},{5,7},{6,4},{7,5},{8,10},{9,11},{10,... | collective-permute-start | bytes 393224 | tf_op jit(solution)/shard_map/ppermute | solution.py:249
  17.0 1.5 %collective-permute-start.9 = (bf16[16,4096]{1,0:T(8,128)(2,1)S(1)}, bf16[16,4096]{1,0:T(8,128)(2,1)S(1)}, u32[]{:S(2)}, u32[]{:S(2)}) collective-permute-start(bf16[16,4096]{1,0:T(8,128)(2,1)S(1)} %get-tuple-element.47.refs_0_.refs_4_), channel_id=1, source_target_pairs={{0,1},{1,0},{2,3},{3,2},{4,5},{5,4},{6,7},{7,6},{8,9},{9,8},{10,11... | collective-permute-start | bytes 393224 | tf_op jit(solution)/shard_map/ppermute | solution.py:249
  18.4 3.5 %shard_map.121 = (bf16[256,4096]{1,0:T(8,128)(2,1)S(1)}, bf16[256,4096]{1,0:T(8,128)(2,1)S(1)}, bf16[256,4096]{1,0:T(8,128)(2,1)S(1)}, bf16[16,256]{1,0:T(8,128)(2,1)S(1)}, bf16[16,4096]{1,0:T(8,128)(2,1)S(1)}) custom-call(f32[16,128]{1,0:T(8,128)S(1)} %get-tuple-element.32._, bf16[1,256,4096]{2,1,0:T(8,128)(2,1)} %gate_hbm.1, bf16[1,256,4096]{2,1,0:T(8,128)(2,1)} %up_hbm.1, ...), custom_call_target="tpu_custom_call" | custom-call | flops 33554432 | bytes 12869632 | tf_op jit(solution)/shard_map/pallas_call | solution.py:32
  22.0 1.9 %shard_map.122 = (bf16[16,4096]{1,0:T(8,128)(2,1)S(1)}, bf16[16,4096]{1,0:T(8,128)(2,1)S(1)}, bf16[16,4096]{1,0:T(8,128)(2,1)S(1)}, bf16[16,4096]{1,0:T(8,128)(2...) custom-call(bf16[16,4096]{1,0:T(8,128)(2,1)S(1)} %get-tuple-element., ...), custom_call_target="tpu_custom_call" | custom-call | flops 402653184 | bytes 7514112 | tf_op jit(solution)/shard_map/pallas_call | solution.py:32
  23.9 2.5 %shard_map.124 = (bf16[16,4096]{1,0:T(8,128)(2,1)S(1)}, bf16[16,4096]{1,0:T(8,128)(2,1)S(1)}, bf16[16,4096]{1,0:T(8,128)(2,1)S(1)}, bf16[16,4096]{1,0:T(8,128)(2,1)S(1)}) custom-call(bf16[16,4096]{1,0:T(8,128)(2,1)S(1)} %get-tuple-element.47.refs_0_.refs_4_, bf16[16,4096]{1,0:T(8,128)(2,1)S(1)} %collective-permute-done.9.refs_1_.refs_5_, ...), custom_call_target="tpu_custom_call" | custom-call | flops 402653184 | bytes 7471104 | tf_op jit(solution)/shard_map/pallas_call | solution.py:32
  26.4 0.6 %collective-permute-start.13 = (bf16[16,4096]{1,0:T(8,128)(2,1)S(1)}, bf16[16,4096]{1,0:T(8,128)(2,1)S(1)}, u32[]{:S(2)}, u32[]{:S(2)}) collective-permute-start(bf16[16,4096]{1,0:T(8,128)(2,1)S(1)} %get-tuple-element.51), channel_id=1, source_target_pairs={{0,29},{1,28},{2,31},{3,30},{4,1},{5,0},{6,3},{7,2},{8,5},{9,4},{1... | collective-permute-start | bytes 393224 | tf_op jit(solution)/shard_map/ppermute | solution.py:249
  27.0 1.1 %collective-permute-start.14 = (bf16[16,4096]{1,0:T(8,128)(2,1)S(1)}, bf16[16,4096]{1,0:T(8,128)(2,1)S(1)}, u32[]{:S(2)}, u32[]{:S(2)}) collective-permute-start(bf16[16,4096]{1,0:T(8,128)(2,1)S(1)} %get-tuple-element.52), channel_id=1, source_target_pairs={{0,30},{1,31},{2,28},{3,29},{4,2},{5,3},{6,0},{7,1},{8,6},{9,7},{1... | collective-permute-start | bytes 393224 | tf_op jit(solution)/shard_map/ppermute | solution.py:249
  28.1 0.0 collective-permute-start.15
  28.1 2.5 %collective-permute-start.18 = (bf16[64,16]{1,0:T(8,128)(2,1)S(1)}, bf16[64,16]{1,0:T(8,128)(2,1)S(1)}, u32[]{:S(2)}, u32[]{:S(2)}) collective-permute-start(bf16[64,16]{1,0:T(8,128)(2,1)S(1)} %get-tuple-element.57.refs_0_), channel_id=1, source_target_pairs={{0,3},{1,2},{2,1},{3,0},{4,7},{5,6},{6,5},{7,4},{8,11},{9,10},{10,... | collective-permute-start | bytes 6152 | tf_op jit(solution)/shard_map/ppermute | solution.py:249
  30.6 0.5 collective-permute-start.17
  31.1 2.6 %collective-permute-done.18.refs_3_ = bf16[64,16]{1,0:T(8,128)(2,1)S(1)} collective-permute-done((bf16[64,16]{1,0:T(8,128)(2,1)S(1)}, bf16[64,16]{1,0:T(8,128)(2,1)S(1)}, u32[]{:S(2)}, u32[]{:S(2)}) %collective-permute-start.18) | collective-permute-done | bytes 2080 | tf_op jit(solution)/shard_map/ppermute | solution.py:249
  33.7 3.5 %collective-permute-start.16 = (bf16[64,16]{1,0:T(8,128)(2,1)S(1)}, bf16[64,16]{1,0:T(8,128)(2,1)S(1)}, u32[]{:S(2)}, u32[]{:S(2)}) collective-permute-start(bf16[64,16]{1,0:T(8,128)(2,1)S(1)} %get-tuple-element.57.refs_0_), channel_id=1, source_target_pairs={{0,1},{1,0},{2,3},{3,2},{4,5},{5,4},{6,7},{7,6},{8,9},{9,8},{10,11... | collective-permute-start | bytes 6152 | tf_op jit(solution)/shard_map/ppermute | solution.py:249
  37.2 1.7 %collective-permute-done.16.refs_1_ = bf16[64,16]{1,0:T(8,128)(2,1)S(1)} collective-permute-done((bf16[64,16]{1,0:T(8,128)(2,1)S(1)}, bf16[64,16]{1,0:T(8,128)(2,1)S(1)}, u32[]{:S(2)}, u32[]{:S(2)}) %collective-permute-start.16) | collective-permute-done | bytes 2080 | tf_op jit(solution)/shard_map/ppermute | solution.py:249
  38.9 1.2 %collective-permute-start.6 = (bf16[16,4096]{1,0:T(8,128)(2,1)S(1)}, bf16[16,4096]{1,0:T(8,128)(2,1)S(1)}, u32[]{:S(2)}, u32[]{:S(2)}) collective-permute-start(bf16[16,4096]{1,0:T(8,128)(2,1)S(1)} %get-tuple-element.43), channel_id=1, source_target_pairs={{0,5},{1,4},{2,7},{3,6},{4,9},{5,8},{6,11},{7,10},{8,13},{9,12},{1... | collective-permute-start | bytes 393224 | tf_op jit(solution)/shard_map/ppermute | solution.py:249
  40.1 0.7 %collective-permute-start.7 = (bf16[16,4096]{1,0:T(8,128)(2,1)S(1)}, bf16[16,4096]{1,0:T(8,128)(2,1)S(1)}, u32[]{:S(2)}, u32[]{:S(2)}) collective-permute-start(bf16[16,4096]{1,0:T(8,128)(2,1)S(1)} %get-tuple-element.44), channel_id=1, source_target_pairs={{0,6},{1,7},{2,4},{3,5},{4,10},{5,11},{6,8},{7,9},{8,14},{9,15},{1... | collective-permute-start | bytes 393224 | tf_op jit(solution)/shard_map/ppermute | solution.py:249
  40.8 0.3 collective-permute-start.8
  41.1 1.0 %shard_map.126 = f32[16,256]{1,0:T(8,128)} custom-call(bf16[16,4096]{1,0:T(8,128)(2,1)S(1)} %get-tuple-element.47.refs_0_.refs_4_, bf16[16,4096]{1,0:T(8,128)(2,1)S(1)} %collective-permute-done.9.refs_1_.refs_5_, bf16[16,4096]{1,0:T(8,128)(2,1)S(1)} %collective-permute-done.10.refs_2_.refs_6_, bf16[16,4096]{1,0:T(8,128)(2,1)S(1)} %collective-permute-done.11.refs_3_.refs_7_, ...), custom_call_target="tpu_custom_call" | custom-call | flops 8388608 | bytes 704512 | tf_op jit(solution)/shard_map/pallas_call | solution.py:32
  42.1 0.9 %shard_map.127 = f32[1,1,16,1024]{3,2,1,0:T(8,128)} custom-call(bf16[64,16]{1,0:T(8,128)(2,1)S(1)} %get-tuple-element.57.refs_0_, bf16[64,16]{1,0:T(8,128)(2,1)S(1)} %collective-permute-done.16.refs_1_, bf16[64,16]{1,0:T(8,128)(2,1)S(1)} %collective-permute-done.17.refs_2_, bf16[64,16]{1,0:T(8,128)(2,1)S(1)} %collective-permute-done.18.refs_3_, ...), custom_call_target="tpu_custom_call" | custom-call | flops 4194304 | bytes 598016 | tf_op jit(solution)/shard_map/pallas_call | solution.py:32
  43.0 1.3 %shard_map.125 = bf16[1,128,4096]{2,1,0:T(8,128)(2,1)} custom-call(f32[16,128]{1,0:T(8,128)S(1)} %collective-permute-done.4.place_ref, bf16[16,4096]{1,0:T(8,128)(2,1)S(1)} %collective-permute-done.12.refs_0_, bf16[16,4096]{1,0:T(8,128)(2,1)S(1)} %collective-permute-done.13.refs_1_, bf16[16,4096]{1,0:T(8,128)(2,1)S(1)} %collective-permute-done.14.refs_2_, ...), custom_call_target="tpu_custom_call" | custom-call | flops 16777216 | bytes 1581056 | tf_op jit(solution)/shard_map/pallas_call | solution.py:32
  44.3 0.8 %collective-permute-done.5.refs_0_ = bf16[16,4096]{1,0:T(8,128)(2,1)S(1)} collective-permute-done((bf16[16,4096]{1,0:T(8,128)(2,1)S(1)}, bf16[16,4096]{1,0:T(8,128)(2,1)S(1)}, u32[]{:S(2)}, u32[]{:S(2)}) %collective-permute-start.5) | collective-permute-done | bytes 131104 | tf_op jit(solution)/shard_map/ppermute | solution.py:249
  45.1 2.9 %collective-permute-done.6.refs_1_ = bf16[16,4096]{1,0:T(8,128)(2,1)S(1)} collective-permute-done((bf16[16,4096]{1,0:T(8,128)(2,1)S(1)}, bf16[16,4096]{1,0:T(8,128)(2,1)S(1)}, u32[]{:S(2)}, u32[]{:S(2)}) %collective-permute-start.6) | collective-permute-done | bytes 131104 | tf_op jit(solution)/shard_map/ppermute | solution.py:249
  47.9 0.6 %collective-permute-done.7.refs_2_ = bf16[16,4096]{1,0:T(8,128)(2,1)S(1)} collective-permute-done((bf16[16,4096]{1,0:T(8,128)(2,1)S(1)}, bf16[16,4096]{1,0:T(8,128)(2,1)S(1)}, u32[]{:S(2)}, u32[]{:S(2)}) %collective-permute-start.7) | collective-permute-done | bytes 131104 | tf_op jit(solution)/shard_map/ppermute | solution.py:249
  48.6 2.5 %collective-permute-done.8.refs_3_ = bf16[16,4096]{1,0:T(8,128)(2,1)S(1)} collective-permute-done((bf16[16,4096]{1,0:T(8,128)(2,1)S(1)}, bf16[16,4096]{1,0:T(8,128)(2,1)S(1)}, u32[]{:S(2)}, u32[]{:S(2)}) %collective-permute-start.8) | collective-permute-done | bytes 131104 | tf_op jit(solution)/shard_map/ppermute | solution.py:249
  51.1 1.3 %shard_map.123 = bf16[1,128,4096]{2,1,0:T(8,128)(2,1)} custom-call(f32[16,128]{1,0:T(8,128)S(1)} %collective-permute-done.3.place_ref, bf16[16,4096]{1,0:T(8,128)(2,1)S(1)} %collective-permute-done.5.refs_0_, bf16[16,4096]{1,0:T(8,128)(2,1)S(1)} %collective-permute-done.6.refs_1_, bf16[16,4096]{1,0:T(8,128)(2,1)S(1)} %collective-permute-done.7.refs_2_, ...), custom_call_target="tpu_custom_call" | custom-call | flops 16777216 | bytes 1581056 | tf_op jit(solution)/shard_map/pallas_call | solution.py:32
  (14 shorter events, 0.0 us)
Async XLA Ops:
  3.3 13.6 %collective-permute-start.2 = (bf16[16,4096]{1,0:T(8,128)(2,1)S(1)}, bf16[16,4096]{1,0:T(8,128)(2,1)S(1)}, u32[]{:S(2)}, u32[]{:S(2)}) collective-permute-start(bf16[16,4096]{1,0:T(8,128)(2,1)S(1)} %get-tuple-element.34.refs_0_), channel_id=1, source_target_pairs={{0,3},{1,2},{2,1},{3,0},{4,7},{5,6},{6,5},{7,4},{8,11},{9,10},{10,... | collective-permute-start | bytes 393224 | tf_op jit(solution)/shard_map/ppermute | solution.py:249
  7.3 14.6 %collective-permute-start.1 = (bf16[16,4096]{1,0:T(8,128)(2,1)S(1)}, bf16[16,4096]{1,0:T(8,128)(2,1)S(1)}, u32[]{:S(2)}, u32[]{:S(2)}) collective-permute-start(bf16[16,4096]{1,0:T(8,128)(2,1)S(1)} %get-tuple-element.34.refs_0_), channel_id=1, source_target_pairs={{0,2},{1,3},{2,0},{3,1},{4,6},{5,7},{6,4},{7,5},{8,10},{9,11},{10,... | collective-permute-start | bytes 393224 | tf_op jit(solution)/shard_map/ppermute | solution.py:249
  7.8 14.2 %collective-permute-start = (bf16[16,4096]{1,0:T(8,128)(2,1)S(1)}, bf16[16,4096]{1,0:T(8,128)(2,1)S(1)}, u32[]{:S(2)}, u32[]{:S(2)}) collective-permute-start(bf16[16,4096]{1,0:T(8,128)(2,1)S(1)} %get-tuple-element.34.refs_0_), channel_id=1, source_target_pairs={{0,1},{1,0},{2,3},{3,2},{4,5},{5,4},{6,7},{7,6},{8,9},{9,8},{10,11... | collective-permute-start | bytes 393224 | tf_op jit(solution)/shard_map/ppermute | solution.py:249
  8.0 4.0 %collective-permute-start.4 = (f32[16,128]{1,0:T(8,128)S(1)}, f32[16,128]{1,0:T(8,128)S(1)}, u32[]{:S(2)}, u32[]{:S(2)}) collective-permute-start(f32[16,128]{1,0:T(8,128)S(1)} %get-tuple-element.32._), channel_id=1, source_target_pairs={{0,28},{1,29},{2,30},{3,31},{4,0},{5,1},{6,2},{7,3},{8,4},{9,5},{1... | collective-permute-start | bytes 24584 | tf_op jit(solution)/shard_map/ppermute | solution.py:249
  10.6 4.9 %collective-permute-start.3 = (f32[16,128]{1,0:T(8,128)S(1)}, f32[16,128]{1,0:T(8,128)S(1)}, u32[]{:S(2)}, u32[]{:S(2)}) collective-permute-start(f32[16,128]{1,0:T(8,128)S(1)} %get-tuple-element.32._), channel_id=1, source_target_pairs={{0,4},{1,5},{2,6},{3,7},{4,8},{5,9},{6,10},{7,11},{8,12},{9,13},{1... | collective-permute-start | bytes 24584 | tf_op jit(solution)/shard_map/ppermute | solution.py:249
  11.9 11.9 %collective-permute-start.11 = (bf16[16,4096]{1,0:T(8,128)(2,1)S(1)}, bf16[16,4096]{1,0:T(8,128)(2,1)S(1)}, u32[]{:S(2)}, u32[]{:S(2)}) collective-permute-start(bf16[16,4096]{1,0:T(8,128)(2,1)S(1)} %get-tuple-element.47.refs_0_.refs_4_), channel_id=1, source_target_pairs={{0,3},{1,2},{2,1},{3,0},{4,7},{5,6},{6,5},{7,4},{8,11},{9,10},{10,... | collective-permute-start | bytes 393224 | tf_op jit(solution)/shard_map/ppermute | solution.py:249
  15.4 8.4 %collective-permute-start.10 = (bf16[16,4096]{1,0:T(8,128)(2,1)S(1)}, bf16[16,4096]{1,0:T(8,128)(2,1)S(1)}, u32[]{:S(2)}, u32[]{:S(2)}) collective-permute-start(bf16[16,4096]{1,0:T(8,128)(2,1)S(1)} %get-tuple-element.47.refs_0_.refs_4_), channel_id=1, source_target_pairs={{0,2},{1,3},{2,0},{3,1},{4,6},{5,7},{6,4},{7,5},{8,10},{9,11},{10,... | collective-permute-start | bytes 393224 | tf_op jit(solution)/shard_map/ppermute | solution.py:249
  17.0 6.9 %collective-permute-start.9 = (bf16[16,4096]{1,0:T(8,128)(2,1)S(1)}, bf16[16,4096]{1,0:T(8,128)(2,1)S(1)}, u32[]{:S(2)}, u32[]{:S(2)}) collective-permute-start(bf16[16,4096]{1,0:T(8,128)(2,1)S(1)} %get-tuple-element.47.refs_0_.refs_4_), channel_id=1, source_target_pairs={{0,1},{1,0},{2,3},{3,2},{4,5},{5,4},{6,7},{7,6},{8,9},{9,8},{10,11... | collective-permute-start | bytes 393224 | tf_op jit(solution)/shard_map/ppermute | solution.py:249
  26.4 12.5 %collective-permute-start.13 = (bf16[16,4096]{1,0:T(8,128)(2,1)S(1)}, bf16[16,4096]{1,0:T(8,128)(2,1)S(1)}, u32[]{:S(2)}, u32[]{:S(2)}) collective-permute-start(bf16[16,4096]{1,0:T(8,128)(2,1)S(1)} %get-tuple-element.51), channel_id=1, source_target_pairs={{0,29},{1,28},{2,31},{3,30},{4,1},{5,0},{6,3},{7,2},{8,5},{9,4},{1... | collective-permute-start | bytes 393224 | tf_op jit(solution)/shard_map/ppermute | solution.py:249
  27.0 13.1 %collective-permute-start.14 = (bf16[16,4096]{1,0:T(8,128)(2,1)S(1)}, bf16[16,4096]{1,0:T(8,128)(2,1)S(1)}, u32[]{:S(2)}, u32[]{:S(2)}) collective-permute-start(bf16[16,4096]{1,0:T(8,128)(2,1)S(1)} %get-tuple-element.52), channel_id=1, source_target_pairs={{0,30},{1,31},{2,28},{3,29},{4,2},{5,3},{6,0},{7,1},{8,6},{9,7},{1... | collective-permute-start | bytes 393224 | tf_op jit(solution)/shard_map/ppermute | solution.py:249
  28.1 12.6 %collective-permute-start.15 = (bf16[16,4096]{1,0:T(8,128)(2,1)S(1)}, bf16[16,4096]{1,0:T(8,128)(2,1)S(1)}, u32[]{:S(2)}, u32[]{:S(2)}) collective-permute-start(bf16[16,4096]{1,0:T(8,128)(2,1)S(1)} %get-tuple-element.53), channel_id=1, source_target_pairs={{0,31},{1,30},{2,29},{3,28},{4,3},{5,2},{6,1},{7,0},{8,7},{9,6},{1... | collective-permute-start | bytes 393224 | tf_op jit(solution)/shard_map/ppermute | solution.py:249
  28.1 5.5 %collective-permute-start.18 = (bf16[64,16]{1,0:T(8,128)(2,1)S(1)}, bf16[64,16]{1,0:T(8,128)(2,1)S(1)}, u32[]{:S(2)}, u32[]{:S(2)}) collective-permute-start(bf16[64,16]{1,0:T(8,128)(2,1)S(1)} %get-tuple-element.57.refs_0_), channel_id=1, source_target_pairs={{0,3},{1,2},{2,1},{3,0},{4,7},{5,6},{6,5},{7,4},{8,11},{9,10},{10,... | collective-permute-start | bytes 6152 | tf_op jit(solution)/shard_map/ppermute | solution.py:249
  30.6 6.6 %collective-permute-start.17 = (bf16[64,16]{1,0:T(8,128)(2,1)S(1)}, bf16[64,16]{1,0:T(8,128)(2,1)S(1)}, u32[]{:S(2)}, u32[]{:S(2)}) collective-permute-start(bf16[64,16]{1,0:T(8,128)(2,1)S(1)} %get-tuple-element.57.refs_0_), channel_id=1, source_target_pairs={{0,2},{1,3},{2,0},{3,1},{4,6},{5,7},{6,4},{7,5},{8,10},{9,11},{10,... | collective-permute-start | bytes 6152 | tf_op jit(solution)/shard_map/ppermute | solution.py:249
  33.7 5.2 %collective-permute-start.16 = (bf16[64,16]{1,0:T(8,128)(2,1)S(1)}, bf16[64,16]{1,0:T(8,128)(2,1)S(1)}, u32[]{:S(2)}, u32[]{:S(2)}) collective-permute-start(bf16[64,16]{1,0:T(8,128)(2,1)S(1)} %get-tuple-element.57.refs_0_), channel_id=1, source_target_pairs={{0,1},{1,0},{2,3},{3,2},{4,5},{5,4},{6,7},{7,6},{8,9},{9,8},{10,11... | collective-permute-start | bytes 6152 | tf_op jit(solution)/shard_map/ppermute | solution.py:249
  37.2 5.9 %collective-permute-start.12 = (bf16[16,4096]{1,0:T(8,128)(2,1)S(1)}, bf16[16,4096]{1,0:T(8,128)(2,1)S(1)}, u32[]{:S(2)}, u32[]{:S(2)}) collective-permute-start(bf16[16,4096]{1,0:T(8,128)(2,1)S(1)} %get-tuple-element.50), channel_id=1, source_target_pairs={{0,28},{1,29},{2,30},{3,31},{4,0},{5,1},{6,2},{7,3},{8,4},{9,5},{1... | collective-permute-start | bytes 393224 | tf_op jit(solution)/shard_map/ppermute | solution.py:249
  38.9 6.2 %collective-permute-start.5 = (bf16[16,4096]{1,0:T(8,128)(2,1)S(1)}, bf16[16,4096]{1,0:T(8,128)(2,1)S(1)}, u32[]{:S(2)}, u32[]{:S(2)}) collective-permute-start(bf16[16,4096]{1,0:T(8,128)(2,1)S(1)} %get-tuple-element.42), channel_id=1, source_target_pairs={{0,4},{1,5},{2,6},{3,7},{4,8},{5,9},{6,10},{7,11},{8,12},{9,13},{1... | collective-permute-start | bytes 393224 | tf_op jit(solution)/shard_map/ppermute | solution.py:249
  38.9 9.0 %collective-permute-start.6 = (bf16[16,4096]{1,0:T(8,128)(2,1)S(1)}, bf16[16,4096]{1,0:T(8,128)(2,1)S(1)}, u32[]{:S(2)}, u32[]{:S(2)}) collective-permute-start(bf16[16,4096]{1,0:T(8,128)(2,1)S(1)} %get-tuple-element.43), channel_id=1, source_target_pairs={{0,5},{1,4},{2,7},{3,6},{4,9},{5,8},{6,11},{7,10},{8,13},{9,12},{1... | collective-permute-start | bytes 393224 | tf_op jit(solution)/shard_map/ppermute | solution.py:249
  40.1 8.5 %collective-permute-start.7 = (bf16[16,4096]{1,0:T(8,128)(2,1)S(1)}, bf16[16,4096]{1,0:T(8,128)(2,1)S(1)}, u32[]{:S(2)}, u32[]{:S(2)}) collective-permute-start(bf16[16,4096]{1,0:T(8,128)(2,1)S(1)} %get-tuple-element.44), channel_id=1, source_target_pairs={{0,6},{1,7},{2,4},{3,5},{4,10},{5,11},{6,8},{7,9},{8,14},{9,15},{1... | collective-permute-start | bytes 393224 | tf_op jit(solution)/shard_map/ppermute | solution.py:249
  40.8 10.3 %collective-permute-start.8 = (bf16[16,4096]{1,0:T(8,128)(2,1)S(1)}, bf16[16,4096]{1,0:T(8,128)(2,1)S(1)}, u32[]{:S(2)}, u32[]{:S(2)}) collective-permute-start(bf16[16,4096]{1,0:T(8,128)(2,1)S(1)} %get-tuple-element.45), channel_id=1, source_target_pairs={{0,7},{1,6},{2,5},{3,4},{4,11},{5,10},{6,9},{7,8},{8,15},{9,14},{1... | collective-permute-start | bytes 393224 | tf_op jit(solution)/shard_map/ppermute | solution.py:249

commit v3 on v2

--- a/solution.py
+++ b/solution.py
@@ -38,6 +38,10 @@
         compiler_params=pltpu.CompilerParams(vmem_limit_bytes=grant),
         cost_estimate=pl.CostEstimate(flops=flops, bytes_accessed=moved, transcendentals=0),
     )(*args, *(pltpu.with_memory_space_constraint(a, pltpu.HBM) for a in far_args))
+
+
+def picks(place):
+    return jnp.where(place > 0, 1.0, 0.0).astype(jnp.bfloat16)
 
 
 def gather(
@@ -94,7 +98,7 @@
         index = f32dot(routed.astype(jnp.bfloat16), before)
         place_ref[f * MOST:(f + 1) * MOST, :] = jnp.where(slot == index, level * LEVEL_STEP, 0.0)
     place = place_ref[...]
-    pick = jnp.where(place > 0, 1.0, 0.0).astype(jnp.bfloat16)
+    pick = picks(place)
     gate = jnp.sum(place, axis=1, keepdims=True)
     for c in range(CHUNKS):
         x_copies[c].wait()
@@ -155,25 +159,33 @@
     out_refs = refs[SPLIT + 4:2 * SPLIT + 4]
     pre_gate_ref, pre_up_ref, hidden_ref, latent_ref = refs[2 * SPLIT + 4:]
     rows = jnp.concatenate([r[...] for r in x_refs], axis=0)
-    height = x_refs[0].shape[0]
+    height, width = x_refs[0].shape
     pre_gate = f32dot(rows, gate_ref[...], LAST)
     pre_up = f32dot(rows, up_ref[...], LAST)
     pre_gate_ref[...] = pre_gate
     pre_up_ref[...] = pre_up
     hidden = (pre_gate * jax.nn.sigmoid(pre_gate) * pre_up).astype(jnp.bfloat16)
     hidden_ref[...] = hidden
-    latent_ref[...] = f32dot(hidden, a_ref[...], LAST).astype(jnp.bfloat16)
     result = f32dot(hidden, down_ref[...]).astype(jnp.bfloat16)
     for k, ref in enumerate(out_refs):
-        ref[...] = result[k * height:(k + 1) * height]
+        ref[:, :width] = result[k * height:(k + 1) * height]
+    latent = f32dot(a_ref[...], hidden, LAST).astype(jnp.bfloat16)
+    latent_ref[...] = latent
+    if out_refs[1].shape[1] > width:
+        rank, count = latent.shape
+        tail = jnp.concatenate(
+            [latent, jnp.zeros((rank, out_refs[1].shape[1] - width - count), jnp.bfloat16)], axis=1
+        )
+        for ref in out_refs[1:]:
+            ref[:, width:] = tail
 
 
 def backward(*refs):
     g_refs = refs[:SPLIT]
-    pre_gate_ref, pre_up_ref, gate_ref, up_ref, down_ref = refs[SPLIT:SPLIT + 5]
-    out_refs = refs[SPLIT + 5:]
+    place_ref, pre_gate_ref, pre_up_ref, gate_ref, up_ref, down_ref = refs[SPLIT:SPLIT + 6]
+    out_refs = refs[SPLIT + 6:]
     rows = jnp.concatenate([r[...] for r in g_refs], axis=0)
-    height = g_refs[0].shape[0]
+    height, width = g_refs[0].shape
     grad_hidden = f32dot(rows, down_ref[...], LAST)
     pre_gate = pre_gate_ref[...]
     g = jax.nn.sigmoid(pre_gate)
@@ -183,7 +195,20 @@
     result = result + f32dot(grad_up.astype(jnp.bfloat16), up_ref[...])
     result = result.astype(jnp.bfloat16)
     for k, ref in enumerate(out_refs):
-        ref[...] = result[k * height:(k + 1) * height]
+        ref[:, :width] = result[k * height:(k + 1) * height]
+    out_refs[0][:, width:] = picks(place_ref[...])
+
+
+def combine(gated, place_ref, *refs):
+    *part_refs, out_ref = refs
+    place = place_ref[...]
+    width = part_refs[0].shape[1]
+    rows = sum(r[:, :width].astype(jnp.float32) for r in part_refs)
+    if gated:
+        rows = rows * jnp.sum(place, axis=1, keepdims=True)
+    out_ref[:, :width] = rows.astype(jnp.bfloat16)
+    if out_ref.shape[1] > width:
+        out_ref[:, width:] = picks(place)
 
 
 def down_map_grad(*refs):
@@ -193,42 +218,30 @@
     out_ref[...] = f32dot(lowrank, hidden_ref[...], FIRST)
 
 
-def up_map_grad(*refs):
-    lat_refs, g_refs, out_ref = refs[:SPLIT], refs[SPLIT:2 * SPLIT], refs[2 * SPLIT]
-    width = out_ref.shape[-1]
-    column = pl.multiple_of(lax.axis_index("expert") * width, 128)
-    height = g_refs[0].shape[0]
-    total = jnp.zeros(out_ref.shape[2:], jnp.float32)
-    for i in range(SPLIT):
-        block = sum(
-            lat_refs[k][(i ^ k) * height:((i ^ k) + 1) * height, :].astype(jnp.float32)
-            for k in range(SPLIT)
-        )
-        high = block.astype(jnp.bfloat16)
-        low = (block - high.astype(jnp.float32)).astype(jnp.bfloat16)
-        rows = g_refs[i][:, pl.ds(column, width)]
-        total = total + f32dot(high, rows, FIRST) + f32dot(low, rows, FIRST)
+def up_map_grad(latent_ref, *refs):
+    message_refs, g_refs, out_ref = refs[:SPLIT - 1], refs[SPLIT - 1:2 * SPLIT - 1], refs[-1]
+    span = out_ref.shape[-1]
+    column = pl.multiple_of(lax.axis_index("expert") * span, 128)
+    count = latent_ref.shape[1]
+    width = g_refs[0].shape[1]
+    latents = [latent_ref[...]] + [r[:, width:width + count] for r in message_refs]
+    rows = [g_refs[i ^ k][:, pl.ds(column, span)] for k in range(SPLIT) for i in range(SPLIT)]
+    total = f32dot(jnp.concatenate(latents, axis=1), jnp.concatenate(rows, axis=0))
     out_ref[0, 0] = LOWRANK_SCALE * total
 
 
-def expand(gated, place_ref, *refs):
+def expand(*refs):
     *part_refs, out_hbm, out_ref, sems = refs
-    place = place_ref[...]
-    pick = jnp.where(place > 0, 1.0, 0.0).astype(jnp.bfloat16)
-    gate = jnp.sum(place, axis=1, keepdims=True)
-    span = out_ref.shape[1] // CHUNKS
+    width = out_ref.shape[1]
+    pick = part_refs[0][:, width:]
+    span = width // CHUNKS
     copies = []
     for c in range(CHUNKS):
         part = slice(c * span, (c + 1) * span)
-        rows = sum(r[:, part].astype(jnp.float32) for r in part_refs)
-        if gated:
-            rows = rows * gate
-        high = rows.astype(jnp.bfloat16)
-        spread = f32dot(pick, high, FIRST)
-        if place.shape[0] > MOST:
-            low = (rows - high.astype(jnp.float32)).astype(jnp.bfloat16)
-            spread = spread + f32dot(pick, low, FIRST)
-        out_ref[:, part] = spread.astype(jnp.bfloat16)
+        rows = part_refs[0][:, part]
+        if len(part_refs) > 1:
+            rows = sum(r[:, part].astype(jnp.float32) for r in part_refs).astype(jnp.bfloat16)
+        out_ref[:, part] = f32dot(pick, rows, FIRST).astype(jnp.bfloat16)
         columns = pl.ds(c * span, span)
         copy = pltpu.make_async_copy(
             out_ref.at[:, columns], out_hbm.at[0, :, columns], sems.at[c]
@@ -309,9 +322,6 @@
     g_rows = between_groups(g_rows, flight)
     x_blocks = [x_rows] + [shifted(x_rows, 0, k) for k in flips[1:]]
     g_blocks = [g_rows] + [shifted(g_rows, 0, k) for k in flips[1:]]
-    place_before = shifted(place, 1, 0)
-    place_after = shifted(place, -1, 0)
-
     gate_near, up_near, down_near, a_near, b_near = call(
         load,
         [sds(units, width)] * 3 + [sds(rank, units), sds(rank, width)],
@@ -325,27 +335,32 @@
         flops=2 * units * rank * width,
     )
 
-    x_blocks, place_before, place_after = lax.optimization_barrier(
-        (x_blocks, place_before, place_after)
-    )
-    block_outs = [sds(slots, width)] * SPLIT
-    *out_blocks, pre_gate, pre_up, hidden, latent = call(
+    wide = width + tokens
+    out_blocks = call(
         forward,
-        block_outs
+        [sds(slots, width)]
+        + [sds(slots, wide if flight == 1 else width)] * (SPLIT - 1)
         + [sds(rows, units, dtype=jnp.float32)] * 2
-        + [sds(rows, units), sds(rows, rank)],
+        + [sds(rows, units), sds(rank, rows)],
         (*x_blocks, gate_near, up_near, down_near, a_near),
         flops=6 * rows * units * width,
     )
-    latents = [latent] + [shifted(latent, 0, k) for k in flips[1:]]
-    out_parts = [shifted(out_blocks[k], 1, k) for k in flips]
+    *out_blocks, pre_gate, pre_up, hidden, latent = out_blocks
+    out_parts = [out_blocks[0]] + [shifted(out_blocks[k], 0, k) for k in flips[1:]]
     grad_blocks = call(
         backward,
-        block_outs,
-        (*g_blocks, pre_gate, pre_up, gate_near, up_near, down_near),
+        [sds(slots, wide)] + [sds(slots, width)] * (SPLIT - 1),
+        (*g_blocks, place, pre_gate, pre_up, gate_near, up_near, down_near),
         flops=6 * rows * units * width,
     )
     grad_parts = [shifted(grad_blocks[k], -1, k) for k in flips]
+
+    def merged(parts, gated, columns):
+        return call(functools.partial(combine, gated), [sds(slots, columns)], (place, *parts))[0]
+
+    if flight > 1:
+        out_parts = [between_groups(merged(out_parts, False, width), flight)]
+    message = shifted(merged(out_parts, True, wide), 1, 0)
 
     hidden, _ = lax.optimization_barrier((hidden, grad_blocks[0]))
     (a_grad,) = call(
@@ -358,30 +373,31 @@
         (b_grad,) = call(
             up_map_grad,
             [sds(1, 1, rank, width // SPLIT, dtype=jnp.float32)],
-            (*latents, *g_blocks),
-            flops=4 * rows * rank * width // SPLIT,
+            (latent, *out_parts[1:], *g_blocks),
+            flops=2 * SPLIT * rows * rank * width // SPLIT,
         )
     else:
-        part = LOWRANK_SCALE * f32dot(latent, jnp.concatenate(g_blocks, axis=0), FIRST)
+        part = LOWRANK_SCALE * f32dot(latent, jnp.concatenate(g_blocks, axis=0))
         mine = jnp.arange(flight, dtype=jnp.int32) == group
         spread = jnp.where(mine[:, None, None], part[None], 0.0)
         b_grad = lax.psum_scatter(spread, "expert", scatter_dimension=2, tiled=True)[None]
 
-    def finish(parts, place, gated):
-        if flight > 1:
-            total = sum(p.astype(jnp.float32) for p in parts).astype(jnp.bfloat16)
-            parts = [between_groups(total, flight)]
+    def expanded(parts):
         return call(
-            functools.partial(expand, gated),
+            expand,
             [sds(1, tokens, width)],
-            (place, *parts),
+            tuple(parts),
             far_outs=True,
             scratch=[pltpu.VMEM((tokens, width), jnp.bfloat16), dma((CHUNKS,))],
             flops=2 * slots * tokens * width,
         )[0]
 
-    next_input = finish(out_parts, place_before, True)
-    prev_grad = finish(grad_parts, place_after, False)
+    next_input = expanded([message])
+    if flight > 1:
+        total = sum(p[:, :width].astype(jnp.float32) for p in grad_parts).astype(jnp.bfloat16)
+        total = between_groups(total, flight)
+        grad_parts = [jnp.concatenate([total, grad_parts[0][:, width:]], axis=1)]
+    prev_grad = expanded(grad_parts)
     return next_input, prev_grad, jnp.swapaxes(a_grad, 0, 1)[None], b_grad
 
 

time: 52.5 us -> 42.4 us (0.81)
  waiting for transfers between devices: 13.5 us -> 6.3 us
  starting transfers between devices: 23.1 us -> 20.2 us
    ppermute x19 -> x14, waiting for transfers between devices: 13.5 us -> 6.3 us  [shifted(): return lax.ppermute(block, ('section', 'expert'), route)]
    ppermute x19 -> x14, starting transfers between devices: 23.1 us -> 20.2 us  [shifted(): return lax.ppermute(block, ('section', 'expert'), route)]
    pallas_call x8 -> x9, Pallas kernels: 15.1 us -> 15 us  [call(): pl.pallas_call(body, out_shape=outs, in_specs=[NEAR] * len(args) + [FAR]...]
  transfers between devices with their start and end apart: 19 -> 14, of which waited for: 8 -> 3; matrix products, arithmetic and copies ran while one was open for 0% -> 0% of each run, Pallas kernels for 16% -> 26%
where the time goes in v3:
time: 42.4 us; the launch traced here: 42.2 us
  starting transfers between devices  20.2 us (48%)
  Pallas kernels  15 us (35%)
  waiting for transfers between devices  6.3 us (15%)
  between operations  0.7 us (2%)
    ppermute x14, starting transfers between devices, shifted(): return lax.ppermute(block, ('section', 'expert'), route)  20.2 us
    pallas_call x9, Pallas kernels, call(): pl.pallas_call(body, out_shape=outs, in_specs=[NEAR] * len(args) + [FAR]...  15 us
    ppermute x14, waiting for transfers between devices, shifted(): return lax.ppermute(block, ('section', 'expert'), route)  6.3 us
  transfers between devices with their start and end apart: 14, of which 3 were waited for; matrix products, arithmetic and copies ran while one was open for 0% of the time, Pallas kernels for 26%

profile of v3, /device:TPU:0, one launch (start us, length us, event | category | flops | bytes accessed | tf_op | source)
XLA Modules:
  0.0 42.2 jit_solution(16667731796784670178)
XLA Ops:
  0.6 2.7 %shard_map.120 = (bf16[16,4096]{1,0:T(8,128)(2,1)S(1)}, bf16[16,4096]{1,0:T(8,128)(2,1)S(1)}, f32[16,128]{1,0:T(8,128)S(1)}) custom-call(s32[8,128]{1,0:T(8,128)} %bitcast.16, s32[8,128]{1,0:T(8,128)} %bitcast.17, bf16[1,128,4096]{2,1,0:T(8,128)(2,1)} %x_hbm.1, bf16[1,128,4096]{2,1,0:T(8,128)(2,1)} %cot_hbm.1), custom_call_target="tpu_custom_call" | custom-call | flops 33554432 | bytes 2375680 | tf_op jit(solution)/shard_map/pallas_call | solution.py:32
  3.3 4.0 %collective-permute-start.2 = (bf16[16,4096]{1,0:T(8,128)(2,1)S(1)}, bf16[16,4096]{1,0:T(8,128)(2,1)S(1)}, u32[]{:S(2)}, u32[]{:S(2)}) collective-permute-start(bf16[16,4096]{1,0:T(8,128)(2,1)S(1)} %get-tuple-element.26.refs_0_), channel_id=1, source_target_pairs={{0,3},{1,2},{2,1},{3,0},{4,7},{5,6},{6,5},{7,4},{8,11},{9,10},{10,... | collective-permute-start | bytes 393224 | tf_op jit(solution)/shard_map/ppermute | solution.py:262
  7.3 0.5 %collective-permute-start.1 = (bf16[16,4096]{1,0:T(8,128)(2,1)S(1)}, bf16[16,4096]{1,0:T(8,128)(2,1)S(1)}, u32[]{:S(2)}, u32[]{:S(2)}) collective-permute-start(bf16[16,4096]{1,0:T(8,128)(2,1)S(1)} %get-tuple-element.26.refs_0_), channel_id=1, source_target_pairs={{0,2},{1,3},{2,0},{3,1},{4,6},{5,7},{6,4},{7,5},{8,10},{9,11},{10,... | collective-permute-start | bytes 393224 | tf_op jit(solution)/shard_map/ppermute | solution.py:262
  7.8 0.1 collective-permute-start
  8.0 2.8 %collective-permute-start.9 = (bf16[16,4096]{1,0:T(8,128)(2,1)S(1)}, bf16[16,4096]{1,0:T(8,128)(2,1)S(1)}, u32[]{:S(2)}, u32[]{:S(2)}) collective-permute-start(bf16[16,4096]{1,0:T(8,128)(2,1)S(1)} %get-tuple-element.35.refs_0_.refs_3_), channel_id=1, source_target_pairs={{0,3},{1,2},{2,1},{3,0},{4,7},{5,6},{6,5},{7,4},{8,11},{9,10},{10,... | collective-permute-start | bytes 393224 | tf_op jit(solution)/shard_map/ppermute | solution.py:262
  10.8 0.5 %collective-permute-start.8 = (bf16[16,4096]{1,0:T(8,128)(2,1)S(1)}, bf16[16,4096]{1,0:T(8,128)(2,1)S(1)}, u32[]{:S(2)}, u32[]{:S(2)}) collective-permute-start(bf16[16,4096]{1,0:T(8,128)(2,1)S(1)} %get-tuple-element.35.refs_0_.refs_3_), channel_id=1, source_target_pairs={{0,2},{1,3},{2,0},{3,1},{4,6},{5,7},{6,4},{7,5},{8,10},{9,11},{10,... | collective-permute-start | bytes 393224 | tf_op jit(solution)/shard_map/ppermute | solution.py:262
  11.3 3.5 %shard_map.121 = (bf16[256,4096]{1,0:T(8,128)(2,1)S(1)}, bf16[256,4096]{1,0:T(8,128)(2,1)S(1)}, bf16[256,4096]{1,0:T(8,128)(2,1)S(1)}, bf16[16,256]{1,0:T(8,128)(2,1)S(1)}, bf16[16,4096]{1,0:T(8,128)(2,1)S(1)}) custom-call(f32[16,128]{1,0:T(8,128)S(1)} %get-tuple-element.25._.place_ref.refs_4_, bf16[1,256,4096]{2,1,0:T(8,128)(2,1)} %gate_hbm.1, ...), custom_call_target="tpu_custom_call" | custom-call | flops 33554432 | bytes 12869632 | tf_op jit(solution)/shard_map/pallas_call | solution.py:32
  14.8 0.2 collective-permute-start.7
  15.0 1.5 %collective-permute-done.1.refs_2_ = bf16[16,4096]{1,0:T(8,128)(2,1)S(1)} collective-permute-done((bf16[16,4096]{1,0:T(8,128)(2,1)S(1)}, bf16[16,4096]{1,0:T(8,128)(2,1)S(1)}, u32[]{:S(2)}, u32[]{:S(2)}) %collective-permute-start.1) | collective-permute-done | bytes 131104 | tf_op jit(solution)/shard_map/ppermute | solution.py:262
  16.5 0.0 collective-permute-done.refs_1_
  16.5 1.8 %shard_map.122 = (bf16[16,4096]{1,0:T(8,128)(2,1)S(1)}, bf16[16,4224]{1,0:T(8,128)(2,1)S(1)}, bf16[16,4224]{1,0:T(8,128)(2,1)S(1)}, bf16[16,4224]{1,0:T(8,128)(2...) custom-call(bf16[16,4096]{1,0:T(8,128)(2,1)S(1)} %get-tuple-element., ...), custom_call_target="tpu_custom_call" | custom-call | flops 402653184 | bytes 7526400 | tf_op jit(solution)/shard_map/pallas_call | solution.py:32
  18.4 0.5 %collective-permute-start.3 = (bf16[16,4224]{1,0:T(8,128)(2,1)S(1)}, bf16[16,4224]{1,0:T(8,128)(2,1)S(1)}, u32[]{:S(2)}, u32[]{:S(2)}) collective-permute-start(bf16[16,4224]{1,0:T(8,128)(2,1)S(1)} %get-tuple-element.32), channel_id=1, source_target_pairs={{0,1},{1,0},{2,3},{3,2},{4,5},{5,4},{6,7},{7,6},{8,9},{9,8},{10,11... | collective-permute-start | bytes 405512 | tf_op jit(solution)/shard_map/ppermute | solution.py:262
  18.8 1.5 %collective-permute-start.4 = (bf16[16,4224]{1,0:T(8,128)(2,1)S(1)}, bf16[16,4224]{1,0:T(8,128)(2,1)S(1)}, u32[]{:S(2)}, u32[]{:S(2)}) collective-permute-start(bf16[16,4224]{1,0:T(8,128)(2,1)S(1)} %get-tuple-element.33), channel_id=1, source_target_pairs={{0,2},{1,3},{2,0},{3,1},{4,6},{5,7},{6,4},{7,5},{8,10},{9,11},{10,... | collective-permute-start | bytes 405512 | tf_op jit(solution)/shard_map/ppermute | solution.py:262
  20.4 1.6 %collective-permute-start.5 = (bf16[16,4224]{1,0:T(8,128)(2,1)S(1)}, bf16[16,4224]{1,0:T(8,128)(2,1)S(1)}, u32[]{:S(2)}, u32[]{:S(2)}) collective-permute-start(bf16[16,4224]{1,0:T(8,128)(2,1)S(1)} %get-tuple-element.34), channel_id=1, source_target_pairs={{0,3},{1,2},{2,1},{3,0},{4,7},{5,6},{6,5},{7,4},{8,11},{9,10},{10,... | collective-permute-start | bytes 405512 | tf_op jit(solution)/shard_map/ppermute | solution.py:262
  21.9 0.0 collective-permute-done.8.refs_2_.refs_5_
  21.9 0.0 collective-permute-done.7.refs_1_.refs_4_
  21.9 2.5 %shard_map.125 = (bf16[16,4224]{1,0:T(8,128)(2,1)S(1)}, bf16[16,4096]{1,0:T(8,128)(2,1)S(1)}, bf16[16,4096]{1,0:T(8,128)(2,1)S(1)}, bf16[16,4096]{1,0:T(8,128)(2,1)S(1)}) custom-call(bf16[16,4096]{1,0:T(8,128)(2,1)S(1)} %get-tuple-element.35.refs_0_.refs_3_, bf16[16,4096]{1,0:T(8,128)(2,1)S(1)} %collective-permute-done.7.refs_1_.refs_4_, ...), custom_call_target="tpu_custom_call" | custom-call | flops 402653184 | bytes 7483392 | tf_op jit(solution)/shard_map/pallas_call | solution.py:32
  24.4 1.0 %collective-permute-start.10 = (bf16[16,4224]{1,0:T(8,128)(2,1)S(1)}, bf16[16,4224]{1,0:T(8,128)(2,1)S(1)}, u32[]{:S(2)}, u32[]{:S(2)}) collective-permute-start(bf16[16,4224]{1,0:T(8,128)(2,1)S(1)} %get-tuple-element.38), channel_id=1, source_target_pairs={{0,28},{1,29},{2,30},{3,31},{4,0},{5,1},{6,2},{7,3},{8,4},{9,5},{1... | collective-permute-start | bytes 405512 | tf_op jit(solution)/shard_map/ppermute | solution.py:262
  25.4 0.0 collective-permute-done.3.refs_1_.refs_0_
  25.4 1.3 %collective-permute-done.4.refs_2_.refs_1_ = bf16[16,4224]{1,0:T(8,128)(2,1)S(1)} collective-permute-done((bf16[16,4224]{1,0:T(8,128)(2,1)S(1)}, bf16[16,4224]{1,0:T(8,128)(2,1)S(1)}, u32[]{:S(2)}, u32[]{:S(2)}) %collective-permute-start.4) | collective-permute-done | bytes 135200 | tf_op jit(solution)/shard_map/ppermute | solution.py:262
  26.7 0.0 collective-permute-done.5.refs_3_.refs_2_
  26.8 0.1 shard_map.123
  26.9 0.1 collective-permute-start.6
  26.9 4.2 %collective-permute-start.11 = (bf16[16,4096]{1,0:T(8,128)(2,1)S(1)}, bf16[16,4096]{1,0:T(8,128)(2,1)S(1)}, u32[]{:S(2)}, u32[]{:S(2)}) collective-permute-start(bf16[16,4096]{1,0:T(8,128)(2,1)S(1)} %get-tuple-element.39), channel_id=1, source_target_pairs={{0,29},{1,28},{2,31},{3,30},{4,1},{5,0},{6,3},{7,2},{8,5},{9,4},{1... | collective-permute-start | bytes 393224 | tf_op jit(solution)/shard_map/ppermute | solution.py:262
  31.1 0.5 %collective-permute-start.12 = (bf16[16,4096]{1,0:T(8,128)(2,1)S(1)}, bf16[16,4096]{1,0:T(8,128)(2,1)S(1)}, u32[]{:S(2)}, u32[]{:S(2)}) collective-permute-start(bf16[16,4096]{1,0:T(8,128)(2,1)S(1)} %get-tuple-element.40), channel_id=1, source_target_pairs={{0,30},{1,31},{2,28},{3,29},{4,2},{5,3},{6,0},{7,1},{8,6},{9,7},{1... | collective-permute-start | bytes 393224 | tf_op jit(solution)/shard_map/ppermute | solution.py:262
  31.6 2.8 %collective-permute-start.13 = (bf16[16,4096]{1,0:T(8,128)(2,1)S(1)}, bf16[16,4096]{1,0:T(8,128)(2,1)S(1)}, u32[]{:S(2)}, u32[]{:S(2)}) collective-permute-start(bf16[16,4096]{1,0:T(8,128)(2,1)S(1)} %get-tuple-element.41), channel_id=1, source_target_pairs={{0,31},{1,30},{2,29},{3,28},{4,3},{5,2},{6,1},{7,0},{8,7},{9,6},{1... | collective-permute-start | bytes 393224 | tf_op jit(solution)/shard_map/ppermute | solution.py:262
  34.3 1.0 %shard_map.127 = f32[16,256]{1,0:T(8,128)} custom-call(bf16[16,4096]{1,0:T(8,128)(2,1)S(1)} %get-tuple-element.35.refs_0_.refs_3_, bf16[16,4096]{1,0:T(8,128)(2,1)S(1)} %collective-permute-done.7.refs_1_.refs_4_, bf16[16,4096]{1,0:T(8,128)(2,1)S(1)} %collective-permute-done.8.refs_2_.refs_5_, bf16[16,4096]{1,0:T(8,128)(2,1)S(1)} %collective-permute-done.9.refs_3_.refs_6_, ...), custom_call_target="tpu_custom_call" | custom-call | flops 8388608 | bytes 704512 | tf_op jit(solution)/shard_map/pallas_call | solution.py:32
  35.4 0.8 %shard_map.128 = f32[1,1,16,1024]{3,2,1,0:T(8,128)} custom-call(bf16[16,64]{1,0:T(8,128)(2,1)S(1)} %get-tuple-element.45.latent_ref, bf16[16,4224]{1,0:T(8,128)(2,1)S(1)} %collective-permute-done.3.refs_1_.refs_0_, bf16[16,4224]{1,0:T(8,128)(2,1)S(1)} %collective-permute-done.4.refs_2_.refs_1_, bf16[16,4224]{1,0:T(8,128)(2,1)S(1)} %collective-permute-done.5.refs_3_.refs_2_, ...), custom_call_target="tpu_custom_call" | custom-call | flops 8388608 | bytes 997376 | tf_op jit(solution)/shard_map/pallas_call | solution.py:32
  36.2 3.5 %collective-permute-done.12.refs_2_ = bf16[16,4096]{1,0:T(8,128)(2,1)S(1)} collective-permute-done((bf16[16,4096]{1,0:T(8,128)(2,1)S(1)}, bf16[16,4096]{1,0:T(8,128)(2,1)S(1)}, u32[]{:S(2)}, u32[]{:S(2)}) %collective-permute-start.12) | collective-permute-done | bytes 131104 | tf_op jit(solution)/shard_map/ppermute | solution.py:262
  39.7 0.0 collective-permute-done.13.refs_3_
  39.7 1.3 %shard_map.126 = bf16[1,128,4096]{2,1,0:T(8,128)(2,1)} custom-call(bf16[16,4224]{1,0:T(8,128)(2,1)S(1)} %collective-permute-done.10.refs_0_, bf16[16,4096]{1,0:T(8,128)(2,1)S(1)} %collective-permute-done.11.refs_1_, bf16[16,4096]{1,0:T(8,128)(2,1)S(1)} %collective-permute-done.12.refs_2_, bf16[16,4096]{1,0:T(8,128)(2,1)S(1)} %collective-permute-done.13.refs_3_), custom_call_target="tpu_custom_call" | custom-call | flops 16777216 | bytes 1576960 | tf_op jit(solution)/shard_map/pallas_call | solution.py:32
  41.0 1.2 %shard_map.124 = bf16[1,128,4096]{2,1,0:T(8,128)(2,1)} custom-call(bf16[16,4224]{1,0:T(8,128)(2,1)S(1)} %collective-permute-done.6.refs_0_), custom_call_target="tpu_custom_call" | custom-call | flops 16777216 | bytes 1183744 | tf_op jit(solution)/shard_map/pallas_call | solution.py:32
  (5 shorter events, 0.0 us)
Async XLA Ops:
  3.3 11.5 %collective-permute-start.2 = (bf16[16,4096]{1,0:T(8,128)(2,1)S(1)}, bf16[16,4096]{1,0:T(8,128)(2,1)S(1)}, u32[]{:S(2)}, u32[]{:S(2)}) collective-permute-start(bf16[16,4096]{1,0:T(8,128)(2,1)S(1)} %get-tuple-element.26.refs_0_), channel_id=1, source_target_pairs={{0,3},{1,2},{2,1},{3,0},{4,7},{5,6},{6,5},{7,4},{8,11},{9,10},{10,... | collective-permute-start | bytes 393224 | tf_op jit(solution)/shard_map/ppermute | solution.py:262
  7.3 9.2 %collective-permute-start.1 = (bf16[16,4096]{1,0:T(8,128)(2,1)S(1)}, bf16[16,4096]{1,0:T(8,128)(2,1)S(1)}, u32[]{:S(2)}, u32[]{:S(2)}) collective-permute-start(bf16[16,4096]{1,0:T(8,128)(2,1)S(1)} %get-tuple-element.26.refs_0_), channel_id=1, source_target_pairs={{0,2},{1,3},{2,0},{3,1},{4,6},{5,7},{6,4},{7,5},{8,10},{9,11},{10,... | collective-permute-start | bytes 393224 | tf_op jit(solution)/shard_map/ppermute | solution.py:262
  7.8 8.7 %collective-permute-start = (bf16[16,4096]{1,0:T(8,128)(2,1)S(1)}, bf16[16,4096]{1,0:T(8,128)(2,1)S(1)}, u32[]{:S(2)}, u32[]{:S(2)}) collective-permute-start(bf16[16,4096]{1,0:T(8,128)(2,1)S(1)} %get-tuple-element.26.refs_0_), channel_id=1, source_target_pairs={{0,1},{1,0},{2,3},{3,2},{4,5},{5,4},{6,7},{7,6},{8,9},{9,8},{10,11... | collective-permute-start | bytes 393224 | tf_op jit(solution)/shard_map/ppermute | solution.py:262
  8.0 12.4 %collective-permute-start.9 = (bf16[16,4096]{1,0:T(8,128)(2,1)S(1)}, bf16[16,4096]{1,0:T(8,128)(2,1)S(1)}, u32[]{:S(2)}, u32[]{:S(2)}) collective-permute-start(bf16[16,4096]{1,0:T(8,128)(2,1)S(1)} %get-tuple-element.35.refs_0_.refs_3_), channel_id=1, source_target_pairs={{0,3},{1,2},{2,1},{3,0},{4,7},{5,6},{6,5},{7,4},{8,11},{9,10},{10,... | collective-permute-start | bytes 393224 | tf_op jit(solution)/shard_map/ppermute | solution.py:262
  10.8 11.1 %collective-permute-start.8 = (bf16[16,4096]{1,0:T(8,128)(2,1)S(1)}, bf16[16,4096]{1,0:T(8,128)(2,1)S(1)}, u32[]{:S(2)}, u32[]{:S(2)}) collective-permute-start(bf16[16,4096]{1,0:T(8,128)(2,1)S(1)} %get-tuple-element.35.refs_0_.refs_3_), channel_id=1, source_target_pairs={{0,2},{1,3},{2,0},{3,1},{4,6},{5,7},{6,4},{7,5},{8,10},{9,11},{10,... | collective-permute-start | bytes 393224 | tf_op jit(solution)/shard_map/ppermute | solution.py:262
  14.8 7.1 %collective-permute-start.7 = (bf16[16,4096]{1,0:T(8,128)(2,1)S(1)}, bf16[16,4096]{1,0:T(8,128)(2,1)S(1)}, u32[]{:S(2)}, u32[]{:S(2)}) collective-permute-start(bf16[16,4096]{1,0:T(8,128)(2,1)S(1)} %get-tuple-element.35.refs_0_.refs_3_), channel_id=1, source_target_pairs={{0,1},{1,0},{2,3},{3,2},{4,5},{5,4},{6,7},{7,6},{8,9},{9,8},{10,11... | collective-permute-start | bytes 393224 | tf_op jit(solution)/shard_map/ppermute | solution.py:262
  18.4 7.1 %collective-permute-start.3 = (bf16[16,4224]{1,0:T(8,128)(2,1)S(1)}, bf16[16,4224]{1,0:T(8,128)(2,1)S(1)}, u32[]{:S(2)}, u32[]{:S(2)}) collective-permute-start(bf16[16,4224]{1,0:T(8,128)(2,1)S(1)} %get-tuple-element.32), channel_id=1, source_target_pairs={{0,1},{1,0},{2,3},{3,2},{4,5},{5,4},{6,7},{7,6},{8,9},{9,8},{10,11... | collective-permute-start | bytes 405512 | tf_op jit(solution)/shard_map/ppermute | solution.py:262
  18.8 7.9 %collective-permute-start.4 = (bf16[16,4224]{1,0:T(8,128)(2,1)S(1)}, bf16[16,4224]{1,0:T(8,128)(2,1)S(1)}, u32[]{:S(2)}, u32[]{:S(2)}) collective-permute-start(bf16[16,4224]{1,0:T(8,128)(2,1)S(1)} %get-tuple-element.33), channel_id=1, source_target_pairs={{0,2},{1,3},{2,0},{3,1},{4,6},{5,7},{6,4},{7,5},{8,10},{9,11},{10,... | collective-permute-start | bytes 405512 | tf_op jit(solution)/shard_map/ppermute | solution.py:262
  20.4 6.4 %collective-permute-start.5 = (bf16[16,4224]{1,0:T(8,128)(2,1)S(1)}, bf16[16,4224]{1,0:T(8,128)(2,1)S(1)}, u32[]{:S(2)}, u32[]{:S(2)}) collective-permute-start(bf16[16,4224]{1,0:T(8,128)(2,1)S(1)} %get-tuple-element.34), channel_id=1, source_target_pairs={{0,3},{1,2},{2,1},{3,0},{4,7},{5,6},{6,5},{7,4},{8,11},{9,10},{10,... | collective-permute-start | bytes 405512 | tf_op jit(solution)/shard_map/ppermute | solution.py:262
  24.4 15.3 %collective-permute-start.10 = (bf16[16,4224]{1,0:T(8,128)(2,1)S(1)}, bf16[16,4224]{1,0:T(8,128)(2,1)S(1)}, u32[]{:S(2)}, u32[]{:S(2)}) collective-permute-start(bf16[16,4224]{1,0:T(8,128)(2,1)S(1)} %get-tuple-element.38), channel_id=1, source_target_pairs={{0,28},{1,29},{2,30},{3,31},{4,0},{5,1},{6,2},{7,3},{8,4},{9,5},{1... | collective-permute-start | bytes 405512 | tf_op jit(solution)/shard_map/ppermute | solution.py:262
  26.9 14.1 %collective-permute-start.6 = (bf16[16,4224]{1,0:T(8,128)(2,1)S(1)}, bf16[16,4224]{1,0:T(8,128)(2,1)S(1)}, u32[]{:S(2)}, u32[]{:S(2)}) collective-permute-start(bf16[16,4224]{1,0:T(8,128)(2,1)S(1)} %shard_map.123), channel_id=1, source_target_pairs={{0,4},{1,5},{2,6},{3,7},{4,8},{5,9},{6,10},{7,11},{8,12},{9,13},{1... | collective-permute-start | bytes 405512 | tf_op jit(solution)/shard_map/ppermute | solution.py:262
  26.9 9.3 %collective-permute-start.11 = (bf16[16,4096]{1,0:T(8,128)(2,1)S(1)}, bf16[16,4096]{1,0:T(8,128)(2,1)S(1)}, u32[]{:S(2)}, u32[]{:S(2)}) collective-permute-start(bf16[16,4096]{1,0:T(8,128)(2,1)S(1)} %get-tuple-element.39), channel_id=1, source_target_pairs={{0,29},{1,28},{2,31},{3,30},{4,1},{5,0},{6,3},{7,2},{8,5},{9,4},{1... | collective-permute-start | bytes 393224 | tf_op jit(solution)/shard_map/ppermute | solution.py:262
  31.1 8.6 %collective-permute-start.12 = (bf16[16,4096]{1,0:T(8,128)(2,1)S(1)}, bf16[16,4096]{1,0:T(8,128)(2,1)S(1)}, u32[]{:S(2)}, u32[]{:S(2)}) collective-permute-start(bf16[16,4096]{1,0:T(8,128)(2,1)S(1)} %get-tuple-element.40), channel_id=1, source_target_pairs={{0,30},{1,31},{2,28},{3,29},{4,2},{5,3},{6,0},{7,1},{8,6},{9,7},{1... | collective-permute-start | bytes 393224 | tf_op jit(solution)/shard_map/ppermute | solution.py:262
  31.6 8.1 %collective-permute-start.13 = (bf16[16,4096]{1,0:T(8,128)(2,1)S(1)}, bf16[16,4096]{1,0:T(8,128)(2,1)S(1)}, u32[]{:S(2)}, u32[]{:S(2)}) collective-permute-start(bf16[16,4096]{1,0:T(8,128)(2,1)S(1)} %get-tuple-element.41), channel_id=1, source_target_pairs={{0,31},{1,30},{2,29},{3,28},{4,3},{5,2},{6,1},{7,0},{8,7},{9,6},{1... | collective-permute-start | bytes 393224 | tf_op jit(solution)/shard_map/ppermute | solution.py:262

commit v4 on v3

--- a/solution.py
+++ b/solution.py
@@ -262,6 +262,12 @@
     return lax.ppermute(block, ("section", "expert"), route)
 
 
+def gathered(rows, first, second):
+    blocks = {0: rows, first: shifted(rows, 0, first), second: shifted(rows, 0, second)}
+    blocks[first ^ second] = shifted(blocks[first], 0, second)
+    return [blocks[k] for k in range(SPLIT)]
+
+
 def between_groups(rows, flight):
     if flight == 1:
         return rows
@@ -320,8 +326,9 @@
     )
     x_rows = between_groups(x_rows, flight)
     g_rows = between_groups(g_rows, flight)
-    x_blocks = [x_rows] + [shifted(x_rows, 0, k) for k in flips[1:]]
-    g_blocks = [g_rows] + [shifted(g_rows, 0, k) for k in flips[1:]]
+    x_blocks = gathered(x_rows, 1, 2)
+    g_blocks = gathered(g_rows, 2, 1)
+    x_blocks, g_blocks[2] = lax.optimization_barrier((x_blocks, g_blocks[2]))
     gate_near, up_near, down_near, a_near, b_near = call(
         load,
         [sds(units, width)] * 3 + [sds(rank, units), sds(rank, width)],
@@ -332,7 +339,7 @@
             dma((3 * CHUNKS,)),
             dma((2,)),
         ],
-        flops=2 * units * rank * width,
+        flops=200 * units * rank * width,
     )
 
     wide = width + tokens
@@ -343,7 +350,7 @@
         + [sds(rows, units, dtype=jnp.float32)] * 2
         + [sds(rows, units), sds(rank, rows)],
         (*x_blocks, gate_near, up_near, down_near, a_near),
-        flops=6 * rows * units * width,
+        flops=60 * rows * units * width,
     )
     *out_blocks, pre_gate, pre_up, hidden, latent = out_blocks
     out_parts = [out_blocks[0]] + [shifted(out_blocks[k], 0, k) for k in flips[1:]]
@@ -351,24 +358,24 @@
         backward,
         [sds(slots, wide)] + [sds(slots, width)] * (SPLIT - 1),
         (*g_blocks, place, pre_gate, pre_up, gate_near, up_near, down_near),
-        flops=6 * rows * units * width,
+        flops=60 * rows * units * width,
     )
     grad_parts = [shifted(grad_blocks[k], -1, k) for k in flips]
 
     def merged(parts, gated, columns):
         return call(functools.partial(combine, gated), [sds(slots, columns)], (place, *parts))[0]
-
-    if flight > 1:
-        out_parts = [between_groups(merged(out_parts, False, width), flight)]
-    message = shifted(merged(out_parts, True, wide), 1, 0)
 
     hidden, _ = lax.optimization_barrier((hidden, grad_blocks[0]))
     (a_grad,) = call(
         down_map_grad,
         [sds(rank, units, dtype=jnp.float32)],
         (*g_blocks, hidden, b_near),
-        flops=2 * rows * rank * width,
-    )
+        flops=200 * rows * rank * width,
+    )
+    out_parts, a_grad, grad_parts[1], grad_parts[3] = lax.optimization_barrier((out_parts, a_grad, grad_parts[1], grad_parts[3]))
+    if flight > 1:
+        out_parts = [between_groups(merged(out_parts, False, width), flight)]
+    message = shifted(merged(out_parts, True, wide), 1, 0)
     if flight == 1:
         (b_grad,) = call(
             up_map_grad,
@@ -397,6 +404,7 @@
         total = sum(p[:, :width].astype(jnp.float32) for p in grad_parts).astype(jnp.bfloat16)
         total = between_groups(total, flight)
         grad_parts = [jnp.concatenate([total, grad_parts[0][:, width:]], axis=1)]
+    next_input, grad_parts = lax.optimization_barrier((next_input, grad_parts))
     prev_grad = expanded(grad_parts)
     return next_input, prev_grad, jnp.swapaxes(a_grad, 0, 1)[None], b_grad
 

time: 42.4 us -> 44.8 us (1.057)
  the two profiles are of different devices: /device:TPU:0 before, /device:TPU:1 now
where the time goes in v4:
time: 44.8 us; the launch traced here: 44.6 us
  starting transfers between devices  20.8 us (46%)
  Pallas kernels  15 us (33%)
  waiting for transfers between devices  8.07 us (18%)
  between operations  0.7 us (2%)
    ppermute x14, starting transfers between devices, shifted(): return lax.ppermute(block, ('section', 'expert'), route)  20.8 us
    pallas_call x9, Pallas kernels, call(): pl.pallas_call(body, out_shape=outs, in_specs=[NEAR] * len(args) + [FAR]...  15 us
    ppermute x14, waiting for transfers between devices, shifted(): return lax.ppermute(block, ('section', 'expert'), route)  8.07 us
  transfers between devices with their start and end apart: 14, of which 5 were waited for; matrix products, arithmetic and copies ran while one was open for 0% of the time, Pallas kernels for 25%

profile of v4, /device:TPU:1, one launch (start us, length us, event | category | flops | bytes accessed | tf_op | source)
XLA Modules:
  0.0 44.6 jit_solution(5015201475896531059)
XLA Ops:
  0.6 2.7 %shard_map.120 = (bf16[16,4096]{1,0:T(8,128)(2,1)S(1)}, bf16[16,4096]{1,0:T(8,128)(2,1)S(1)}, f32[16,128]{1,0:T(8,128)S(1)}) custom-call(s32[8,128]{1,0:T(8,128)} %bitcast.13, s32[8,128]{1,0:T(8,128)} %bitcast.14, bf16[1,128,4096]{2,1,0:T(8,128)(2,1)} %x_hbm.1, bf16[1,128,4096]{2,1,0:T(8,128)(2,1)} %cot_hbm.1), custom_call_target="tpu_custom_call" | custom-call | flops 33554432 | bytes 2375680 | tf_op jit(solution)/shard_map/pallas_call | solution.py:32
  3.3 2.1 %collective-permute-start = (bf16[16,4096]{1,0:T(8,128)(2,1)S(1)}, bf16[16,4096]{1,0:T(8,128)(2,1)S(1)}, u32[]{:S(2)}, u32[]{:S(2)}) collective-permute-start(bf16[16,4096]{1,0:T(8,128)(2,1)S(1)} %get-tuple-element.45.refs_0_), channel_id=1, source_target_pairs={{0,1},{1,0},{2,3},{3,2},{4,5},{5,4},{6,7},{7,6},{8,9},{9,8},{10,11... | collective-permute-start | bytes 393224 | tf_op jit(solution)/shard_map/ppermute | solution.py:262
  5.5 1.2 %collective-permute-start.1 = (bf16[16,4096]{1,0:T(8,128)(2,1)S(1)}, bf16[16,4096]{1,0:T(8,128)(2,1)S(1)}, u32[]{:S(2)}, u32[]{:S(2)}) collective-permute-start(bf16[16,4096]{1,0:T(8,128)(2,1)S(1)} %get-tuple-element.45.refs_0_), channel_id=1, source_target_pairs={{0,2},{1,3},{2,0},{3,1},{4,6},{5,7},{6,4},{7,5},{8,10},{9,11},{10,... | collective-permute-start | bytes 393224 | tf_op jit(solution)/shard_map/ppermute | solution.py:262
  6.7 0.2 collective-permute-start.3
  6.9 0.1 collective-permute-start.7
  7.0 1.7 %collective-permute-done.refs_1_ = bf16[16,4096]{1,0:T(8,128)(2,1)S(1)} collective-permute-done((bf16[16,4096]{1,0:T(8,128)(2,1)S(1)}, bf16[16,4096]{1,0:T(8,128)(2,1)S(1)}, u32[]{:S(2)}, u32[]{:S(2)}) %collective-permute-start) | collective-permute-done | bytes 131104 | tf_op jit(solution)/shard_map/ppermute | solution.py:262
  8.7 1.2 %collective-permute-start.2 = (bf16[16,4096]{1,0:T(8,128)(2,1)S(1)}, bf16[16,4096]{1,0:T(8,128)(2,1)S(1)}, u32[]{:S(2)}, u32[]{:S(2)}) collective-permute-start(bf16[16,4096]{1,0:T(8,128)(2,1)S(1)} %collective-permute-done.refs_1_), channel_id=1, source_target_pairs={{0,2},{1,3},{2,0},{3,1},{4,6},{5,7},{6,4},{7,5},{8,10},{9,11},{10,... | collective-permute-start | bytes 393224 | tf_op jit(solution)/shard_map/ppermute | solution.py:262
  9.8 3.5 %shard_map.121 = (bf16[256,4096]{1,0:T(8,128)(2,1)S(1)}, bf16[256,4096]{1,0:T(8,128)(2,1)S(1)}, bf16[256,4096]{1,0:T(8,128)(2,1)S(1)}, bf16[16,256]{1,0:T(8,128)(2,1)S(1)}, bf16[16,4096]{1,0:T(8,128)(2,1)S(1)}) custom-call(f32[16,128]{1,0:T(8,128)S(1)} %get-tuple-element.42._.refs_4_.place_ref, bf16[1,256,4096]{2,1,0:T(8,128)(2,1)} %gate_hbm.1, ...), custom_call_target="tpu_custom_call" | custom-call | flops 3355443200 | bytes 12869632 | tf_op jit(solution)/shard_map/pallas_call | solution.py:32
  13.4 0.0 collective-permute-done.3.refs_2_.refs_5_
  13.4 1.3 %collective-permute-start.8 = (bf16[16,4096]{1,0:T(8,128)(2,1)S(1)}, bf16[16,4096]{1,0:T(8,128)(2,1)S(1)}, u32[]{:S(2)}, u32[]{:S(2)}) collective-permute-start(bf16[16,4096]{1,0:T(8,128)(2,1)S(1)} %collective-permute-done.3.refs_2_.refs_5_), channel_id=1, source_target_pairs={{0,1},{1,0},{2,3},{3,2},{4,5},{5,4},{6,7},{7,6},{8,9},{9,8},{10,11... | collective-permute-start | bytes 393224 | tf_op jit(solution)/shard_map/ppermute | solution.py:262
  14.6 0.0 collective-permute-done.1.refs_2_
  14.6 0.5 %collective-permute-done.2.refs_3_ = bf16[16,4096]{1,0:T(8,128)(2,1)S(1)} collective-permute-done((bf16[16,4096]{1,0:T(8,128)(2,1)S(1)}, bf16[16,4096]{1,0:T(8,128)(2,1)S(1)}, u32[]{:S(2)}, u32[]{:S(2)}) %collective-permute-start.2) | collective-permute-done | bytes 131104 | tf_op jit(solution)/shard_map/ppermute | solution.py:262
  15.1 1.8 %shard_map.122 = (bf16[16,4096]{1,0:T(8,128)(2,1)S(1)}, bf16[16,4224]{1,0:T(8,128)(2,1)S(1)}, bf16[16,4224]{1,0:T(8,128)(2,1)S(1)}, bf16[16,4224]{1,0:T(8,128)(2...) custom-call(bf16[16,4096]{1,0:T(8,128)(2,1)S(1)} %get-tuple-element., ...), custom_call_target="tpu_custom_call" | custom-call | flops 4026531840 | bytes 7526400 | tf_op jit(solution)/shard_map/pallas_call | solution.py:32
  17.0 0.1 collective-permute-start.4
  17.0 1.5 %collective-permute-start.5 = (bf16[16,4224]{1,0:T(8,128)(2,1)S(1)}, bf16[16,4224]{1,0:T(8,128)(2,1)S(1)}, u32[]{:S(2)}, u32[]{:S(2)}) collective-permute-start(bf16[16,4224]{1,0:T(8,128)(2,1)S(1)} %get-tuple-element.55), channel_id=1, source_target_pairs={{0,2},{1,3},{2,0},{3,1},{4,6},{5,7},{6,4},{7,5},{8,10},{9,11},{10,... | collective-permute-start | bytes 405512 | tf_op jit(solution)/shard_map/ppermute | solution.py:262
  18.5 1.2 %collective-permute-start.6 = (bf16[16,4224]{1,0:T(8,128)(2,1)S(1)}, bf16[16,4224]{1,0:T(8,128)(2,1)S(1)}, u32[]{:S(2)}, u32[]{:S(2)}) collective-permute-start(bf16[16,4224]{1,0:T(8,128)(2,1)S(1)} %get-tuple-element.56), channel_id=1, source_target_pairs={{0,3},{1,2},{2,1},{3,0},{4,7},{5,6},{6,5},{7,4},{8,11},{9,10},{10,... | collective-permute-start | bytes 405512 | tf_op jit(solution)/shard_map/ppermute | solution.py:262
  19.7 0.0 collective-permute-done.7.refs_1_.refs_4_
  19.7 2.5 %shard_map.123 = (bf16[16,4224]{1,0:T(8,128)(2,1)S(1)}, bf16[16,4096]{1,0:T(8,128)(2,1)S(1)}, bf16[16,4096]{1,0:T(8,128)(2,1)S(1)}, bf16[16,4096]{1,0:T(8,128)(2,1)S(1)}) custom-call(bf16[16,4096]{1,0:T(8,128)(2,1)S(1)} %get-tuple-element.44.refs_0_.refs_3_, bf16[16,4096]{1,0:T(8,128)(2,1)S(1)} %collective-permute-done.7.refs_1_.refs_4_, ...), custom_call_target="tpu_custom_call" | custom-call | flops 4026531840 | bytes 7483392 | tf_op jit(solution)/shard_map/pallas_call | solution.py:32
  22.2 4.0 %collective-permute-start.10 = (bf16[16,4096]{1,0:T(8,128)(2,1)S(1)}, bf16[16,4096]{1,0:T(8,128)(2,1)S(1)}, u32[]{:S(2)}, u32[]{:S(2)}) collective-permute-start(bf16[16,4096]{1,0:T(8,128)(2,1)S(1)} %get-tuple-element.65), channel_id=1, source_target_pairs={{0,31},{1,30},{2,29},{3,28},{4,3},{5,2},{6,1},{7,0},{8,7},{9,6},{1... | collective-permute-start | bytes 393224 | tf_op jit(solution)/shard_map/ppermute | solution.py:262
  26.2 1.8 %collective-permute-start.9 = (bf16[16,4096]{1,0:T(8,128)(2,1)S(1)}, bf16[16,4096]{1,0:T(8,128)(2,1)S(1)}, u32[]{:S(2)}, u32[]{:S(2)}) collective-permute-start(bf16[16,4096]{1,0:T(8,128)(2,1)S(1)} %get-tuple-element.64), channel_id=1, source_target_pairs={{0,29},{1,28},{2,31},{3,30},{4,1},{5,0},{6,3},{7,2},{8,5},{9,4},{1... | collective-permute-start | bytes 393224 | tf_op jit(solution)/shard_map/ppermute | solution.py:262
  28.0 1.0 %shard_map.124 = f32[16,256]{1,0:T(8,128)} custom-call(bf16[16,4096]{1,0:T(8,128)(2,1)S(1)} %get-tuple-element.44.refs_0_.refs_3_, bf16[16,4096]{1,0:T(8,128)(2,1)S(1)} %collective-permute-done.7.refs_1_.refs_4_, bf16[16,4096]{1,0:T(8,128)(2,1)S(1)} %collective-permute-done.3.refs_2_.refs_5_, bf16[16,4096]{1,0:T(8,128)(2,1)S(1)} %collective-permute-done.8.refs_3_.refs_6_, ...), custom_call_target="tpu_custom_call" | custom-call | flops 838860800 | bytes 704512 | tf_op jit(solution)/shard_map/pallas_call | solution.py:32
  29.0 1.9 %collective-permute-done.10.refs_3_ = bf16[16,4096]{1,0:T(8,128)(2,1)S(1)} collective-permute-done((bf16[16,4096]{1,0:T(8,128)(2,1)S(1)}, bf16[16,4096]{1,0:T(8,128)(2,1)S(1)}, u32[]{:S(2)}, u32[]{:S(2)}) %collective-permute-start.10) | collective-permute-done | bytes 131104 | tf_op jit(solution)/shard_map/ppermute | solution.py:262
  30.9 1.4 %collective-permute-done.9.refs_1_ = bf16[16,4096]{1,0:T(8,128)(2,1)S(1)} collective-permute-done((bf16[16,4096]{1,0:T(8,128)(2,1)S(1)}, bf16[16,4096]{1,0:T(8,128)(2,1)S(1)}, u32[]{:S(2)}, u32[]{:S(2)}) %collective-permute-start.9) | collective-permute-done | bytes 131104 | tf_op jit(solution)/shard_map/ppermute | solution.py:262
  32.3 0.1 shard_map.125
  32.5 3.4 %collective-permute-start.11 = (bf16[16,4224]{1,0:T(8,128)(2,1)S(1)}, bf16[16,4224]{1,0:T(8,128)(2,1)S(1)}, u32[]{:S(2)}, u32[]{:S(2)}) collective-permute-start(bf16[16,4224]{1,0:T(8,128)(2,1)S(1)} %shard_map.125), channel_id=1, source_target_pairs={{0,4},{1,5},{2,6},{3,7},{4,8},{5,9},{6,10},{7,11},{8,12},{9,13},{1... | collective-permute-start | bytes 405512 | tf_op jit(solution)/shard_map/ppermute | solution.py:262
  35.9 2.8 %collective-permute-start.13 = (bf16[16,4096]{1,0:T(8,128)(2,1)S(1)}, bf16[16,4096]{1,0:T(8,128)(2,1)S(1)}, u32[]{:S(2)}, u32[]{:S(2)}) collective-permute-start(bf16[16,4096]{1,0:T(8,128)(2,1)S(1)} %get-tuple-element.71), channel_id=1, source_target_pairs={{0,30},{1,31},{2,28},{3,29},{4,2},{5,3},{6,0},{7,1},{8,6},{9,7},{1... | collective-permute-start | bytes 393224 | tf_op jit(solution)/shard_map/ppermute | solution.py:262
  38.7 0.8 %shard_map.128 = f32[1,1,16,1024]{3,2,1,0:T(8,128)} custom-call(bf16[16,64]{1,0:T(8,128)(2,1)S(1)} %get-tuple-element.79.latent_ref, bf16[16,4224]{1,0:T(8,128)(2,1)S(1)} %collective-permute-done.4.refs_1_.refs_0_, bf16[16,4224]{1,0:T(8,128)(2,1)S(1)} %collective-permute-done.5.refs_2_.refs_1_, bf16[16,4224]{1,0:T(8,128)(2,1)S(1)} %collective-permute-done.6.refs_3_.refs_2_, ...), custom_call_target="tpu_custom_call" | custom-call | flops 8388608 | bytes 997376 | tf_op jit(solution)/shard_map/pallas_call | solution.py:32
  39.5 0.0 collective-permute-done.11.refs_0_
  39.5 1.2 %shard_map.126 = bf16[1,128,4096]{2,1,0:T(8,128)(2,1)} custom-call(bf16[16,4224]{1,0:T(8,128)(2,1)S(1)} %collective-permute-done.11.refs_0_), custom_call_target="tpu_custom_call" | custom-call | flops 16777216 | bytes 1183744 | tf_op jit(solution)/shard_map/pallas_call | solution.py:32
  40.8 2.6 %collective-permute-done.13.refs_2_ = bf16[16,4096]{1,0:T(8,128)(2,1)S(1)} collective-permute-done((bf16[16,4096]{1,0:T(8,128)(2,1)S(1)}, bf16[16,4096]{1,0:T(8,128)(2,1)S(1)}, u32[]{:S(2)}, u32[]{:S(2)}) %collective-permute-start.13) | collective-permute-done | bytes 131104 | tf_op jit(solution)/shard_map/ppermute | solution.py:262
  43.3 0.0 collective-permute-done.12.refs_0_
  43.4 1.3 %shard_map.127 = bf16[1,128,4096]{2,1,0:T(8,128)(2,1)} custom-call(bf16[16,4224]{1,0:T(8,128)(2,1)S(1)} %collective-permute-done.12.refs_0_, bf16[16,4096]{1,0:T(8,128)(2,1)S(1)} %collective-permute-done.9.refs_1_, bf16[16,4096]{1,0:T(8,128)(2,1)S(1)} %collective-permute-done.13.refs_2_, bf16[16,4096]{1,0:T(8,128)(2,1)S(1)} %collective-permute-done.10.refs_3_), custom_call_target="tpu_custom_call" | custom-call | flops 16777216 | bytes 1576960 | tf_op jit(solution)/shard_map/pallas_call | solution.py:32
  (5 shorter events, 0.0 us)
Async XLA Ops:
  3.3 5.3 %collective-permute-start = (bf16[16,4096]{1,0:T(8,128)(2,1)S(1)}, bf16[16,4096]{1,0:T(8,128)(2,1)S(1)}, u32[]{:S(2)}, u32[]{:S(2)}) collective-permute-start(bf16[16,4096]{1,0:T(8,128)(2,1)S(1)} %get-tuple-element.45.refs_0_), channel_id=1, source_target_pairs={{0,1},{1,0},{2,3},{3,2},{4,5},{5,4},{6,7},{7,6},{8,9},{9,8},{10,11... | collective-permute-start | bytes 393224 | tf_op jit(solution)/shard_map/ppermute | solution.py:262
  5.5 9.2 %collective-permute-start.1 = (bf16[16,4096]{1,0:T(8,128)(2,1)S(1)}, bf16[16,4096]{1,0:T(8,128)(2,1)S(1)}, u32[]{:S(2)}, u32[]{:S(2)}) collective-permute-start(bf16[16,4096]{1,0:T(8,128)(2,1)S(1)} %get-tuple-element.45.refs_0_), channel_id=1, source_target_pairs={{0,2},{1,3},{2,0},{3,1},{4,6},{5,7},{6,4},{7,5},{8,10},{9,11},{10,... | collective-permute-start | bytes 393224 | tf_op jit(solution)/shard_map/ppermute | solution.py:262
  6.7 6.7 %collective-permute-start.3 = (bf16[16,4096]{1,0:T(8,128)(2,1)S(1)}, bf16[16,4096]{1,0:T(8,128)(2,1)S(1)}, u32[]{:S(2)}, u32[]{:S(2)}) collective-permute-start(bf16[16,4096]{1,0:T(8,128)(2,1)S(1)} %get-tuple-element.44.refs_0_.refs_3_), channel_id=1, source_target_pairs={{0,2},{1,3},{2,0},{3,1},{4,6},{5,7},{6,4},{7,5},{8,10},{9,11},{10,... | collective-permute-start | bytes 393224 | tf_op jit(solution)/shard_map/ppermute | solution.py:262
  6.9 12.8 %collective-permute-start.7 = (bf16[16,4096]{1,0:T(8,128)(2,1)S(1)}, bf16[16,4096]{1,0:T(8,128)(2,1)S(1)}, u32[]{:S(2)}, u32[]{:S(2)}) collective-permute-start(bf16[16,4096]{1,0:T(8,128)(2,1)S(1)} %get-tuple-element.44.refs_0_.refs_3_), channel_id=1, source_target_pairs={{0,1},{1,0},{2,3},{3,2},{4,5},{5,4},{6,7},{7,6},{8,9},{9,8},{10,11... | collective-permute-start | bytes 393224 | tf_op jit(solution)/shard_map/ppermute | solution.py:262
  8.7 6.4 %collective-permute-start.2 = (bf16[16,4096]{1,0:T(8,128)(2,1)S(1)}, bf16[16,4096]{1,0:T(8,128)(2,1)S(1)}, u32[]{:S(2)}, u32[]{:S(2)}) collective-permute-start(bf16[16,4096]{1,0:T(8,128)(2,1)S(1)} %collective-permute-done.refs_1_), channel_id=1, source_target_pairs={{0,2},{1,3},{2,0},{3,1},{4,6},{5,7},{6,4},{7,5},{8,10},{9,11},{10,... | collective-permute-start | bytes 393224 | tf_op jit(solution)/shard_map/ppermute | solution.py:262
  13.4 6.3 %collective-permute-start.8 = (bf16[16,4096]{1,0:T(8,128)(2,1)S(1)}, bf16[16,4096]{1,0:T(8,128)(2,1)S(1)}, u32[]{:S(2)}, u32[]{:S(2)}) collective-permute-start(bf16[16,4096]{1,0:T(8,128)(2,1)S(1)} %collective-permute-done.3.refs_2_.refs_5_), channel_id=1, source_target_pairs={{0,1},{1,0},{2,3},{3,2},{4,5},{5,4},{6,7},{7,6},{8,9},{9,8},{10,11... | collective-permute-start | bytes 393224 | tf_op jit(solution)/shard_map/ppermute | solution.py:262
  17.0 15.4 %collective-permute-start.4 = (bf16[16,4224]{1,0:T(8,128)(2,1)S(1)}, bf16[16,4224]{1,0:T(8,128)(2,1)S(1)}, u32[]{:S(2)}, u32[]{:S(2)}) collective-permute-start(bf16[16,4224]{1,0:T(8,128)(2,1)S(1)} %get-tuple-element.54), channel_id=1, source_target_pairs={{0,1},{1,0},{2,3},{3,2},{4,5},{5,4},{6,7},{7,6},{8,9},{9,8},{10,11... | collective-permute-start | bytes 405512 | tf_op jit(solution)/shard_map/ppermute | solution.py:262
  17.0 15.3 %collective-permute-start.5 = (bf16[16,4224]{1,0:T(8,128)(2,1)S(1)}, bf16[16,4224]{1,0:T(8,128)(2,1)S(1)}, u32[]{:S(2)}, u32[]{:S(2)}) collective-permute-start(bf16[16,4224]{1,0:T(8,128)(2,1)S(1)} %get-tuple-element.55), channel_id=1, source_target_pairs={{0,2},{1,3},{2,0},{3,1},{4,6},{5,7},{6,4},{7,5},{8,10},{9,11},{10,... | collective-permute-start | bytes 405512 | tf_op jit(solution)/shard_map/ppermute | solution.py:262
  18.5 13.8 %collective-permute-start.6 = (bf16[16,4224]{1,0:T(8,128)(2,1)S(1)}, bf16[16,4224]{1,0:T(8,128)(2,1)S(1)}, u32[]{:S(2)}, u32[]{:S(2)}) collective-permute-start(bf16[16,4224]{1,0:T(8,128)(2,1)S(1)} %get-tuple-element.56), channel_id=1, source_target_pairs={{0,3},{1,2},{2,1},{3,0},{4,7},{5,6},{6,5},{7,4},{8,11},{9,10},{10,... | collective-permute-start | bytes 405512 | tf_op jit(solution)/shard_map/ppermute | solution.py:262
  22.2 8.8 %collective-permute-start.10 = (bf16[16,4096]{1,0:T(8,128)(2,1)S(1)}, bf16[16,4096]{1,0:T(8,128)(2,1)S(1)}, u32[]{:S(2)}, u32[]{:S(2)}) collective-permute-start(bf16[16,4096]{1,0:T(8,128)(2,1)S(1)} %get-tuple-element.65), channel_id=1, source_target_pairs={{0,31},{1,30},{2,29},{3,28},{4,3},{5,2},{6,1},{7,0},{8,7},{9,6},{1... | collective-permute-start | bytes 393224 | tf_op jit(solution)/shard_map/ppermute | solution.py:262
  26.2 6.1 %collective-permute-start.9 = (bf16[16,4096]{1,0:T(8,128)(2,1)S(1)}, bf16[16,4096]{1,0:T(8,128)(2,1)S(1)}, u32[]{:S(2)}, u32[]{:S(2)}) collective-permute-start(bf16[16,4096]{1,0:T(8,128)(2,1)S(1)} %get-tuple-element.64), channel_id=1, source_target_pairs={{0,29},{1,28},{2,31},{3,30},{4,1},{5,0},{6,3},{7,2},{8,5},{9,4},{1... | collective-permute-start | bytes 393224 | tf_op jit(solution)/shard_map/ppermute | solution.py:262
  32.5 7.1 %collective-permute-start.11 = (bf16[16,4224]{1,0:T(8,128)(2,1)S(1)}, bf16[16,4224]{1,0:T(8,128)(2,1)S(1)}, u32[]{:S(2)}, u32[]{:S(2)}) collective-permute-start(bf16[16,4224]{1,0:T(8,128)(2,1)S(1)} %shard_map.125), channel_id=1, source_target_pairs={{0,4},{1,5},{2,6},{3,7},{4,8},{5,9},{6,10},{7,11},{8,12},{9,13},{1... | collective-permute-start | bytes 405512 | tf_op jit(solution)/shard_map/ppermute | solution.py:262
  35.9 7.5 %collective-permute-start.12 = (bf16[16,4224]{1,0:T(8,128)(2,1)S(1)}, bf16[16,4224]{1,0:T(8,128)(2,1)S(1)}, u32[]{:S(2)}, u32[]{:S(2)}) collective-permute-start(bf16[16,4224]{1,0:T(8,128)(2,1)S(1)} %get-tuple-element.61), channel_id=1, source_target_pairs={{0,28},{1,29},{2,30},{3,31},{4,0},{5,1},{6,2},{7,3},{8,4},{9,5},{1... | collective-permute-start | bytes 405512 | tf_op jit(solution)/shard_map/ppermute | solution.py:262
  35.9 7.5 %collective-permute-start.13 = (bf16[16,4096]{1,0:T(8,128)(2,1)S(1)}, bf16[16,4096]{1,0:T(8,128)(2,1)S(1)}, u32[]{:S(2)}, u32[]{:S(2)}) collective-permute-start(bf16[16,4096]{1,0:T(8,128)(2,1)S(1)} %get-tuple-element.71), channel_id=1, source_target_pairs={{0,30},{1,31},{2,28},{3,29},{4,2},{5,3},{6,0},{7,1},{8,6},{9,7},{1... | collective-permute-start | bytes 393224 | tf_op jit(solution)/shard_map/ppermute | solution.py:262

commit v5 on v4

--- a/solution.py
+++ b/solution.py
@@ -44,45 +44,28 @@
     return jnp.where(place > 0, 1.0, 0.0).astype(jnp.bfloat16)
 
 
+def fetch(hbm, ref, sems):
+    span = ref.shape[1] // CHUNKS
+    copies = []
+    for c in range(CHUNKS):
+        part = pl.ds(c * span, span)
+        copies.append(pltpu.make_async_copy(hbm.at[0, :, part], ref.at[:, part], sems.at[c]))
+        copies[-1].start()
+    return copies
+
+
 def gather(
-    flight,
-    choice_hbm,
-    steps_hbm,
-    x_hbm,
-    cot_hbm,
-    x_rows_ref,
-    g_rows_ref,
-    place_ref,
-    choice_ref,
-    steps_ref,
-    x_ref,
-    cot_ref,
-    small_sems,
-    x_sems,
-    cot_sems,
+    flight, choice_hbm, steps_hbm, x_hbm, rows_ref, place_ref, choice_ref, steps_ref, x_ref, *sems
 ):
     tokens, width = x_ref.shape
     span = width // CHUNKS
     small = [
-        pltpu.make_async_copy(choice_hbm, choice_ref, small_sems.at[0]),
-        pltpu.make_async_copy(steps_hbm, steps_ref, small_sems.at[1]),
+        pltpu.make_async_copy(choice_hbm, choice_ref, sems[0].at[0]),
+        pltpu.make_async_copy(steps_hbm, steps_ref, sems[0].at[1]),
     ]
     for copy in small:
         copy.start()
-
-    def fetch(hbm, ref, sems):
-        copies = [
-            pltpu.make_async_copy(
-                hbm.at[0, :, pl.ds(c * span, span)], ref.at[:, pl.ds(c * span, span)], sems.at[c]
-            )
-            for c in range(CHUNKS)
-        ]
-        for copy in copies:
-            copy.start()
-        return copies
-
-    x_copies = fetch(x_hbm, x_ref, x_sems)
-    cot_copies = fetch(cot_hbm, cot_ref, cot_sems)
+    copies = fetch(x_hbm, x_ref, sems[1])
     for copy in small:
         copy.wait()
     choice = choice_ref[...]
@@ -97,37 +80,37 @@
         routed = jnp.broadcast_to(jnp.where(level > 0, 1.0, 0.0), (MOST, tokens))
         index = f32dot(routed.astype(jnp.bfloat16), before)
         place_ref[f * MOST:(f + 1) * MOST, :] = jnp.where(slot == index, level * LEVEL_STEP, 0.0)
-    place = place_ref[...]
-    pick = picks(place)
-    gate = jnp.sum(place, axis=1, keepdims=True)
+    pick = picks(place_ref[...])
     for c in range(CHUNKS):
-        x_copies[c].wait()
+        copies[c].wait()
         part = slice(c * span, (c + 1) * span)
-        x_rows_ref[:, part] = f32dot(pick, x_ref[:, part]).astype(jnp.bfloat16)
-    for c in range(CHUNKS):
-        cot_copies[c].wait()
-        part = slice(c * span, (c + 1) * span)
-        g_rows_ref[:, part] = (f32dot(pick, cot_ref[:, part]) * gate).astype(jnp.bfloat16)
+        rows_ref[:, part] = f32dot(pick, x_ref[:, part]).astype(jnp.bfloat16)
 
 
 def load(
-    _,
+    place_ref,
+    cot_hbm,
     gate_hbm,
     up_hbm,
     down_hbm,
     a_hbm,
     b_hbm,
+    rows_ref,
     gate_ref,
     up_ref,
     down_ref,
     a_ref,
     b_ref,
+    cot_ref,
     raw_ref,
+    cot_sems,
     weight_sems,
     small_sems,
 ):
     units, width = raw_ref.shape
     band = units // CHUNKS
+    span = width // CHUNKS
+    cot_copies = fetch(cot_hbm, cot_ref, cot_sems)
     small = [
         pltpu.make_async_copy(a_hbm, a_ref, small_sems.at[0]),
         pltpu.make_async_copy(b_hbm, b_ref, small_sems.at[1]),
@@ -143,6 +126,13 @@
             )
             copy.start()
             copies.append(copy)
+    place = place_ref[...]
+    pick = picks(place)
+    gate = jnp.sum(place, axis=1, keepdims=True)
+    for c in range(CHUNKS):
+        cot_copies[c].wait()
+        part = slice(c * span, (c + 1) * span)
+        rows_ref[:, part] = (f32dot(pick, cot_ref[:, part]) * gate).astype(jnp.bfloat16)
     for copy in small + copies[:CHUNKS]:
         copy.wait()
     span = 512
@@ -197,6 +187,8 @@
     for k, ref in enumerate(out_refs):
         ref[:, :width] = result[k * height:(k + 1) * height]
     out_refs[0][:, width:] = picks(place_ref[...])
+    for ref in out_refs[1:]:
+        ref[:, width:] = jnp.zeros((height, ref.shape[1] - width), jnp.bfloat16)
 
 
 def combine(gated, place_ref, *refs):
@@ -260,12 +252,6 @@
         for e in range(experts)
     ]
     return lax.ppermute(block, ("section", "expert"), route)
-
-
-def gathered(rows, first, second):
-    blocks = {0: rows, first: shifted(rows, 0, first), second: shifted(rows, 0, second)}
-    blocks[first ^ second] = shifted(blocks[first], 0, second)
-    return [blocks[k] for k in range(SPLIT)]
 
 
 def between_groups(rows, flight):
@@ -303,44 +289,45 @@
         up_map = lax.dynamic_index_in_dim(adapter_up_maps[0], group, 0, keepdims=False)
     down_map = jnp.swapaxes(adapter_down_maps[0], 0, 1)
 
-    x_rows, g_rows, place = call(
+    x_rows, place = call(
         functools.partial(gather, flight),
-        [sds(slots, width), sds(slots, width), sds(slots, tokens, dtype=jnp.float32)],
+        [sds(slots, width), sds(slots, tokens, dtype=jnp.float32)],
         (),
         (
             jnp.swapaxes(token_expert_choice[0], 0, 1),
             jnp.swapaxes(route_gate_steps[0], 0, 1),
             section_layer_input,
-            cotangent,
         ),
         scratch=[
             pltpu.VMEM((top, tokens), jnp.int32),
             pltpu.VMEM((top, tokens), jnp.int32),
             pltpu.VMEM((tokens, width), jnp.bfloat16),
-            pltpu.VMEM((tokens, width), jnp.bfloat16),
             dma((2,)),
             dma((CHUNKS,)),
+        ],
+        flops=2 * slots * tokens * width,
+    )
+    x_rows = between_groups(x_rows, flight)
+    x_blocks = [x_rows] + [shifted(x_rows, 0, k) for k in flips[1:]]
+
+    g_rows, gate_near, up_near, down_near, a_near, b_near = call(
+        load,
+        [sds(slots, width)]
+        + [sds(units, width)] * 3
+        + [sds(rank, units), sds(rank, width)],
+        (place,),
+        (cotangent, gate_weight, up_weight, down_weight, down_map, up_map),
+        scratch=[
+            pltpu.VMEM((tokens, width), jnp.bfloat16),
+            pltpu.VMEM((units, width), jnp.bfloat16),
             dma((CHUNKS,)),
-        ],
-        flops=4 * slots * tokens * width,
-    )
-    x_rows = between_groups(x_rows, flight)
-    g_rows = between_groups(g_rows, flight)
-    x_blocks = gathered(x_rows, 1, 2)
-    g_blocks = gathered(g_rows, 2, 1)
-    x_blocks, g_blocks[2] = lax.optimization_barrier((x_blocks, g_blocks[2]))
-    gate_near, up_near, down_near, a_near, b_near = call(
-        load,
-        [sds(units, width)] * 3 + [sds(rank, units), sds(rank, width)],
-        (place,),
-        (gate_weight, up_weight, down_weight, down_map, up_map),
-        scratch=[
-            pltpu.VMEM((units, width), jnp.bfloat16),
             dma((3 * CHUNKS,)),
             dma((2,)),
         ],
         flops=200 * units * rank * width,
     )
+    g_rows = between_groups(g_rows, flight)
+    g_blocks = [g_rows] + [shifted(g_rows, 0, k) for k in flips[1:]]
 
     wide = width + tokens
     out_blocks = call(
@@ -356,7 +343,7 @@
     out_parts = [out_blocks[0]] + [shifted(out_blocks[k], 0, k) for k in flips[1:]]
     grad_blocks = call(
         backward,
-        [sds(slots, wide)] + [sds(slots, width)] * (SPLIT - 1),
+        [sds(slots, wide)] + [sds(slots, wide + tokens)] * (SPLIT - 1),
         (*g_blocks, place, pre_gate, pre_up, gate_near, up_near, down_near),
         flops=60 * rows * units * width,
     )
@@ -365,29 +352,30 @@
     def merged(parts, gated, columns):
         return call(functools.partial(combine, gated), [sds(slots, columns)], (place, *parts))[0]
 
-    hidden, _ = lax.optimization_barrier((hidden, grad_blocks[0]))
+    hidden, latent, _ = lax.optimization_barrier((hidden, latent, grad_blocks[0]))
     (a_grad,) = call(
         down_map_grad,
         [sds(rank, units, dtype=jnp.float32)],
         (*g_blocks, hidden, b_near),
         flops=200 * rows * rank * width,
     )
-    out_parts, a_grad, grad_parts[1], grad_parts[3] = lax.optimization_barrier((out_parts, a_grad, grad_parts[1], grad_parts[3]))
-    if flight > 1:
-        out_parts = [between_groups(merged(out_parts, False, width), flight)]
-    message = shifted(merged(out_parts, True, wide), 1, 0)
     if flight == 1:
         (b_grad,) = call(
             up_map_grad,
             [sds(1, 1, rank, width // SPLIT, dtype=jnp.float32)],
             (latent, *out_parts[1:], *g_blocks),
-            flops=2 * SPLIT * rows * rank * width // SPLIT,
+            flops=200 * rows * rank * width,
         )
     else:
         part = LOWRANK_SCALE * f32dot(latent, jnp.concatenate(g_blocks, axis=0))
         mine = jnp.arange(flight, dtype=jnp.int32) == group
         spread = jnp.where(mine[:, None, None], part[None], 0.0)
         b_grad = lax.psum_scatter(spread, "expert", scatter_dimension=2, tiled=True)[None]
+
+    out_parts, b_grad = lax.optimization_barrier((out_parts, b_grad))
+    if flight > 1:
+        out_parts = [between_groups(merged(out_parts, False, width), flight)]
+    message = shifted(merged(out_parts, True, wide), 1, 0)
 
     def expanded(parts):
         return call(

time: 44.8 us -> 40.3 us (0.90)
  the two profiles are of different devices: /device:TPU:1 before, /device:TPU:0 now
where the time goes in v5:
time: 40.3 us; the launch traced here: 40.1 us
  starting transfers between devices  22.5 us (56%)
  Pallas kernels  14.5 us (36%)
  waiting for transfers between devices  2.34 us (6%)
  between operations  0.71 us (2%)
    ppermute x14, starting transfers between devices, shifted(): return lax.ppermute(block, ('section', 'expert'), route)  22.5 us
    pallas_call x9, Pallas kernels, call(): pl.pallas_call(body, out_shape=outs, in_specs=[NEAR] * len(args) + [FAR]...  14.5 us
    ppermute x14, waiting for transfers between devices, shifted(): return lax.ppermute(block, ('section', 'expert'), route)  2.34 us
  transfers between devices with their start and end apart: 14, of which 2 were waited for; matrix products, arithmetic and copies ran while one was open for 0% of the time, Pallas kernels for 29%

profile of v5, /device:TPU:0, one launch (start us, length us, event | category | flops | bytes accessed | tf_op | source)
XLA Modules:
  0.0 40.1 jit_solution(14751268786472772900)
XLA Ops:
  0.6 1.7 %shard_map.120 = (bf16[16,4096]{1,0:T(8,128)(2,1)S(1)}, f32[16,128]{1,0:T(8,128)S(1)}) custom-call(s32[8,128]{1,0:T(8,128)} %bitcast.13, s32[8,128]{1,0:T(8,128)} %bitcast.14, bf16[1,128,4096]{2,1,0:T(8,128)(2,1)} %x_hbm.1), custom_call_target="tpu_custom_call" | custom-call | flops 16777216 | bytes 1196032 | tf_op jit(solution)/shard_map/pallas_call | solution.py:32
  2.4 4.0 %collective-permute-start.2 = (bf16[16,4096]{1,0:T(8,128)(2,1)S(1)}, bf16[16,4096]{1,0:T(8,128)(2,1)S(1)}, u32[]{:S(2)}, u32[]{:S(2)}) collective-permute-start(bf16[16,4096]{1,0:T(8,128)(2,1)S(1)} %get-tuple-element.37.refs_0_), channel_id=1, source_target_pairs={{0,3},{1,2},{2,1},{3,0},{4,7},{5,6},{6,5},{7,4},{8,11},{9,10},{10,... | collective-permute-start | bytes 393224 | tf_op jit(solution)/shard_map/ppermute | solution.py:254
  6.3 0.5 %collective-permute-start.1 = (bf16[16,4096]{1,0:T(8,128)(2,1)S(1)}, bf16[16,4096]{1,0:T(8,128)(2,1)S(1)}, u32[]{:S(2)}, u32[]{:S(2)}) collective-permute-start(bf16[16,4096]{1,0:T(8,128)(2,1)S(1)} %get-tuple-element.37.refs_0_), channel_id=1, source_target_pairs={{0,2},{1,3},{2,0},{3,1},{4,6},{5,7},{6,4},{7,5},{8,10},{9,11},{10,... | collective-permute-start | bytes 393224 | tf_op jit(solution)/shard_map/ppermute | solution.py:254
  6.8 0.1 collective-permute-start
  7.0 4.0 %shard_map.121 = (bf16[16,4096]{1,0:T(8,128)(2,1)S(1)}, bf16[256,4096]{1,0:T(8,128)(2,1)S(1)}, bf16[256,4096]{1,0:T(8,128)(2,1)S(1)}, bf16[256,4096]{1,0:T(8,128...) custom-call(f32[16,128]{1,0:T(8,128)S(1)} %get-tuple-element.36.place_ref.refs_4_, ...), custom_call_target="tpu_custom_call" | custom-call | flops 3355443200 | bytes 14049280 | tf_op jit(solution)/shard_map/pallas_call | solution.py:32
  11.0 2.9 %collective-permute-start.8 = (bf16[16,4096]{1,0:T(8,128)(2,1)S(1)}, bf16[16,4096]{1,0:T(8,128)(2,1)S(1)}, u32[]{:S(2)}, u32[]{:S(2)}) collective-permute-start(bf16[16,4096]{1,0:T(8,128)(2,1)S(1)} %get-tuple-element.48.refs_0_.refs_3_), channel_id=1, source_target_pairs={{0,3},{1,2},{2,1},{3,0},{4,7},{5,6},{6,5},{7,4},{8,11},{9,10},{10,... | collective-permute-start | bytes 393224 | tf_op jit(solution)/shard_map/ppermute | solution.py:254
  13.9 0.5 %collective-permute-start.7 = (bf16[16,4096]{1,0:T(8,128)(2,1)S(1)}, bf16[16,4096]{1,0:T(8,128)(2,1)S(1)}, u32[]{:S(2)}, u32[]{:S(2)}) collective-permute-start(bf16[16,4096]{1,0:T(8,128)(2,1)S(1)} %get-tuple-element.48.refs_0_.refs_3_), channel_id=1, source_target_pairs={{0,2},{1,3},{2,0},{3,1},{4,6},{5,7},{6,4},{7,5},{8,10},{9,11},{10,... | collective-permute-start | bytes 393224 | tf_op jit(solution)/shard_map/ppermute | solution.py:254
  14.4 0.1 collective-permute-start.6
  14.5 0.0 collective-permute-done.1.refs_2_
  14.5 0.0 collective-permute-done.refs_1_
  14.5 1.8 %shard_map.122 = (bf16[16,4096]{1,0:T(8,128)(2,1)S(1)}, bf16[16,4224]{1,0:T(8,128)(2,1)S(1)}, bf16[16,4224]{1,0:T(8,128)(2,1)S(1)}, bf16[16,4224]{1,0:T(8,128)(2...) custom-call(bf16[16,4096]{1,0:T(8,128)(2,1)S(1)} %get-tuple-element., ...), custom_call_target="tpu_custom_call" | custom-call | flops 4026531840 | bytes 7526400 | tf_op jit(solution)/shard_map/pallas_call | solution.py:32
  16.4 1.9 %collective-permute-start.3 = (bf16[16,4224]{1,0:T(8,128)(2,1)S(1)}, bf16[16,4224]{1,0:T(8,128)(2,1)S(1)}, u32[]{:S(2)}, u32[]{:S(2)}) collective-permute-start(bf16[16,4224]{1,0:T(8,128)(2,1)S(1)} %get-tuple-element.43), channel_id=1, source_target_pairs={{0,1},{1,0},{2,3},{3,2},{4,5},{5,4},{6,7},{7,6},{8,9},{9,8},{10,11... | collective-permute-start | bytes 405512 | tf_op jit(solution)/shard_map/ppermute | solution.py:254
  18.3 1.5 %collective-permute-start.4 = (bf16[16,4224]{1,0:T(8,128)(2,1)S(1)}, bf16[16,4224]{1,0:T(8,128)(2,1)S(1)}, u32[]{:S(2)}, u32[]{:S(2)}) collective-permute-start(bf16[16,4224]{1,0:T(8,128)(2,1)S(1)} %get-tuple-element.44), channel_id=1, source_target_pairs={{0,2},{1,3},{2,0},{3,1},{4,6},{5,7},{6,4},{7,5},{8,10},{9,11},{10,... | collective-permute-start | bytes 405512 | tf_op jit(solution)/shard_map/ppermute | solution.py:254
  19.9 1.4 %collective-permute-start.5 = (bf16[16,4224]{1,0:T(8,128)(2,1)S(1)}, bf16[16,4224]{1,0:T(8,128)(2,1)S(1)}, u32[]{:S(2)}, u32[]{:S(2)}) collective-permute-start(bf16[16,4224]{1,0:T(8,128)(2,1)S(1)} %get-tuple-element.45), channel_id=1, source_target_pairs={{0,3},{1,2},{2,1},{3,0},{4,7},{5,6},{6,5},{7,4},{8,11},{9,10},{10,... | collective-permute-start | bytes 405512 | tf_op jit(solution)/shard_map/ppermute | solution.py:254
  21.2 0.0 collective-permute-done.7.refs_2_.refs_5_
  21.2 0.3 collective-permute-done.6.refs_1_.refs_4_
  21.5 2.5 %shard_map.123 = (bf16[16,4224]{1,0:T(8,128)(2,1)S(1)}, bf16[16,4352]{1,0:T(8,128)(2,1)S(1)}, bf16[16,4352]{1,0:T(8,128)(2,1)S(1)}, bf16[16,4352]{1,0:T(8,128)(2,1)S(1)}) custom-call(bf16[16,4096]{1,0:T(8,128)(2,1)S(1)} %get-tuple-element.48.refs_0_.refs_3_, bf16[16,4096]{1,0:T(8,128)(2,1)S(1)} %collective-permute-done.6.refs_1_.refs_4_, ...), custom_call_target="tpu_custom_call" | custom-call | flops 4026531840 | bytes 7507968 | tf_op jit(solution)/shard_map/pallas_call | solution.py:32
  24.0 1.4 %collective-permute-start.11 = (bf16[16,4352]{1,0:T(8,128)(2,1)S(1)}, bf16[16,4352]{1,0:T(8,128)(2,1)S(1)}, u32[]{:S(2)}, u32[]{:S(2)}) collective-permute-start(bf16[16,4352]{1,0:T(8,128)(2,1)S(1)} %get-tuple-element.57), channel_id=1, source_target_pairs={{0,29},{1,28},{2,31},{3,30},{4,1},{5,0},{6,3},{7,2},{8,5},{9,4},{1... | collective-permute-start | bytes 417800 | tf_op jit(solution)/shard_map/ppermute | solution.py:254
  25.4 3.2 %collective-permute-start.12 = (bf16[16,4352]{1,0:T(8,128)(2,1)S(1)}, bf16[16,4352]{1,0:T(8,128)(2,1)S(1)}, u32[]{:S(2)}, u32[]{:S(2)}) collective-permute-start(bf16[16,4352]{1,0:T(8,128)(2,1)S(1)} %get-tuple-element.58), channel_id=1, source_target_pairs={{0,30},{1,31},{2,28},{3,29},{4,2},{5,3},{6,0},{7,1},{8,6},{9,7},{1... | collective-permute-start | bytes 417800 | tf_op jit(solution)/shard_map/ppermute | solution.py:254
  28.7 0.0 collective-permute-done.3.refs_0_.refs_1_
  28.7 1.3 %collective-permute-start.13 = (bf16[16,4352]{1,0:T(8,128)(2,1)S(1)}, bf16[16,4352]{1,0:T(8,128)(2,1)S(1)}, u32[]{:S(2)}, u32[]{:S(2)}) collective-permute-start(bf16[16,4352]{1,0:T(8,128)(2,1)S(1)} %get-tuple-element.59), channel_id=1, source_target_pairs={{0,31},{1,30},{2,29},{3,28},{4,3},{5,2},{6,1},{7,0},{8,7},{9,6},{1... | collective-permute-start | bytes 417800 | tf_op jit(solution)/shard_map/ppermute | solution.py:254
  30.0 0.0 collective-permute-done.4.refs_1_.refs_2_
  30.0 0.0 collective-permute-done.5.refs_2_.refs_3_
  30.0 0.9 %shard_map.124 = f32[1,1,16,1024]{3,2,1,0:T(8,128)} custom-call(bf16[16,64]{1,0:T(8,128)(2,1)S(1)} %get-tuple-element.52.latent_ref, bf16[16,4224]{1,0:T(8,128)(2,1)S(1)} %collective-permute-done.3.refs_0_.refs_1_, bf16[16,4224]{1,0:T(8,128)(2,1)S(1)} %collective-permute-done.4.refs_1_.refs_2_, bf16[16,4224]{1,0:T(8,128)(2,1)S(1)} %collective-permute-done.5.refs_2_.refs_3_, ...), custom_call_target="tpu_custom_call" | custom-call | flops 838860800 | bytes 997376 | tf_op jit(solution)/shard_map/pallas_call | solution.py:32
  30.8 0.1 shard_map.125
  30.9 0.5 %collective-permute-start.9 = (bf16[16,4224]{1,0:T(8,128)(2,1)S(1)}, bf16[16,4224]{1,0:T(8,128)(2,1)S(1)}, u32[]{:S(2)}, u32[]{:S(2)}) collective-permute-start(bf16[16,4224]{1,0:T(8,128)(2,1)S(1)} %shard_map.125), channel_id=1, source_target_pairs={{0,4},{1,5},{2,6},{3,7},{4,8},{5,9},{6,10},{7,11},{8,12},{9,13},{1... | collective-permute-start | bytes 405512 | tf_op jit(solution)/shard_map/ppermute | solution.py:254
  31.4 3.1 %collective-permute-start.10 = (bf16[16,4224]{1,0:T(8,128)(2,1)S(1)}, bf16[16,4224]{1,0:T(8,128)(2,1)S(1)}, u32[]{:S(2)}, u32[]{:S(2)}) collective-permute-start(bf16[16,4224]{1,0:T(8,128)(2,1)S(1)} %get-tuple-element.51), channel_id=1, source_target_pairs={{0,28},{1,29},{2,30},{3,31},{4,0},{5,1},{6,2},{7,3},{8,4},{9,5},{1... | collective-permute-start | bytes 405512 | tf_op jit(solution)/shard_map/ppermute | solution.py:254
  34.5 1.0 %shard_map.128 = f32[16,256]{1,0:T(8,128)} custom-call(bf16[16,4096]{1,0:T(8,128)(2,1)S(1)} %get-tuple-element.48.refs_0_.refs_3_, bf16[16,4096]{1,0:T(8,128)(2,1)S(1)} %collective-permute-done.6.refs_1_.refs_4_, bf16[16,4096]{1,0:T(8,128)(2,1)S(1)} %collective-permute-done.7.refs_2_.refs_5_, bf16[16,4096]{1,0:T(8,128)(2,1)S(1)} %collective-permute-done.8.refs_3_.refs_6_, ...), custom_call_target="tpu_custom_call" | custom-call | flops 838860800 | bytes 704512 | tf_op jit(solution)/shard_map/pallas_call | solution.py:32
  35.6 2.0 %collective-permute-done.9.refs_0_ = bf16[16,4224]{1,0:T(8,128)(2,1)S(1)} collective-permute-done((bf16[16,4224]{1,0:T(8,128)(2,1)S(1)}, bf16[16,4224]{1,0:T(8,128)(2,1)S(1)}, u32[]{:S(2)}, u32[]{:S(2)}) %collective-permute-start.9) | collective-permute-done | bytes 135200 | tf_op jit(solution)/shard_map/ppermute | solution.py:254
  37.6 1.2 %shard_map.126 = bf16[1,128,4096]{2,1,0:T(8,128)(2,1)} custom-call(bf16[16,4224]{1,0:T(8,128)(2,1)S(1)} %collective-permute-done.9.refs_0_), custom_call_target="tpu_custom_call" | custom-call | flops 16777216 | bytes 1183744 | tf_op jit(solution)/shard_map/pallas_call | solution.py:32
  38.9 0.0 collective-permute-done.10.refs_0_
  38.9 1.2 %shard_map.127 = bf16[1,128,4096]{2,1,0:T(8,128)(2,1)} custom-call(bf16[16,4224]{1,0:T(8,128)(2,1)S(1)} %collective-permute-done.10.refs_0_, bf16[16,4352]{1,0:T(8,128)(2,1)S(1)} %collective-permute-done.11.refs_1_, bf16[16,4352]{1,0:T(8,128)(2,1)S(1)} %collective-permute-done.12.refs_2_, bf16[16,4352]{1,0:T(8,128)(2,1)S(1)} %collective-permute-done.13.refs_3_), custom_call_target="tpu_custom_call" | custom-call | flops 16777216 | bytes 1601536 | tf_op jit(solution)/shard_map/pallas_call | solution.py:32
  (5 shorter events, 0.0 us)
Async XLA Ops:
  2.4 12.0 %collective-permute-start.2 = (bf16[16,4096]{1,0:T(8,128)(2,1)S(1)}, bf16[16,4096]{1,0:T(8,128)(2,1)S(1)}, u32[]{:S(2)}, u32[]{:S(2)}) collective-permute-start(bf16[16,4096]{1,0:T(8,128)(2,1)S(1)} %get-tuple-element.37.refs_0_), channel_id=1, source_target_pairs={{0,3},{1,2},{2,1},{3,0},{4,7},{5,6},{6,5},{7,4},{8,11},{9,10},{10,... | collective-permute-start | bytes 393224 | tf_op jit(solution)/shard_map/ppermute | solution.py:254
  6.3 8.2 %collective-permute-start.1 = (bf16[16,4096]{1,0:T(8,128)(2,1)S(1)}, bf16[16,4096]{1,0:T(8,128)(2,1)S(1)}, u32[]{:S(2)}, u32[]{:S(2)}) collective-permute-start(bf16[16,4096]{1,0:T(8,128)(2,1)S(1)} %get-tuple-element.37.refs_0_), channel_id=1, source_target_pairs={{0,2},{1,3},{2,0},{3,1},{4,6},{5,7},{6,4},{7,5},{8,10},{9,11},{10,... | collective-permute-start | bytes 393224 | tf_op jit(solution)/shard_map/ppermute | solution.py:254
  6.8 7.7 %collective-permute-start = (bf16[16,4096]{1,0:T(8,128)(2,1)S(1)}, bf16[16,4096]{1,0:T(8,128)(2,1)S(1)}, u32[]{:S(2)}, u32[]{:S(2)}) collective-permute-start(bf16[16,4096]{1,0:T(8,128)(2,1)S(1)} %get-tuple-element.37.refs_0_), channel_id=1, source_target_pairs={{0,1},{1,0},{2,3},{3,2},{4,5},{5,4},{6,7},{7,6},{8,9},{9,8},{10,11... | collective-permute-start | bytes 393224 | tf_op jit(solution)/shard_map/ppermute | solution.py:254
  11.0 8.9 %collective-permute-start.8 = (bf16[16,4096]{1,0:T(8,128)(2,1)S(1)}, bf16[16,4096]{1,0:T(8,128)(2,1)S(1)}, u32[]{:S(2)}, u32[]{:S(2)}) collective-permute-start(bf16[16,4096]{1,0:T(8,128)(2,1)S(1)} %get-tuple-element.48.refs_0_.refs_3_), channel_id=1, source_target_pairs={{0,3},{1,2},{2,1},{3,0},{4,7},{5,6},{6,5},{7,4},{8,11},{9,10},{10,... | collective-permute-start | bytes 393224 | tf_op jit(solution)/shard_map/ppermute | solution.py:254
  13.9 7.3 %collective-permute-start.7 = (bf16[16,4096]{1,0:T(8,128)(2,1)S(1)}, bf16[16,4096]{1,0:T(8,128)(2,1)S(1)}, u32[]{:S(2)}, u32[]{:S(2)}) collective-permute-start(bf16[16,4096]{1,0:T(8,128)(2,1)S(1)} %get-tuple-element.48.refs_0_.refs_3_), channel_id=1, source_target_pairs={{0,2},{1,3},{2,0},{3,1},{4,6},{5,7},{6,4},{7,5},{8,10},{9,11},{10,... | collective-permute-start | bytes 393224 | tf_op jit(solution)/shard_map/ppermute | solution.py:254
  14.4 7.1 %collective-permute-start.6 = (bf16[16,4096]{1,0:T(8,128)(2,1)S(1)}, bf16[16,4096]{1,0:T(8,128)(2,1)S(1)}, u32[]{:S(2)}, u32[]{:S(2)}) collective-permute-start(bf16[16,4096]{1,0:T(8,128)(2,1)S(1)} %get-tuple-element.48.refs_0_.refs_3_), channel_id=1, source_target_pairs={{0,1},{1,0},{2,3},{3,2},{4,5},{5,4},{6,7},{7,6},{8,9},{9,8},{10,11... | collective-permute-start | bytes 393224 | tf_op jit(solution)/shard_map/ppermute | solution.py:254
  16.4 12.3 %collective-permute-start.3 = (bf16[16,4224]{1,0:T(8,128)(2,1)S(1)}, bf16[16,4224]{1,0:T(8,128)(2,1)S(1)}, u32[]{:S(2)}, u32[]{:S(2)}) collective-permute-start(bf16[16,4224]{1,0:T(8,128)(2,1)S(1)} %get-tuple-element.43), channel_id=1, source_target_pairs={{0,1},{1,0},{2,3},{3,2},{4,5},{5,4},{6,7},{7,6},{8,9},{9,8},{10,11... | collective-permute-start | bytes 405512 | tf_op jit(solution)/shard_map/ppermute | solution.py:254
  18.3 11.6 %collective-permute-start.4 = (bf16[16,4224]{1,0:T(8,128)(2,1)S(1)}, bf16[16,4224]{1,0:T(8,128)(2,1)S(1)}, u32[]{:S(2)}, u32[]{:S(2)}) collective-permute-start(bf16[16,4224]{1,0:T(8,128)(2,1)S(1)} %get-tuple-element.44), channel_id=1, source_target_pairs={{0,2},{1,3},{2,0},{3,1},{4,6},{5,7},{6,4},{7,5},{8,10},{9,11},{10,... | collective-permute-start | bytes 405512 | tf_op jit(solution)/shard_map/ppermute | solution.py:254
  19.9 10.1 %collective-permute-start.5 = (bf16[16,4224]{1,0:T(8,128)(2,1)S(1)}, bf16[16,4224]{1,0:T(8,128)(2,1)S(1)}, u32[]{:S(2)}, u32[]{:S(2)}) collective-permute-start(bf16[16,4224]{1,0:T(8,128)(2,1)S(1)} %get-tuple-element.45), channel_id=1, source_target_pairs={{0,3},{1,2},{2,1},{3,0},{4,7},{5,6},{6,5},{7,4},{8,11},{9,10},{10,... | collective-permute-start | bytes 405512 | tf_op jit(solution)/shard_map/ppermute | solution.py:254
  24.0 14.9 %collective-permute-start.11 = (bf16[16,4352]{1,0:T(8,128)(2,1)S(1)}, bf16[16,4352]{1,0:T(8,128)(2,1)S(1)}, u32[]{:S(2)}, u32[]{:S(2)}) collective-permute-start(bf16[16,4352]{1,0:T(8,128)(2,1)S(1)} %get-tuple-element.57), channel_id=1, source_target_pairs={{0,29},{1,28},{2,31},{3,30},{4,1},{5,0},{6,3},{7,2},{8,5},{9,4},{1... | collective-permute-start | bytes 417800 | tf_op jit(solution)/shard_map/ppermute | solution.py:254
  25.4 13.4 %collective-permute-start.12 = (bf16[16,4352]{1,0:T(8,128)(2,1)S(1)}, bf16[16,4352]{1,0:T(8,128)(2,1)S(1)}, u32[]{:S(2)}, u32[]{:S(2)}) collective-permute-start(bf16[16,4352]{1,0:T(8,128)(2,1)S(1)} %get-tuple-element.58), channel_id=1, source_target_pairs={{0,30},{1,31},{2,28},{3,29},{4,2},{5,3},{6,0},{7,1},{8,6},{9,7},{1... | collective-permute-start | bytes 417800 | tf_op jit(solution)/shard_map/ppermute | solution.py:254
  28.7 10.2 %collective-permute-start.13 = (bf16[16,4352]{1,0:T(8,128)(2,1)S(1)}, bf16[16,4352]{1,0:T(8,128)(2,1)S(1)}, u32[]{:S(2)}, u32[]{:S(2)}) collective-permute-start(bf16[16,4352]{1,0:T(8,128)(2,1)S(1)} %get-tuple-element.59), channel_id=1, source_target_pairs={{0,31},{1,30},{2,29},{3,28},{4,3},{5,2},{6,1},{7,0},{8,7},{9,6},{1... | collective-permute-start | bytes 417800 | tf_op jit(solution)/shard_map/ppermute | solution.py:254
  30.9 6.7 %collective-permute-start.9 = (bf16[16,4224]{1,0:T(8,128)(2,1)S(1)}, bf16[16,4224]{1,0:T(8,128)(2,1)S(1)}, u32[]{:S(2)}, u32[]{:S(2)}) collective-permute-start(bf16[16,4224]{1,0:T(8,128)(2,1)S(1)} %shard_map.125), channel_id=1, source_target_pairs={{0,4},{1,5},{2,6},{3,7},{4,8},{5,9},{6,10},{7,11},{8,12},{9,13},{1... | collective-permute-start | bytes 405512 | tf_op jit(solution)/shard_map/ppermute | solution.py:254
  31.4 7.4 %collective-permute-start.10 = (bf16[16,4224]{1,0:T(8,128)(2,1)S(1)}, bf16[16,4224]{1,0:T(8,128)(2,1)S(1)}, u32[]{:S(2)}, u32[]{:S(2)}) collective-permute-start(bf16[16,4224]{1,0:T(8,128)(2,1)S(1)} %get-tuple-element.51), channel_id=1, source_target_pairs={{0,28},{1,29},{2,30},{3,31},{4,0},{5,1},{6,2},{7,3},{8,4},{9,5},{1... | collective-permute-start | bytes 405512 | tf_op jit(solution)/shard_map/ppermute | solution.py:254

commit v6 on v5

--- a/solution.py
+++ b/solution.py
@@ -145,9 +145,9 @@
 
 
 def forward(*refs):
-    x_refs, (gate_ref, up_ref, down_ref, a_ref) = refs[:SPLIT], refs[SPLIT:SPLIT + 4]
-    out_refs = refs[SPLIT + 4:2 * SPLIT + 4]
-    pre_gate_ref, pre_up_ref, hidden_ref, latent_ref = refs[2 * SPLIT + 4:]
+    x_refs, (place_ref, gate_ref, up_ref, down_ref, a_ref) = refs[:SPLIT], refs[SPLIT:SPLIT + 5]
+    out_refs = refs[SPLIT + 5:2 * SPLIT + 5]
+    pre_gate_ref, pre_up_ref, hidden_ref, latent_ref = refs[2 * SPLIT + 5:]
     rows = jnp.concatenate([r[...] for r in x_refs], axis=0)
     height, width = x_refs[0].shape
     pre_gate = f32dot(rows, gate_ref[...], LAST)
@@ -159,15 +159,12 @@
     result = f32dot(hidden, down_ref[...]).astype(jnp.bfloat16)
     for k, ref in enumerate(out_refs):
         ref[:, :width] = result[k * height:(k + 1) * height]
-    latent = f32dot(a_ref[...], hidden, LAST).astype(jnp.bfloat16)
-    latent_ref[...] = latent
-    if out_refs[1].shape[1] > width:
-        rank, count = latent.shape
-        tail = jnp.concatenate(
-            [latent, jnp.zeros((rank, out_refs[1].shape[1] - width - count), jnp.bfloat16)], axis=1
-        )
-        for ref in out_refs[1:]:
-            ref[:, width:] = tail
+    place = place_ref[...]
+    tokens = place.shape[1]
+    high = place.astype(jnp.bfloat16)
+    out_refs[0][:, width:width + tokens] = high
+    out_refs[0][:, width + tokens:] = (place - high.astype(jnp.float32)).astype(jnp.bfloat16)
+    latent_ref[...] = f32dot(a_ref[...], hidden, LAST).astype(jnp.bfloat16).astype(jnp.float32)
 
 
 def backward(*refs):
@@ -187,20 +184,16 @@
     for k, ref in enumerate(out_refs):
         ref[:, :width] = result[k * height:(k + 1) * height]
     out_refs[0][:, width:] = picks(place_ref[...])
-    for ref in out_refs[1:]:
-        ref[:, width:] = jnp.zeros((height, ref.shape[1] - width), jnp.bfloat16)
-
-
-def combine(gated, place_ref, *refs):
-    *part_refs, out_ref = refs
-    place = place_ref[...]
-    width = part_refs[0].shape[1]
-    rows = sum(r[:, :width].astype(jnp.float32) for r in part_refs)
-    if gated:
-        rows = rows * jnp.sum(place, axis=1, keepdims=True)
-    out_ref[:, :width] = rows.astype(jnp.bfloat16)
-    if out_ref.shape[1] > width:
-        out_ref[:, width:] = picks(place)
+
+
+def joined(own, other, flip):
+    height = own.shape[1] // SPLIT
+    blocks = [other[:, (i ^ flip) * height:((i ^ flip) + 1) * height] for i in range(SPLIT)]
+    return own + jnp.concatenate(blocks, axis=1)
+
+
+def join(own_ref, other_ref, out_ref):
+    out_ref[...] = joined(own_ref[...], other_ref[...], 1)
 
 
 def down_map_grad(*refs):
@@ -210,30 +203,33 @@
     out_ref[...] = f32dot(lowrank, hidden_ref[...], FIRST)
 
 
-def up_map_grad(latent_ref, *refs):
-    message_refs, g_refs, out_ref = refs[:SPLIT - 1], refs[SPLIT - 1:2 * SPLIT - 1], refs[-1]
+def up_map_grad(pair_ref, other_ref, *refs):
+    *g_refs, out_ref = refs
     span = out_ref.shape[-1]
     column = pl.multiple_of(lax.axis_index("expert") * span, 128)
-    count = latent_ref.shape[1]
-    width = g_refs[0].shape[1]
-    latents = [latent_ref[...]] + [r[:, width:width + count] for r in message_refs]
-    rows = [g_refs[i ^ k][:, pl.ds(column, span)] for k in range(SPLIT) for i in range(SPLIT)]
-    total = f32dot(jnp.concatenate(latents, axis=1), jnp.concatenate(rows, axis=0))
-    out_ref[0, 0] = LOWRANK_SCALE * total
-
-
-def expand(*refs):
+    latent = joined(pair_ref[...], other_ref[...], 2)
+    high = latent.astype(jnp.bfloat16)
+    low = (latent - high.astype(jnp.float32)).astype(jnp.bfloat16)
+    rows = jnp.concatenate([r[:, pl.ds(column, span)] for r in g_refs], axis=0)
+    out_ref[0, 0] = LOWRANK_SCALE * (f32dot(high, rows) + f32dot(low, rows))
+
+
+def expand(gated, *refs):
     *part_refs, out_hbm, out_ref, sems = refs
-    width = out_ref.shape[1]
-    pick = part_refs[0][:, width:]
+    tokens, width = out_ref.shape
+    high = part_refs[0][:, width:width + tokens]
+    pick = picks(high)
+    if gated:
+        low = part_refs[0][:, width + tokens:]
+        gate = jnp.sum(high.astype(jnp.float32) + low.astype(jnp.float32), axis=1, keepdims=True)
     span = width // CHUNKS
     copies = []
     for c in range(CHUNKS):
         part = slice(c * span, (c + 1) * span)
-        rows = part_refs[0][:, part]
-        if len(part_refs) > 1:
-            rows = sum(r[:, part].astype(jnp.float32) for r in part_refs).astype(jnp.bfloat16)
-        out_ref[:, part] = f32dot(pick, rows, FIRST).astype(jnp.bfloat16)
+        rows = sum(r[:, part].astype(jnp.float32) for r in part_refs)
+        if gated:
+            rows = rows * gate
+        out_ref[:, part] = f32dot(pick, rows.astype(jnp.bfloat16), FIRST).astype(jnp.bfloat16)
         columns = pl.ds(c * span, span)
         copy = pltpu.make_async_copy(
             out_ref.at[:, columns], out_hbm.at[0, :, columns], sems.at[c]
@@ -329,57 +325,38 @@
     g_rows = between_groups(g_rows, flight)
     g_blocks = [g_rows] + [shifted(g_rows, 0, k) for k in flips[1:]]
 
-    wide = width + tokens
-    out_blocks = call(
+    *out_blocks, pre_gate, pre_up, hidden, latent = call(
         forward,
-        [sds(slots, width)]
-        + [sds(slots, wide if flight == 1 else width)] * (SPLIT - 1)
+        [sds(slots, width + 2 * tokens)]
+        + [sds(slots, width)] * (SPLIT - 1)
         + [sds(rows, units, dtype=jnp.float32)] * 2
-        + [sds(rows, units), sds(rank, rows)],
-        (*x_blocks, gate_near, up_near, down_near, a_near),
+        + [sds(rows, units), sds(rank, rows, dtype=jnp.float32)],
+        (*x_blocks, place, gate_near, up_near, down_near, a_near),
         flops=60 * rows * units * width,
     )
-    *out_blocks, pre_gate, pre_up, hidden, latent = out_blocks
-    out_parts = [out_blocks[0]] + [shifted(out_blocks[k], 0, k) for k in flips[1:]]
+    out_parts = [shifted(out_blocks[k], 1, k) for k in flips]
     grad_blocks = call(
         backward,
-        [sds(slots, wide)] + [sds(slots, wide + tokens)] * (SPLIT - 1),
+        [sds(slots, width + tokens)] + [sds(slots, width)] * (SPLIT - 1),
         (*g_blocks, place, pre_gate, pre_up, gate_near, up_near, down_near),
         flops=60 * rows * units * width,
     )
     grad_parts = [shifted(grad_blocks[k], -1, k) for k in flips]
 
-    def merged(parts, gated, columns):
-        return call(functools.partial(combine, gated), [sds(slots, columns)], (place, *parts))[0]
-
-    hidden, latent, _ = lax.optimization_barrier((hidden, latent, grad_blocks[0]))
+    hidden, _ = lax.optimization_barrier((hidden, grad_blocks[0]))
     (a_grad,) = call(
         down_map_grad,
         [sds(rank, units, dtype=jnp.float32)],
         (*g_blocks, hidden, b_near),
-        flops=200 * rows * rank * width,
-    )
-    if flight == 1:
-        (b_grad,) = call(
-            up_map_grad,
-            [sds(1, 1, rank, width // SPLIT, dtype=jnp.float32)],
-            (latent, *out_parts[1:], *g_blocks),
-            flops=200 * rows * rank * width,
-        )
-    else:
-        part = LOWRANK_SCALE * f32dot(latent, jnp.concatenate(g_blocks, axis=0))
-        mine = jnp.arange(flight, dtype=jnp.int32) == group
-        spread = jnp.where(mine[:, None, None], part[None], 0.0)
-        b_grad = lax.psum_scatter(spread, "expert", scatter_dimension=2, tiled=True)[None]
-
-    out_parts, b_grad = lax.optimization_barrier((out_parts, b_grad))
-    if flight > 1:
-        out_parts = [between_groups(merged(out_parts, False, width), flight)]
-    message = shifted(merged(out_parts, True, wide), 1, 0)
-
-    def expanded(parts):
+        flops=2 * rows * rank * width,
+    )
+    def expanded(parts, gated):
+        if flight > 1:
+            total = sum(p[:, :width].astype(jnp.float32) for p in parts).astype(jnp.bfloat16)
+            total = between_groups(total, flight)
+            parts = [jnp.concatenate([total, parts[0][:, width:]], axis=1)]
         return call(
-            expand,
+            functools.partial(expand, gated),
             [sds(1, tokens, width)],
             tuple(parts),
             far_outs=True,
@@ -387,13 +364,27 @@
             flops=2 * slots * tokens * width,
         )[0]
 
-    next_input = expanded([message])
-    if flight > 1:
-        total = sum(p[:, :width].astype(jnp.float32) for p in grad_parts).astype(jnp.bfloat16)
-        total = between_groups(total, flight)
-        grad_parts = [jnp.concatenate([total, grad_parts[0][:, width:]], axis=1)]
-    next_input, grad_parts = lax.optimization_barrier((next_input, grad_parts))
-    prev_grad = expanded(grad_parts)
+    next_input = expanded(out_parts, True)
+    latent, next_input = lax.optimization_barrier((latent, next_input))
+    if flight == 1:
+        (pair,) = call(
+            join, [sds(rank, rows, dtype=jnp.float32)], (latent, shifted(latent, 0, 1))
+        )
+        (b_grad,) = call(
+            up_map_grad,
+            [sds(1, 1, rank, width // SPLIT, dtype=jnp.float32)],
+            (pair, shifted(pair, 0, 2), *g_blocks),
+            flops=4 * rows * rank * width // SPLIT,
+        )
+    else:
+        latent = latent.astype(jnp.bfloat16)
+        part = LOWRANK_SCALE * f32dot(latent, jnp.concatenate(g_blocks, axis=0))
+        mine = jnp.arange(flight, dtype=jnp.int32) == group
+        spread = jnp.where(mine[:, None, None], part[None], 0.0)
+        b_grad = lax.psum_scatter(spread, "expert", scatter_dimension=2, tiled=True)[None]
+
+    next_input, b_grad, grad_parts = lax.optimization_barrier((next_input, b_grad, grad_parts))
+    prev_grad = expanded(grad_parts, False)
     return next_input, prev_grad, jnp.swapaxes(a_grad, 0, 1)[None], b_grad
 
 

time: 40.3 us -> 42.8 us (1.062)
  waiting for transfers between devices: 2.34 us -> 4.41 us
  starting transfers between devices: 22.5 us -> 23 us
    ppermute x14 -> x16, waiting for transfers between devices: 2.34 us -> 4.41 us  [shifted(): return lax.ppermute(block, ('section', 'expert'), route)]
    ppermute x14 -> x16, starting transfers between devices: 22.5 us -> 23 us  [shifted(): return lax.ppermute(block, ('section', 'expert'), route)]
  transfers between devices with their start and end apart: 14 -> 16, of which waited for: 2 -> 3; matrix products, arithmetic and copies ran while one was open for 0% -> 0% of each run, Pallas kernels for 29% -> 27%
where the time goes in v6:
time: 42.8 us; the launch traced here: 42.7 us
  starting transfers between devices  23 us (54%)
  Pallas kernels  14.6 us (34%)
  waiting for transfers between devices  4.41 us (10%)
  between operations  0.7 us (2%)
    ppermute x16, starting transfers between devices, shifted(): return lax.ppermute(block, ('section', 'expert'), route)  23 us
    pallas_call x9, Pallas kernels, call(): pl.pallas_call(body, out_shape=outs, in_specs=[NEAR] * len(args) + [FAR]...  14.6 us
    ppermute x16, waiting for transfers between devices, shifted(): return lax.ppermute(block, ('section', 'expert'), route)  4.41 us
  transfers between devices with their start and end apart: 16, of which 3 were waited for; matrix products, arithmetic and copies ran while one was open for 0% of the time, Pallas kernels for 27%

profile of v6, /device:TPU:0, one launch (start us, length us, event | category | flops | bytes accessed | tf_op | source)
XLA Modules:
  0.0 42.7 jit_solution(9469124642658412901)
XLA Ops:
  0.6 1.7 %shard_map.120 = (bf16[16,4096]{1,0:T(8,128)(2,1)S(1)}, f32[16,128]{1,0:T(8,128)S(1)}) custom-call(s32[8,128]{1,0:T(8,128)} %bitcast.14, s32[8,128]{1,0:T(8,128)} %bitcast.15, bf16[1,128,4096]{2,1,0:T(8,128)(2,1)} %x_hbm.1), custom_call_target="tpu_custom_call" | custom-call | flops 16777216 | bytes 1196032 | tf_op jit(solution)/shard_map/pallas_call | solution.py:32
  2.4 3.0 %collective-permute-start = (bf16[16,4096]{1,0:T(8,128)(2,1)S(1)}, bf16[16,4096]{1,0:T(8,128)(2,1)S(1)}, u32[]{:S(2)}, u32[]{:S(2)}) collective-permute-start(bf16[16,4096]{1,0:T(8,128)(2,1)S(1)} %get-tuple-element.33.refs_0_), channel_id=1, source_target_pairs={{0,1},{1,0},{2,3},{3,2},{4,5},{5,4},{6,7},{7,6},{8,9},{9,8},{10,11... | collective-permute-start | bytes 393224 | tf_op jit(solution)/shard_map/ppermute | solution.py:250
  5.4 1.5 %collective-permute-start.1 = (bf16[16,4096]{1,0:T(8,128)(2,1)S(1)}, bf16[16,4096]{1,0:T(8,128)(2,1)S(1)}, u32[]{:S(2)}, u32[]{:S(2)}) collective-permute-start(bf16[16,4096]{1,0:T(8,128)(2,1)S(1)} %get-tuple-element.33.refs_0_), channel_id=1, source_target_pairs={{0,2},{1,3},{2,0},{3,1},{4,6},{5,7},{6,4},{7,5},{8,10},{9,11},{10,... | collective-permute-start | bytes 393224 | tf_op jit(solution)/shard_map/ppermute | solution.py:250
  6.9 0.0 collective-permute-start.2
  6.9 4.0 %shard_map.121 = (bf16[16,4096]{1,0:T(8,128)(2,1)S(1)}, bf16[256,4096]{1,0:T(8,128)(2,1)S(1)}, bf16[256,4096]{1,0:T(8,128)(2,1)S(1)}, bf16[256,4096]{1,0:T(8,128...) custom-call(f32[16,128]{1,0:T(8,128)S(1)} %get-tuple-element.34.place_ref.refs_4_, ...), custom_call_target="tpu_custom_call" | custom-call | flops 3355443200 | bytes 14049280 | tf_op jit(solution)/shard_map/pallas_call | solution.py:32
  10.9 2.0 %collective-permute-start.10 = (bf16[16,4096]{1,0:T(8,128)(2,1)S(1)}, bf16[16,4096]{1,0:T(8,128)(2,1)S(1)}, u32[]{:S(2)}, u32[]{:S(2)}) collective-permute-start(bf16[16,4096]{1,0:T(8,128)(2,1)S(1)} %get-tuple-element.46.refs_0_), channel_id=1, source_target_pairs={{0,2},{1,3},{2,0},{3,1},{4,6},{5,7},{6,4},{7,5},{8,10},{9,11},{10,... | collective-permute-start | bytes 393224 | tf_op jit(solution)/shard_map/ppermute | solution.py:250
  12.9 1.4 %collective-permute-start.11 = (bf16[16,4096]{1,0:T(8,128)(2,1)S(1)}, bf16[16,4096]{1,0:T(8,128)(2,1)S(1)}, u32[]{:S(2)}, u32[]{:S(2)}) collective-permute-start(bf16[16,4096]{1,0:T(8,128)(2,1)S(1)} %get-tuple-element.46.refs_0_), channel_id=1, source_target_pairs={{0,3},{1,2},{2,1},{3,0},{4,7},{5,6},{6,5},{7,4},{8,11},{9,10},{10,... | collective-permute-start | bytes 393224 | tf_op jit(solution)/shard_map/ppermute | solution.py:250
  14.4 0.0 collective-permute-done.refs_1_
  14.4 0.1 collective-permute-start.9
  14.5 0.0 collective-permute-done.1.refs_2_
  14.5 0.0 collective-permute-done.2.refs_3_
  14.5 1.8 %shard_map.122 = (bf16[16,4352]{1,0:T(8,128)(2,1)S(1)}, bf16[16,4096]{1,0:T(8,128)(2,1)S(1)}, bf16[16,4096]{1,0:T(8,128)(2,1)S(1)}, bf16[16,4096]{1,0:T(8,128)(2...) custom-call(bf16[16,4096]{1,0:T(8,128)(2,1)S(1)} %get-tuple-element., ...), custom_call_target="tpu_custom_call" | custom-call | flops 4026531840 | bytes 7532544 | tf_op jit(solution)/shard_map/pallas_call | solution.py:32
  16.3 0.1 collective-permute-start.3
  16.4 3.2 %collective-permute-start.4 = (bf16[16,4096]{1,0:T(8,128)(2,1)S(1)}, bf16[16,4096]{1,0:T(8,128)(2,1)S(1)}, u32[]{:S(2)}, u32[]{:S(2)}) collective-permute-start(bf16[16,4096]{1,0:T(8,128)(2,1)S(1)} %get-tuple-element.41), channel_id=1, source_target_pairs={{0,5},{1,4},{2,7},{3,6},{4,9},{5,8},{6,11},{7,10},{8,13},{9,12},{1... | collective-permute-start | bytes 393224 | tf_op jit(solution)/shard_map/ppermute | solution.py:250
  19.6 0.0 collective-permute-done.10.refs_2_
  19.6 1.0 %collective-permute-start.5 = (bf16[16,4096]{1,0:T(8,128)(2,1)S(1)}, bf16[16,4096]{1,0:T(8,128)(2,1)S(1)}, u32[]{:S(2)}, u32[]{:S(2)}) collective-permute-start(bf16[16,4096]{1,0:T(8,128)(2,1)S(1)} %get-tuple-element.42), channel_id=1, source_target_pairs={{0,6},{1,7},{2,4},{3,5},{4,10},{5,11},{6,8},{7,9},{8,14},{9,15},{1... | collective-permute-start | bytes 393224 | tf_op jit(solution)/shard_map/ppermute | solution.py:250
  20.6 1.7 %collective-permute-start.6 = (bf16[16,4096]{1,0:T(8,128)(2,1)S(1)}, bf16[16,4096]{1,0:T(8,128)(2,1)S(1)}, u32[]{:S(2)}, u32[]{:S(2)}) collective-permute-start(bf16[16,4096]{1,0:T(8,128)(2,1)S(1)} %get-tuple-element.43), channel_id=1, source_target_pairs={{0,7},{1,6},{2,5},{3,4},{4,11},{5,10},{6,9},{7,8},{8,15},{9,14},{1... | collective-permute-start | bytes 393224 | tf_op jit(solution)/shard_map/ppermute | solution.py:250
  22.4 2.5 %shard_map.126 = (bf16[16,4224]{1,0:T(8,128)(2,1)S(1)}, bf16[16,4096]{1,0:T(8,128)(2,1)S(1)}, bf16[16,4096]{1,0:T(8,128)(2,1)S(1)}, bf16[16,4096]{1,0:T(8,128)(2,1)S(1)}) custom-call(bf16[16,4096]{1,0:T(8,128)(2,1)S(1)} %get-tuple-element.46.refs_0_, bf16[16,4096]{1,0:T(8,128)(2,1)S(1)} %collective-permute-done.9.refs_1_, ...), custom_call_target="tpu_custom_call" | custom-call | flops 4026531840 | bytes 7483392 | tf_op jit(solution)/shard_map/pallas_call | solution.py:32
  24.9 1.8 %collective-permute-start.12 = (bf16[16,4224]{1,0:T(8,128)(2,1)S(1)}, bf16[16,4224]{1,0:T(8,128)(2,1)S(1)}, u32[]{:S(2)}, u32[]{:S(2)}) collective-permute-start(bf16[16,4224]{1,0:T(8,128)(2,1)S(1)} %get-tuple-element.49), channel_id=1, source_target_pairs={{0,28},{1,29},{2,30},{3,31},{4,0},{5,1},{6,2},{7,3},{8,4},{9,5},{1... | collective-permute-start | bytes 405512 | tf_op jit(solution)/shard_map/ppermute | solution.py:250
  26.7 1.5 %collective-permute-start.13 = (bf16[16,4096]{1,0:T(8,128)(2,1)S(1)}, bf16[16,4096]{1,0:T(8,128)(2,1)S(1)}, u32[]{:S(2)}, u32[]{:S(2)}) collective-permute-start(bf16[16,4096]{1,0:T(8,128)(2,1)S(1)} %get-tuple-element.50), channel_id=1, source_target_pairs={{0,29},{1,28},{2,31},{3,30},{4,1},{5,0},{6,3},{7,2},{8,5},{9,4},{1... | collective-permute-start | bytes 393224 | tf_op jit(solution)/shard_map/ppermute | solution.py:250
  28.2 1.2 %collective-permute-start.14 = (bf16[16,4096]{1,0:T(8,128)(2,1)S(1)}, bf16[16,4096]{1,0:T(8,128)(2,1)S(1)}, u32[]{:S(2)}, u32[]{:S(2)}) collective-permute-start(bf16[16,4096]{1,0:T(8,128)(2,1)S(1)} %get-tuple-element.51), channel_id=1, source_target_pairs={{0,30},{1,31},{2,28},{3,29},{4,2},{5,3},{6,0},{7,1},{8,6},{9,7},{1... | collective-permute-start | bytes 393224 | tf_op jit(solution)/shard_map/ppermute | solution.py:250
  29.4 0.3 collective-permute-done.6.refs_3_
  29.7 2.1 %collective-permute-start.15 = (bf16[16,4096]{1,0:T(8,128)(2,1)S(1)}, bf16[16,4096]{1,0:T(8,128)(2,1)S(1)}, u32[]{:S(2)}, u32[]{:S(2)}) collective-permute-start(bf16[16,4096]{1,0:T(8,128)(2,1)S(1)} %get-tuple-element.52), channel_id=1, source_target_pairs={{0,31},{1,30},{2,29},{3,28},{4,3},{5,2},{6,1},{7,0},{8,7},{9,6},{1... | collective-permute-start | bytes 393224 | tf_op jit(solution)/shard_map/ppermute | solution.py:250
  31.8 1.3 %shard_map.123 = bf16[1,128,4096]{2,1,0:T(8,128)(2,1)} custom-call(bf16[16,4352]{1,0:T(8,128)(2,1)S(1)} %collective-permute-done.3.refs_0_, bf16[16,4096]{1,0:T(8,128)(2,1)S(1)} %collective-permute-done.4.refs_1_, bf16[16,4096]{1,0:T(8,128)(2,1)S(1)} %collective-permute-done.5.refs_2_, bf16[16,4096]{1,0:T(8,128)(2,1)S(1)} %collective-permute-done.6.refs_3_), custom_call_target="tpu_custom_call" | custom-call | flops 16777216 | bytes 1581056 | tf_op jit(solution)/shard_map/pallas_call | solution.py:32
  33.1 0.7 %collective-permute-start.7 = (f32[16,64]{1,0:T(8,128)S(1)}, f32[16,64]{1,0:T(8,128)S(1)}, u32[]{:S(2)}, u32[]{:S(2)}) collective-permute-start(f32[16,64]{1,0:T(8,128)S(1)} %get-tuple-element.45.own_ref), channel_id=1, source_target_pairs={{0,1},{1,0},{2,3},{3,2},{4,5},{5,4},{6,7},{7,6},{8,9},{9,8},{10,11... | collective-permute-start | bytes 12296 | tf_op jit(solution)/shard_map/ppermute | solution.py:250
  33.7 3.1 %collective-permute-done.7.other_ref = f32[16,64]{1,0:T(8,128)S(1)} collective-permute-done((f32[16,64]{1,0:T(8,128)S(1)}, f32[16,64]{1,0:T(8,128)S(1)}, u32[]{:S(2)}, u32[]{:S(2)}) %collective-permute-start.7) | collective-permute-done | bytes 4128 | tf_op jit(solution)/shard_map/ppermute | solution.py:250
  36.8 0.1 shard_map.124.pair_ref
  36.9 1.6 %collective-permute-start.8 = (f32[16,64]{1,0:T(8,128)S(1)}, f32[16,64]{1,0:T(8,128)S(1)}, u32[]{:S(2)}, u32[]{:S(2)}) collective-permute-start(f32[16,64]{1,0:T(8,128)S(1)} %shard_map.124.pair_ref), channel_id=1, source_target_pairs={{0,2},{1,3},{2,0},{3,1},{4,6},{5,7},{6,4},{7,5},{8,10},{9,11},{10,... | collective-permute-start | bytes 12296 | tf_op jit(solution)/shard_map/ppermute | solution.py:250
  38.5 1.0 %shard_map.128 = f32[16,256]{1,0:T(8,128)} custom-call(bf16[16,4096]{1,0:T(8,128)(2,1)S(1)} %get-tuple-element.46.refs_0_, bf16[16,4096]{1,0:T(8,128)(2,1)S(1)} %collective-permute-done.9.refs_1_, bf16[16,4096]{1,0:T(8,128)(2,1)S(1)} %collective-permute-done.10.refs_2_, bf16[16,4096]{1,0:T(8,128)(2,1)S(1)} %collective-permute-done.11.refs_3_, ...), custom_call_target="tpu_custom_call" | custom-call | flops 8388608 | bytes 704512 | tf_op jit(solution)/shard_map/pallas_call | solution.py:32
  39.5 1.0 %collective-permute-done.8.other_ref = f32[16,64]{1,0:T(8,128)S(1)} collective-permute-done((f32[16,64]{1,0:T(8,128)S(1)}, f32[16,64]{1,0:T(8,128)S(1)}, u32[]{:S(2)}, u32[]{:S(2)}) %collective-permute-start.8) | collective-permute-done | bytes 4128 | tf_op jit(solution)/shard_map/ppermute | solution.py:250
  40.6 0.9 %shard_map.125 = f32[1,1,16,1024]{3,2,1,0:T(8,128)} custom-call(f32[16,64]{1,0:T(8,128)S(1)} %shard_map.124.pair_ref, f32[16,64]{1,0:T(8,128)S(1)} %collective-permute-done.8.other_ref, bf16[16,4096]{1,0:T(8,128)(2,1)S(1)} %get-tuple-element.46.refs_0_, bf16[16,4096]{1,0:T(8,128)(2,1)S(1)} %collective-permute-done.9.refs_1_, ...), custom_call_target="tpu_custom_call" | custom-call | flops 4194304 | bytes 598016 | tf_op jit(solution)/shard_map/pallas_call | solution.py:32
  41.4 1.3 %shard_map.127 = bf16[1,128,4096]{2,1,0:T(8,128)(2,1)} custom-call(bf16[16,4224]{1,0:T(8,128)(2,1)S(1)} %collective-permute-done.12.refs_0_, bf16[16,4096]{1,0:T(8,128)(2,1)S(1)} %collective-permute-done.13.refs_1_, bf16[16,4096]{1,0:T(8,128)(2,1)S(1)} %collective-permute-done.14.refs_2_, bf16[16,4096]{1,0:T(8,128)(2,1)S(1)} %collective-permute-done.15.refs_3_), custom_call_target="tpu_custom_call" | custom-call | flops 16777216 | bytes 1576960 | tf_op jit(solution)/shard_map/pallas_call | solution.py:32
  (9 shorter events, 0.0 us)
Async XLA Ops:
  2.4 12.0 %collective-permute-start = (bf16[16,4096]{1,0:T(8,128)(2,1)S(1)}, bf16[16,4096]{1,0:T(8,128)(2,1)S(1)}, u32[]{:S(2)}, u32[]{:S(2)}) collective-permute-start(bf16[16,4096]{1,0:T(8,128)(2,1)S(1)} %get-tuple-element.33.refs_0_), channel_id=1, source_target_pairs={{0,1},{1,0},{2,3},{3,2},{4,5},{5,4},{6,7},{7,6},{8,9},{9,8},{10,11... | collective-permute-start | bytes 393224 | tf_op jit(solution)/shard_map/ppermute | solution.py:250
  5.4 9.1 %collective-permute-start.1 = (bf16[16,4096]{1,0:T(8,128)(2,1)S(1)}, bf16[16,4096]{1,0:T(8,128)(2,1)S(1)}, u32[]{:S(2)}, u32[]{:S(2)}) collective-permute-start(bf16[16,4096]{1,0:T(8,128)(2,1)S(1)} %get-tuple-element.33.refs_0_), channel_id=1, source_target_pairs={{0,2},{1,3},{2,0},{3,1},{4,6},{5,7},{6,4},{7,5},{8,10},{9,11},{10,... | collective-permute-start | bytes 393224 | tf_op jit(solution)/shard_map/ppermute | solution.py:250
  6.9 7.6 %collective-permute-start.2 = (bf16[16,4096]{1,0:T(8,128)(2,1)S(1)}, bf16[16,4096]{1,0:T(8,128)(2,1)S(1)}, u32[]{:S(2)}, u32[]{:S(2)}) collective-permute-start(bf16[16,4096]{1,0:T(8,128)(2,1)S(1)} %get-tuple-element.33.refs_0_), channel_id=1, source_target_pairs={{0,3},{1,2},{2,1},{3,0},{4,7},{5,6},{6,5},{7,4},{8,11},{9,10},{10,... | collective-permute-start | bytes 393224 | tf_op jit(solution)/shard_map/ppermute | solution.py:250
  10.9 8.7 %collective-permute-start.10 = (bf16[16,4096]{1,0:T(8,128)(2,1)S(1)}, bf16[16,4096]{1,0:T(8,128)(2,1)S(1)}, u32[]{:S(2)}, u32[]{:S(2)}) collective-permute-start(bf16[16,4096]{1,0:T(8,128)(2,1)S(1)} %get-tuple-element.46.refs_0_), channel_id=1, source_target_pairs={{0,2},{1,3},{2,0},{3,1},{4,6},{5,7},{6,4},{7,5},{8,10},{9,11},{10,... | collective-permute-start | bytes 393224 | tf_op jit(solution)/shard_map/ppermute | solution.py:250
  12.9 7.7 %collective-permute-start.11 = (bf16[16,4096]{1,0:T(8,128)(2,1)S(1)}, bf16[16,4096]{1,0:T(8,128)(2,1)S(1)}, u32[]{:S(2)}, u32[]{:S(2)}) collective-permute-start(bf16[16,4096]{1,0:T(8,128)(2,1)S(1)} %get-tuple-element.46.refs_0_), channel_id=1, source_target_pairs={{0,3},{1,2},{2,1},{3,0},{4,7},{5,6},{6,5},{7,4},{8,11},{9,10},{10,... | collective-permute-start | bytes 393224 | tf_op jit(solution)/shard_map/ppermute | solution.py:250
  14.4 8.0 %collective-permute-start.9 = (bf16[16,4096]{1,0:T(8,128)(2,1)S(1)}, bf16[16,4096]{1,0:T(8,128)(2,1)S(1)}, u32[]{:S(2)}, u32[]{:S(2)}) collective-permute-start(bf16[16,4096]{1,0:T(8,128)(2,1)S(1)} %get-tuple-element.46.refs_0_), channel_id=1, source_target_pairs={{0,1},{1,0},{2,3},{3,2},{4,5},{5,4},{6,7},{7,6},{8,9},{9,8},{10,11... | collective-permute-start | bytes 393224 | tf_op jit(solution)/shard_map/ppermute | solution.py:250
  16.3 15.4 %collective-permute-start.3 = (bf16[16,4352]{1,0:T(8,128)(2,1)S(1)}, bf16[16,4352]{1,0:T(8,128)(2,1)S(1)}, u32[]{:S(2)}, u32[]{:S(2)}) collective-permute-start(bf16[16,4352]{1,0:T(8,128)(2,1)S(1)} %get-tuple-element.40), channel_id=1, source_target_pairs={{0,4},{1,5},{2,6},{3,7},{4,8},{5,9},{6,10},{7,11},{8,12},{9,13},{1... | collective-permute-start | bytes 417800 | tf_op jit(solution)/shard_map/ppermute | solution.py:250
  16.4 10.3 %collective-permute-start.4 = (bf16[16,4096]{1,0:T(8,128)(2,1)S(1)}, bf16[16,4096]{1,0:T(8,128)(2,1)S(1)}, u32[]{:S(2)}, u32[]{:S(2)}) collective-permute-start(bf16[16,4096]{1,0:T(8,128)(2,1)S(1)} %get-tuple-element.41), channel_id=1, source_target_pairs={{0,5},{1,4},{2,7},{3,6},{4,9},{5,8},{6,11},{7,10},{8,13},{9,12},{1... | collective-permute-start | bytes 393224 | tf_op jit(solution)/shard_map/ppermute | solution.py:250
  19.6 8.6 %collective-permute-start.5 = (bf16[16,4096]{1,0:T(8,128)(2,1)S(1)}, bf16[16,4096]{1,0:T(8,128)(2,1)S(1)}, u32[]{:S(2)}, u32[]{:S(2)}) collective-permute-start(bf16[16,4096]{1,0:T(8,128)(2,1)S(1)} %get-tuple-element.42), channel_id=1, source_target_pairs={{0,6},{1,7},{2,4},{3,5},{4,10},{5,11},{6,8},{7,9},{8,14},{9,15},{1... | collective-permute-start | bytes 393224 | tf_op jit(solution)/shard_map/ppermute | solution.py:250
  20.6 9.0 %collective-permute-start.6 = (bf16[16,4096]{1,0:T(8,128)(2,1)S(1)}, bf16[16,4096]{1,0:T(8,128)(2,1)S(1)}, u32[]{:S(2)}, u32[]{:S(2)}) collective-permute-start(bf16[16,4096]{1,0:T(8,128)(2,1)S(1)} %get-tuple-element.43), channel_id=1, source_target_pairs={{0,7},{1,6},{2,5},{3,4},{4,11},{5,10},{6,9},{7,8},{8,15},{9,14},{1... | collective-permute-start | bytes 393224 | tf_op jit(solution)/shard_map/ppermute | solution.py:250
  24.9 16.6 %collective-permute-start.12 = (bf16[16,4224]{1,0:T(8,128)(2,1)S(1)}, bf16[16,4224]{1,0:T(8,128)(2,1)S(1)}, u32[]{:S(2)}, u32[]{:S(2)}) collective-permute-start(bf16[16,4224]{1,0:T(8,128)(2,1)S(1)} %get-tuple-element.49), channel_id=1, source_target_pairs={{0,28},{1,29},{2,30},{3,31},{4,0},{5,1},{6,2},{7,3},{8,4},{9,5},{1... | collective-permute-start | bytes 405512 | tf_op jit(solution)/shard_map/ppermute | solution.py:250
  26.7 14.7 %collective-permute-start.13 = (bf16[16,4096]{1,0:T(8,128)(2,1)S(1)}, bf16[16,4096]{1,0:T(8,128)(2,1)S(1)}, u32[]{:S(2)}, u32[]{:S(2)}) collective-permute-start(bf16[16,4096]{1,0:T(8,128)(2,1)S(1)} %get-tuple-element.50), channel_id=1, source_target_pairs={{0,29},{1,28},{2,31},{3,30},{4,1},{5,0},{6,3},{7,2},{8,5},{9,4},{1... | collective-permute-start | bytes 393224 | tf_op jit(solution)/shard_map/ppermute | solution.py:250
  28.2 13.2 %collective-permute-start.14 = (bf16[16,4096]{1,0:T(8,128)(2,1)S(1)}, bf16[16,4096]{1,0:T(8,128)(2,1)S(1)}, u32[]{:S(2)}, u32[]{:S(2)}) collective-permute-start(bf16[16,4096]{1,0:T(8,128)(2,1)S(1)} %get-tuple-element.51), channel_id=1, source_target_pairs={{0,30},{1,31},{2,28},{3,29},{4,2},{5,3},{6,0},{7,1},{8,6},{9,7},{1... | collective-permute-start | bytes 393224 | tf_op jit(solution)/shard_map/ppermute | solution.py:250
  29.7 11.7 %collective-permute-start.15 = (bf16[16,4096]{1,0:T(8,128)(2,1)S(1)}, bf16[16,4096]{1,0:T(8,128)(2,1)S(1)}, u32[]{:S(2)}, u32[]{:S(2)}) collective-permute-start(bf16[16,4096]{1,0:T(8,128)(2,1)S(1)} %get-tuple-element.52), channel_id=1, source_target_pairs={{0,31},{1,30},{2,29},{3,28},{4,3},{5,2},{6,1},{7,0},{8,7},{9,6},{1... | collective-permute-start | bytes 393224 | tf_op jit(solution)/shard_map/ppermute | solution.py:250
  33.1 3.8 %collective-permute-start.7 = (f32[16,64]{1,0:T(8,128)S(1)}, f32[16,64]{1,0:T(8,128)S(1)}, u32[]{:S(2)}, u32[]{:S(2)}) collective-permute-start(f32[16,64]{1,0:T(8,128)S(1)} %get-tuple-element.45.own_ref), channel_id=1, source_target_pairs={{0,1},{1,0},{2,3},{3,2},{4,5},{5,4},{6,7},{7,6},{8,9},{9,8},{10,11... | collective-permute-start | bytes 12296 | tf_op jit(solution)/shard_map/ppermute | solution.py:250
  36.9 3.7 %collective-permute-start.8 = (f32[16,64]{1,0:T(8,128)S(1)}, f32[16,64]{1,0:T(8,128)S(1)}, u32[]{:S(2)}, u32[]{:S(2)}) collective-permute-start(f32[16,64]{1,0:T(8,128)S(1)} %shard_map.124.pair_ref), channel_id=1, source_target_pairs={{0,2},{1,3},{2,0},{3,1},{4,6},{5,7},{6,4},{7,5},{8,10},{9,11},{10,... | collective-permute-start | bytes 12296 | tf_op jit(solution)/shard_map/ppermute | solution.py:250

commit v7 on v5

--- a/solution.py
+++ b/solution.py
@@ -87,67 +87,22 @@
         rows_ref[:, part] = f32dot(pick, x_ref[:, part]).astype(jnp.bfloat16)
 
 
-def load(
-    place_ref,
-    cot_hbm,
-    gate_hbm,
-    up_hbm,
-    down_hbm,
-    a_hbm,
-    b_hbm,
-    rows_ref,
-    gate_ref,
-    up_ref,
-    down_ref,
-    a_ref,
-    b_ref,
-    cot_ref,
-    raw_ref,
-    cot_sems,
-    weight_sems,
-    small_sems,
-):
-    units, width = raw_ref.shape
-    band = units // CHUNKS
-    span = width // CHUNKS
-    cot_copies = fetch(cot_hbm, cot_ref, cot_sems)
-    small = [
-        pltpu.make_async_copy(a_hbm, a_ref, small_sems.at[0]),
-        pltpu.make_async_copy(b_hbm, b_ref, small_sems.at[1]),
-    ]
-    for copy in small:
-        copy.start()
-    copies = []
-    for i, (hbm, ref) in enumerate(((down_hbm, raw_ref), (gate_hbm, gate_ref), (up_hbm, up_ref))):
-        for c in range(CHUNKS):
-            bands = pl.ds(c * band, band)
-            copy = pltpu.make_async_copy(
-                hbm.at[0, bands, :], ref.at[bands, :], weight_sems.at[i * CHUNKS + c]
-            )
-            copy.start()
-            copies.append(copy)
+def gather_grads(place_ref, cot_hbm, rows_ref, cot_ref, sems):
+    copies = fetch(cot_hbm, cot_ref, sems)
+    span = cot_ref.shape[1] // CHUNKS
     place = place_ref[...]
     pick = picks(place)
     gate = jnp.sum(place, axis=1, keepdims=True)
     for c in range(CHUNKS):
-        cot_copies[c].wait()
+        copies[c].wait()
         part = slice(c * span, (c + 1) * span)
         rows_ref[:, part] = (f32dot(pick, cot_ref[:, part]) * gate).astype(jnp.bfloat16)
-    for copy in small + copies[:CHUNKS]:
-        copy.wait()
-    span = 512
-    for c in range(width // span):
-        part = slice(c * span, (c + 1) * span)
-        adapter = LOWRANK_SCALE * f32dot(a_ref[...], b_ref[:, part], FIRST)
-        down_ref[:, part] = (raw_ref[:, part].astype(jnp.float32) + adapter).astype(jnp.bfloat16)
-    for copy in copies[CHUNKS:]:
-        copy.wait()
 
 
 def forward(*refs):
-    x_refs, (gate_ref, up_ref, down_ref, a_ref) = refs[:SPLIT], refs[SPLIT:SPLIT + 4]
-    out_refs = refs[SPLIT + 4:2 * SPLIT + 4]
-    pre_gate_ref, pre_up_ref, hidden_ref, latent_ref = refs[2 * SPLIT + 4:]
+    x_refs, (gate_ref, up_ref, down_ref, a_ref, b_ref) = refs[:SPLIT], refs[SPLIT:SPLIT + 5]
+    out_refs = refs[SPLIT + 5:2 * SPLIT + 5]
+    pre_gate_ref, pre_up_ref, hidden_ref, latent_ref = refs[2 * SPLIT + 5:]
     rows = jnp.concatenate([r[...] for r in x_refs], axis=0)
     height, width = x_refs[0].shape
     pre_gate = f32dot(rows, gate_ref[...], LAST)
@@ -156,11 +111,13 @@
     pre_up_ref[...] = pre_up
     hidden = (pre_gate * jax.nn.sigmoid(pre_gate) * pre_up).astype(jnp.bfloat16)
     hidden_ref[...] = hidden
-    result = f32dot(hidden, down_ref[...]).astype(jnp.bfloat16)
+    latent = f32dot(a_ref[...], hidden, LAST).astype(jnp.bfloat16)
+    latent_ref[...] = latent
+    result = f32dot(hidden, down_ref[...])
+    result = result + f32dot(LOWRANK_SCALE * latent, b_ref[...], FIRST)
+    result = result.astype(jnp.bfloat16)
     for k, ref in enumerate(out_refs):
         ref[:, :width] = result[k * height:(k + 1) * height]
-    latent = f32dot(a_ref[...], hidden, LAST).astype(jnp.bfloat16)
-    latent_ref[...] = latent
     if out_refs[1].shape[1] > width:
         rank, count = latent.shape
         tail = jnp.concatenate(
@@ -172,11 +129,13 @@
 
 def backward(*refs):
     g_refs = refs[:SPLIT]
-    place_ref, pre_gate_ref, pre_up_ref, gate_ref, up_ref, down_ref = refs[SPLIT:SPLIT + 6]
-    out_refs = refs[SPLIT + 6:]
+    pre_gate_ref, pre_up_ref, gate_ref, up_ref, down_ref, a_ref, b_ref = refs[SPLIT:SPLIT + 7]
+    *out_refs, lowrank_ref = refs[SPLIT + 7:]
     rows = jnp.concatenate([r[...] for r in g_refs], axis=0)
     height, width = g_refs[0].shape
-    grad_hidden = f32dot(rows, down_ref[...], LAST)
+    lowrank = (LOWRANK_SCALE * f32dot(rows, b_ref[...], LAST)).astype(jnp.bfloat16)
+    lowrank_ref[...] = lowrank
+    grad_hidden = f32dot(rows, down_ref[...], LAST) + f32dot(lowrank, a_ref[...])
     pre_gate = pre_gate_ref[...]
     g = jax.nn.sigmoid(pre_gate)
     grad_gate = grad_hidden * pre_up_ref[...] * g * (1.0 + pre_gate * (1.0 - g))
@@ -185,10 +144,7 @@
     result = result + f32dot(grad_up.astype(jnp.bfloat16), up_ref[...])
     result = result.astype(jnp.bfloat16)
     for k, ref in enumerate(out_refs):
-        ref[:, :width] = result[k * height:(k + 1) * height]
-    out_refs[0][:, width:] = picks(place_ref[...])
-    for ref in out_refs[1:]:
-        ref[:, width:] = jnp.zeros((height, ref.shape[1] - width), jnp.bfloat16)
+        ref[...] = result[k * height:(k + 1) * height]
 
 
 def combine(gated, place_ref, *refs):
@@ -203,11 +159,8 @@
         out_ref[:, width:] = picks(place)
 
 
-def down_map_grad(*refs):
-    g_refs, (hidden_ref, b_ref, out_ref) = refs[:SPLIT], refs[SPLIT:]
-    rows = jnp.concatenate([r[...] for r in g_refs], axis=0)
-    lowrank = (LOWRANK_SCALE * f32dot(rows, b_ref[...], LAST)).astype(jnp.bfloat16)
-    out_ref[...] = f32dot(lowrank, hidden_ref[...], FIRST)
+def down_map_grad(lowrank_ref, hidden_ref, out_ref):
+    out_ref[...] = f32dot(lowrank_ref[...], hidden_ref[...], FIRST)
 
 
 def up_map_grad(latent_ref, *refs):
@@ -222,18 +175,14 @@
     out_ref[0, 0] = LOWRANK_SCALE * total
 
 
-def expand(*refs):
-    *part_refs, out_hbm, out_ref, sems = refs
+def expand(message_ref, out_hbm, out_ref, sems):
     width = out_ref.shape[1]
-    pick = part_refs[0][:, width:]
+    pick = message_ref[:, width:]
     span = width // CHUNKS
     copies = []
     for c in range(CHUNKS):
         part = slice(c * span, (c + 1) * span)
-        rows = part_refs[0][:, part]
-        if len(part_refs) > 1:
-            rows = sum(r[:, part].astype(jnp.float32) for r in part_refs).astype(jnp.bfloat16)
-        out_ref[:, part] = f32dot(pick, rows, FIRST).astype(jnp.bfloat16)
+        out_ref[:, part] = f32dot(pick, message_ref[:, part], FIRST).astype(jnp.bfloat16)
         columns = pl.ds(c * span, span)
         copy = pltpu.make_async_copy(
             out_ref.at[:, columns], out_hbm.at[0, :, columns], sems.at[c]
@@ -310,53 +259,45 @@
     x_rows = between_groups(x_rows, flight)
     x_blocks = [x_rows] + [shifted(x_rows, 0, k) for k in flips[1:]]
 
-    g_rows, gate_near, up_near, down_near, a_near, b_near = call(
-        load,
-        [sds(slots, width)]
-        + [sds(units, width)] * 3
-        + [sds(rank, units), sds(rank, width)],
+    (g_rows,) = call(
+        gather_grads,
+        [sds(slots, width)],
         (place,),
-        (cotangent, gate_weight, up_weight, down_weight, down_map, up_map),
-        scratch=[
-            pltpu.VMEM((tokens, width), jnp.bfloat16),
-            pltpu.VMEM((units, width), jnp.bfloat16),
-            dma((CHUNKS,)),
-            dma((3 * CHUNKS,)),
-            dma((2,)),
-        ],
+        (cotangent,),
+        scratch=[pltpu.VMEM((tokens, width), jnp.bfloat16), dma((CHUNKS,))],
         flops=200 * units * rank * width,
     )
+    weights = [
+        pltpu.with_memory_space_constraint(a, pltpu.VMEM)
+        for a in (gate_weight[0], up_weight[0], down_weight[0], down_map, up_map)
+    ]
     g_rows = between_groups(g_rows, flight)
     g_blocks = [g_rows] + [shifted(g_rows, 0, k) for k in flips[1:]]
 
     wide = width + tokens
-    out_blocks = call(
+    *out_blocks, pre_gate, pre_up, hidden, latent = call(
         forward,
         [sds(slots, width)]
         + [sds(slots, wide if flight == 1 else width)] * (SPLIT - 1)
         + [sds(rows, units, dtype=jnp.float32)] * 2
         + [sds(rows, units), sds(rank, rows)],
-        (*x_blocks, gate_near, up_near, down_near, a_near),
+        (*x_blocks, *weights),
         flops=60 * rows * units * width,
     )
-    *out_blocks, pre_gate, pre_up, hidden, latent = out_blocks
     out_parts = [out_blocks[0]] + [shifted(out_blocks[k], 0, k) for k in flips[1:]]
-    grad_blocks = call(
+    *grad_blocks, lowrank = call(
         backward,
-        [sds(slots, wide)] + [sds(slots, wide + tokens)] * (SPLIT - 1),
-        (*g_blocks, place, pre_gate, pre_up, gate_near, up_near, down_near),
+        [sds(slots, width)] * SPLIT + [sds(rows, rank)],
+        (*g_blocks, pre_gate, pre_up, *weights),
         flops=60 * rows * units * width,
     )
-    grad_parts = [shifted(grad_blocks[k], -1, k) for k in flips]
-
-    def merged(parts, gated, columns):
-        return call(functools.partial(combine, gated), [sds(slots, columns)], (place, *parts))[0]
+    grad_parts = [grad_blocks[0]] + [shifted(grad_blocks[k], 0, k) for k in flips[1:]]
 
     hidden, latent, _ = lax.optimization_barrier((hidden, latent, grad_blocks[0]))
     (a_grad,) = call(
         down_map_grad,
         [sds(rank, units, dtype=jnp.float32)],
-        (*g_blocks, hidden, b_near),
+        (lowrank, hidden),
         flops=200 * rows * rank * width,
     )
     if flight == 1:
@@ -372,28 +313,30 @@
         spread = jnp.where(mine[:, None, None], part[None], 0.0)
         b_grad = lax.psum_scatter(spread, "expert", scatter_dimension=2, tiled=True)[None]
 
-    out_parts, b_grad = lax.optimization_barrier((out_parts, b_grad))
-    if flight > 1:
-        out_parts = [between_groups(merged(out_parts, False, width), flight)]
-    message = shifted(merged(out_parts, True, wide), 1, 0)
-
-    def expanded(parts):
+    def merged(parts, gated, columns):
+        return call(functools.partial(combine, gated), [sds(slots, columns)], (place, *parts))[0]
+
+    def reduced(parts, gated):
+        if flight > 1:
+            parts = [between_groups(merged(parts, False, width), flight)]
+        return merged(parts, gated, wide)
+
+    def expanded(message):
         return call(
             expand,
             [sds(1, tokens, width)],
-            tuple(parts),
+            (message,),
             far_outs=True,
             scratch=[pltpu.VMEM((tokens, width), jnp.bfloat16), dma((CHUNKS,))],
             flops=2 * slots * tokens * width,
         )[0]
 
-    next_input = expanded([message])
-    if flight > 1:
-        total = sum(p[:, :width].astype(jnp.float32) for p in grad_parts).astype(jnp.bfloat16)
-        total = between_groups(total, flight)
-        grad_parts = [jnp.concatenate([total, grad_parts[0][:, width:]], axis=1)]
-    next_input, grad_parts = lax.optimization_barrier((next_input, grad_parts))
-    prev_grad = expanded(grad_parts)
+    out_message = shifted(reduced(out_parts, True), 1, 0)
+    grad_parts, a_grad, b_grad = lax.optimization_barrier((grad_parts, a_grad, b_grad))
+    grad_message = shifted(reduced(grad_parts, False), -1, 0)
+    next_input = expanded(out_message)
+    next_input, grad_message = lax.optimization_barrier((next_input, grad_message))
+    prev_grad = expanded(grad_message)
     return next_input, prev_grad, jnp.swapaxes(a_grad, 0, 1)[None], b_grad
 
 

time: 40.3 us -> 37.7 us (0.935); the launches traced: 40.1 us -> 37 us
  starting transfers between devices: 22.5 us -> 17.2 us
  waiting for transfers between devices: 2.34 us -> 6.31 us
  Pallas kernels: 14.5 us -> 12.7 us
    ppermute x14, starting transfers between devices: 22.5 us -> 17.2 us  [shifted(): return lax.ppermute(block, ('section', 'expert'), route)]
    ppermute x14, waiting for transfers between devices: 2.34 us -> 6.31 us  [shifted(): return lax.ppermute(block, ('section', 'expert'), route)]
    pallas_call x9 -> x10, Pallas kernels: 14.5 us -> 12.7 us  [call(): pl.pallas_call(body, out_shape=outs, in_specs=[NEAR] * len(args) + [FAR]...]
  transfers between devices with their start and end apart: 14 -> 14, of which waited for: 2 -> 6; matrix products, arithmetic and copies ran while one was open for 0% -> 0% of each run, Pallas kernels for 29% -> 26%
where the time goes in v7:
time: 37.7 us; the launch traced here: 37 us
  starting transfers between devices  17.2 us (46%)
  Pallas kernels  12.7 us (34%)
  waiting for transfers between devices  6.31 us (17%)
  between operations  0.73 us (2%)
    ppermute x14, starting transfers between devices, shifted(): return lax.ppermute(block, ('section', 'expert'), route)  17.2 us
    pallas_call x10, Pallas kernels, call(): pl.pallas_call(body, out_shape=outs, in_specs=[NEAR] * len(args) + [FAR]...  12.7 us
    ppermute x14, waiting for transfers between devices, shifted(): return lax.ppermute(block, ('section', 'expert'), route)  6.31 us
  transfers between devices with their start and end apart: 14, of which 6 were waited for; matrix products, arithmetic and copies ran while one was open for 0% of the time, Pallas kernels for 26%

profile of v7, /device:TPU:0, one launch (start us, length us, event | category | flops | bytes accessed | tf_op | source)
XLA Modules:
  0.0 37.0 jit_solution(10775870164590377337)
XLA Ops:
  0.6 1.7 %shard_map.120 = (bf16[16,4096]{1,0:T(8,128)(2,1)S(1)}, f32[16,128]{1,0:T(8,128)S(1)}) custom-call(s32[8,128]{1,0:T(8,128)} %bitcast.26, s32[8,128]{1,0:T(8,128)} %bitcast.27, bf16[1,128,4096]{2,1,0:T(8,128)(2,1)} %x_hbm.1), custom_call_target="tpu_custom_call" | custom-call | flops 16777216 | bytes 1196032 | tf_op jit(solution)/shard_map/pallas_call | solution.py:32
  2.4 4.0 %collective-permute-start.2 = (bf16[16,4096]{1,0:T(8,128)(2,1)S(1)}, bf16[16,4096]{1,0:T(8,128)(2,1)S(1)}, u32[]{:S(2)}, u32[]{:S(2)}) collective-permute-start(bf16[16,4096]{1,0:T(8,128)(2,1)S(1)} %get-tuple-element.30.refs_0_), channel_id=1, source_target_pairs={{0,3},{1,2},{2,1},{3,0},{4,7},{5,6},{6,5},{7,4},{8,11},{9,10},{10,... | collective-permute-start | bytes 393224 | tf_op jit(solution)/shard_map/ppermute | solution.py:203
  6.3 0.5 %collective-permute-start.1 = (bf16[16,4096]{1,0:T(8,128)(2,1)S(1)}, bf16[16,4096]{1,0:T(8,128)(2,1)S(1)}, u32[]{:S(2)}, u32[]{:S(2)}) collective-permute-start(bf16[16,4096]{1,0:T(8,128)(2,1)S(1)} %get-tuple-element.30.refs_0_), channel_id=1, source_target_pairs={{0,2},{1,3},{2,0},{3,1},{4,6},{5,7},{6,4},{7,5},{8,10},{9,11},{10,... | collective-permute-start | bytes 393224 | tf_op jit(solution)/shard_map/ppermute | solution.py:203
  6.8 0.1 collective-permute-start
  7.0 0.0 copy-start.4
  7.0 1.8 %shard_map.124.refs_0_.refs_3_ = bf16[16,4096]{1,0:T(8,128)(2,1)S(1)} custom-call(f32[16,128]{1,0:T(8,128)S(1)} %get-tuple-element.29.place_ref, bf16[1,128,4096]{2,1,0:T(8,128)(2,1)} %cot_hbm.1), custom_call_target="tpu_custom_call" | custom-call | flops 3355443200 | bytes 1187840 | tf_op jit(solution)/shard_map/pallas_call | solution.py:32
  8.8 2.9 %collective-permute-start.9 = (bf16[16,4096]{1,0:T(8,128)(2,1)S(1)}, bf16[16,4096]{1,0:T(8,128)(2,1)S(1)}, u32[]{:S(2)}, u32[]{:S(2)}) collective-permute-start(bf16[16,4096]{1,0:T(8,128)(2,1)S(1)} %shard_map.124.refs_0_.refs_3_), channel_id=1, source_target_pairs={{0,3},{1,2},{2,1},{3,0},{4,7},{5,6},{6,5},{7,4},{8,11},{9,10},{10,... | collective-permute-start | bytes 393224 | tf_op jit(solution)/shard_map/ppermute | solution.py:203
  11.7 0.5 %collective-permute-start.8 = (bf16[16,4096]{1,0:T(8,128)(2,1)S(1)}, bf16[16,4096]{1,0:T(8,128)(2,1)S(1)}, u32[]{:S(2)}, u32[]{:S(2)}) collective-permute-start(bf16[16,4096]{1,0:T(8,128)(2,1)S(1)} %shard_map.124.refs_0_.refs_3_), channel_id=1, source_target_pairs={{0,2},{1,3},{2,0},{3,1},{4,6},{5,7},{6,4},{7,5},{8,10},{9,11},{10,... | collective-permute-start | bytes 393224 | tf_op jit(solution)/shard_map/ppermute | solution.py:203
  12.2 0.5 %collective-permute-start.7 = (bf16[16,4096]{1,0:T(8,128)(2,1)S(1)}, bf16[16,4096]{1,0:T(8,128)(2,1)S(1)}, u32[]{:S(2)}, u32[]{:S(2)}) collective-permute-start(bf16[16,4096]{1,0:T(8,128)(2,1)S(1)} %shard_map.124.refs_0_.refs_3_), channel_id=1, source_target_pairs={{0,1},{1,0},{2,3},{3,2},{4,5},{5,4},{6,7},{7,6},{8,9},{9,8},{10,11... | collective-permute-start | bytes 393224 | tf_op jit(solution)/shard_map/ppermute | solution.py:203
  12.7 1.2 %collective-permute-done.1.refs_2_ = bf16[16,4096]{1,0:T(8,128)(2,1)S(1)} collective-permute-done((bf16[16,4096]{1,0:T(8,128)(2,1)S(1)}, bf16[16,4096]{1,0:T(8,128)(2,1)S(1)}, u32[]{:S(2)}, u32[]{:S(2)}) %collective-permute-start.1) | collective-permute-done | bytes 131104 | tf_op jit(solution)/shard_map/ppermute | solution.py:203
  13.9 0.1 collective-permute-done.refs_1_
  14.0 2.2 %shard_map.121 = (bf16[16,4096]{1,0:T(8,128)(2,1)S(1)}, bf16[16,4224]{1,0:T(8,128)(2,1)S(1)}, bf16[16,4224]{1,0:T(8,128)(2,1)S(1)}, bf16[16,4224]{1,0:T(8,128)(2...) custom-call(bf16[16,4096]{1,0:T(8,128)(2,1)S(1)} %get-tuple-element., ...), custom_call_target="tpu_custom_call" | custom-call | flops 4026531840 | bytes 7657472 | tf_op jit(solution)/shard_map/pallas_call | solution.py:32
  16.2 1.7 %collective-permute-start.3 = (bf16[16,4224]{1,0:T(8,128)(2,1)S(1)}, bf16[16,4224]{1,0:T(8,128)(2,1)S(1)}, u32[]{:S(2)}, u32[]{:S(2)}) collective-permute-start(bf16[16,4224]{1,0:T(8,128)(2,1)S(1)} %get-tuple-element.32), channel_id=1, source_target_pairs={{0,1},{1,0},{2,3},{3,2},{4,5},{5,4},{6,7},{7,6},{8,9},{9,8},{10,11... | collective-permute-start | bytes 405512 | tf_op jit(solution)/shard_map/ppermute | solution.py:203
  17.8 1.6 %collective-permute-start.4 = (bf16[16,4224]{1,0:T(8,128)(2,1)S(1)}, bf16[16,4224]{1,0:T(8,128)(2,1)S(1)}, u32[]{:S(2)}, u32[]{:S(2)}) collective-permute-start(bf16[16,4224]{1,0:T(8,128)(2,1)S(1)} %get-tuple-element.33), channel_id=1, source_target_pairs={{0,2},{1,3},{2,0},{3,1},{4,6},{5,7},{6,4},{7,5},{8,10},{9,11},{10,... | collective-permute-start | bytes 405512 | tf_op jit(solution)/shard_map/ppermute | solution.py:203
  19.4 0.3 collective-permute-start.5
  19.7 2.8 %shard_map.125 = (bf16[16,4096]{1,0:T(8,128)(2,1)S(1)}, bf16[16,4096]{1,0:T(8,128)(2,1)S(1)}, bf16[16,4096]{1,0:T(8,128)(2,1)S(1)}, bf16[16,4096]{1,0:T(8,128)(2,1)S(1)}, bf16[64,16]{1,0:T(8,128)(2,1)S(1)}) custom-call(bf16[16,4096]{1,0:T(8,128)(2,1)S(1)} %shard_map.124.refs_0_.refs_3_, bf16[16,4096]{1,0:T(8,128)(2,1)S(1)} %collective-permute-done.7.refs_1_.refs_4_, ...), custom_call_target="tpu_custom_call" | custom-call | flops 4026531840 | bytes 7612416 | tf_op jit(solution)/shard_map/pallas_call | solution.py:32
  22.5 1.7 %collective-permute-start.10 = (bf16[16,4096]{1,0:T(8,128)(2,1)S(1)}, bf16[16,4096]{1,0:T(8,128)(2,1)S(1)}, u32[]{:S(2)}, u32[]{:S(2)}) collective-permute-start(bf16[16,4096]{1,0:T(8,128)(2,1)S(1)} %get-tuple-element.38), channel_id=1, source_target_pairs={{0,1},{1,0},{2,3},{3,2},{4,5},{5,4},{6,7},{7,6},{8,9},{9,8},{10,11... | collective-permute-start | bytes 393224 | tf_op jit(solution)/shard_map/ppermute | solution.py:203
  24.2 1.6 %collective-permute-start.11 = (bf16[16,4096]{1,0:T(8,128)(2,1)S(1)}, bf16[16,4096]{1,0:T(8,128)(2,1)S(1)}, u32[]{:S(2)}, u32[]{:S(2)}) collective-permute-start(bf16[16,4096]{1,0:T(8,128)(2,1)S(1)} %get-tuple-element.39), channel_id=1, source_target_pairs={{0,2},{1,3},{2,0},{3,1},{4,6},{5,7},{6,4},{7,5},{8,10},{9,11},{10,... | collective-permute-start | bytes 393224 | tf_op jit(solution)/shard_map/ppermute | solution.py:203
  25.7 0.3 collective-permute-start.12
  26.1 0.8 %shard_map.126 = f32[16,256]{1,0:T(8,128)} custom-call(bf16[64,16]{1,0:T(8,128)(2,1)S(1)} %get-tuple-element.41.lowrank_ref, bf16[64,256]{1,0:T(8,128)(2,1)S(1)} %get-tuple-element.44.hidden_ref), custom_call_target="tpu_custom_call" | custom-call | flops 838860800 | bytes 51200 | tf_op jit(solution)/shard_map/pallas_call | solution.py:32
  26.8 0.1 shard_map.122
  26.9 0.1 collective-permute-start.6
  27.0 0.9 %shard_map.127 = f32[1,1,16,1024]{3,2,1,0:T(8,128)} custom-call(bf16[16,64]{1,0:T(8,128)(2,1)S(1)} %get-tuple-element.45.latent_ref, bf16[16,4224]{1,0:T(8,128)(2,1)S(1)} %collective-permute-done.3.refs_1_.refs_0_, bf16[16,4224]{1,0:T(8,128)(2,1)S(1)} %collective-permute-done.4.refs_2_.refs_1_, bf16[16,4224]{1,0:T(8,128)(2,1)S(1)} %collective-permute-done.5.refs_3_.refs_2_, ...), custom_call_target="tpu_custom_call" | custom-call | flops 838860800 | bytes 997376 | tf_op jit(solution)/shard_map/pallas_call | solution.py:32
  27.9 0.7 %collective-permute-done.10.refs_1_ = bf16[16,4096]{1,0:T(8,128)(2,1)S(1)} collective-permute-done((bf16[16,4096]{1,0:T(8,128)(2,1)S(1)}, bf16[16,4096]{1,0:T(8,128)(2,1)S(1)}, u32[]{:S(2)}, u32[]{:S(2)}) %collective-permute-start.10) | collective-permute-done | bytes 131104 | tf_op jit(solution)/shard_map/ppermute | solution.py:203
  28.5 1.8 %collective-permute-done.11.refs_2_ = bf16[16,4096]{1,0:T(8,128)(2,1)S(1)} collective-permute-done((bf16[16,4096]{1,0:T(8,128)(2,1)S(1)}, bf16[16,4096]{1,0:T(8,128)(2,1)S(1)}, u32[]{:S(2)}, u32[]{:S(2)}) %collective-permute-start.11) | collective-permute-done | bytes 131104 | tf_op jit(solution)/shard_map/ppermute | solution.py:203
  30.4 1.2 %collective-permute-done.12.refs_3_ = bf16[16,4096]{1,0:T(8,128)(2,1)S(1)} collective-permute-done((bf16[16,4096]{1,0:T(8,128)(2,1)S(1)}, bf16[16,4096]{1,0:T(8,128)(2,1)S(1)}, u32[]{:S(2)}, u32[]{:S(2)}) %collective-permute-start.12) | collective-permute-done | bytes 131104 | tf_op jit(solution)/shard_map/ppermute | solution.py:203
  31.6 0.1 shard_map.128
  31.6 1.6 %collective-permute-start.13 = (bf16[16,4224]{1,0:T(8,128)(2,1)S(1)}, bf16[16,4224]{1,0:T(8,128)(2,1)S(1)}, u32[]{:S(2)}, u32[]{:S(2)}) collective-permute-start(bf16[16,4224]{1,0:T(8,128)(2,1)S(1)} %shard_map.128), channel_id=1, source_target_pairs={{0,28},{1,29},{2,30},{3,31},{4,0},{5,1},{6,2},{7,3},{8,4},{9,5},{1... | collective-permute-start | bytes 405512 | tf_op jit(solution)/shard_map/ppermute | solution.py:203
  33.2 0.0 collective-permute-done.6.message_ref
  33.2 1.2 %shard_map.123 = bf16[1,128,4096]{2,1,0:T(8,128)(2,1)} custom-call(bf16[16,4224]{1,0:T(8,128)(2,1)S(1)} %collective-permute-done.6.message_ref), custom_call_target="tpu_custom_call" | custom-call | flops 16777216 | bytes 1183744 | tf_op jit(solution)/shard_map/pallas_call | solution.py:32
  34.5 1.3 %collective-permute-done.13.message_ref = bf16[16,4224]{1,0:T(8,128)(2,1)S(1)} collective-permute-done((bf16[16,4224]{1,0:T(8,128)(2,1)S(1)}, bf16[16,4224]{1,0:T(8,128)(2,1)S(1)}, u32[]{:S(2)}, u32[]{:S(2)}) %collective-permute-start.13) | collective-permute-done | bytes 135200 | tf_op jit(solution)/shard_map/ppermute | solution.py:203
  35.8 1.2 %shard_map.129 = bf16[1,128,4096]{2,1,0:T(8,128)(2,1)} custom-call(bf16[16,4224]{1,0:T(8,128)(2,1)S(1)} %collective-permute-done.13.message_ref), custom_call_target="tpu_custom_call" | custom-call | flops 16777216 | bytes 1183744 | tf_op jit(solution)/shard_map/pallas_call | solution.py:32
  (16 shorter events, 0.0 us)
Async XLA Ops:
  2.4 9.8 %collective-permute-start.2 = (bf16[16,4096]{1,0:T(8,128)(2,1)S(1)}, bf16[16,4096]{1,0:T(8,128)(2,1)S(1)}, u32[]{:S(2)}, u32[]{:S(2)}) collective-permute-start(bf16[16,4096]{1,0:T(8,128)(2,1)S(1)} %get-tuple-element.30.refs_0_), channel_id=1, source_target_pairs={{0,3},{1,2},{2,1},{3,0},{4,7},{5,6},{6,5},{7,4},{8,11},{9,10},{10,... | collective-permute-start | bytes 393224 | tf_op jit(solution)/shard_map/ppermute | solution.py:203
  6.3 7.5 %collective-permute-start.1 = (bf16[16,4096]{1,0:T(8,128)(2,1)S(1)}, bf16[16,4096]{1,0:T(8,128)(2,1)S(1)}, u32[]{:S(2)}, u32[]{:S(2)}) collective-permute-start(bf16[16,4096]{1,0:T(8,128)(2,1)S(1)} %get-tuple-element.30.refs_0_), channel_id=1, source_target_pairs={{0,2},{1,3},{2,0},{3,1},{4,6},{5,7},{6,4},{7,5},{8,10},{9,11},{10,... | collective-permute-start | bytes 393224 | tf_op jit(solution)/shard_map/ppermute | solution.py:203
  6.8 7.1 %collective-permute-start = (bf16[16,4096]{1,0:T(8,128)(2,1)S(1)}, bf16[16,4096]{1,0:T(8,128)(2,1)S(1)}, u32[]{:S(2)}, u32[]{:S(2)}) collective-permute-start(bf16[16,4096]{1,0:T(8,128)(2,1)S(1)} %get-tuple-element.30.refs_0_), channel_id=1, source_target_pairs={{0,1},{1,0},{2,3},{3,2},{4,5},{5,4},{6,7},{7,6},{8,9},{9,8},{10,11... | collective-permute-start | bytes 393224 | tf_op jit(solution)/shard_map/ppermute | solution.py:203
  7.0 7.0 %copy-start = (bf16[1,256,4096]{2,1,0:T(8,128)(2,1)S(1)}, bf16[1,256,4096]{2,1,0:T(8,128)(2,1)}, u32[]{:S(2)}) copy-start(bf16[1,256,4096]{2,1,0:T(8,128)(2,1)} %param.12) | copy-start | bytes 6291460
  7.0 7.0 %copy-start.1 = (bf16[1,256,4096]{2,1,0:T(8,128)(2,1)S(1)}, bf16[1,256,4096]{2,1,0:T(8,128)(2,1)}, u32[]{:S(2)}) copy-start(bf16[1,256,4096]{2,1,0:T(8,128)(2,1)} %param.13) | copy-start | bytes 6291460
  7.0 7.0 %copy-start.2 = (bf16[1,256,4096]{2,1,0:T(8,128)(2,1)S(1)}, bf16[1,256,4096]{2,1,0:T(8,128)(2,1)}, u32[]{:S(2)}) copy-start(bf16[1,256,4096]{2,1,0:T(8,128)(2,1)} %param.14) | copy-start | bytes 6291460
  7.0 7.0 %copy-start.3 = (bf16[1,1,16,4096]{3,2,1,0:T(8,128)(2,1)S(1)}, bf16[1,1,16,4096]{3,2,1,0:T(8,128)(2,1)}, u32[]{:S(2)}) copy-start(bf16[1,1,16,4096]{3,2,1,0:T(8,128)(2,1)} %param.16) | copy-start | bytes 393220
  7.0 7.0 %copy-start.4 = (bf16[1,256,16]{1,2,0:T(8,128)(2,1)S(1)}, bf16[1,256,16]{1,2,0:T(8,128)(2,1)}, u32[]{:S(2)}) copy-start(bf16[1,256,16]{1,2,0:T(8,128)(2,1)} %param.15) | copy-start | bytes 24580
  8.8 10.6 %collective-permute-start.9 = (bf16[16,4096]{1,0:T(8,128)(2,1)S(1)}, bf16[16,4096]{1,0:T(8,128)(2,1)S(1)}, u32[]{:S(2)}, u32[]{:S(2)}) collective-permute-start(bf16[16,4096]{1,0:T(8,128)(2,1)S(1)} %shard_map.124.refs_0_.refs_3_), channel_id=1, source_target_pairs={{0,3},{1,2},{2,1},{3,0},{4,7},{5,6},{6,5},{7,4},{8,11},{9,10},{10,... | collective-permute-start | bytes 393224 | tf_op jit(solution)/shard_map/ppermute | solution.py:203
  11.7 8.0 %collective-permute-start.8 = (bf16[16,4096]{1,0:T(8,128)(2,1)S(1)}, bf16[16,4096]{1,0:T(8,128)(2,1)S(1)}, u32[]{:S(2)}, u32[]{:S(2)}) collective-permute-start(bf16[16,4096]{1,0:T(8,128)(2,1)S(1)} %shard_map.124.refs_0_.refs_3_), channel_id=1, source_target_pairs={{0,2},{1,3},{2,0},{3,1},{4,6},{5,7},{6,4},{7,5},{8,10},{9,11},{10,... | collective-permute-start | bytes 393224 | tf_op jit(solution)/shard_map/ppermute | solution.py:203
  12.2 7.5 %collective-permute-start.7 = (bf16[16,4096]{1,0:T(8,128)(2,1)S(1)}, bf16[16,4096]{1,0:T(8,128)(2,1)S(1)}, u32[]{:S(2)}, u32[]{:S(2)}) collective-permute-start(bf16[16,4096]{1,0:T(8,128)(2,1)S(1)} %shard_map.124.refs_0_.refs_3_), channel_id=1, source_target_pairs={{0,1},{1,0},{2,3},{3,2},{4,5},{5,4},{6,7},{7,6},{8,9},{9,8},{10,11... | collective-permute-start | bytes 393224 | tf_op jit(solution)/shard_map/ppermute | solution.py:203
  16.2 9.5 %collective-permute-start.3 = (bf16[16,4224]{1,0:T(8,128)(2,1)S(1)}, bf16[16,4224]{1,0:T(8,128)(2,1)S(1)}, u32[]{:S(2)}, u32[]{:S(2)}) collective-permute-start(bf16[16,4224]{1,0:T(8,128)(2,1)S(1)} %get-tuple-element.32), channel_id=1, source_target_pairs={{0,1},{1,0},{2,3},{3,2},{4,5},{5,4},{6,7},{7,6},{8,9},{9,8},{10,11... | collective-permute-start | bytes 405512 | tf_op jit(solution)/shard_map/ppermute | solution.py:203
  17.8 9.0 %collective-permute-start.4 = (bf16[16,4224]{1,0:T(8,128)(2,1)S(1)}, bf16[16,4224]{1,0:T(8,128)(2,1)S(1)}, u32[]{:S(2)}, u32[]{:S(2)}) collective-permute-start(bf16[16,4224]{1,0:T(8,128)(2,1)S(1)} %get-tuple-element.33), channel_id=1, source_target_pairs={{0,2},{1,3},{2,0},{3,1},{4,6},{5,7},{6,4},{7,5},{8,10},{9,11},{10,... | collective-permute-start | bytes 405512 | tf_op jit(solution)/shard_map/ppermute | solution.py:203
  19.4 7.5 %collective-permute-start.5 = (bf16[16,4224]{1,0:T(8,128)(2,1)S(1)}, bf16[16,4224]{1,0:T(8,128)(2,1)S(1)}, u32[]{:S(2)}, u32[]{:S(2)}) collective-permute-start(bf16[16,4224]{1,0:T(8,128)(2,1)S(1)} %get-tuple-element.34), channel_id=1, source_target_pairs={{0,3},{1,2},{2,1},{3,0},{4,7},{5,6},{6,5},{7,4},{8,11},{9,10},{10,... | collective-permute-start | bytes 405512 | tf_op jit(solution)/shard_map/ppermute | solution.py:203
  22.5 6.0 %collective-permute-start.10 = (bf16[16,4096]{1,0:T(8,128)(2,1)S(1)}, bf16[16,4096]{1,0:T(8,128)(2,1)S(1)}, u32[]{:S(2)}, u32[]{:S(2)}) collective-permute-start(bf16[16,4096]{1,0:T(8,128)(2,1)S(1)} %get-tuple-element.38), channel_id=1, source_target_pairs={{0,1},{1,0},{2,3},{3,2},{4,5},{5,4},{6,7},{7,6},{8,9},{9,8},{10,11... | collective-permute-start | bytes 393224 | tf_op jit(solution)/shard_map/ppermute | solution.py:203
  24.2 6.2 %collective-permute-start.11 = (bf16[16,4096]{1,0:T(8,128)(2,1)S(1)}, bf16[16,4096]{1,0:T(8,128)(2,1)S(1)}, u32[]{:S(2)}, u32[]{:S(2)}) collective-permute-start(bf16[16,4096]{1,0:T(8,128)(2,1)S(1)} %get-tuple-element.39), channel_id=1, source_target_pairs={{0,2},{1,3},{2,0},{3,1},{4,6},{5,7},{6,4},{7,5},{8,10},{9,11},{10,... | collective-permute-start | bytes 393224 | tf_op jit(solution)/shard_map/ppermute | solution.py:203
  25.7 5.9 %collective-permute-start.12 = (bf16[16,4096]{1,0:T(8,128)(2,1)S(1)}, bf16[16,4096]{1,0:T(8,128)(2,1)S(1)}, u32[]{:S(2)}, u32[]{:S(2)}) collective-permute-start(bf16[16,4096]{1,0:T(8,128)(2,1)S(1)} %get-tuple-element.40), channel_id=1, source_target_pairs={{0,3},{1,2},{2,1},{3,0},{4,7},{5,6},{6,5},{7,4},{8,11},{9,10},{10,... | collective-permute-start | bytes 393224 | tf_op jit(solution)/shard_map/ppermute | solution.py:203
  26.9 6.3 %collective-permute-start.6 = (bf16[16,4224]{1,0:T(8,128)(2,1)S(1)}, bf16[16,4224]{1,0:T(8,128)(2,1)S(1)}, u32[]{:S(2)}, u32[]{:S(2)}) collective-permute-start(bf16[16,4224]{1,0:T(8,128)(2,1)S(1)} %shard_map.122), channel_id=1, source_target_pairs={{0,4},{1,5},{2,6},{3,7},{4,8},{5,9},{6,10},{7,11},{8,12},{9,13},{1... | collective-permute-start | bytes 405512 | tf_op jit(solution)/shard_map/ppermute | solution.py:203
  31.6 4.1 %collective-permute-start.13 = (bf16[16,4224]{1,0:T(8,128)(2,1)S(1)}, bf16[16,4224]{1,0:T(8,128)(2,1)S(1)}, u32[]{:S(2)}, u32[]{:S(2)}) collective-permute-start(bf16[16,4224]{1,0:T(8,128)(2,1)S(1)} %shard_map.128), channel_id=1, source_target_pairs={{0,28},{1,29},{2,30},{3,31},{4,0},{5,1},{6,2},{7,3},{8,4},{9,5},{1... | collective-permute-start | bytes 405512 | tf_op jit(solution)/shard_map/ppermute | solution.py:203

commit v8 on v7

--- a/solution.py
+++ b/solution.py
@@ -12,6 +12,7 @@
 LOWRANK_SCALE = 2.0
 LEVEL_STEP = 1.0 / 4096.0
 CHUNKS = 4
+DIAGONAL_FIRST = (3, 1, 2)
 MIB = 1 << 20
 LAST = (((1,), (1,)), ((), ()))
 FIRST = (((0,), (0,)), ((), ()))
@@ -129,8 +130,8 @@
 
 def backward(*refs):
     g_refs = refs[:SPLIT]
-    pre_gate_ref, pre_up_ref, gate_ref, up_ref, down_ref, a_ref, b_ref = refs[SPLIT:SPLIT + 7]
-    *out_refs, lowrank_ref = refs[SPLIT + 7:]
+    place_ref, pre_gate_ref, pre_up_ref, gate_ref, up_ref, down_ref = refs[SPLIT:SPLIT + 6]
+    a_ref, b_ref, *out_refs, lowrank_ref = refs[SPLIT + 6:]
     rows = jnp.concatenate([r[...] for r in g_refs], axis=0)
     height, width = g_refs[0].shape
     lowrank = (LOWRANK_SCALE * f32dot(rows, b_ref[...], LAST)).astype(jnp.bfloat16)
@@ -144,7 +145,8 @@
     result = result + f32dot(grad_up.astype(jnp.bfloat16), up_ref[...])
     result = result.astype(jnp.bfloat16)
     for k, ref in enumerate(out_refs):
-        ref[...] = result[k * height:(k + 1) * height]
+        ref[:, :width] = result[k * height:(k + 1) * height]
+    out_refs[0][:, width:] = picks(place_ref[...])
 
 
 def combine(gated, place_ref, *refs):
@@ -164,25 +166,30 @@
 
 
 def up_map_grad(latent_ref, *refs):
-    message_refs, g_refs, out_ref = refs[:SPLIT - 1], refs[SPLIT - 1:2 * SPLIT - 1], refs[-1]
+    g_refs, out_ref = refs[SPLIT - 1:2 * SPLIT - 1], refs[-1]
+    distances = (0, *DIAGONAL_FIRST)
     span = out_ref.shape[-1]
     column = pl.multiple_of(lax.axis_index("expert") * span, 128)
     count = latent_ref.shape[1]
     width = g_refs[0].shape[1]
-    latents = [latent_ref[...]] + [r[:, width:width + count] for r in message_refs]
-    rows = [g_refs[i ^ k][:, pl.ds(column, span)] for k in range(SPLIT) for i in range(SPLIT)]
+    latents = [latent_ref[...]] + [r[:, width:width + count] for r in refs[:SPLIT - 1]]
+    rows = [g_refs[i ^ k][:, pl.ds(column, span)] for k in distances for i in range(SPLIT)]
     total = f32dot(jnp.concatenate(latents, axis=1), jnp.concatenate(rows, axis=0))
     out_ref[0, 0] = LOWRANK_SCALE * total
 
 
-def expand(message_ref, out_hbm, out_ref, sems):
-    width = out_ref.shape[1]
-    pick = message_ref[:, width:]
+def expand(*refs):
+    *part_refs, out_hbm, out_ref, sems = refs
+    tokens, width = out_ref.shape
+    pick = part_refs[0][:, width:width + tokens]
     span = width // CHUNKS
     copies = []
     for c in range(CHUNKS):
         part = slice(c * span, (c + 1) * span)
-        out_ref[:, part] = f32dot(pick, message_ref[:, part], FIRST).astype(jnp.bfloat16)
+        rows = part_refs[0][:, part]
+        if len(part_refs) > 1:
+            rows = sum(r[:, part].astype(jnp.float32) for r in part_refs).astype(jnp.bfloat16)
+        out_ref[:, part] = f32dot(pick, rows, FIRST).astype(jnp.bfloat16)
         columns = pl.ds(c * span, span)
         copy = pltpu.make_async_copy(
             out_ref.at[:, columns], out_hbm.at[0, :, columns], sems.at[c]
@@ -284,14 +291,14 @@
         (*x_blocks, *weights),
         flops=60 * rows * units * width,
     )
-    out_parts = [out_blocks[0]] + [shifted(out_blocks[k], 0, k) for k in flips[1:]]
+    out_parts = [out_blocks[0]] + [shifted(out_blocks[k], 0, k) for k in DIAGONAL_FIRST]
     *grad_blocks, lowrank = call(
         backward,
-        [sds(slots, width)] * SPLIT + [sds(rows, rank)],
-        (*g_blocks, pre_gate, pre_up, *weights),
+        [sds(slots, wide)] + [sds(slots, width)] * (SPLIT - 1) + [sds(rows, rank)],
+        (*g_blocks, place, pre_gate, pre_up, *weights),
         flops=60 * rows * units * width,
     )
-    grad_parts = [grad_blocks[0]] + [shifted(grad_blocks[k], 0, k) for k in flips[1:]]
+    grad_parts = [shifted(grad_blocks[k], -1, k) for k in (0, *DIAGONAL_FIRST)]
 
     hidden, latent, _ = lax.optimization_barrier((hidden, latent, grad_blocks[0]))
     (a_grad,) = call(
@@ -321,22 +328,27 @@
             parts = [between_groups(merged(parts, False, width), flight)]
         return merged(parts, gated, wide)
 
-    def expanded(message):
+    def expanded(parts):
         return call(
             expand,
             [sds(1, tokens, width)],
-            (message,),
+            tuple(parts),
             far_outs=True,
             scratch=[pltpu.VMEM((tokens, width), jnp.bfloat16), dma((CHUNKS,))],
             flops=2 * slots * tokens * width,
         )[0]
 
     out_message = shifted(reduced(out_parts, True), 1, 0)
-    grad_parts, a_grad, b_grad = lax.optimization_barrier((grad_parts, a_grad, b_grad))
-    grad_message = shifted(reduced(grad_parts, False), -1, 0)
-    next_input = expanded(out_message)
-    next_input, grad_message = lax.optimization_barrier((next_input, grad_message))
-    prev_grad = expanded(grad_message)
+    out_message = shifted(reduced(out_parts, True), 1, 0)
+    next_input = expanded([out_message])
+    next_input, grad_parts, a_grad, b_grad = lax.optimization_barrier(
+        (next_input, grad_parts, a_grad, b_grad)
+    )
+    if flight > 1:
+        total = sum(p[:, :width].astype(jnp.float32) for p in grad_parts).astype(jnp.bfloat16)
+        total = between_groups(total, flight)
+        grad_parts = [jnp.concatenate([total, grad_parts[0][:, width:]], axis=1)]
+    prev_grad = expanded(grad_parts)
     return next_input, prev_grad, jnp.swapaxes(a_grad, 0, 1)[None], b_grad
 
 

time: 37.7 us -> 39.3 us (1.042); the launches traced: 37 us -> 39.2 us
  starting transfers between devices: 17.2 us -> 19.2 us
    ppermute x14, starting transfers between devices: 17.2 us -> 19.2 us  [shifted(): return lax.ppermute(block, ('section', 'expert'), route)]
    pallas_call x10 -> x9, Pallas kernels: 12.7 us -> 12.7 us  [call(): pl.pallas_call(body, out_shape=outs, in_specs=[NEAR] * len(args) + [FAR]...]
  transfers between devices with their start and end apart: 14 -> 14, of which waited for: 6 -> 3; matrix products, arithmetic and copies ran while one was open for 0% -> 0% of each run, Pallas kernels for 26% -> 25%
where the time goes in v8:
time: 39.3 us; the launch traced here: 39.2 us
  starting transfers between devices  19.2 us (49%)
  Pallas kernels  12.7 us (32%)
  waiting for transfers between devices  6.52 us (17%)
  between operations  0.75 us (2%)
    ppermute x14, starting transfers between devices, shifted(): return lax.ppermute(block, ('section', 'expert'), route)  19.2 us
    pallas_call x9, Pallas kernels, call(): pl.pallas_call(body, out_shape=outs, in_specs=[NEAR] * len(args) + [FAR]...  12.7 us
    ppermute x14, waiting for transfers between devices, shifted(): return lax.ppermute(block, ('section', 'expert'), route)  6.52 us
  transfers between devices with their start and end apart: 14, of which 3 were waited for; matrix products, arithmetic and copies ran while one was open for 0% of the time, Pallas kernels for 25%

profile of v8, /device:TPU:0, one launch (start us, length us, event | category | flops | bytes accessed | tf_op | source)
XLA Modules:
  0.0 39.2 jit_solution(271306770173530240)
XLA Ops:
  0.6 1.7 %shard_map.120 = (bf16[16,4096]{1,0:T(8,128)(2,1)S(1)}, f32[16,128]{1,0:T(8,128)S(1)}) custom-call(s32[8,128]{1,0:T(8,128)} %bitcast.26, s32[8,128]{1,0:T(8,128)} %bitcast.27, bf16[1,128,4096]{2,1,0:T(8,128)(2,1)} %x_hbm.1), custom_call_target="tpu_custom_call" | custom-call | flops 16777216 | bytes 1196032 | tf_op jit(solution)/shard_map/pallas_call | solution.py:33
  2.4 4.0 %collective-permute-start.2 = (bf16[16,4096]{1,0:T(8,128)(2,1)S(1)}, bf16[16,4096]{1,0:T(8,128)(2,1)S(1)}, u32[]{:S(2)}, u32[]{:S(2)}) collective-permute-start(bf16[16,4096]{1,0:T(8,128)(2,1)S(1)} %get-tuple-element.29.refs_0_), channel_id=1, source_target_pairs={{0,3},{1,2},{2,1},{3,0},{4,7},{5,6},{6,5},{7,4},{8,11},{9,10},{10,... | collective-permute-start | bytes 393224 | tf_op jit(solution)/shard_map/ppermute | solution.py:210
  6.3 0.5 %collective-permute-start.1 = (bf16[16,4096]{1,0:T(8,128)(2,1)S(1)}, bf16[16,4096]{1,0:T(8,128)(2,1)S(1)}, u32[]{:S(2)}, u32[]{:S(2)}) collective-permute-start(bf16[16,4096]{1,0:T(8,128)(2,1)S(1)} %get-tuple-element.29.refs_0_), channel_id=1, source_target_pairs={{0,2},{1,3},{2,0},{3,1},{4,6},{5,7},{6,4},{7,5},{8,10},{9,11},{10,... | collective-permute-start | bytes 393224 | tf_op jit(solution)/shard_map/ppermute | solution.py:210
  6.8 0.1 collective-permute-start
  7.0 0.0 copy-start.4
  7.0 1.8 %shard_map.124.refs_0_.refs_3_ = bf16[16,4096]{1,0:T(8,128)(2,1)S(1)} custom-call(f32[16,128]{1,0:T(8,128)S(1)} %get-tuple-element.28.place_ref.refs_4_, bf16[1,128,4096]{2,1,0:T(8,128)(2,1)} %cot_hbm.1), custom_call_target="tpu_custom_call" | custom-call | flops 3355443200 | bytes 1187840 | tf_op jit(solution)/shard_map/pallas_call | solution.py:33
  8.8 2.9 %collective-permute-start.9 = (bf16[16,4096]{1,0:T(8,128)(2,1)S(1)}, bf16[16,4096]{1,0:T(8,128)(2,1)S(1)}, u32[]{:S(2)}, u32[]{:S(2)}) collective-permute-start(bf16[16,4096]{1,0:T(8,128)(2,1)S(1)} %shard_map.124.refs_0_.refs_3_), channel_id=1, source_target_pairs={{0,3},{1,2},{2,1},{3,0},{4,7},{5,6},{6,5},{7,4},{8,11},{9,10},{10,... | collective-permute-start | bytes 393224 | tf_op jit(solution)/shard_map/ppermute | solution.py:210
  11.7 0.5 %collective-permute-start.8 = (bf16[16,4096]{1,0:T(8,128)(2,1)S(1)}, bf16[16,4096]{1,0:T(8,128)(2,1)S(1)}, u32[]{:S(2)}, u32[]{:S(2)}) collective-permute-start(bf16[16,4096]{1,0:T(8,128)(2,1)S(1)} %shard_map.124.refs_0_.refs_3_), channel_id=1, source_target_pairs={{0,2},{1,3},{2,0},{3,1},{4,6},{5,7},{6,4},{7,5},{8,10},{9,11},{10,... | collective-permute-start | bytes 393224 | tf_op jit(solution)/shard_map/ppermute | solution.py:210
  12.2 0.5 %collective-permute-start.7 = (bf16[16,4096]{1,0:T(8,128)(2,1)S(1)}, bf16[16,4096]{1,0:T(8,128)(2,1)S(1)}, u32[]{:S(2)}, u32[]{:S(2)}) collective-permute-start(bf16[16,4096]{1,0:T(8,128)(2,1)S(1)} %shard_map.124.refs_0_.refs_3_), channel_id=1, source_target_pairs={{0,1},{1,0},{2,3},{3,2},{4,5},{5,4},{6,7},{7,6},{8,9},{9,8},{10,11... | collective-permute-start | bytes 393224 | tf_op jit(solution)/shard_map/ppermute | solution.py:210
  12.7 1.2 %collective-permute-done.1.refs_2_ = bf16[16,4096]{1,0:T(8,128)(2,1)S(1)} collective-permute-done((bf16[16,4096]{1,0:T(8,128)(2,1)S(1)}, bf16[16,4096]{1,0:T(8,128)(2,1)S(1)}, u32[]{:S(2)}, u32[]{:S(2)}) %collective-permute-start.1) | collective-permute-done | bytes 131104 | tf_op jit(solution)/shard_map/ppermute | solution.py:210
  13.9 0.1 collective-permute-done.refs_1_
  14.0 2.2 %shard_map.121 = (bf16[16,4096]{1,0:T(8,128)(2,1)S(1)}, bf16[16,4224]{1,0:T(8,128)(2,1)S(1)}, bf16[16,4224]{1,0:T(8,128)(2,1)S(1)}, bf16[16,4224]{1,0:T(8,128)(2...) custom-call(bf16[16,4096]{1,0:T(8,128)(2,1)S(1)} %get-tuple-element., ...), custom_call_target="tpu_custom_call" | custom-call | flops 4026531840 | bytes 7657472 | tf_op jit(solution)/shard_map/pallas_call | solution.py:33
  16.2 2.6 %collective-permute-start.3 = (bf16[16,4224]{1,0:T(8,128)(2,1)S(1)}, bf16[16,4224]{1,0:T(8,128)(2,1)S(1)}, u32[]{:S(2)}, u32[]{:S(2)}) collective-permute-start(bf16[16,4224]{1,0:T(8,128)(2,1)S(1)} %get-tuple-element.31), channel_id=1, source_target_pairs={{0,3},{1,2},{2,1},{3,0},{4,7},{5,6},{6,5},{7,4},{8,11},{9,10},{10,... | collective-permute-start | bytes 405512 | tf_op jit(solution)/shard_map/ppermute | solution.py:210
  18.8 0.5 %collective-permute-start.4 = (bf16[16,4224]{1,0:T(8,128)(2,1)S(1)}, bf16[16,4224]{1,0:T(8,128)(2,1)S(1)}, u32[]{:S(2)}, u32[]{:S(2)}) collective-permute-start(bf16[16,4224]{1,0:T(8,128)(2,1)S(1)} %get-tuple-element.32), channel_id=1, source_target_pairs={{0,1},{1,0},{2,3},{3,2},{4,5},{5,4},{6,7},{7,6},{8,9},{9,8},{10,11... | collective-permute-start | bytes 405512 | tf_op jit(solution)/shard_map/ppermute | solution.py:210
  19.3 0.0 collective-permute-done.9.refs_3_.refs_6_
  19.3 0.4 %collective-permute-start.5 = (bf16[16,4224]{1,0:T(8,128)(2,1)S(1)}, bf16[16,4224]{1,0:T(8,128)(2,1)S(1)}, u32[]{:S(2)}, u32[]{:S(2)}) collective-permute-start(bf16[16,4224]{1,0:T(8,128)(2,1)S(1)} %get-tuple-element.33), channel_id=1, source_target_pairs={{0,2},{1,3},{2,0},{3,1},{4,6},{5,7},{6,4},{7,5},{8,10},{9,11},{10,... | collective-permute-start | bytes 405512 | tf_op jit(solution)/shard_map/ppermute | solution.py:210
  19.7 0.0 collective-permute-done.7.refs_1_.refs_4_
  19.7 2.8 %shard_map.125 = (bf16[16,4224]{1,0:T(8,128)(2,1)S(1)}, bf16[16,4096]{1,0:T(8,128)(2,1)S(1)}, bf16[16,4096]{1,0:T(8,128)(2,1)S(1)}, bf16[16,4096]{1,0:T(8,128)(2,1)S(1)}, bf16[64,16]{1,0:T(8,128)(2,1)S(1)}) custom-call(bf16[16,4096]{1,0:T(8,128)(2,1)S(1)} %shard_map.124.refs_0_.refs_3_, bf16[16,4096]{1,0:T(8,128)(2,1)S(1)} %collective-permute-done.7.refs_1_.refs_4_, ...), custom_call_target="tpu_custom_call" | custom-call | flops 4026531840 | bytes 7624704 | tf_op jit(solution)/shard_map/pallas_call | solution.py:33
  22.5 2.3 %collective-permute-start.10 = (bf16[16,4224]{1,0:T(8,128)(2,1)S(1)}, bf16[16,4224]{1,0:T(8,128)(2,1)S(1)}, u32[]{:S(2)}, u32[]{:S(2)}) collective-permute-start(bf16[16,4224]{1,0:T(8,128)(2,1)S(1)} %get-tuple-element.36), channel_id=1, source_target_pairs={{0,28},{1,29},{2,30},{3,31},{4,0},{5,1},{6,2},{7,3},{8,4},{9,5},{1... | collective-permute-start | bytes 405512 | tf_op jit(solution)/shard_map/ppermute | solution.py:210
  24.9 4.1 %collective-permute-start.11 = (bf16[16,4096]{1,0:T(8,128)(2,1)S(1)}, bf16[16,4096]{1,0:T(8,128)(2,1)S(1)}, u32[]{:S(2)}, u32[]{:S(2)}) collective-permute-start(bf16[16,4096]{1,0:T(8,128)(2,1)S(1)} %get-tuple-element.37), channel_id=1, source_target_pairs={{0,31},{1,30},{2,29},{3,28},{4,3},{5,2},{6,1},{7,0},{8,7},{9,6},{1... | collective-permute-start | bytes 393224 | tf_op jit(solution)/shard_map/ppermute | solution.py:210
  29.0 0.0 collective-permute-done.3.refs_1_.refs_0_
  29.0 0.0 collective-permute-start.12
  29.0 0.3 collective-permute-start.13
  29.3 0.1 shard_map.122
  29.4 0.4 %collective-permute-start.6 = (bf16[16,4224]{1,0:T(8,128)(2,1)S(1)}, bf16[16,4224]{1,0:T(8,128)(2,1)S(1)}, u32[]{:S(2)}, u32[]{:S(2)}) collective-permute-start(bf16[16,4224]{1,0:T(8,128)(2,1)S(1)} %shard_map.122), channel_id=1, source_target_pairs={{0,4},{1,5},{2,6},{3,7},{4,8},{5,9},{6,10},{7,11},{8,12},{9,13},{1... | collective-permute-start | bytes 405512 | tf_op jit(solution)/shard_map/ppermute | solution.py:210
  29.8 0.8 %shard_map.126 = f32[16,256]{1,0:T(8,128)} custom-call(bf16[64,16]{1,0:T(8,128)(2,1)S(1)} %get-tuple-element.40.lowrank_ref, bf16[64,256]{1,0:T(8,128)(2,1)S(1)} %get-tuple-element.43.hidden_ref), custom_call_target="tpu_custom_call" | custom-call | flops 838860800 | bytes 51200 | tf_op jit(solution)/shard_map/pallas_call | solution.py:33
  30.6 0.8 %shard_map.127 = f32[1,1,16,1024]{3,2,1,0:T(8,128)} custom-call(bf16[16,64]{1,0:T(8,128)(2,1)S(1)} %get-tuple-element.44.latent_ref, bf16[16,4224]{1,0:T(8,128)(2,1)S(1)} %collective-permute-done.3.refs_1_.refs_0_, bf16[16,4224]{1,0:T(8,128)(2,1)S(1)} %collective-permute-done.4.refs_2_.refs_1_, bf16[16,4224]{1,0:T(8,128)(2,1)S(1)} %collective-permute-done.5.refs_3_.refs_2_, ...), custom_call_target="tpu_custom_call" | custom-call | flops 838860800 | bytes 997376 | tf_op jit(solution)/shard_map/pallas_call | solution.py:33
  31.4 5.2 %collective-permute-done.6.refs_0_ = bf16[16,4224]{1,0:T(8,128)(2,1)S(1)} collective-permute-done((bf16[16,4224]{1,0:T(8,128)(2,1)S(1)}, bf16[16,4224]{1,0:T(8,128)(2,1)S(1)}, u32[]{:S(2)}, u32[]{:S(2)}) %collective-permute-start.6) | collective-permute-done | bytes 135200 | tf_op jit(solution)/shard_map/ppermute | solution.py:210
  36.7 1.2 %shard_map.123 = bf16[1,128,4096]{2,1,0:T(8,128)(2,1)} custom-call(bf16[16,4224]{1,0:T(8,128)(2,1)S(1)} %collective-permute-done.6.refs_0_), custom_call_target="tpu_custom_call" | custom-call | flops 16777216 | bytes 1183744 | tf_op jit(solution)/shard_map/pallas_call | solution.py:33
  37.9 0.0 collective-permute-done.11.refs_1_
  37.9 0.0 collective-permute-done.12.refs_2_
  37.9 1.2 %shard_map.128 = bf16[1,128,4096]{2,1,0:T(8,128)(2,1)} custom-call(bf16[16,4224]{1,0:T(8,128)(2,1)S(1)} %collective-permute-done.10.refs_0_, bf16[16,4096]{1,0:T(8,128)(2,1)S(1)} %collective-permute-done.11.refs_1_, bf16[16,4096]{1,0:T(8,128)(2,1)S(1)} %collective-permute-done.12.refs_2_, bf16[16,4096]{1,0:T(8,128)(2,1)S(1)} %collective-permute-done.13.refs_3_), custom_call_target="tpu_custom_call" | custom-call | flops 16777216 | bytes 1576960 | tf_op jit(solution)/shard_map/pallas_call | solution.py:33
  (15 shorter events, 0.0 us)
Async XLA Ops:
  2.4 9.8 %collective-permute-start.2 = (bf16[16,4096]{1,0:T(8,128)(2,1)S(1)}, bf16[16,4096]{1,0:T(8,128)(2,1)S(1)}, u32[]{:S(2)}, u32[]{:S(2)}) collective-permute-start(bf16[16,4096]{1,0:T(8,128)(2,1)S(1)} %get-tuple-element.29.refs_0_), channel_id=1, source_target_pairs={{0,3},{1,2},{2,1},{3,0},{4,7},{5,6},{6,5},{7,4},{8,11},{9,10},{10,... | collective-permute-start | bytes 393224 | tf_op jit(solution)/shard_map/ppermute | solution.py:210
  6.3 7.5 %collective-permute-start.1 = (bf16[16,4096]{1,0:T(8,128)(2,1)S(1)}, bf16[16,4096]{1,0:T(8,128)(2,1)S(1)}, u32[]{:S(2)}, u32[]{:S(2)}) collective-permute-start(bf16[16,4096]{1,0:T(8,128)(2,1)S(1)} %get-tuple-element.29.refs_0_), channel_id=1, source_target_pairs={{0,2},{1,3},{2,0},{3,1},{4,6},{5,7},{6,4},{7,5},{8,10},{9,11},{10,... | collective-permute-start | bytes 393224 | tf_op jit(solution)/shard_map/ppermute | solution.py:210
  6.8 7.1 %collective-permute-start = (bf16[16,4096]{1,0:T(8,128)(2,1)S(1)}, bf16[16,4096]{1,0:T(8,128)(2,1)S(1)}, u32[]{:S(2)}, u32[]{:S(2)}) collective-permute-start(bf16[16,4096]{1,0:T(8,128)(2,1)S(1)} %get-tuple-element.29.refs_0_), channel_id=1, source_target_pairs={{0,1},{1,0},{2,3},{3,2},{4,5},{5,4},{6,7},{7,6},{8,9},{9,8},{10,11... | collective-permute-start | bytes 393224 | tf_op jit(solution)/shard_map/ppermute | solution.py:210
  7.0 7.0 %copy-start = (bf16[1,256,4096]{2,1,0:T(8,128)(2,1)S(1)}, bf16[1,256,4096]{2,1,0:T(8,128)(2,1)}, u32[]{:S(2)}) copy-start(bf16[1,256,4096]{2,1,0:T(8,128)(2,1)} %param.12) | copy-start | bytes 6291460
  7.0 7.0 %copy-start.1 = (bf16[1,256,4096]{2,1,0:T(8,128)(2,1)S(1)}, bf16[1,256,4096]{2,1,0:T(8,128)(2,1)}, u32[]{:S(2)}) copy-start(bf16[1,256,4096]{2,1,0:T(8,128)(2,1)} %param.13) | copy-start | bytes 6291460
  7.0 7.0 %copy-start.2 = (bf16[1,256,4096]{2,1,0:T(8,128)(2,1)S(1)}, bf16[1,256,4096]{2,1,0:T(8,128)(2,1)}, u32[]{:S(2)}) copy-start(bf16[1,256,4096]{2,1,0:T(8,128)(2,1)} %param.14) | copy-start | bytes 6291460
  7.0 7.0 %copy-start.3 = (bf16[1,1,16,4096]{3,2,1,0:T(8,128)(2,1)S(1)}, bf16[1,1,16,4096]{3,2,1,0:T(8,128)(2,1)}, u32[]{:S(2)}) copy-start(bf16[1,1,16,4096]{3,2,1,0:T(8,128)(2,1)} %param.16) | copy-start | bytes 393220
  7.0 7.0 %copy-start.4 = (bf16[1,256,16]{1,2,0:T(8,128)(2,1)S(1)}, bf16[1,256,16]{1,2,0:T(8,128)(2,1)}, u32[]{:S(2)}) copy-start(bf16[1,256,16]{1,2,0:T(8,128)(2,1)} %param.15) | copy-start | bytes 24580
  8.8 10.5 %collective-permute-start.9 = (bf16[16,4096]{1,0:T(8,128)(2,1)S(1)}, bf16[16,4096]{1,0:T(8,128)(2,1)S(1)}, u32[]{:S(2)}, u32[]{:S(2)}) collective-permute-start(bf16[16,4096]{1,0:T(8,128)(2,1)S(1)} %shard_map.124.refs_0_.refs_3_), channel_id=1, source_target_pairs={{0,3},{1,2},{2,1},{3,0},{4,7},{5,6},{6,5},{7,4},{8,11},{9,10},{10,... | collective-permute-start | bytes 393224 | tf_op jit(solution)/shard_map/ppermute | solution.py:210
  11.7 8.1 %collective-permute-start.8 = (bf16[16,4096]{1,0:T(8,128)(2,1)S(1)}, bf16[16,4096]{1,0:T(8,128)(2,1)S(1)}, u32[]{:S(2)}, u32[]{:S(2)}) collective-permute-start(bf16[16,4096]{1,0:T(8,128)(2,1)S(1)} %shard_map.124.refs_0_.refs_3_), channel_id=1, source_target_pairs={{0,2},{1,3},{2,0},{3,1},{4,6},{5,7},{6,4},{7,5},{8,10},{9,11},{10,... | collective-permute-start | bytes 393224 | tf_op jit(solution)/shard_map/ppermute | solution.py:210
  12.2 7.5 %collective-permute-start.7 = (bf16[16,4096]{1,0:T(8,128)(2,1)S(1)}, bf16[16,4096]{1,0:T(8,128)(2,1)S(1)}, u32[]{:S(2)}, u32[]{:S(2)}) collective-permute-start(bf16[16,4096]{1,0:T(8,128)(2,1)S(1)} %shard_map.124.refs_0_.refs_3_), channel_id=1, source_target_pairs={{0,1},{1,0},{2,3},{3,2},{4,5},{5,4},{6,7},{7,6},{8,9},{9,8},{10,11... | collective-permute-start | bytes 393224 | tf_op jit(solution)/shard_map/ppermute | solution.py:210
  16.2 12.8 %collective-permute-start.3 = (bf16[16,4224]{1,0:T(8,128)(2,1)S(1)}, bf16[16,4224]{1,0:T(8,128)(2,1)S(1)}, u32[]{:S(2)}, u32[]{:S(2)}) collective-permute-start(bf16[16,4224]{1,0:T(8,128)(2,1)S(1)} %get-tuple-element.31), channel_id=1, source_target_pairs={{0,3},{1,2},{2,1},{3,0},{4,7},{5,6},{6,5},{7,4},{8,11},{9,10},{10,... | collective-permute-start | bytes 405512 | tf_op jit(solution)/shard_map/ppermute | solution.py:210
  18.8 10.1 %collective-permute-start.4 = (bf16[16,4224]{1,0:T(8,128)(2,1)S(1)}, bf16[16,4224]{1,0:T(8,128)(2,1)S(1)}, u32[]{:S(2)}, u32[]{:S(2)}) collective-permute-start(bf16[16,4224]{1,0:T(8,128)(2,1)S(1)} %get-tuple-element.32), channel_id=1, source_target_pairs={{0,1},{1,0},{2,3},{3,2},{4,5},{5,4},{6,7},{7,6},{8,9},{9,8},{10,11... | collective-permute-start | bytes 405512 | tf_op jit(solution)/shard_map/ppermute | solution.py:210
  19.3 10.0 %collective-permute-start.5 = (bf16[16,4224]{1,0:T(8,128)(2,1)S(1)}, bf16[16,4224]{1,0:T(8,128)(2,1)S(1)}, u32[]{:S(2)}, u32[]{:S(2)}) collective-permute-start(bf16[16,4224]{1,0:T(8,128)(2,1)S(1)} %get-tuple-element.33), channel_id=1, source_target_pairs={{0,2},{1,3},{2,0},{3,1},{4,6},{5,7},{6,4},{7,5},{8,10},{9,11},{10,... | collective-permute-start | bytes 405512 | tf_op jit(solution)/shard_map/ppermute | solution.py:210
  22.5 15.4 %collective-permute-start.10 = (bf16[16,4224]{1,0:T(8,128)(2,1)S(1)}, bf16[16,4224]{1,0:T(8,128)(2,1)S(1)}, u32[]{:S(2)}, u32[]{:S(2)}) collective-permute-start(bf16[16,4224]{1,0:T(8,128)(2,1)S(1)} %get-tuple-element.36), channel_id=1, source_target_pairs={{0,28},{1,29},{2,30},{3,31},{4,0},{5,1},{6,2},{7,3},{8,4},{9,5},{1... | collective-permute-start | bytes 405512 | tf_op jit(solution)/shard_map/ppermute | solution.py:210
  24.9 13.0 %collective-permute-start.11 = (bf16[16,4096]{1,0:T(8,128)(2,1)S(1)}, bf16[16,4096]{1,0:T(8,128)(2,1)S(1)}, u32[]{:S(2)}, u32[]{:S(2)}) collective-permute-start(bf16[16,4096]{1,0:T(8,128)(2,1)S(1)} %get-tuple-element.37), channel_id=1, source_target_pairs={{0,31},{1,30},{2,29},{3,28},{4,3},{5,2},{6,1},{7,0},{8,7},{9,6},{1... | collective-permute-start | bytes 393224 | tf_op jit(solution)/shard_map/ppermute | solution.py:210
  29.0 9.0 %collective-permute-start.12 = (bf16[16,4096]{1,0:T(8,128)(2,1)S(1)}, bf16[16,4096]{1,0:T(8,128)(2,1)S(1)}, u32[]{:S(2)}, u32[]{:S(2)}) collective-permute-start(bf16[16,4096]{1,0:T(8,128)(2,1)S(1)} %get-tuple-element.38), channel_id=1, source_target_pairs={{0,29},{1,28},{2,31},{3,30},{4,1},{5,0},{6,3},{7,2},{8,5},{9,4},{1... | collective-permute-start | bytes 393224 | tf_op jit(solution)/shard_map/ppermute | solution.py:210
  29.0 9.0 %collective-permute-start.13 = (bf16[16,4096]{1,0:T(8,128)(2,1)S(1)}, bf16[16,4096]{1,0:T(8,128)(2,1)S(1)}, u32[]{:S(2)}, u32[]{:S(2)}) collective-permute-start(bf16[16,4096]{1,0:T(8,128)(2,1)S(1)} %get-tuple-element.39), channel_id=1, source_target_pairs={{0,30},{1,31},{2,28},{3,29},{4,2},{5,3},{6,0},{7,1},{8,6},{9,7},{1... | collective-permute-start | bytes 393224 | tf_op jit(solution)/shard_map/ppermute | solution.py:210
  29.4 7.3 %collective-permute-start.6 = (bf16[16,4224]{1,0:T(8,128)(2,1)S(1)}, bf16[16,4224]{1,0:T(8,128)(2,1)S(1)}, u32[]{:S(2)}, u32[]{:S(2)}) collective-permute-start(bf16[16,4224]{1,0:T(8,128)(2,1)S(1)} %shard_map.122), channel_id=1, source_target_pairs={{0,4},{1,5},{2,6},{3,7},{4,8},{5,9},{6,10},{7,11},{8,12},{9,13},{1... | collective-permute-start | bytes 405512 | tf_op jit(solution)/shard_map/ppermute | solution.py:210

commit v9 on v8

--- a/solution.py
+++ b/solution.py
@@ -292,15 +292,28 @@
         flops=60 * rows * units * width,
     )
     out_parts = [out_blocks[0]] + [shifted(out_blocks[k], 0, k) for k in DIAGONAL_FIRST]
+    def merged(parts, gated, columns):
+        return call(functools.partial(combine, gated), [sds(slots, columns)], (place, *parts))[0]
+
+    def reduced(parts, gated):
+        if flight > 1:
+            parts = [between_groups(merged(parts, False, width), flight)]
+        return merged(parts, gated, wide)
+
     *grad_blocks, lowrank = call(
         backward,
         [sds(slots, wide)] + [sds(slots, width)] * (SPLIT - 1) + [sds(rows, rank)],
         (*g_blocks, place, pre_gate, pre_up, *weights),
         flops=60 * rows * units * width,
     )
+
+    out_message = reduced(out_parts, True)
+    out_message, *late = lax.optimization_barrier((out_message, grad_blocks[0], grad_blocks[2]))
+    grad_blocks[0], grad_blocks[2] = late
+    out_message = shifted(out_message, 1, 0)
     grad_parts = [shifted(grad_blocks[k], -1, k) for k in (0, *DIAGONAL_FIRST)]
 
-    hidden, latent, _ = lax.optimization_barrier((hidden, latent, grad_blocks[0]))
+    hidden, latent, _ = lax.optimization_barrier((hidden, latent, grad_blocks[3]))
     (a_grad,) = call(
         down_map_grad,
         [sds(rank, units, dtype=jnp.float32)],
@@ -320,14 +333,6 @@
         spread = jnp.where(mine[:, None, None], part[None], 0.0)
         b_grad = lax.psum_scatter(spread, "expert", scatter_dimension=2, tiled=True)[None]
 
-    def merged(parts, gated, columns):
-        return call(functools.partial(combine, gated), [sds(slots, columns)], (place, *parts))[0]
-
-    def reduced(parts, gated):
-        if flight > 1:
-            parts = [between_groups(merged(parts, False, width), flight)]
-        return merged(parts, gated, wide)
-
     def expanded(parts):
         return call(
             expand,
@@ -339,7 +344,6 @@
         )[0]
 
     out_message = shifted(reduced(out_parts, True), 1, 0)
-    out_message = shifted(reduced(out_parts, True), 1, 0)
     next_input = expanded([out_message])
     next_input, grad_parts, a_grad, b_grad = lax.optimization_barrier(
         (next_input, grad_parts, a_grad, b_grad)

time: 39.3 us -> 39.1 us (level)
  waiting for transfers between devices: 6.52 us -> 3.74 us
  starting transfers between devices: 19.2 us -> 21.8 us
    ppermute x14, waiting for transfers between devices: 6.52 us -> 3.74 us  [shifted(): return lax.ppermute(block, ('section', 'expert'), route)]
    ppermute x14, starting transfers between devices: 19.2 us -> 21.8 us  [shifted(): return lax.ppermute(block, ('section', 'expert'), route)]
where the time goes in v9:
time: 39.1 us; the launch traced here: 39 us
  starting transfers between devices  21.8 us (56%)
  Pallas kernels  12.7 us (32%)
  waiting for transfers between devices  3.74 us (10%)
  between operations  0.75 us (2%)
    ppermute x14, starting transfers between devices, shifted(): return lax.ppermute(block, ('section', 'expert'), route)  21.8 us
    pallas_call x9, Pallas kernels, call(): pl.pallas_call(body, out_shape=outs, in_specs=[NEAR] * len(args) + [FAR]...  12.7 us
    ppermute x14, waiting for transfers between devices, shifted(): return lax.ppermute(block, ('section', 'expert'), route)  3.74 us
  transfers between devices with their start and end apart: 14, of which 3 were waited for; matrix products, arithmetic and copies ran while one was open for 0% of the time, Pallas kernels for 25%

profile of v9, /device:TPU:0, one launch (start us, length us, event | category | flops | bytes accessed | tf_op | source)
XLA Modules:
  0.0 39.0 jit_solution(2584798491087852089)
XLA Ops:
  0.6 1.7 %shard_map.120 = (bf16[16,4096]{1,0:T(8,128)(2,1)S(1)}, f32[16,128]{1,0:T(8,128)S(1)}) custom-call(s32[8,128]{1,0:T(8,128)} %bitcast.26, s32[8,128]{1,0:T(8,128)} %bitcast.27, bf16[1,128,4096]{2,1,0:T(8,128)(2,1)} %x_hbm.1), custom_call_target="tpu_custom_call" | custom-call | flops 16777216 | bytes 1196032 | tf_op jit(solution)/shard_map/pallas_call | solution.py:33
  2.4 4.0 %collective-permute-start.2 = (bf16[16,4096]{1,0:T(8,128)(2,1)S(1)}, bf16[16,4096]{1,0:T(8,128)(2,1)S(1)}, u32[]{:S(2)}, u32[]{:S(2)}) collective-permute-start(bf16[16,4096]{1,0:T(8,128)(2,1)S(1)} %get-tuple-element.31.refs_0_), channel_id=1, source_target_pairs={{0,3},{1,2},{2,1},{3,0},{4,7},{5,6},{6,5},{7,4},{8,11},{9,10},{10,... | collective-permute-start | bytes 393224 | tf_op jit(solution)/shard_map/ppermute | solution.py:210
  6.3 0.5 %collective-permute-start.1 = (bf16[16,4096]{1,0:T(8,128)(2,1)S(1)}, bf16[16,4096]{1,0:T(8,128)(2,1)S(1)}, u32[]{:S(2)}, u32[]{:S(2)}) collective-permute-start(bf16[16,4096]{1,0:T(8,128)(2,1)S(1)} %get-tuple-element.31.refs_0_), channel_id=1, source_target_pairs={{0,2},{1,3},{2,0},{3,1},{4,6},{5,7},{6,4},{7,5},{8,10},{9,11},{10,... | collective-permute-start | bytes 393224 | tf_op jit(solution)/shard_map/ppermute | solution.py:210
  6.8 0.1 collective-permute-start
  7.0 0.0 copy-start.4
  7.0 1.8 %shard_map.124.refs_0_.refs_3_ = bf16[16,4096]{1,0:T(8,128)(2,1)S(1)} custom-call(f32[16,128]{1,0:T(8,128)S(1)} %get-tuple-element.30.place_ref.refs_4_, bf16[1,128,4096]{2,1,0:T(8,128)(2,1)} %cot_hbm.1), custom_call_target="tpu_custom_call" | custom-call | flops 3355443200 | bytes 1187840 | tf_op jit(solution)/shard_map/pallas_call | solution.py:33
  8.8 2.9 %collective-permute-start.9 = (bf16[16,4096]{1,0:T(8,128)(2,1)S(1)}, bf16[16,4096]{1,0:T(8,128)(2,1)S(1)}, u32[]{:S(2)}, u32[]{:S(2)}) collective-permute-start(bf16[16,4096]{1,0:T(8,128)(2,1)S(1)} %shard_map.124.refs_0_.refs_3_), channel_id=1, source_target_pairs={{0,3},{1,2},{2,1},{3,0},{4,7},{5,6},{6,5},{7,4},{8,11},{9,10},{10,... | collective-permute-start | bytes 393224 | tf_op jit(solution)/shard_map/ppermute | solution.py:210
  11.7 0.5 %collective-permute-start.8 = (bf16[16,4096]{1,0:T(8,128)(2,1)S(1)}, bf16[16,4096]{1,0:T(8,128)(2,1)S(1)}, u32[]{:S(2)}, u32[]{:S(2)}) collective-permute-start(bf16[16,4096]{1,0:T(8,128)(2,1)S(1)} %shard_map.124.refs_0_.refs_3_), channel_id=1, source_target_pairs={{0,2},{1,3},{2,0},{3,1},{4,6},{5,7},{6,4},{7,5},{8,10},{9,11},{10,... | collective-permute-start | bytes 393224 | tf_op jit(solution)/shard_map/ppermute | solution.py:210
  12.2 0.0 collective-permute-done.2.refs_3_
  12.2 0.5 %collective-permute-start.7 = (bf16[16,4096]{1,0:T(8,128)(2,1)S(1)}, bf16[16,4096]{1,0:T(8,128)(2,1)S(1)}, u32[]{:S(2)}, u32[]{:S(2)}) collective-permute-start(bf16[16,4096]{1,0:T(8,128)(2,1)S(1)} %shard_map.124.refs_0_.refs_3_), channel_id=1, source_target_pairs={{0,1},{1,0},{2,3},{3,2},{4,5},{5,4},{6,7},{7,6},{8,9},{9,8},{10,11... | collective-permute-start | bytes 393224 | tf_op jit(solution)/shard_map/ppermute | solution.py:210
  12.7 1.2 %collective-permute-done.1.refs_2_ = bf16[16,4096]{1,0:T(8,128)(2,1)S(1)} collective-permute-done((bf16[16,4096]{1,0:T(8,128)(2,1)S(1)}, bf16[16,4096]{1,0:T(8,128)(2,1)S(1)}, u32[]{:S(2)}, u32[]{:S(2)}) %collective-permute-start.1) | collective-permute-done | bytes 131104 | tf_op jit(solution)/shard_map/ppermute | solution.py:210
  13.9 0.1 collective-permute-done.refs_1_
  14.0 2.2 %shard_map.121 = (bf16[16,4096]{1,0:T(8,128)(2,1)S(1)}, bf16[16,4224]{1,0:T(8,128)(2,1)S(1)}, bf16[16,4224]{1,0:T(8,128)(2,1)S(1)}, bf16[16,4224]{1,0:T(8,128)(2...) custom-call(bf16[16,4096]{1,0:T(8,128)(2,1)S(1)} %get-tuple-element., ...), custom_call_target="tpu_custom_call" | custom-call | flops 4026531840 | bytes 7657472 | tf_op jit(solution)/shard_map/pallas_call | solution.py:33
  16.2 2.6 %collective-permute-start.3 = (bf16[16,4224]{1,0:T(8,128)(2,1)S(1)}, bf16[16,4224]{1,0:T(8,128)(2,1)S(1)}, u32[]{:S(2)}, u32[]{:S(2)}) collective-permute-start(bf16[16,4224]{1,0:T(8,128)(2,1)S(1)} %get-tuple-element.33), channel_id=1, source_target_pairs={{0,3},{1,2},{2,1},{3,0},{4,7},{5,6},{6,5},{7,4},{8,11},{9,10},{10,... | collective-permute-start | bytes 405512 | tf_op jit(solution)/shard_map/ppermute | solution.py:210
  18.8 0.5 %collective-permute-start.4 = (bf16[16,4224]{1,0:T(8,128)(2,1)S(1)}, bf16[16,4224]{1,0:T(8,128)(2,1)S(1)}, u32[]{:S(2)}, u32[]{:S(2)}) collective-permute-start(bf16[16,4224]{1,0:T(8,128)(2,1)S(1)} %get-tuple-element.34), channel_id=1, source_target_pairs={{0,1},{1,0},{2,3},{3,2},{4,5},{5,4},{6,7},{7,6},{8,9},{9,8},{10,11... | collective-permute-start | bytes 405512 | tf_op jit(solution)/shard_map/ppermute | solution.py:210
  19.3 0.4 %collective-permute-start.5 = (bf16[16,4224]{1,0:T(8,128)(2,1)S(1)}, bf16[16,4224]{1,0:T(8,128)(2,1)S(1)}, u32[]{:S(2)}, u32[]{:S(2)}) collective-permute-start(bf16[16,4224]{1,0:T(8,128)(2,1)S(1)} %get-tuple-element.35), channel_id=1, source_target_pairs={{0,2},{1,3},{2,0},{3,1},{4,6},{5,7},{6,4},{7,5},{8,10},{9,11},{10,... | collective-permute-start | bytes 405512 | tf_op jit(solution)/shard_map/ppermute | solution.py:210
  19.7 0.0 collective-permute-done.8.refs_2_.refs_5_
  19.7 0.0 collective-permute-done.7.refs_1_.refs_4_
  19.7 2.8 %shard_map.125 = (bf16[16,4224]{1,0:T(8,128)(2,1)S(1)}, bf16[16,4096]{1,0:T(8,128)(2,1)S(1)}, bf16[16,4096]{1,0:T(8,128)(2,1)S(1)}, bf16[16,4096]{1,0:T(8,128)(2,1)S(1)}, bf16[64,16]{1,0:T(8,128)(2,1)S(1)}) custom-call(bf16[16,4096]{1,0:T(8,128)(2,1)S(1)} %shard_map.124.refs_0_.refs_3_, bf16[16,4096]{1,0:T(8,128)(2,1)S(1)} %collective-permute-done.7.refs_1_.refs_4_, ...), custom_call_target="tpu_custom_call" | custom-call | flops 4026531840 | bytes 7624704 | tf_op jit(solution)/shard_map/pallas_call | solution.py:33
  22.5 3.0 %collective-permute-start.11 = (bf16[16,4096]{1,0:T(8,128)(2,1)S(1)}, bf16[16,4096]{1,0:T(8,128)(2,1)S(1)}, u32[]{:S(2)}, u32[]{:S(2)}) collective-permute-start(bf16[16,4096]{1,0:T(8,128)(2,1)S(1)} %get-tuple-element.41), channel_id=1, source_target_pairs={{0,31},{1,30},{2,29},{3,28},{4,3},{5,2},{6,1},{7,0},{8,7},{9,6},{1... | collective-permute-start | bytes 393224 | tf_op jit(solution)/shard_map/ppermute | solution.py:210
  25.5 3.1 %collective-permute-start.12 = (bf16[16,4096]{1,0:T(8,128)(2,1)S(1)}, bf16[16,4096]{1,0:T(8,128)(2,1)S(1)}, u32[]{:S(2)}, u32[]{:S(2)}) collective-permute-start(bf16[16,4096]{1,0:T(8,128)(2,1)S(1)} %get-tuple-element.42), channel_id=1, source_target_pairs={{0,29},{1,28},{2,31},{3,30},{4,1},{5,0},{6,3},{7,2},{8,5},{9,4},{1... | collective-permute-start | bytes 393224 | tf_op jit(solution)/shard_map/ppermute | solution.py:210
  28.6 0.0 collective-permute-done.3.refs_1_.refs_0_
  28.6 0.0 collective-permute-done.4.refs_2_.refs_1_
  28.6 0.1 shard_map.122
  28.7 0.1 collective-permute-start.6
  28.8 3.6 %collective-permute-start.13 = (bf16[16,4096]{1,0:T(8,128)(2,1)S(1)}, bf16[16,4096]{1,0:T(8,128)(2,1)S(1)}, u32[]{:S(2)}, u32[]{:S(2)}) collective-permute-start(bf16[16,4096]{1,0:T(8,128)(2,1)S(1)} %get-tuple-element.43), channel_id=1, source_target_pairs={{0,30},{1,31},{2,28},{3,29},{4,2},{5,3},{6,0},{7,1},{8,6},{9,7},{1... | collective-permute-start | bytes 393224 | tf_op jit(solution)/shard_map/ppermute | solution.py:210
  32.4 0.8 %shard_map.126 = f32[16,256]{1,0:T(8,128)} custom-call(bf16[64,16]{1,0:T(8,128)(2,1)S(1)} %get-tuple-element.44.lowrank_ref, bf16[64,256]{1,0:T(8,128)(2,1)S(1)} %get-tuple-element.47.hidden_ref), custom_call_target="tpu_custom_call" | custom-call | flops 838860800 | bytes 51200 | tf_op jit(solution)/shard_map/pallas_call | solution.py:33
  33.1 0.8 %shard_map.127 = f32[1,1,16,1024]{3,2,1,0:T(8,128)} custom-call(bf16[16,64]{1,0:T(8,128)(2,1)S(1)} %get-tuple-element.48.latent_ref, bf16[16,4224]{1,0:T(8,128)(2,1)S(1)} %collective-permute-done.3.refs_1_.refs_0_, bf16[16,4224]{1,0:T(8,128)(2,1)S(1)} %collective-permute-done.4.refs_2_.refs_1_, bf16[16,4224]{1,0:T(8,128)(2,1)S(1)} %collective-permute-done.5.refs_3_.refs_2_, ...), custom_call_target="tpu_custom_call" | custom-call | flops 838860800 | bytes 997376 | tf_op jit(solution)/shard_map/pallas_call | solution.py:33
  34.0 2.4 %collective-permute-done.6.refs_0_ = bf16[16,4224]{1,0:T(8,128)(2,1)S(1)} collective-permute-done((bf16[16,4224]{1,0:T(8,128)(2,1)S(1)}, bf16[16,4224]{1,0:T(8,128)(2,1)S(1)}, u32[]{:S(2)}, u32[]{:S(2)}) %collective-permute-start.6) | collective-permute-done | bytes 135200 | tf_op jit(solution)/shard_map/ppermute | solution.py:210
  36.4 1.2 %shard_map.123 = bf16[1,128,4096]{2,1,0:T(8,128)(2,1)} custom-call(bf16[16,4224]{1,0:T(8,128)(2,1)S(1)} %collective-permute-done.6.refs_0_), custom_call_target="tpu_custom_call" | custom-call | flops 16777216 | bytes 1183744 | tf_op jit(solution)/shard_map/pallas_call | solution.py:33
  37.7 0.0 collective-permute-done.11.refs_1_
  37.7 1.2 %shard_map.128 = bf16[1,128,4096]{2,1,0:T(8,128)(2,1)} custom-call(bf16[16,4224]{1,0:T(8,128)(2,1)S(1)} %collective-permute-done.10.refs_0_, bf16[16,4096]{1,0:T(8,128)(2,1)S(1)} %collective-permute-done.11.refs_1_, bf16[16,4096]{1,0:T(8,128)(2,1)S(1)} %collective-permute-done.12.refs_2_, bf16[16,4096]{1,0:T(8,128)(2,1)S(1)} %collective-permute-done.13.refs_3_), custom_call_target="tpu_custom_call" | custom-call | flops 16777216 | bytes 1576960 | tf_op jit(solution)/shard_map/pallas_call | solution.py:33
  (15 shorter events, 0.0 us)
Async XLA Ops:
  2.4 9.8 %collective-permute-start.2 = (bf16[16,4096]{1,0:T(8,128)(2,1)S(1)}, bf16[16,4096]{1,0:T(8,128)(2,1)S(1)}, u32[]{:S(2)}, u32[]{:S(2)}) collective-permute-start(bf16[16,4096]{1,0:T(8,128)(2,1)S(1)} %get-tuple-element.31.refs_0_), channel_id=1, source_target_pairs={{0,3},{1,2},{2,1},{3,0},{4,7},{5,6},{6,5},{7,4},{8,11},{9,10},{10,... | collective-permute-start | bytes 393224 | tf_op jit(solution)/shard_map/ppermute | solution.py:210
  6.3 7.5 %collective-permute-start.1 = (bf16[16,4096]{1,0:T(8,128)(2,1)S(1)}, bf16[16,4096]{1,0:T(8,128)(2,1)S(1)}, u32[]{:S(2)}, u32[]{:S(2)}) collective-permute-start(bf16[16,4096]{1,0:T(8,128)(2,1)S(1)} %get-tuple-element.31.refs_0_), channel_id=1, source_target_pairs={{0,2},{1,3},{2,0},{3,1},{4,6},{5,7},{6,4},{7,5},{8,10},{9,11},{10,... | collective-permute-start | bytes 393224 | tf_op jit(solution)/shard_map/ppermute | solution.py:210
  6.8 7.1 %collective-permute-start = (bf16[16,4096]{1,0:T(8,128)(2,1)S(1)}, bf16[16,4096]{1,0:T(8,128)(2,1)S(1)}, u32[]{:S(2)}, u32[]{:S(2)}) collective-permute-start(bf16[16,4096]{1,0:T(8,128)(2,1)S(1)} %get-tuple-element.31.refs_0_), channel_id=1, source_target_pairs={{0,1},{1,0},{2,3},{3,2},{4,5},{5,4},{6,7},{7,6},{8,9},{9,8},{10,11... | collective-permute-start | bytes 393224 | tf_op jit(solution)/shard_map/ppermute | solution.py:210
  7.0 7.0 %copy-start = (bf16[1,256,4096]{2,1,0:T(8,128)(2,1)S(1)}, bf16[1,256,4096]{2,1,0:T(8,128)(2,1)}, u32[]{:S(2)}) copy-start(bf16[1,256,4096]{2,1,0:T(8,128)(2,1)} %param.12) | copy-start | bytes 6291460
  7.0 7.0 %copy-start.1 = (bf16[1,256,4096]{2,1,0:T(8,128)(2,1)S(1)}, bf16[1,256,4096]{2,1,0:T(8,128)(2,1)}, u32[]{:S(2)}) copy-start(bf16[1,256,4096]{2,1,0:T(8,128)(2,1)} %param.13) | copy-start | bytes 6291460
  7.0 7.0 %copy-start.2 = (bf16[1,256,4096]{2,1,0:T(8,128)(2,1)S(1)}, bf16[1,256,4096]{2,1,0:T(8,128)(2,1)}, u32[]{:S(2)}) copy-start(bf16[1,256,4096]{2,1,0:T(8,128)(2,1)} %param.14) | copy-start | bytes 6291460
  7.0 7.0 %copy-start.3 = (bf16[1,1,16,4096]{3,2,1,0:T(8,128)(2,1)S(1)}, bf16[1,1,16,4096]{3,2,1,0:T(8,128)(2,1)}, u32[]{:S(2)}) copy-start(bf16[1,1,16,4096]{3,2,1,0:T(8,128)(2,1)} %param.16) | copy-start | bytes 393220
  7.0 7.0 %copy-start.4 = (bf16[1,256,16]{1,2,0:T(8,128)(2,1)S(1)}, bf16[1,256,16]{1,2,0:T(8,128)(2,1)}, u32[]{:S(2)}) copy-start(bf16[1,256,16]{1,2,0:T(8,128)(2,1)} %param.15) | copy-start | bytes 24580
  8.8 10.5 %collective-permute-start.9 = (bf16[16,4096]{1,0:T(8,128)(2,1)S(1)}, bf16[16,4096]{1,0:T(8,128)(2,1)S(1)}, u32[]{:S(2)}, u32[]{:S(2)}) collective-permute-start(bf16[16,4096]{1,0:T(8,128)(2,1)S(1)} %shard_map.124.refs_0_.refs_3_), channel_id=1, source_target_pairs={{0,3},{1,2},{2,1},{3,0},{4,7},{5,6},{6,5},{7,4},{8,11},{9,10},{10,... | collective-permute-start | bytes 393224 | tf_op jit(solution)/shard_map/ppermute | solution.py:210
  11.7 8.1 %collective-permute-start.8 = (bf16[16,4096]{1,0:T(8,128)(2,1)S(1)}, bf16[16,4096]{1,0:T(8,128)(2,1)S(1)}, u32[]{:S(2)}, u32[]{:S(2)}) collective-permute-start(bf16[16,4096]{1,0:T(8,128)(2,1)S(1)} %shard_map.124.refs_0_.refs_3_), channel_id=1, source_target_pairs={{0,2},{1,3},{2,0},{3,1},{4,6},{5,7},{6,4},{7,5},{8,10},{9,11},{10,... | collective-permute-start | bytes 393224 | tf_op jit(solution)/shard_map/ppermute | solution.py:210
  12.2 7.5 %collective-permute-start.7 = (bf16[16,4096]{1,0:T(8,128)(2,1)S(1)}, bf16[16,4096]{1,0:T(8,128)(2,1)S(1)}, u32[]{:S(2)}, u32[]{:S(2)}) collective-permute-start(bf16[16,4096]{1,0:T(8,128)(2,1)S(1)} %shard_map.124.refs_0_.refs_3_), channel_id=1, source_target_pairs={{0,1},{1,0},{2,3},{3,2},{4,5},{5,4},{6,7},{7,6},{8,9},{9,8},{10,11... | collective-permute-start | bytes 393224 | tf_op jit(solution)/shard_map/ppermute | solution.py:210
  16.2 12.4 %collective-permute-start.3 = (bf16[16,4224]{1,0:T(8,128)(2,1)S(1)}, bf16[16,4224]{1,0:T(8,128)(2,1)S(1)}, u32[]{:S(2)}, u32[]{:S(2)}) collective-permute-start(bf16[16,4224]{1,0:T(8,128)(2,1)S(1)} %get-tuple-element.33), channel_id=1, source_target_pairs={{0,3},{1,2},{2,1},{3,0},{4,7},{5,6},{6,5},{7,4},{8,11},{9,10},{10,... | collective-permute-start | bytes 405512 | tf_op jit(solution)/shard_map/ppermute | solution.py:210
  18.8 9.8 %collective-permute-start.4 = (bf16[16,4224]{1,0:T(8,128)(2,1)S(1)}, bf16[16,4224]{1,0:T(8,128)(2,1)S(1)}, u32[]{:S(2)}, u32[]{:S(2)}) collective-permute-start(bf16[16,4224]{1,0:T(8,128)(2,1)S(1)} %get-tuple-element.34), channel_id=1, source_target_pairs={{0,1},{1,0},{2,3},{3,2},{4,5},{5,4},{6,7},{7,6},{8,9},{9,8},{10,11... | collective-permute-start | bytes 405512 | tf_op jit(solution)/shard_map/ppermute | solution.py:210
  19.3 9.3 %collective-permute-start.5 = (bf16[16,4224]{1,0:T(8,128)(2,1)S(1)}, bf16[16,4224]{1,0:T(8,128)(2,1)S(1)}, u32[]{:S(2)}, u32[]{:S(2)}) collective-permute-start(bf16[16,4224]{1,0:T(8,128)(2,1)S(1)} %get-tuple-element.35), channel_id=1, source_target_pairs={{0,2},{1,3},{2,0},{3,1},{4,6},{5,7},{6,4},{7,5},{8,10},{9,11},{10,... | collective-permute-start | bytes 405512 | tf_op jit(solution)/shard_map/ppermute | solution.py:210
  22.5 15.2 %collective-permute-start.11 = (bf16[16,4096]{1,0:T(8,128)(2,1)S(1)}, bf16[16,4096]{1,0:T(8,128)(2,1)S(1)}, u32[]{:S(2)}, u32[]{:S(2)}) collective-permute-start(bf16[16,4096]{1,0:T(8,128)(2,1)S(1)} %get-tuple-element.41), channel_id=1, source_target_pairs={{0,31},{1,30},{2,29},{3,28},{4,3},{5,2},{6,1},{7,0},{8,7},{9,6},{1... | collective-permute-start | bytes 393224 | tf_op jit(solution)/shard_map/ppermute | solution.py:210
  25.5 12.2 %collective-permute-start.12 = (bf16[16,4096]{1,0:T(8,128)(2,1)S(1)}, bf16[16,4096]{1,0:T(8,128)(2,1)S(1)}, u32[]{:S(2)}, u32[]{:S(2)}) collective-permute-start(bf16[16,4096]{1,0:T(8,128)(2,1)S(1)} %get-tuple-element.42), channel_id=1, source_target_pairs={{0,29},{1,28},{2,31},{3,30},{4,1},{5,0},{6,3},{7,2},{8,5},{9,4},{1... | collective-permute-start | bytes 393224 | tf_op jit(solution)/shard_map/ppermute | solution.py:210
  28.7 7.7 %collective-permute-start.6 = (bf16[16,4224]{1,0:T(8,128)(2,1)S(1)}, bf16[16,4224]{1,0:T(8,128)(2,1)S(1)}, u32[]{:S(2)}, u32[]{:S(2)}) collective-permute-start(bf16[16,4224]{1,0:T(8,128)(2,1)S(1)} %shard_map.122), channel_id=1, source_target_pairs={{0,4},{1,5},{2,6},{3,7},{4,8},{5,9},{6,10},{7,11},{8,12},{9,13},{1... | collective-permute-start | bytes 405512 | tf_op jit(solution)/shard_map/ppermute | solution.py:210
  28.8 8.9 %collective-permute-start.13 = (bf16[16,4096]{1,0:T(8,128)(2,1)S(1)}, bf16[16,4096]{1,0:T(8,128)(2,1)S(1)}, u32[]{:S(2)}, u32[]{:S(2)}) collective-permute-start(bf16[16,4096]{1,0:T(8,128)(2,1)S(1)} %get-tuple-element.43), channel_id=1, source_target_pairs={{0,30},{1,31},{2,28},{3,29},{4,2},{5,3},{6,0},{7,1},{8,6},{9,7},{1... | collective-permute-start | bytes 393224 | tf_op jit(solution)/shard_map/ppermute | solution.py:210
  32.4 5.3 %collective-permute-start.10 = (bf16[16,4224]{1,0:T(8,128)(2,1)S(1)}, bf16[16,4224]{1,0:T(8,128)(2,1)S(1)}, u32[]{:S(2)}, u32[]{:S(2)}) collective-permute-start(bf16[16,4224]{1,0:T(8,128)(2,1)S(1)} %get-tuple-element.40), channel_id=1, source_target_pairs={{0,28},{1,29},{2,30},{3,31},{4,0},{5,1},{6,2},{7,3},{8,4},{9,5},{1... | collective-permute-start | bytes 405512 | tf_op jit(solution)/shard_map/ppermute | solution.py:210

commit v10 on v7

--- a/solution.py
+++ b/solution.py
@@ -12,6 +12,7 @@
 LOWRANK_SCALE = 2.0
 LEVEL_STEP = 1.0 / 4096.0
 CHUNKS = 4
+DIAGONAL_FIRST = (3, 1, 2)
 MIB = 1 << 20
 LAST = (((1,), (1,)), ((), ()))
 FIRST = (((0,), (0,)), ((), ()))
@@ -27,8 +28,10 @@
     return jax.ShapeDtypeStruct(shape, dtype)
 
 
-def call(body, outs, args, far_args=(), far_outs=False, scratch=(), flops=0, grant=24 * MIB):
-    moved = sum(a.size * a.dtype.itemsize for a in (*args, *far_args, *outs))
+def call(
+    body, outs, args, far_args=(), far_outs=False, scratch=(), flops=0, moved=None, grant=24 * MIB
+):
+    moved = moved or sum(a.size * a.dtype.itemsize for a in (*args, *far_args, *outs))
     return pl.pallas_call(
         body,
         out_shape=outs,
@@ -54,9 +57,8 @@
     return copies
 
 
-def gather(
-    flight, choice_hbm, steps_hbm, x_hbm, rows_ref, place_ref, choice_ref, steps_ref, x_ref, *sems
-):
+def gather(flight, choice_hbm, steps_hbm, x_hbm, cot_hbm, *refs):
+    rows_ref, place_ref, cot_ref, choice_ref, steps_ref, x_ref, *sems = refs
     tokens, width = x_ref.shape
     span = width // CHUNKS
     small = [
@@ -66,15 +68,17 @@
     for copy in small:
         copy.start()
     copies = fetch(x_hbm, x_ref, sems[1])
+    cot_copy = pltpu.make_async_copy(cot_hbm.at[0], cot_ref, sems[0].at[2])
+    cot_copy.start()
+    before = lax.broadcasted_iota(jnp.int32, (tokens, tokens), 0) < lax.broadcasted_iota(
+        jnp.int32, (tokens, tokens), 1
+    )
+    before = jnp.where(before, 1.0, 0.0).astype(jnp.bfloat16)
+    slot = lax.broadcasted_iota(jnp.int32, (MOST, tokens), 0).astype(jnp.float32)
     for copy in small:
         copy.wait()
     choice = choice_ref[...]
     steps = steps_ref[...].astype(jnp.float32)
-    before = lax.broadcasted_iota(jnp.int32, (tokens, tokens), 0) < lax.broadcasted_iota(
-        jnp.int32, (tokens, tokens), 1
-    )
-    before = jnp.where(before, 1.0, 0.0).astype(jnp.bfloat16)
-    slot = lax.broadcasted_iota(jnp.int32, (MOST, tokens), 0).astype(jnp.float32)
     for f in range(flight):
         level = jnp.sum(jnp.where(choice == f, steps, 0.0), axis=0, keepdims=True)
         routed = jnp.broadcast_to(jnp.where(level > 0, 1.0, 0.0), (MOST, tokens))
@@ -85,24 +89,28 @@
         copies[c].wait()
         part = slice(c * span, (c + 1) * span)
         rows_ref[:, part] = f32dot(pick, x_ref[:, part]).astype(jnp.bfloat16)
-
-
-def gather_grads(place_ref, cot_hbm, rows_ref, cot_ref, sems):
-    copies = fetch(cot_hbm, cot_ref, sems)
-    span = cot_ref.shape[1] // CHUNKS
+    cot_copy.wait()
+
+
+def gather_grads(place_ref, cot_ref, rows_ref):
     place = place_ref[...]
-    pick = picks(place)
     gate = jnp.sum(place, axis=1, keepdims=True)
-    for c in range(CHUNKS):
-        copies[c].wait()
+    rows_ref[...] = (f32dot(picks(place), cot_ref[...]) * gate).astype(jnp.bfloat16)
+
+
+def add_adapter(down_ref, a_ref, b_ref, _, out_ref):
+    width = down_ref.shape[1]
+    span = width // 8
+    for c in range(8):
         part = slice(c * span, (c + 1) * span)
-        rows_ref[:, part] = (f32dot(pick, cot_ref[:, part]) * gate).astype(jnp.bfloat16)
+        adapter = LOWRANK_SCALE * f32dot(a_ref[...], b_ref[:, part], FIRST)
+        out_ref[:, part] = (down_ref[:, part].astype(jnp.float32) + adapter).astype(jnp.bfloat16)
 
 
 def forward(*refs):
-    x_refs, (gate_ref, up_ref, down_ref, a_ref, b_ref) = refs[:SPLIT], refs[SPLIT:SPLIT + 5]
-    out_refs = refs[SPLIT + 5:2 * SPLIT + 5]
-    pre_gate_ref, pre_up_ref, hidden_ref, latent_ref = refs[2 * SPLIT + 5:]
+    x_refs, (gate_ref, up_ref, down_ref, a_ref) = refs[:SPLIT], refs[SPLIT:SPLIT + 4]
+    out_refs = refs[SPLIT + 4:2 * SPLIT + 4]
+    pre_gate_ref, pre_up_ref, hidden_ref, latent_ref = refs[2 * SPLIT + 4:]
     rows = jnp.concatenate([r[...] for r in x_refs], axis=0)
     height, width = x_refs[0].shape
     pre_gate = f32dot(rows, gate_ref[...], LAST)
@@ -111,13 +119,11 @@
     pre_up_ref[...] = pre_up
     hidden = (pre_gate * jax.nn.sigmoid(pre_gate) * pre_up).astype(jnp.bfloat16)
     hidden_ref[...] = hidden
+    result = f32dot(hidden, down_ref[...]).astype(jnp.bfloat16)
+    for k, ref in enumerate(out_refs):
+        ref[:, :width] = result[k * height:(k + 1) * height]
     latent = f32dot(a_ref[...], hidden, LAST).astype(jnp.bfloat16)
     latent_ref[...] = latent
-    result = f32dot(hidden, down_ref[...])
-    result = result + f32dot(LOWRANK_SCALE * latent, b_ref[...], FIRST)
-    result = result.astype(jnp.bfloat16)
-    for k, ref in enumerate(out_refs):
-        ref[:, :width] = result[k * height:(k + 1) * height]
     if out_refs[1].shape[1] > width:
         rank, count = latent.shape
         tail = jnp.concatenate(
@@ -129,13 +135,11 @@
 
 def backward(*refs):
     g_refs = refs[:SPLIT]
-    pre_gate_ref, pre_up_ref, gate_ref, up_ref, down_ref, a_ref, b_ref = refs[SPLIT:SPLIT + 7]
-    *out_refs, lowrank_ref = refs[SPLIT + 7:]
+    pre_gate_ref, pre_up_ref, gate_ref, up_ref, down_ref = refs[SPLIT:SPLIT + 5]
+    out_refs = refs[SPLIT + 5:]
     rows = jnp.concatenate([r[...] for r in g_refs], axis=0)
-    height, width = g_refs[0].shape
-    lowrank = (LOWRANK_SCALE * f32dot(rows, b_ref[...], LAST)).astype(jnp.bfloat16)
-    lowrank_ref[...] = lowrank
-    grad_hidden = f32dot(rows, down_ref[...], LAST) + f32dot(lowrank, a_ref[...])
+    height = g_refs[0].shape[0]
+    grad_hidden = f32dot(rows, down_ref[...], LAST)
     pre_gate = pre_gate_ref[...]
     g = jax.nn.sigmoid(pre_gate)
     grad_gate = grad_hidden * pre_up_ref[...] * g * (1.0 + pre_gate * (1.0 - g))
@@ -159,18 +163,22 @@
         out_ref[:, width:] = picks(place)
 
 
-def down_map_grad(lowrank_ref, hidden_ref, out_ref):
-    out_ref[...] = f32dot(lowrank_ref[...], hidden_ref[...], FIRST)
+def down_map_grad(*refs):
+    g_refs, (hidden_ref, b_ref, out_ref) = refs[:SPLIT], refs[SPLIT:]
+    rows = jnp.concatenate([r[...] for r in g_refs], axis=0)
+    lowrank = (LOWRANK_SCALE * f32dot(rows, b_ref[...], LAST)).astype(jnp.bfloat16)
+    out_ref[...] = f32dot(lowrank, hidden_ref[...], FIRST)
 
 
 def up_map_grad(latent_ref, *refs):
-    message_refs, g_refs, out_ref = refs[:SPLIT - 1], refs[SPLIT - 1:2 * SPLIT - 1], refs[-1]
+    g_refs, out_ref = refs[SPLIT - 1:2 * SPLIT - 1], refs[-1]
+    distances = (0, *DIAGONAL_FIRST)
     span = out_ref.shape[-1]
     column = pl.multiple_of(lax.axis_index("expert") * span, 128)
     count = latent_ref.shape[1]
     width = g_refs[0].shape[1]
-    latents = [latent_ref[...]] + [r[:, width:width + count] for r in message_refs]
-    rows = [g_refs[i ^ k][:, pl.ds(column, span)] for k in range(SPLIT) for i in range(SPLIT)]
+    latents = [latent_ref[...]] + [r[:, width:width + count] for r in refs[:SPLIT - 1]]
+    rows = [g_refs[i ^ k][:, pl.ds(column, span)] for k in distances for i in range(SPLIT)]
     total = f32dot(jnp.concatenate(latents, axis=1), jnp.concatenate(rows, axis=0))
     out_ref[0, 0] = LOWRANK_SCALE * total
 
@@ -238,20 +246,25 @@
         up_map = lax.dynamic_index_in_dim(adapter_up_maps[0], group, 0, keepdims=False)
     down_map = jnp.swapaxes(adapter_down_maps[0], 0, 1)
 
-    x_rows, place = call(
+    x_rows, place, cot_near = call(
         functools.partial(gather, flight),
-        [sds(slots, width), sds(slots, tokens, dtype=jnp.float32)],
+        [
+            sds(slots, width),
+            sds(slots, tokens, dtype=jnp.float32),
+            sds(tokens, width),
+        ],
         (),
         (
             jnp.swapaxes(token_expert_choice[0], 0, 1),
             jnp.swapaxes(route_gate_steps[0], 0, 1),
             section_layer_input,
+            cotangent,
         ),
         scratch=[
             pltpu.VMEM((top, tokens), jnp.int32),
             pltpu.VMEM((top, tokens), jnp.int32),
             pltpu.VMEM((tokens, width), jnp.bfloat16),
-            dma((2,)),
+            dma((3,)),
             dma((CHUNKS,)),
         ],
         flops=2 * slots * tokens * width,
@@ -259,20 +272,25 @@
     x_rows = between_groups(x_rows, flight)
     x_blocks = [x_rows] + [shifted(x_rows, 0, k) for k in flips[1:]]
 
+    near = functools.partial(pltpu.with_memory_space_constraint, memory_space=pltpu.VMEM)
     (g_rows,) = call(
         gather_grads,
         [sds(slots, width)],
-        (place,),
-        (cotangent,),
-        scratch=[pltpu.VMEM((tokens, width), jnp.bfloat16), dma((CHUNKS,))],
+        (place, cot_near),
         flops=200 * units * rank * width,
     )
-    weights = [
-        pltpu.with_memory_space_constraint(a, pltpu.VMEM)
-        for a in (gate_weight[0], up_weight[0], down_weight[0], down_map, up_map)
-    ]
     g_rows = between_groups(g_rows, flight)
     g_blocks = [g_rows] + [shifted(g_rows, 0, k) for k in flips[1:]]
+
+    gate_near, up_near, down_near, a_near, b_near = map(
+        near, (gate_weight[0], up_weight[0], down_weight[0], down_map, up_map)
+    )
+    (down_near,) = call(
+        add_adapter,
+        [sds(units, width)],
+        (down_near, a_near, b_near, g_rows),
+        moved=1,
+    )
 
     wide = width + tokens
     *out_blocks, pre_gate, pre_up, hidden, latent = call(
@@ -281,23 +299,23 @@
         + [sds(slots, wide if flight == 1 else width)] * (SPLIT - 1)
         + [sds(rows, units, dtype=jnp.float32)] * 2
         + [sds(rows, units), sds(rank, rows)],
-        (*x_blocks, *weights),
+        (*x_blocks, gate_near, up_near, down_near, a_near),
         flops=60 * rows * units * width,
     )
-    out_parts = [out_blocks[0]] + [shifted(out_blocks[k], 0, k) for k in flips[1:]]
-    *grad_blocks, lowrank = call(
+    out_parts = [out_blocks[0]] + [shifted(out_blocks[k], 0, k) for k in DIAGONAL_FIRST]
+    grad_blocks = call(
         backward,
-        [sds(slots, width)] * SPLIT + [sds(rows, rank)],
-        (*g_blocks, pre_gate, pre_up, *weights),
+        [sds(slots, width)] * SPLIT,
+        (*g_blocks, pre_gate, pre_up, gate_near, up_near, down_near),
         flops=60 * rows * units * width,
     )
-    grad_parts = [grad_blocks[0]] + [shifted(grad_blocks[k], 0, k) for k in flips[1:]]
+    grad_parts = [grad_blocks[0]] + [shifted(grad_blocks[k], 0, k) for k in DIAGONAL_FIRST]
 
     hidden, latent, _ = lax.optimization_barrier((hidden, latent, grad_blocks[0]))
     (a_grad,) = call(
         down_map_grad,
         [sds(rank, units, dtype=jnp.float32)],
-        (lowrank, hidden),
+        (*g_blocks, hidden, b_near),
         flops=200 * rows * rank * width,
     )
     if flight == 1:

time: 37.7 us -> 37.2 us (0.987); the launches traced: 37 us -> 37 us
  starting transfers between devices: 17.2 us -> 18.8 us
  Pallas kernels: 12.7 us -> 11.6 us
    ppermute x14, starting transfers between devices: 17.2 us -> 18.8 us  [shifted(): return lax.ppermute(block, ('section', 'expert'), route)]
    pallas_call x10 -> x11, Pallas kernels: 12.7 us -> 11.6 us  [call(): pl.pallas_call(body, out_shape=outs, in_specs=[NEAR] * len(args) + [FAR]...]
  transfers between devices with their start and end apart: 14 -> 14, of which waited for: 6 -> 5; matrix products, arithmetic and copies ran while one was open for 0% -> 0% of each run, Pallas kernels for 26% -> 23%
where the time goes in v10:
time: 37.2 us; the launch traced here: 37 us
  starting transfers between devices  18.8 us (51%)
  Pallas kernels  11.6 us (31%)
  waiting for transfers between devices  5.99 us (16%)
  between operations  0.72 us (2%)
    ppermute x14, starting transfers between devices, shifted(): return lax.ppermute(block, ('section', 'expert'), route)  18.8 us
    pallas_call x11, Pallas kernels, call(): pl.pallas_call(body, out_shape=outs, in_specs=[NEAR] * len(args) + [FAR]...  11.6 us
    ppermute x14, waiting for transfers between devices, shifted(): return lax.ppermute(block, ('section', 'expert'), route)  5.99 us
  transfers between devices with their start and end apart: 14, of which 5 were waited for; matrix products, arithmetic and copies ran while one was open for 0% of the time, Pallas kernels for 23%

profile of v10, /device:TPU:0, one launch (start us, length us, event | category | flops | bytes accessed | tf_op | source)
XLA Modules:
  0.0 37.0 jit_solution(12926333267994072433)
XLA Ops:
  0.6 1.7 %shard_map.120 = (bf16[16,4096]{1,0:T(8,128)(2,1)S(1)}, f32[16,128]{1,0:T(8,128)S(1)}, bf16[128,4096]{1,0:T(8,128)(2,1)S(1)}) custom-call(s32[8,128]{1,0:T(8,128)} %bitcast.25, s32[8,128]{1,0:T(8,128)} %bitcast.26, bf16[1,128,4096]{2,1,0:T(8,128)(2,1)} %x_hbm.1, bf16[1,128,4096]{2,1,0:T(8,128)(2,1)} %cot_hbm.1), custom_call_target="tpu_custom_call" | custom-call | flops 16777216 | bytes 3293184 | tf_op jit(solution)/shard_map/pallas_call | solution.py:35
  2.3 4.0 %collective-permute-start.2 = (bf16[16,4096]{1,0:T(8,128)(2,1)S(1)}, bf16[16,4096]{1,0:T(8,128)(2,1)S(1)}, u32[]{:S(2)}, u32[]{:S(2)}) collective-permute-start(bf16[16,4096]{1,0:T(8,128)(2,1)S(1)} %get-tuple-element.30.refs_0_), channel_id=1, source_target_pairs={{0,3},{1,2},{2,1},{3,0},{4,7},{5,6},{6,5},{7,4},{8,11},{9,10},{10,... | collective-permute-start | bytes 393224 | tf_op jit(solution)/shard_map/ppermute | solution.py:211
  6.3 0.5 %collective-permute-start.1 = (bf16[16,4096]{1,0:T(8,128)(2,1)S(1)}, bf16[16,4096]{1,0:T(8,128)(2,1)S(1)}, u32[]{:S(2)}, u32[]{:S(2)}) collective-permute-start(bf16[16,4096]{1,0:T(8,128)(2,1)S(1)} %get-tuple-element.30.refs_0_), channel_id=1, source_target_pairs={{0,2},{1,3},{2,0},{3,1},{4,6},{5,7},{6,4},{7,5},{8,10},{9,11},{10,... | collective-permute-start | bytes 393224 | tf_op jit(solution)/shard_map/ppermute | solution.py:211
  6.8 0.1 collective-permute-start
  6.9 0.2 shard_map.121._.refs_0_.refs_3_
  7.2 2.9 %collective-permute-start.9 = (bf16[16,4096]{1,0:T(8,128)(2,1)S(1)}, bf16[16,4096]{1,0:T(8,128)(2,1)S(1)}, u32[]{:S(2)}, u32[]{:S(2)}) collective-permute-start(bf16[16,4096]{1,0:T(8,128)(2,1)S(1)} %shard_map.121._.refs_0_.refs_3_), channel_id=1, source_target_pairs={{0,3},{1,2},{2,1},{3,0},{4,7},{5,6},{6,5},{7,4},{8,11},{9,10},{10,... | collective-permute-start | bytes 393224 | tf_op jit(solution)/shard_map/ppermute | solution.py:211
  10.1 0.5 %collective-permute-start.8 = (bf16[16,4096]{1,0:T(8,128)(2,1)S(1)}, bf16[16,4096]{1,0:T(8,128)(2,1)S(1)}, u32[]{:S(2)}, u32[]{:S(2)}) collective-permute-start(bf16[16,4096]{1,0:T(8,128)(2,1)S(1)} %shard_map.121._.refs_0_.refs_3_), channel_id=1, source_target_pairs={{0,2},{1,3},{2,0},{3,1},{4,6},{5,7},{6,4},{7,5},{8,10},{9,11},{10,... | collective-permute-start | bytes 393224 | tf_op jit(solution)/shard_map/ppermute | solution.py:211
  10.6 0.0 copy-start.4
  10.6 0.7 %shard_map.122.refs_6_.refs_8_ = bf16[256,4096]{1,0:T(8,128)(2,1)S(1)} custom-call(bf16[256,4096]{1,0:T(8,128)(2,1)S(1)} %bitcast.16, bf16[16,256]{1,0:T(8,128)(2,1)S(1)} %bitcast.19, bf16[16,4096]{1,0:T(8,128)(2,1)S(1)} %bitcast.17, bf16[16,4096]{1,0:T(8,128)(2,1)S(1)} %shard_map.121._.refs_0_.refs_3_), custom_call_target="tpu_custom_call" | custom-call | bytes 1 | tf_op jit(solution)/shard_map/pallas_call | solution.py:35
  11.3 0.0 collective-permute-done.2.refs_3_
  11.3 1.3 %collective-permute-start.7 = (bf16[16,4096]{1,0:T(8,128)(2,1)S(1)}, bf16[16,4096]{1,0:T(8,128)(2,1)S(1)}, u32[]{:S(2)}, u32[]{:S(2)}) collective-permute-start(bf16[16,4096]{1,0:T(8,128)(2,1)S(1)} %shard_map.121._.refs_0_.refs_3_), channel_id=1, source_target_pairs={{0,1},{1,0},{2,3},{3,2},{4,5},{5,4},{6,7},{7,6},{8,9},{9,8},{10,11... | collective-permute-start | bytes 393224 | tf_op jit(solution)/shard_map/ppermute | solution.py:211
  12.6 1.5 %collective-permute-done.1.refs_2_ = bf16[16,4096]{1,0:T(8,128)(2,1)S(1)} collective-permute-done((bf16[16,4096]{1,0:T(8,128)(2,1)S(1)}, bf16[16,4096]{1,0:T(8,128)(2,1)S(1)}, u32[]{:S(2)}, u32[]{:S(2)}) %collective-permute-start.1) | collective-permute-done | bytes 131104 | tf_op jit(solution)/shard_map/ppermute | solution.py:211
  14.1 1.9 %shard_map.123 = (bf16[16,4096]{1,0:T(8,128)(2,1)S(1)}, bf16[16,4224]{1,0:T(8,128)(2,1)S(1)}, bf16[16,4224]{1,0:T(8,128)(2,1)S(1)}, bf16[16,4224]{1,0:T(8,128)(2...) custom-call(bf16[16,4096]{1,0:T(8,128)(2,1)S(1)} %get-tuple-element., ...), custom_call_target="tpu_custom_call" | custom-call | flops 4026531840 | bytes 7526400 | tf_op jit(solution)/shard_map/pallas_call | solution.py:35
  15.9 2.4 %collective-permute-start.3 = (bf16[16,4224]{1,0:T(8,128)(2,1)S(1)}, bf16[16,4224]{1,0:T(8,128)(2,1)S(1)}, u32[]{:S(2)}, u32[]{:S(2)}) collective-permute-start(bf16[16,4224]{1,0:T(8,128)(2,1)S(1)} %get-tuple-element.33), channel_id=1, source_target_pairs={{0,3},{1,2},{2,1},{3,0},{4,7},{5,6},{6,5},{7,4},{8,11},{9,10},{10,... | collective-permute-start | bytes 405512 | tf_op jit(solution)/shard_map/ppermute | solution.py:211
  18.4 0.6 %collective-permute-start.4 = (bf16[16,4224]{1,0:T(8,128)(2,1)S(1)}, bf16[16,4224]{1,0:T(8,128)(2,1)S(1)}, u32[]{:S(2)}, u32[]{:S(2)}) collective-permute-start(bf16[16,4224]{1,0:T(8,128)(2,1)S(1)} %get-tuple-element.34), channel_id=1, source_target_pairs={{0,1},{1,0},{2,3},{3,2},{4,5},{5,4},{6,7},{7,6},{8,9},{9,8},{10,11... | collective-permute-start | bytes 405512 | tf_op jit(solution)/shard_map/ppermute | solution.py:211
  18.9 0.6 %collective-permute-start.5 = (bf16[16,4224]{1,0:T(8,128)(2,1)S(1)}, bf16[16,4224]{1,0:T(8,128)(2,1)S(1)}, u32[]{:S(2)}, u32[]{:S(2)}) collective-permute-start(bf16[16,4224]{1,0:T(8,128)(2,1)S(1)} %get-tuple-element.35), channel_id=1, source_target_pairs={{0,2},{1,3},{2,0},{3,1},{4,6},{5,7},{6,4},{7,5},{8,10},{9,11},{10,... | collective-permute-start | bytes 405512 | tf_op jit(solution)/shard_map/ppermute | solution.py:211
  19.5 2.5 %shard_map.126 = (bf16[16,4096]{1,0:T(8,128)(2,1)S(1)}, bf16[16,4096]{1,0:T(8,128)(2,1)S(1)}, bf16[16,4096]{1,0:T(8,128)(2,1)S(1)}, bf16[16,4096]{1,0:T(8,128)(2,1)S(1)}) custom-call(bf16[16,4096]{1,0:T(8,128)(2,1)S(1)} %shard_map.121._.refs_0_.refs_3_, bf16[16,4096]{1,0:T(8,128)(2,1)S(1)} %collective-permute-done.7.refs_1_.refs_4_, ...), custom_call_target="tpu_custom_call" | custom-call | flops 4026531840 | bytes 7471104 | tf_op jit(solution)/shard_map/pallas_call | solution.py:35
  22.0 2.4 %collective-permute-start.10 = (bf16[16,4096]{1,0:T(8,128)(2,1)S(1)}, bf16[16,4096]{1,0:T(8,128)(2,1)S(1)}, u32[]{:S(2)}, u32[]{:S(2)}) collective-permute-start(bf16[16,4096]{1,0:T(8,128)(2,1)S(1)} %get-tuple-element.39), channel_id=1, source_target_pairs={{0,3},{1,2},{2,1},{3,0},{4,7},{5,6},{6,5},{7,4},{8,11},{9,10},{10,... | collective-permute-start | bytes 393224 | tf_op jit(solution)/shard_map/ppermute | solution.py:211
  24.4 0.6 %collective-permute-start.11 = (bf16[16,4096]{1,0:T(8,128)(2,1)S(1)}, bf16[16,4096]{1,0:T(8,128)(2,1)S(1)}, u32[]{:S(2)}, u32[]{:S(2)}) collective-permute-start(bf16[16,4096]{1,0:T(8,128)(2,1)S(1)} %get-tuple-element.40), channel_id=1, source_target_pairs={{0,1},{1,0},{2,3},{3,2},{4,5},{5,4},{6,7},{7,6},{8,9},{9,8},{10,11... | collective-permute-start | bytes 393224 | tf_op jit(solution)/shard_map/ppermute | solution.py:211
  25.0 0.6 %collective-permute-start.12 = (bf16[16,4096]{1,0:T(8,128)(2,1)S(1)}, bf16[16,4096]{1,0:T(8,128)(2,1)S(1)}, u32[]{:S(2)}, u32[]{:S(2)}) collective-permute-start(bf16[16,4096]{1,0:T(8,128)(2,1)S(1)} %get-tuple-element.41), channel_id=1, source_target_pairs={{0,2},{1,3},{2,0},{3,1},{4,6},{5,7},{6,4},{7,5},{8,10},{9,11},{10,... | collective-permute-start | bytes 393224 | tf_op jit(solution)/shard_map/ppermute | solution.py:211
  25.6 1.0 %shard_map.127 = f32[16,256]{1,0:T(8,128)} custom-call(bf16[16,4096]{1,0:T(8,128)(2,1)S(1)} %shard_map.121._.refs_0_.refs_3_, bf16[16,4096]{1,0:T(8,128)(2,1)S(1)} %collective-permute-done.7.refs_1_.refs_4_, bf16[16,4096]{1,0:T(8,128)(2,1)S(1)} %collective-permute-done.8.refs_2_.refs_5_, bf16[16,4096]{1,0:T(8,128)(2,1)S(1)} %collective-permute-done.9.refs_3_.refs_6_, ...), custom_call_target="tpu_custom_call" | custom-call | flops 838860800 | bytes 704512 | tf_op jit(solution)/shard_map/pallas_call | solution.py:35
  26.6 0.1 shard_map.124
  26.7 0.1 collective-permute-start.6
  26.8 0.9 %shard_map.128 = f32[1,1,16,1024]{3,2,1,0:T(8,128)} custom-call(bf16[16,64]{1,0:T(8,128)(2,1)S(1)} %get-tuple-element.45.latent_ref, bf16[16,4224]{1,0:T(8,128)(2,1)S(1)} %collective-permute-done.3.refs_1_.refs_0_, bf16[16,4224]{1,0:T(8,128)(2,1)S(1)} %collective-permute-done.4.refs_2_.refs_1_, bf16[16,4224]{1,0:T(8,128)(2,1)S(1)} %collective-permute-done.5.refs_3_.refs_2_, ...), custom_call_target="tpu_custom_call" | custom-call | flops 838860800 | bytes 997376 | tf_op jit(solution)/shard_map/pallas_call | solution.py:35
  27.6 1.8 %collective-permute-done.10.refs_1_ = bf16[16,4096]{1,0:T(8,128)(2,1)S(1)} collective-permute-done((bf16[16,4096]{1,0:T(8,128)(2,1)S(1)}, bf16[16,4096]{1,0:T(8,128)(2,1)S(1)}, u32[]{:S(2)}, u32[]{:S(2)}) %collective-permute-start.10) | collective-permute-done | bytes 131104 | tf_op jit(solution)/shard_map/ppermute | solution.py:211
  29.4 1.3 %collective-permute-done.11.refs_2_ = bf16[16,4096]{1,0:T(8,128)(2,1)S(1)} collective-permute-done((bf16[16,4096]{1,0:T(8,128)(2,1)S(1)}, bf16[16,4096]{1,0:T(8,128)(2,1)S(1)}, u32[]{:S(2)}, u32[]{:S(2)}) %collective-permute-start.11) | collective-permute-done | bytes 131104 | tf_op jit(solution)/shard_map/ppermute | solution.py:211
  30.7 0.1 collective-permute-done.12.refs_3_
  30.8 0.1 shard_map.129
  30.9 2.3 %collective-permute-start.13 = (bf16[16,4224]{1,0:T(8,128)(2,1)S(1)}, bf16[16,4224]{1,0:T(8,128)(2,1)S(1)}, u32[]{:S(2)}, u32[]{:S(2)}) collective-permute-start(bf16[16,4224]{1,0:T(8,128)(2,1)S(1)} %shard_map.129), channel_id=1, source_target_pairs={{0,28},{1,29},{2,30},{3,31},{4,0},{5,1},{6,2},{7,3},{8,4},{9,5},{1... | collective-permute-start | bytes 405512 | tf_op jit(solution)/shard_map/ppermute | solution.py:211
  33.2 1.2 %shard_map.125 = bf16[1,128,4096]{2,1,0:T(8,128)(2,1)} custom-call(bf16[16,4224]{1,0:T(8,128)(2,1)S(1)} %collective-permute-done.6.message_ref), custom_call_target="tpu_custom_call" | custom-call | flops 16777216 | bytes 1183744 | tf_op jit(solution)/shard_map/pallas_call | solution.py:35
  34.5 1.3 %collective-permute-done.13.message_ref = bf16[16,4224]{1,0:T(8,128)(2,1)S(1)} collective-permute-done((bf16[16,4224]{1,0:T(8,128)(2,1)S(1)}, bf16[16,4224]{1,0:T(8,128)(2,1)S(1)}, u32[]{:S(2)}, u32[]{:S(2)}) %collective-permute-start.13) | collective-permute-done | bytes 135200 | tf_op jit(solution)/shard_map/ppermute | solution.py:211
  35.8 1.2 %shard_map.130 = bf16[1,128,4096]{2,1,0:T(8,128)(2,1)} custom-call(bf16[16,4224]{1,0:T(8,128)(2,1)S(1)} %collective-permute-done.13.message_ref), custom_call_target="tpu_custom_call" | custom-call | flops 16777216 | bytes 1183744 | tf_op jit(solution)/shard_map/pallas_call | solution.py:35
  (17 shorter events, 0.0 us)
Async XLA Ops:
  2.3 9.0 %collective-permute-start.2 = (bf16[16,4096]{1,0:T(8,128)(2,1)S(1)}, bf16[16,4096]{1,0:T(8,128)(2,1)S(1)}, u32[]{:S(2)}, u32[]{:S(2)}) collective-permute-start(bf16[16,4096]{1,0:T(8,128)(2,1)S(1)} %get-tuple-element.30.refs_0_), channel_id=1, source_target_pairs={{0,3},{1,2},{2,1},{3,0},{4,7},{5,6},{6,5},{7,4},{8,11},{9,10},{10,... | collective-permute-start | bytes 393224 | tf_op jit(solution)/shard_map/ppermute | solution.py:211
  6.3 7.8 %collective-permute-start.1 = (bf16[16,4096]{1,0:T(8,128)(2,1)S(1)}, bf16[16,4096]{1,0:T(8,128)(2,1)S(1)}, u32[]{:S(2)}, u32[]{:S(2)}) collective-permute-start(bf16[16,4096]{1,0:T(8,128)(2,1)S(1)} %get-tuple-element.30.refs_0_), channel_id=1, source_target_pairs={{0,2},{1,3},{2,0},{3,1},{4,6},{5,7},{6,4},{7,5},{8,10},{9,11},{10,... | collective-permute-start | bytes 393224 | tf_op jit(solution)/shard_map/ppermute | solution.py:211
  6.8 7.3 %collective-permute-start = (bf16[16,4096]{1,0:T(8,128)(2,1)S(1)}, bf16[16,4096]{1,0:T(8,128)(2,1)S(1)}, u32[]{:S(2)}, u32[]{:S(2)}) collective-permute-start(bf16[16,4096]{1,0:T(8,128)(2,1)S(1)} %get-tuple-element.30.refs_0_), channel_id=1, source_target_pairs={{0,1},{1,0},{2,3},{3,2},{4,5},{5,4},{6,7},{7,6},{8,9},{9,8},{10,11... | collective-permute-start | bytes 393224 | tf_op jit(solution)/shard_map/ppermute | solution.py:211
  6.9 3.7 %copy-start = (bf16[1,256,4096]{2,1,0:T(8,128)(2,1)S(1)}, bf16[1,256,4096]{2,1,0:T(8,128)(2,1)}, u32[]{:S(2)}) copy-start(bf16[1,256,4096]{2,1,0:T(8,128)(2,1)} %param.14) | copy-start | bytes 6291460
  6.9 3.7 %copy-start.1 = (bf16[1,1,16,4096]{3,2,1,0:T(8,128)(2,1)S(1)}, bf16[1,1,16,4096]{3,2,1,0:T(8,128)(2,1)}, u32[]{:S(2)}) copy-start(bf16[1,1,16,4096]{3,2,1,0:T(8,128)(2,1)} %param.16) | copy-start | bytes 393220
  6.9 3.7 %copy-start.2 = (bf16[1,256,16]{1,2,0:T(8,128)(2,1)S(1)}, bf16[1,256,16]{1,2,0:T(8,128)(2,1)}, u32[]{:S(2)}) copy-start(bf16[1,256,16]{1,2,0:T(8,128)(2,1)} %param.15) | copy-start | bytes 24580
  7.2 11.8 %collective-permute-start.9 = (bf16[16,4096]{1,0:T(8,128)(2,1)S(1)}, bf16[16,4096]{1,0:T(8,128)(2,1)S(1)}, u32[]{:S(2)}, u32[]{:S(2)}) collective-permute-start(bf16[16,4096]{1,0:T(8,128)(2,1)S(1)} %shard_map.121._.refs_0_.refs_3_), channel_id=1, source_target_pairs={{0,3},{1,2},{2,1},{3,0},{4,7},{5,6},{6,5},{7,4},{8,11},{9,10},{10,... | collective-permute-start | bytes 393224 | tf_op jit(solution)/shard_map/ppermute | solution.py:211
  10.1 9.4 %collective-permute-start.8 = (bf16[16,4096]{1,0:T(8,128)(2,1)S(1)}, bf16[16,4096]{1,0:T(8,128)(2,1)S(1)}, u32[]{:S(2)}, u32[]{:S(2)}) collective-permute-start(bf16[16,4096]{1,0:T(8,128)(2,1)S(1)} %shard_map.121._.refs_0_.refs_3_), channel_id=1, source_target_pairs={{0,2},{1,3},{2,0},{3,1},{4,6},{5,7},{6,4},{7,5},{8,10},{9,11},{10,... | collective-permute-start | bytes 393224 | tf_op jit(solution)/shard_map/ppermute | solution.py:211
  10.6 3.5 %copy-start.3 = (bf16[1,256,4096]{2,1,0:T(8,128)(2,1)S(1)}, bf16[1,256,4096]{2,1,0:T(8,128)(2,1)}, u32[]{:S(2)}) copy-start(bf16[1,256,4096]{2,1,0:T(8,128)(2,1)} %param.12) | copy-start | bytes 6291460
  10.6 3.5 %copy-start.4 = (bf16[1,256,4096]{2,1,0:T(8,128)(2,1)S(1)}, bf16[1,256,4096]{2,1,0:T(8,128)(2,1)}, u32[]{:S(2)}) copy-start(bf16[1,256,4096]{2,1,0:T(8,128)(2,1)} %param.13) | copy-start | bytes 6291460
  11.3 8.2 %collective-permute-start.7 = (bf16[16,4096]{1,0:T(8,128)(2,1)S(1)}, bf16[16,4096]{1,0:T(8,128)(2,1)S(1)}, u32[]{:S(2)}, u32[]{:S(2)}) collective-permute-start(bf16[16,4096]{1,0:T(8,128)(2,1)S(1)} %shard_map.121._.refs_0_.refs_3_), channel_id=1, source_target_pairs={{0,1},{1,0},{2,3},{3,2},{4,5},{5,4},{6,7},{7,6},{8,9},{9,8},{10,11... | collective-permute-start | bytes 393224 | tf_op jit(solution)/shard_map/ppermute | solution.py:211
  15.9 9.0 %collective-permute-start.3 = (bf16[16,4224]{1,0:T(8,128)(2,1)S(1)}, bf16[16,4224]{1,0:T(8,128)(2,1)S(1)}, u32[]{:S(2)}, u32[]{:S(2)}) collective-permute-start(bf16[16,4224]{1,0:T(8,128)(2,1)S(1)} %get-tuple-element.33), channel_id=1, source_target_pairs={{0,3},{1,2},{2,1},{3,0},{4,7},{5,6},{6,5},{7,4},{8,11},{9,10},{10,... | collective-permute-start | bytes 405512 | tf_op jit(solution)/shard_map/ppermute | solution.py:211
  18.4 8.2 %collective-permute-start.4 = (bf16[16,4224]{1,0:T(8,128)(2,1)S(1)}, bf16[16,4224]{1,0:T(8,128)(2,1)S(1)}, u32[]{:S(2)}, u32[]{:S(2)}) collective-permute-start(bf16[16,4224]{1,0:T(8,128)(2,1)S(1)} %get-tuple-element.34), channel_id=1, source_target_pairs={{0,1},{1,0},{2,3},{3,2},{4,5},{5,4},{6,7},{7,6},{8,9},{9,8},{10,11... | collective-permute-start | bytes 405512 | tf_op jit(solution)/shard_map/ppermute | solution.py:211
  18.9 7.7 %collective-permute-start.5 = (bf16[16,4224]{1,0:T(8,128)(2,1)S(1)}, bf16[16,4224]{1,0:T(8,128)(2,1)S(1)}, u32[]{:S(2)}, u32[]{:S(2)}) collective-permute-start(bf16[16,4224]{1,0:T(8,128)(2,1)S(1)} %get-tuple-element.35), channel_id=1, source_target_pairs={{0,2},{1,3},{2,0},{3,1},{4,6},{5,7},{6,4},{7,5},{8,10},{9,11},{10,... | collective-permute-start | bytes 405512 | tf_op jit(solution)/shard_map/ppermute | solution.py:211
  22.0 7.4 %collective-permute-start.10 = (bf16[16,4096]{1,0:T(8,128)(2,1)S(1)}, bf16[16,4096]{1,0:T(8,128)(2,1)S(1)}, u32[]{:S(2)}, u32[]{:S(2)}) collective-permute-start(bf16[16,4096]{1,0:T(8,128)(2,1)S(1)} %get-tuple-element.39), channel_id=1, source_target_pairs={{0,3},{1,2},{2,1},{3,0},{4,7},{5,6},{6,5},{7,4},{8,11},{9,10},{10,... | collective-permute-start | bytes 393224 | tf_op jit(solution)/shard_map/ppermute | solution.py:211
  24.4 6.3 %collective-permute-start.11 = (bf16[16,4096]{1,0:T(8,128)(2,1)S(1)}, bf16[16,4096]{1,0:T(8,128)(2,1)S(1)}, u32[]{:S(2)}, u32[]{:S(2)}) collective-permute-start(bf16[16,4096]{1,0:T(8,128)(2,1)S(1)} %get-tuple-element.40), channel_id=1, source_target_pairs={{0,1},{1,0},{2,3},{3,2},{4,5},{5,4},{6,7},{7,6},{8,9},{9,8},{10,11... | collective-permute-start | bytes 393224 | tf_op jit(solution)/shard_map/ppermute | solution.py:211
  25.0 5.8 %collective-permute-start.12 = (bf16[16,4096]{1,0:T(8,128)(2,1)S(1)}, bf16[16,4096]{1,0:T(8,128)(2,1)S(1)}, u32[]{:S(2)}, u32[]{:S(2)}) collective-permute-start(bf16[16,4096]{1,0:T(8,128)(2,1)S(1)} %get-tuple-element.41), channel_id=1, source_target_pairs={{0,2},{1,3},{2,0},{3,1},{4,6},{5,7},{6,4},{7,5},{8,10},{9,11},{10,... | collective-permute-start | bytes 393224 | tf_op jit(solution)/shard_map/ppermute | solution.py:211
  26.7 6.5 %collective-permute-start.6 = (bf16[16,4224]{1,0:T(8,128)(2,1)S(1)}, bf16[16,4224]{1,0:T(8,128)(2,1)S(1)}, u32[]{:S(2)}, u32[]{:S(2)}) collective-permute-start(bf16[16,4224]{1,0:T(8,128)(2,1)S(1)} %shard_map.124), channel_id=1, source_target_pairs={{0,4},{1,5},{2,6},{3,7},{4,8},{5,9},{6,10},{7,11},{8,12},{9,13},{1... | collective-permute-start | bytes 405512 | tf_op jit(solution)/shard_map/ppermute | solution.py:211
  30.9 4.9 %collective-permute-start.13 = (bf16[16,4224]{1,0:T(8,128)(2,1)S(1)}, bf16[16,4224]{1,0:T(8,128)(2,1)S(1)}, u32[]{:S(2)}, u32[]{:S(2)}) collective-permute-start(bf16[16,4224]{1,0:T(8,128)(2,1)S(1)} %shard_map.129), channel_id=1, source_target_pairs={{0,28},{1,29},{2,30},{3,31},{4,0},{5,1},{6,2},{7,3},{8,4},{9,5},{1... | collective-permute-start | bytes 405512 | tf_op jit(solution)/shard_map/ppermute | solution.py:211

commit v11 on v10

--- a/solution.py
+++ b/solution.py
@@ -12,6 +12,7 @@
 LOWRANK_SCALE = 2.0
 LEVEL_STEP = 1.0 / 4096.0
 CHUNKS = 4
+SPAN = 512
 DIAGONAL_FIRST = (3, 1, 2)
 MIB = 1 << 20
 LAST = (((1,), (1,)), ((), ()))
@@ -22,6 +23,10 @@
 
 def f32dot(a, b, dims=(((1,), (0,)), ((), ()))):
     return lax.dot_general(a, b, dims, preferred_element_type=jnp.float32)
+
+
+def spans(width, start=0):
+    return [slice(start + c, start + c + SPAN) for c in range(0, width, SPAN)]
 
 
 def sds(*shape, dtype=jnp.bfloat16):
@@ -119,9 +124,10 @@
     pre_up_ref[...] = pre_up
     hidden = (pre_gate * jax.nn.sigmoid(pre_gate) * pre_up).astype(jnp.bfloat16)
     hidden_ref[...] = hidden
-    result = f32dot(hidden, down_ref[...]).astype(jnp.bfloat16)
-    for k, ref in enumerate(out_refs):
-        ref[:, :width] = result[k * height:(k + 1) * height]
+    for part in spans(width):
+        result = f32dot(hidden, down_ref[:, part]).astype(jnp.bfloat16)
+        for k, ref in enumerate(out_refs):
+            ref[:, part] = result[k * height:(k + 1) * height]
     latent = f32dot(a_ref[...], hidden, LAST).astype(jnp.bfloat16)
     latent_ref[...] = latent
     if out_refs[1].shape[1] > width:
@@ -138,17 +144,19 @@
     pre_gate_ref, pre_up_ref, gate_ref, up_ref, down_ref = refs[SPLIT:SPLIT + 5]
     out_refs = refs[SPLIT + 5:]
     rows = jnp.concatenate([r[...] for r in g_refs], axis=0)
-    height = g_refs[0].shape[0]
+    height, width = g_refs[0].shape
     grad_hidden = f32dot(rows, down_ref[...], LAST)
     pre_gate = pre_gate_ref[...]
     g = jax.nn.sigmoid(pre_gate)
     grad_gate = grad_hidden * pre_up_ref[...] * g * (1.0 + pre_gate * (1.0 - g))
     grad_up = grad_hidden * pre_gate * g
-    result = f32dot(grad_gate.astype(jnp.bfloat16), gate_ref[...])
-    result = result + f32dot(grad_up.astype(jnp.bfloat16), up_ref[...])
-    result = result.astype(jnp.bfloat16)
-    for k, ref in enumerate(out_refs):
-        ref[...] = result[k * height:(k + 1) * height]
+    grad_gate = grad_gate.astype(jnp.bfloat16)
+    grad_up = grad_up.astype(jnp.bfloat16)
+    for part in spans(width):
+        result = f32dot(grad_gate, gate_ref[:, part]) + f32dot(grad_up, up_ref[:, part])
+        result = result.astype(jnp.bfloat16)
+        for k, ref in enumerate(out_refs):
+            ref[:, part] = result[k * height:(k + 1) * height]
 
 
 def combine(gated, place_ref, *refs):
@@ -189,8 +197,8 @@
     span = width // CHUNKS
     copies = []
     for c in range(CHUNKS):
-        part = slice(c * span, (c + 1) * span)
-        out_ref[:, part] = f32dot(pick, message_ref[:, part], FIRST).astype(jnp.bfloat16)
+        for part in spans(span, c * span):
+            out_ref[:, part] = f32dot(pick, message_ref[:, part], FIRST).astype(jnp.bfloat16)
         columns = pl.ds(c * span, span)
         copy = pltpu.make_async_copy(
             out_ref.at[:, columns], out_hbm.at[0, :, columns], sems.at[c]

time: 37.2 us -> 37.2 us (level)
  no operation moved by 1% of the time
where the time goes in v11:
time: 37.2 us; the launch traced here: 37 us
  starting transfers between devices  18.8 us (51%)
  Pallas kernels  11.6 us (31%)
  waiting for transfers between devices  5.99 us (16%)
  between operations  0.72 us (2%)
    ppermute x14, starting transfers between devices, shifted(): return lax.ppermute(block, ('section', 'expert'), route)  18.8 us
    pallas_call x11, Pallas kernels, call(): pl.pallas_call(body, out_shape=outs, in_specs=[NEAR] * len(args) + [FAR]...  11.6 us
    ppermute x14, waiting for transfers between devices, shifted(): return lax.ppermute(block, ('section', 'expert'), route)  5.99 us
  transfers between devices with their start and end apart: 14, of which 5 were waited for; matrix products, arithmetic and copies ran while one was open for 0% of the time, Pallas kernels for 23%

profile of v11, /device:TPU:0, one launch (start us, length us, event | category | flops | bytes accessed | tf_op | source)
XLA Modules:
  0.0 37.0 jit_solution(16483721070814628858)
XLA Ops:
  0.6 1.7 %shard_map.120 = (bf16[16,4096]{1,0:T(8,128)(2,1)S(1)}, f32[16,128]{1,0:T(8,128)S(1)}, bf16[128,4096]{1,0:T(8,128)(2,1)S(1)}) custom-call(s32[8,128]{1,0:T(8,128)} %bitcast.25, s32[8,128]{1,0:T(8,128)} %bitcast.26, bf16[1,128,4096]{2,1,0:T(8,128)(2,1)} %x_hbm.1, bf16[1,128,4096]{2,1,0:T(8,128)(2,1)} %cot_hbm.1), custom_call_target="tpu_custom_call" | custom-call | flops 16777216 | bytes 3293184 | tf_op jit(solution)/shard_map/pallas_call | solution.py:40
  2.3 4.0 %collective-permute-start.2 = (bf16[16,4096]{1,0:T(8,128)(2,1)S(1)}, bf16[16,4096]{1,0:T(8,128)(2,1)S(1)}, u32[]{:S(2)}, u32[]{:S(2)}) collective-permute-start(bf16[16,4096]{1,0:T(8,128)(2,1)S(1)} %get-tuple-element.30.refs_0_), channel_id=1, source_target_pairs={{0,3},{1,2},{2,1},{3,0},{4,7},{5,6},{6,5},{7,4},{8,11},{9,10},{10,... | collective-permute-start | bytes 393224 | tf_op jit(solution)/shard_map/ppermute | solution.py:219
  6.3 0.5 %collective-permute-start.1 = (bf16[16,4096]{1,0:T(8,128)(2,1)S(1)}, bf16[16,4096]{1,0:T(8,128)(2,1)S(1)}, u32[]{:S(2)}, u32[]{:S(2)}) collective-permute-start(bf16[16,4096]{1,0:T(8,128)(2,1)S(1)} %get-tuple-element.30.refs_0_), channel_id=1, source_target_pairs={{0,2},{1,3},{2,0},{3,1},{4,6},{5,7},{6,4},{7,5},{8,10},{9,11},{10,... | collective-permute-start | bytes 393224 | tf_op jit(solution)/shard_map/ppermute | solution.py:219
  6.8 0.1 collective-permute-start
  6.9 0.2 shard_map.121._.refs_0_.refs_3_
  7.2 2.9 %collective-permute-start.9 = (bf16[16,4096]{1,0:T(8,128)(2,1)S(1)}, bf16[16,4096]{1,0:T(8,128)(2,1)S(1)}, u32[]{:S(2)}, u32[]{:S(2)}) collective-permute-start(bf16[16,4096]{1,0:T(8,128)(2,1)S(1)} %shard_map.121._.refs_0_.refs_3_), channel_id=1, source_target_pairs={{0,3},{1,2},{2,1},{3,0},{4,7},{5,6},{6,5},{7,4},{8,11},{9,10},{10,... | collective-permute-start | bytes 393224 | tf_op jit(solution)/shard_map/ppermute | solution.py:219
  10.1 0.5 %collective-permute-start.8 = (bf16[16,4096]{1,0:T(8,128)(2,1)S(1)}, bf16[16,4096]{1,0:T(8,128)(2,1)S(1)}, u32[]{:S(2)}, u32[]{:S(2)}) collective-permute-start(bf16[16,4096]{1,0:T(8,128)(2,1)S(1)} %shard_map.121._.refs_0_.refs_3_), channel_id=1, source_target_pairs={{0,2},{1,3},{2,0},{3,1},{4,6},{5,7},{6,4},{7,5},{8,10},{9,11},{10,... | collective-permute-start | bytes 393224 | tf_op jit(solution)/shard_map/ppermute | solution.py:219
  10.6 0.0 copy-start.4
  10.6 0.7 %shard_map.122.refs_6_.refs_8_ = bf16[256,4096]{1,0:T(8,128)(2,1)S(1)} custom-call(bf16[256,4096]{1,0:T(8,128)(2,1)S(1)} %bitcast.16, bf16[16,256]{1,0:T(8,128)(2,1)S(1)} %bitcast.19, bf16[16,4096]{1,0:T(8,128)(2,1)S(1)} %bitcast.17, bf16[16,4096]{1,0:T(8,128)(2,1)S(1)} %shard_map.121._.refs_0_.refs_3_), custom_call_target="tpu_custom_call" | custom-call | bytes 1 | tf_op jit(solution)/shard_map/pallas_call | solution.py:40
  11.3 0.0 collective-permute-done.2.refs_3_
  11.3 1.3 %collective-permute-start.7 = (bf16[16,4096]{1,0:T(8,128)(2,1)S(1)}, bf16[16,4096]{1,0:T(8,128)(2,1)S(1)}, u32[]{:S(2)}, u32[]{:S(2)}) collective-permute-start(bf16[16,4096]{1,0:T(8,128)(2,1)S(1)} %shard_map.121._.refs_0_.refs_3_), channel_id=1, source_target_pairs={{0,1},{1,0},{2,3},{3,2},{4,5},{5,4},{6,7},{7,6},{8,9},{9,8},{10,11... | collective-permute-start | bytes 393224 | tf_op jit(solution)/shard_map/ppermute | solution.py:219
  12.6 1.5 %collective-permute-done.1.refs_2_ = bf16[16,4096]{1,0:T(8,128)(2,1)S(1)} collective-permute-done((bf16[16,4096]{1,0:T(8,128)(2,1)S(1)}, bf16[16,4096]{1,0:T(8,128)(2,1)S(1)}, u32[]{:S(2)}, u32[]{:S(2)}) %collective-permute-start.1) | collective-permute-done | bytes 131104 | tf_op jit(solution)/shard_map/ppermute | solution.py:219
  14.1 1.9 %shard_map.123 = (bf16[16,4096]{1,0:T(8,128)(2,1)S(1)}, bf16[16,4224]{1,0:T(8,128)(2,1)S(1)}, bf16[16,4224]{1,0:T(8,128)(2,1)S(1)}, bf16[16,4224]{1,0:T(8,128)(2...) custom-call(bf16[16,4096]{1,0:T(8,128)(2,1)S(1)} %get-tuple-element., ...), custom_call_target="tpu_custom_call" | custom-call | flops 4026531840 | bytes 7526400 | tf_op jit(solution)/shard_map/pallas_call | solution.py:40
  15.9 2.4 %collective-permute-start.3 = (bf16[16,4224]{1,0:T(8,128)(2,1)S(1)}, bf16[16,4224]{1,0:T(8,128)(2,1)S(1)}, u32[]{:S(2)}, u32[]{:S(2)}) collective-permute-start(bf16[16,4224]{1,0:T(8,128)(2,1)S(1)} %get-tuple-element.33), channel_id=1, source_target_pairs={{0,3},{1,2},{2,1},{3,0},{4,7},{5,6},{6,5},{7,4},{8,11},{9,10},{10,... | collective-permute-start | bytes 405512 | tf_op jit(solution)/shard_map/ppermute | solution.py:219
  18.4 0.6 %collective-permute-start.4 = (bf16[16,4224]{1,0:T(8,128)(2,1)S(1)}, bf16[16,4224]{1,0:T(8,128)(2,1)S(1)}, u32[]{:S(2)}, u32[]{:S(2)}) collective-permute-start(bf16[16,4224]{1,0:T(8,128)(2,1)S(1)} %get-tuple-element.34), channel_id=1, source_target_pairs={{0,1},{1,0},{2,3},{3,2},{4,5},{5,4},{6,7},{7,6},{8,9},{9,8},{10,11... | collective-permute-start | bytes 405512 | tf_op jit(solution)/shard_map/ppermute | solution.py:219
  18.9 0.6 %collective-permute-start.5 = (bf16[16,4224]{1,0:T(8,128)(2,1)S(1)}, bf16[16,4224]{1,0:T(8,128)(2,1)S(1)}, u32[]{:S(2)}, u32[]{:S(2)}) collective-permute-start(bf16[16,4224]{1,0:T(8,128)(2,1)S(1)} %get-tuple-element.35), channel_id=1, source_target_pairs={{0,2},{1,3},{2,0},{3,1},{4,6},{5,7},{6,4},{7,5},{8,10},{9,11},{10,... | collective-permute-start | bytes 405512 | tf_op jit(solution)/shard_map/ppermute | solution.py:219
  19.5 2.5 %shard_map.126 = (bf16[16,4096]{1,0:T(8,128)(2,1)S(1)}, bf16[16,4096]{1,0:T(8,128)(2,1)S(1)}, bf16[16,4096]{1,0:T(8,128)(2,1)S(1)}, bf16[16,4096]{1,0:T(8,128)(2,1)S(1)}) custom-call(bf16[16,4096]{1,0:T(8,128)(2,1)S(1)} %shard_map.121._.refs_0_.refs_3_, bf16[16,4096]{1,0:T(8,128)(2,1)S(1)} %collective-permute-done.7.refs_1_.refs_4_, ...), custom_call_target="tpu_custom_call" | custom-call | flops 4026531840 | bytes 7471104 | tf_op jit(solution)/shard_map/pallas_call | solution.py:40
  22.0 2.4 %collective-permute-start.10 = (bf16[16,4096]{1,0:T(8,128)(2,1)S(1)}, bf16[16,4096]{1,0:T(8,128)(2,1)S(1)}, u32[]{:S(2)}, u32[]{:S(2)}) collective-permute-start(bf16[16,4096]{1,0:T(8,128)(2,1)S(1)} %get-tuple-element.39), channel_id=1, source_target_pairs={{0,3},{1,2},{2,1},{3,0},{4,7},{5,6},{6,5},{7,4},{8,11},{9,10},{10,... | collective-permute-start | bytes 393224 | tf_op jit(solution)/shard_map/ppermute | solution.py:219
  24.4 0.6 %collective-permute-start.11 = (bf16[16,4096]{1,0:T(8,128)(2,1)S(1)}, bf16[16,4096]{1,0:T(8,128)(2,1)S(1)}, u32[]{:S(2)}, u32[]{:S(2)}) collective-permute-start(bf16[16,4096]{1,0:T(8,128)(2,1)S(1)} %get-tuple-element.40), channel_id=1, source_target_pairs={{0,1},{1,0},{2,3},{3,2},{4,5},{5,4},{6,7},{7,6},{8,9},{9,8},{10,11... | collective-permute-start | bytes 393224 | tf_op jit(solution)/shard_map/ppermute | solution.py:219
  25.0 0.6 %collective-permute-start.12 = (bf16[16,4096]{1,0:T(8,128)(2,1)S(1)}, bf16[16,4096]{1,0:T(8,128)(2,1)S(1)}, u32[]{:S(2)}, u32[]{:S(2)}) collective-permute-start(bf16[16,4096]{1,0:T(8,128)(2,1)S(1)} %get-tuple-element.41), channel_id=1, source_target_pairs={{0,2},{1,3},{2,0},{3,1},{4,6},{5,7},{6,4},{7,5},{8,10},{9,11},{10,... | collective-permute-start | bytes 393224 | tf_op jit(solution)/shard_map/ppermute | solution.py:219
  25.6 1.0 %shard_map.127 = f32[16,256]{1,0:T(8,128)} custom-call(bf16[16,4096]{1,0:T(8,128)(2,1)S(1)} %shard_map.121._.refs_0_.refs_3_, bf16[16,4096]{1,0:T(8,128)(2,1)S(1)} %collective-permute-done.7.refs_1_.refs_4_, bf16[16,4096]{1,0:T(8,128)(2,1)S(1)} %collective-permute-done.8.refs_2_.refs_5_, bf16[16,4096]{1,0:T(8,128)(2,1)S(1)} %collective-permute-done.9.refs_3_.refs_6_, ...), custom_call_target="tpu_custom_call" | custom-call | flops 838860800 | bytes 704512 | tf_op jit(solution)/shard_map/pallas_call | solution.py:40
  26.6 0.1 shard_map.124
  26.7 0.1 collective-permute-start.6
  26.8 0.9 %shard_map.128 = f32[1,1,16,1024]{3,2,1,0:T(8,128)} custom-call(bf16[16,64]{1,0:T(8,128)(2,1)S(1)} %get-tuple-element.45.latent_ref, bf16[16,4224]{1,0:T(8,128)(2,1)S(1)} %collective-permute-done.3.refs_1_.refs_0_, bf16[16,4224]{1,0:T(8,128)(2,1)S(1)} %collective-permute-done.4.refs_2_.refs_1_, bf16[16,4224]{1,0:T(8,128)(2,1)S(1)} %collective-permute-done.5.refs_3_.refs_2_, ...), custom_call_target="tpu_custom_call" | custom-call | flops 838860800 | bytes 997376 | tf_op jit(solution)/shard_map/pallas_call | solution.py:40
  27.6 1.8 %collective-permute-done.10.refs_1_ = bf16[16,4096]{1,0:T(8,128)(2,1)S(1)} collective-permute-done((bf16[16,4096]{1,0:T(8,128)(2,1)S(1)}, bf16[16,4096]{1,0:T(8,128)(2,1)S(1)}, u32[]{:S(2)}, u32[]{:S(2)}) %collective-permute-start.10) | collective-permute-done | bytes 131104 | tf_op jit(solution)/shard_map/ppermute | solution.py:219
  29.4 1.3 %collective-permute-done.11.refs_2_ = bf16[16,4096]{1,0:T(8,128)(2,1)S(1)} collective-permute-done((bf16[16,4096]{1,0:T(8,128)(2,1)S(1)}, bf16[16,4096]{1,0:T(8,128)(2,1)S(1)}, u32[]{:S(2)}, u32[]{:S(2)}) %collective-permute-start.11) | collective-permute-done | bytes 131104 | tf_op jit(solution)/shard_map/ppermute | solution.py:219
  30.7 0.1 collective-permute-done.12.refs_3_
  30.8 0.1 shard_map.129
  30.9 2.3 %collective-permute-start.13 = (bf16[16,4224]{1,0:T(8,128)(2,1)S(1)}, bf16[16,4224]{1,0:T(8,128)(2,1)S(1)}, u32[]{:S(2)}, u32[]{:S(2)}) collective-permute-start(bf16[16,4224]{1,0:T(8,128)(2,1)S(1)} %shard_map.129), channel_id=1, source_target_pairs={{0,28},{1,29},{2,30},{3,31},{4,0},{5,1},{6,2},{7,3},{8,4},{9,5},{1... | collective-permute-start | bytes 405512 | tf_op jit(solution)/shard_map/ppermute | solution.py:219
  33.2 1.2 %shard_map.125 = bf16[1,128,4096]{2,1,0:T(8,128)(2,1)} custom-call(bf16[16,4224]{1,0:T(8,128)(2,1)S(1)} %collective-permute-done.6.message_ref), custom_call_target="tpu_custom_call" | custom-call | flops 16777216 | bytes 1183744 | tf_op jit(solution)/shard_map/pallas_call | solution.py:40
  34.5 1.3 %collective-permute-done.13.message_ref = bf16[16,4224]{1,0:T(8,128)(2,1)S(1)} collective-permute-done((bf16[16,4224]{1,0:T(8,128)(2,1)S(1)}, bf16[16,4224]{1,0:T(8,128)(2,1)S(1)}, u32[]{:S(2)}, u32[]{:S(2)}) %collective-permute-start.13) | collective-permute-done | bytes 135200 | tf_op jit(solution)/shard_map/ppermute | solution.py:219
  35.8 1.2 %shard_map.130 = bf16[1,128,4096]{2,1,0:T(8,128)(2,1)} custom-call(bf16[16,4224]{1,0:T(8,128)(2,1)S(1)} %collective-permute-done.13.message_ref), custom_call_target="tpu_custom_call" | custom-call | flops 16777216 | bytes 1183744 | tf_op jit(solution)/shard_map/pallas_call | solution.py:40
  (17 shorter events, 0.0 us)
Async XLA Ops:
  2.3 9.0 %collective-permute-start.2 = (bf16[16,4096]{1,0:T(8,128)(2,1)S(1)}, bf16[16,4096]{1,0:T(8,128)(2,1)S(1)}, u32[]{:S(2)}, u32[]{:S(2)}) collective-permute-start(bf16[16,4096]{1,0:T(8,128)(2,1)S(1)} %get-tuple-element.30.refs_0_), channel_id=1, source_target_pairs={{0,3},{1,2},{2,1},{3,0},{4,7},{5,6},{6,5},{7,4},{8,11},{9,10},{10,... | collective-permute-start | bytes 393224 | tf_op jit(solution)/shard_map/ppermute | solution.py:219
  6.3 7.8 %collective-permute-start.1 = (bf16[16,4096]{1,0:T(8,128)(2,1)S(1)}, bf16[16,4096]{1,0:T(8,128)(2,1)S(1)}, u32[]{:S(2)}, u32[]{:S(2)}) collective-permute-start(bf16[16,4096]{1,0:T(8,128)(2,1)S(1)} %get-tuple-element.30.refs_0_), channel_id=1, source_target_pairs={{0,2},{1,3},{2,0},{3,1},{4,6},{5,7},{6,4},{7,5},{8,10},{9,11},{10,... | collective-permute-start | bytes 393224 | tf_op jit(solution)/shard_map/ppermute | solution.py:219
  6.8 7.3 %collective-permute-start = (bf16[16,4096]{1,0:T(8,128)(2,1)S(1)}, bf16[16,4096]{1,0:T(8,128)(2,1)S(1)}, u32[]{:S(2)}, u32[]{:S(2)}) collective-permute-start(bf16[16,4096]{1,0:T(8,128)(2,1)S(1)} %get-tuple-element.30.refs_0_), channel_id=1, source_target_pairs={{0,1},{1,0},{2,3},{3,2},{4,5},{5,4},{6,7},{7,6},{8,9},{9,8},{10,11... | collective-permute-start | bytes 393224 | tf_op jit(solution)/shard_map/ppermute | solution.py:219
  6.9 3.7 %copy-start = (bf16[1,256,4096]{2,1,0:T(8,128)(2,1)S(1)}, bf16[1,256,4096]{2,1,0:T(8,128)(2,1)}, u32[]{:S(2)}) copy-start(bf16[1,256,4096]{2,1,0:T(8,128)(2,1)} %param.14) | copy-start | bytes 6291460
  6.9 3.7 %copy-start.1 = (bf16[1,1,16,4096]{3,2,1,0:T(8,128)(2,1)S(1)}, bf16[1,1,16,4096]{3,2,1,0:T(8,128)(2,1)}, u32[]{:S(2)}) copy-start(bf16[1,1,16,4096]{3,2,1,0:T(8,128)(2,1)} %param.16) | copy-start | bytes 393220
  6.9 3.7 %copy-start.2 = (bf16[1,256,16]{1,2,0:T(8,128)(2,1)S(1)}, bf16[1,256,16]{1,2,0:T(8,128)(2,1)}, u32[]{:S(2)}) copy-start(bf16[1,256,16]{1,2,0:T(8,128)(2,1)} %param.15) | copy-start | bytes 24580
  7.2 11.8 %collective-permute-start.9 = (bf16[16,4096]{1,0:T(8,128)(2,1)S(1)}, bf16[16,4096]{1,0:T(8,128)(2,1)S(1)}, u32[]{:S(2)}, u32[]{:S(2)}) collective-permute-start(bf16[16,4096]{1,0:T(8,128)(2,1)S(1)} %shard_map.121._.refs_0_.refs_3_), channel_id=1, source_target_pairs={{0,3},{1,2},{2,1},{3,0},{4,7},{5,6},{6,5},{7,4},{8,11},{9,10},{10,... | collective-permute-start | bytes 393224 | tf_op jit(solution)/shard_map/ppermute | solution.py:219
  10.1 9.4 %collective-permute-start.8 = (bf16[16,4096]{1,0:T(8,128)(2,1)S(1)}, bf16[16,4096]{1,0:T(8,128)(2,1)S(1)}, u32[]{:S(2)}, u32[]{:S(2)}) collective-permute-start(bf16[16,4096]{1,0:T(8,128)(2,1)S(1)} %shard_map.121._.refs_0_.refs_3_), channel_id=1, source_target_pairs={{0,2},{1,3},{2,0},{3,1},{4,6},{5,7},{6,4},{7,5},{8,10},{9,11},{10,... | collective-permute-start | bytes 393224 | tf_op jit(solution)/shard_map/ppermute | solution.py:219
  10.6 3.5 %copy-start.3 = (bf16[1,256,4096]{2,1,0:T(8,128)(2,1)S(1)}, bf16[1,256,4096]{2,1,0:T(8,128)(2,1)}, u32[]{:S(2)}) copy-start(bf16[1,256,4096]{2,1,0:T(8,128)(2,1)} %param.12) | copy-start | bytes 6291460
  10.6 3.5 %copy-start.4 = (bf16[1,256,4096]{2,1,0:T(8,128)(2,1)S(1)}, bf16[1,256,4096]{2,1,0:T(8,128)(2,1)}, u32[]{:S(2)}) copy-start(bf16[1,256,4096]{2,1,0:T(8,128)(2,1)} %param.13) | copy-start | bytes 6291460
  11.3 8.2 %collective-permute-start.7 = (bf16[16,4096]{1,0:T(8,128)(2,1)S(1)}, bf16[16,4096]{1,0:T(8,128)(2,1)S(1)}, u32[]{:S(2)}, u32[]{:S(2)}) collective-permute-start(bf16[16,4096]{1,0:T(8,128)(2,1)S(1)} %shard_map.121._.refs_0_.refs_3_), channel_id=1, source_target_pairs={{0,1},{1,0},{2,3},{3,2},{4,5},{5,4},{6,7},{7,6},{8,9},{9,8},{10,11... | collective-permute-start | bytes 393224 | tf_op jit(solution)/shard_map/ppermute | solution.py:219
  15.9 9.0 %collective-permute-start.3 = (bf16[16,4224]{1,0:T(8,128)(2,1)S(1)}, bf16[16,4224]{1,0:T(8,128)(2,1)S(1)}, u32[]{:S(2)}, u32[]{:S(2)}) collective-permute-start(bf16[16,4224]{1,0:T(8,128)(2,1)S(1)} %get-tuple-element.33), channel_id=1, source_target_pairs={{0,3},{1,2},{2,1},{3,0},{4,7},{5,6},{6,5},{7,4},{8,11},{9,10},{10,... | collective-permute-start | bytes 405512 | tf_op jit(solution)/shard_map/ppermute | solution.py:219
  18.4 8.2 %collective-permute-start.4 = (bf16[16,4224]{1,0:T(8,128)(2,1)S(1)}, bf16[16,4224]{1,0:T(8,128)(2,1)S(1)}, u32[]{:S(2)}, u32[]{:S(2)}) collective-permute-start(bf16[16,4224]{1,0:T(8,128)(2,1)S(1)} %get-tuple-element.34), channel_id=1, source_target_pairs={{0,1},{1,0},{2,3},{3,2},{4,5},{5,4},{6,7},{7,6},{8,9},{9,8},{10,11... | collective-permute-start | bytes 405512 | tf_op jit(solution)/shard_map/ppermute | solution.py:219
  18.9 7.7 %collective-permute-start.5 = (bf16[16,4224]{1,0:T(8,128)(2,1)S(1)}, bf16[16,4224]{1,0:T(8,128)(2,1)S(1)}, u32[]{:S(2)}, u32[]{:S(2)}) collective-permute-start(bf16[16,4224]{1,0:T(8,128)(2,1)S(1)} %get-tuple-element.35), channel_id=1, source_target_pairs={{0,2},{1,3},{2,0},{3,1},{4,6},{5,7},{6,4},{7,5},{8,10},{9,11},{10,... | collective-permute-start | bytes 405512 | tf_op jit(solution)/shard_map/ppermute | solution.py:219
  22.0 7.4 %collective-permute-start.10 = (bf16[16,4096]{1,0:T(8,128)(2,1)S(1)}, bf16[16,4096]{1,0:T(8,128)(2,1)S(1)}, u32[]{:S(2)}, u32[]{:S(2)}) collective-permute-start(bf16[16,4096]{1,0:T(8,128)(2,1)S(1)} %get-tuple-element.39), channel_id=1, source_target_pairs={{0,3},{1,2},{2,1},{3,0},{4,7},{5,6},{6,5},{7,4},{8,11},{9,10},{10,... | collective-permute-start | bytes 393224 | tf_op jit(solution)/shard_map/ppermute | solution.py:219
  24.4 6.3 %collective-permute-start.11 = (bf16[16,4096]{1,0:T(8,128)(2,1)S(1)}, bf16[16,4096]{1,0:T(8,128)(2,1)S(1)}, u32[]{:S(2)}, u32[]{:S(2)}) collective-permute-start(bf16[16,4096]{1,0:T(8,128)(2,1)S(1)} %get-tuple-element.40), channel_id=1, source_target_pairs={{0,1},{1,0},{2,3},{3,2},{4,5},{5,4},{6,7},{7,6},{8,9},{9,8},{10,11... | collective-permute-start | bytes 393224 | tf_op jit(solution)/shard_map/ppermute | solution.py:219
  25.0 5.8 %collective-permute-start.12 = (bf16[16,4096]{1,0:T(8,128)(2,1)S(1)}, bf16[16,4096]{1,0:T(8,128)(2,1)S(1)}, u32[]{:S(2)}, u32[]{:S(2)}) collective-permute-start(bf16[16,4096]{1,0:T(8,128)(2,1)S(1)} %get-tuple-element.41), channel_id=1, source_target_pairs={{0,2},{1,3},{2,0},{3,1},{4,6},{5,7},{6,4},{7,5},{8,10},{9,11},{10,... | collective-permute-start | bytes 393224 | tf_op jit(solution)/shard_map/ppermute | solution.py:219
  26.7 6.5 %collective-permute-start.6 = (bf16[16,4224]{1,0:T(8,128)(2,1)S(1)}, bf16[16,4224]{1,0:T(8,128)(2,1)S(1)}, u32[]{:S(2)}, u32[]{:S(2)}) collective-permute-start(bf16[16,4224]{1,0:T(8,128)(2,1)S(1)} %shard_map.124), channel_id=1, source_target_pairs={{0,4},{1,5},{2,6},{3,7},{4,8},{5,9},{6,10},{7,11},{8,12},{9,13},{1... | collective-permute-start | bytes 405512 | tf_op jit(solution)/shard_map/ppermute | solution.py:219
  30.9 4.9 %collective-permute-start.13 = (bf16[16,4224]{1,0:T(8,128)(2,1)S(1)}, bf16[16,4224]{1,0:T(8,128)(2,1)S(1)}, u32[]{:S(2)}, u32[]{:S(2)}) collective-permute-start(bf16[16,4224]{1,0:T(8,128)(2,1)S(1)} %shard_map.129), channel_id=1, source_target_pairs={{0,28},{1,29},{2,30},{3,31},{4,0},{5,1},{6,2},{7,3},{8,4},{9,5},{1... | collective-permute-start | bytes 405512 | tf_op jit(solution)/shard_map/ppermute | solution.py:219

commit v12 on v10

--- a/solution.py
+++ b/solution.py
@@ -109,10 +109,9 @@
 
 def forward(*refs):
     x_refs, (gate_ref, up_ref, down_ref, a_ref) = refs[:SPLIT], refs[SPLIT:SPLIT + 4]
-    out_refs = refs[SPLIT + 4:2 * SPLIT + 4]
-    pre_gate_ref, pre_up_ref, hidden_ref, latent_ref = refs[2 * SPLIT + 4:]
+    keep_ref, send_ref, pre_gate_ref, pre_up_ref, hidden_ref, latent_ref = refs[SPLIT + 4:]
     rows = jnp.concatenate([r[...] for r in x_refs], axis=0)
-    height, width = x_refs[0].shape
+    height = x_refs[0].shape[0]
     pre_gate = f32dot(rows, gate_ref[...], LAST)
     pre_up = f32dot(rows, up_ref[...], LAST)
     pre_gate_ref[...] = pre_gate
@@ -120,25 +119,33 @@
     hidden = (pre_gate * jax.nn.sigmoid(pre_gate) * pre_up).astype(jnp.bfloat16)
     hidden_ref[...] = hidden
     result = f32dot(hidden, down_ref[...]).astype(jnp.bfloat16)
-    for k, ref in enumerate(out_refs):
-        ref[:, :width] = result[k * height:(k + 1) * height]
-    latent = f32dot(a_ref[...], hidden, LAST).astype(jnp.bfloat16)
-    latent_ref[...] = latent
-    if out_refs[1].shape[1] > width:
-        rank, count = latent.shape
-        tail = jnp.concatenate(
-            [latent, jnp.zeros((rank, out_refs[1].shape[1] - width - count), jnp.bfloat16)], axis=1
-        )
-        for ref in out_refs[1:]:
-            ref[:, width:] = tail
+    for i in range(2):
+        part = slice(i * height, (i + 1) * height)
+        keep_ref[part] = result[2 * i * height:(2 * i + 1) * height]
+        send_ref[part] = result[(2 * i + 1) * height:(2 * i + 2) * height]
+    latent_ref[...] = f32dot(a_ref[...], hidden, LAST).astype(jnp.bfloat16)
+
+
+def add_pairs(place_ref, keep_ref, other_ref, own_ref, cross_ref):
+    height, width = keep_ref.shape[0] // 2, keep_ref.shape[1]
+    total = keep_ref[...].astype(jnp.float32) + other_ref[...].astype(jnp.float32)
+    total = total.astype(jnp.bfloat16)
+    own_ref[:, :width] = total[:height]
+    cross_ref[:, :width] = total[height:]
+    cross_ref[:, width:] = jnp.zeros((height, cross_ref.shape[1] - width), jnp.bfloat16)
+    place = place_ref[...]
+    tokens = place.shape[1]
+    high = place.astype(jnp.bfloat16)
+    own_ref[:, width:width + tokens] = high
+    own_ref[:, width + tokens:] = (place - high.astype(jnp.float32)).astype(jnp.bfloat16)
 
 
 def backward(*refs):
     g_refs = refs[:SPLIT]
-    pre_gate_ref, pre_up_ref, gate_ref, up_ref, down_ref = refs[SPLIT:SPLIT + 5]
-    out_refs = refs[SPLIT + 5:]
+    latent_ref, pre_gate_ref, pre_up_ref, gate_ref, up_ref, down_ref = refs[SPLIT:SPLIT + 6]
+    out_refs = refs[SPLIT + 6:]
     rows = jnp.concatenate([r[...] for r in g_refs], axis=0)
-    height = g_refs[0].shape[0]
+    height, width = g_refs[0].shape
     grad_hidden = f32dot(rows, down_ref[...], LAST)
     pre_gate = pre_gate_ref[...]
     g = jax.nn.sigmoid(pre_gate)
@@ -148,19 +155,22 @@
     result = result + f32dot(grad_up.astype(jnp.bfloat16), up_ref[...])
     result = result.astype(jnp.bfloat16)
     for k, ref in enumerate(out_refs):
-        ref[...] = result[k * height:(k + 1) * height]
-
-
-def combine(gated, place_ref, *refs):
+        ref[:, :width] = result[k * height:(k + 1) * height]
+    spare = out_refs[1].shape[1] - width
+    if spare:
+        latent = latent_ref[...]
+        rest = jnp.zeros((latent.shape[0], spare - latent.shape[1]), jnp.bfloat16)
+        for ref in out_refs[1:]:
+            ref[:, width:] = jnp.concatenate([latent, rest], axis=1)
+
+
+def combine(place_ref, *refs):
     *part_refs, out_ref = refs
-    place = place_ref[...]
     width = part_refs[0].shape[1]
     rows = sum(r[:, :width].astype(jnp.float32) for r in part_refs)
-    if gated:
-        rows = rows * jnp.sum(place, axis=1, keepdims=True)
     out_ref[:, :width] = rows.astype(jnp.bfloat16)
     if out_ref.shape[1] > width:
-        out_ref[:, width:] = picks(place)
+        out_ref[:, width:] = picks(place_ref[...])
 
 
 def down_map_grad(*refs):
@@ -183,14 +193,23 @@
     out_ref[0, 0] = LOWRANK_SCALE * total
 
 
-def expand(message_ref, out_hbm, out_ref, sems):
-    width = out_ref.shape[1]
-    pick = message_ref[:, width:]
+def expand(gated, *refs):
+    *part_refs, out_hbm, out_ref, sems = refs
+    tokens, width = out_ref.shape
+    high = part_refs[0][:, width:width + tokens]
+    pick = picks(high)
+    if gated:
+        low = part_refs[0][:, width + tokens:]
+        gate = jnp.sum(high.astype(jnp.float32) + low.astype(jnp.float32), axis=1, keepdims=True)
     span = width // CHUNKS
     copies = []
     for c in range(CHUNKS):
         part = slice(c * span, (c + 1) * span)
-        out_ref[:, part] = f32dot(pick, message_ref[:, part], FIRST).astype(jnp.bfloat16)
+        rows = part_refs[0][:, part]
+        if gated:
+            rows = sum(r[:, part].astype(jnp.float32) for r in part_refs) * gate
+            rows = rows.astype(jnp.bfloat16)
+        out_ref[:, part] = f32dot(pick, rows, FIRST).astype(jnp.bfloat16)
         columns = pl.ds(c * span, span)
         copy = pltpu.make_async_copy(
             out_ref.at[:, columns], out_hbm.at[0, :, columns], sems.at[c]
@@ -292,37 +311,53 @@
         moved=1,
     )
 
-    wide = width + tokens
-    *out_blocks, pre_gate, pre_up, hidden, latent = call(
+    keep, send, pre_gate, pre_up, hidden, latent = call(
         forward,
-        [sds(slots, width)]
-        + [sds(slots, wide if flight == 1 else width)] * (SPLIT - 1)
+        [sds(2 * slots, width)] * 2
         + [sds(rows, units, dtype=jnp.float32)] * 2
         + [sds(rows, units), sds(rank, rows)],
         (*x_blocks, gate_near, up_near, down_near, a_near),
         flops=60 * rows * units * width,
     )
-    out_parts = [out_blocks[0]] + [shifted(out_blocks[k], 0, k) for k in DIAGONAL_FIRST]
+    other = shifted(send, 0, 1)
+    wide = width + tokens
     grad_blocks = call(
         backward,
-        [sds(slots, width)] * SPLIT,
-        (*g_blocks, pre_gate, pre_up, gate_near, up_near, down_near),
+        [sds(slots, width)] + [sds(slots, wide if flight == 1 else width)] * (SPLIT - 1),
+        (*g_blocks, latent, pre_gate, pre_up, gate_near, up_near, down_near),
         flops=60 * rows * units * width,
     )
     grad_parts = [grad_blocks[0]] + [shifted(grad_blocks[k], 0, k) for k in DIAGONAL_FIRST]
 
-    hidden, latent, _ = lax.optimization_barrier((hidden, latent, grad_blocks[0]))
+    own, cross = call(
+        add_pairs,
+        [sds(slots, wide + tokens)] * 2,
+        (place, keep, other),
+    )
+    out_parts = [shifted(own, 1, 0), shifted(cross, 1, 2)]
+
+    hidden, _ = lax.optimization_barrier((hidden, grad_blocks[1]))
     (a_grad,) = call(
         down_map_grad,
         [sds(rank, units, dtype=jnp.float32)],
         (*g_blocks, hidden, b_near),
         flops=200 * rows * rank * width,
     )
+    grad_parts, a_grad = lax.optimization_barrier((grad_parts, a_grad))
+
+    def merged(parts, columns):
+        return call(combine, [sds(slots, columns)], (place, *parts))[0]
+
+    grad_message = grad_parts
+    if flight > 1:
+        grad_message = [between_groups(merged(grad_parts, width), flight)]
+    grad_message = shifted(merged(grad_message, wide), -1, 0)
+
     if flight == 1:
         (b_grad,) = call(
             up_map_grad,
             [sds(1, 1, rank, width // SPLIT, dtype=jnp.float32)],
-            (latent, *out_parts[1:], *g_blocks),
+            (latent, *grad_parts[1:], *g_blocks),
             flops=200 * rows * rank * width,
         )
     else:
@@ -331,30 +366,23 @@
         spread = jnp.where(mine[:, None, None], part[None], 0.0)
         b_grad = lax.psum_scatter(spread, "expert", scatter_dimension=2, tiled=True)[None]
 
-    def merged(parts, gated, columns):
-        return call(functools.partial(combine, gated), [sds(slots, columns)], (place, *parts))[0]
-
-    def reduced(parts, gated):
-        if flight > 1:
-            parts = [between_groups(merged(parts, False, width), flight)]
-        return merged(parts, gated, wide)
-
-    def expanded(message):
+    def expanded(parts, gated):
         return call(
-            expand,
+            functools.partial(expand, gated),
             [sds(1, tokens, width)],
-            (message,),
+            tuple(parts),
             far_outs=True,
             scratch=[pltpu.VMEM((tokens, width), jnp.bfloat16), dma((CHUNKS,))],
             flops=2 * slots * tokens * width,
         )[0]
 
-    out_message = shifted(reduced(out_parts, True), 1, 0)
-    grad_parts, a_grad, b_grad = lax.optimization_barrier((grad_parts, a_grad, b_grad))
-    grad_message = shifted(reduced(grad_parts, False), -1, 0)
-    next_input = expanded(out_message)
-    next_input, grad_message = lax.optimization_barrier((next_input, grad_message))
-    prev_grad = expanded(grad_message)
+    if flight > 1:
+        total = sum(p[:, :width].astype(jnp.float32) for p in out_parts).astype(jnp.bfloat16)
+        total = between_groups(total, flight)
+        out_parts = [jnp.concatenate([total, out_parts[0][:, width:]], axis=1)]
+    next_input = expanded(out_parts, True)
+    next_input, b_grad, grad_message = lax.optimization_barrier((next_input, b_grad, grad_message))
+    prev_grad = expanded([grad_message], False)
     return next_input, prev_grad, jnp.swapaxes(a_grad, 0, 1)[None], b_grad
 
 

time: 37.2 us -> 38.3 us (1.030)
  starting transfers between devices: 18.8 us -> 20.8 us
  waiting for transfers between devices: 5.99 us -> 4.84 us
    ppermute x14 -> x13, starting transfers between devices: 18.8 us -> 20.8 us  [shifted(): return lax.ppermute(block, ('section', 'expert'), route)]
    ppermute x14 -> x13, waiting for transfers between devices: 5.99 us -> 4.84 us  [shifted(): return lax.ppermute(block, ('section', 'expert'), route)]
  transfers between devices with their start and end apart: 14 -> 13, of which waited for: 5 -> 6; matrix products, arithmetic and copies ran while one was open for 0% -> 0% of each run, Pallas kernels for 23% -> 23%
where the time goes in v12:
time: 38.3 us; the launch traced here: 38 us
  starting transfers between devices  20.8 us (54%)
  Pallas kernels  11.5 us (30%)
  waiting for transfers between devices  4.84 us (13%)
  between operations  0.72 us (2%)
    ppermute x13, starting transfers between devices, shifted(): return lax.ppermute(block, ('section', 'expert'), route)  20.8 us
    pallas_call x11, Pallas kernels, call(): pl.pallas_call(body, out_shape=outs, in_specs=[NEAR] * len(args) + [FAR]...  11.5 us
    ppermute x13, waiting for transfers between devices, shifted(): return lax.ppermute(block, ('section', 'expert'), route)  4.84 us
  transfers between devices with their start and end apart: 13, of which 6 were waited for; matrix products, arithmetic and copies ran while one was open for 0% of the time, Pallas kernels for 23%

profile of v12, /device:TPU:0, one launch (start us, length us, event | category | flops | bytes accessed | tf_op | source)
XLA Modules:
  0.0 38.0 jit_solution(15127006956194716630)
XLA Ops:
  0.6 1.7 %shard_map.120 = (bf16[16,4096]{1,0:T(8,128)(2,1)S(1)}, f32[16,128]{1,0:T(8,128)S(1)}, bf16[128,4096]{1,0:T(8,128)(2,1)S(1)}) custom-call(s32[8,128]{1,0:T(8,128)} %bitcast.25, s32[8,128]{1,0:T(8,128)} %bitcast.26, bf16[1,128,4096]{2,1,0:T(8,128)(2,1)} %x_hbm.1, bf16[1,128,4096]{2,1,0:T(8,128)(2,1)} %cot_hbm.1), custom_call_target="tpu_custom_call" | custom-call | flops 16777216 | bytes 3293184 | tf_op jit(solution)/shard_map/pallas_call | solution.py:35
  2.3 4.0 %collective-permute-start.2 = (bf16[16,4096]{1,0:T(8,128)(2,1)S(1)}, bf16[16,4096]{1,0:T(8,128)(2,1)S(1)}, u32[]{:S(2)}, u32[]{:S(2)}) collective-permute-start(bf16[16,4096]{1,0:T(8,128)(2,1)S(1)} %get-tuple-element.29.refs_0_), channel_id=1, source_target_pairs={{0,3},{1,2},{2,1},{3,0},{4,7},{5,6},{6,5},{7,4},{8,11},{9,10},{10,... | collective-permute-start | bytes 393224 | tf_op jit(solution)/shard_map/ppermute | solution.py:230
  6.3 0.5 %collective-permute-start.1 = (bf16[16,4096]{1,0:T(8,128)(2,1)S(1)}, bf16[16,4096]{1,0:T(8,128)(2,1)S(1)}, u32[]{:S(2)}, u32[]{:S(2)}) collective-permute-start(bf16[16,4096]{1,0:T(8,128)(2,1)S(1)} %get-tuple-element.29.refs_0_), channel_id=1, source_target_pairs={{0,2},{1,3},{2,0},{3,1},{4,6},{5,7},{6,4},{7,5},{8,10},{9,11},{10,... | collective-permute-start | bytes 393224 | tf_op jit(solution)/shard_map/ppermute | solution.py:230
  6.8 0.1 collective-permute-start
  6.9 0.2 shard_map.121._.refs_0_.refs_3_
  7.2 2.9 %collective-permute-start.8 = (bf16[16,4096]{1,0:T(8,128)(2,1)S(1)}, bf16[16,4096]{1,0:T(8,128)(2,1)S(1)}, u32[]{:S(2)}, u32[]{:S(2)}) collective-permute-start(bf16[16,4096]{1,0:T(8,128)(2,1)S(1)} %shard_map.121._.refs_0_.refs_3_), channel_id=1, source_target_pairs={{0,3},{1,2},{2,1},{3,0},{4,7},{5,6},{6,5},{7,4},{8,11},{9,10},{10,... | collective-permute-start | bytes 393224 | tf_op jit(solution)/shard_map/ppermute | solution.py:230
  10.1 0.5 %collective-permute-start.7 = (bf16[16,4096]{1,0:T(8,128)(2,1)S(1)}, bf16[16,4096]{1,0:T(8,128)(2,1)S(1)}, u32[]{:S(2)}, u32[]{:S(2)}) collective-permute-start(bf16[16,4096]{1,0:T(8,128)(2,1)S(1)} %shard_map.121._.refs_0_.refs_3_), channel_id=1, source_target_pairs={{0,2},{1,3},{2,0},{3,1},{4,6},{5,7},{6,4},{7,5},{8,10},{9,11},{10,... | collective-permute-start | bytes 393224 | tf_op jit(solution)/shard_map/ppermute | solution.py:230
  10.6 0.0 copy-start.4
  10.6 0.7 %shard_map.122.refs_6_.refs_9_ = bf16[256,4096]{1,0:T(8,128)(2,1)S(1)} custom-call(bf16[256,4096]{1,0:T(8,128)(2,1)S(1)} %bitcast.16, bf16[16,256]{1,0:T(8,128)(2,1)S(1)} %bitcast.19, bf16[16,4096]{1,0:T(8,128)(2,1)S(1)} %bitcast.17, bf16[16,4096]{1,0:T(8,128)(2,1)S(1)} %shard_map.121._.refs_0_.refs_3_), custom_call_target="tpu_custom_call" | custom-call | bytes 1 | tf_op jit(solution)/shard_map/pallas_call | solution.py:35
  11.3 1.3 %collective-permute-start.6 = (bf16[16,4096]{1,0:T(8,128)(2,1)S(1)}, bf16[16,4096]{1,0:T(8,128)(2,1)S(1)}, u32[]{:S(2)}, u32[]{:S(2)}) collective-permute-start(bf16[16,4096]{1,0:T(8,128)(2,1)S(1)} %shard_map.121._.refs_0_.refs_3_), channel_id=1, source_target_pairs={{0,1},{1,0},{2,3},{3,2},{4,5},{5,4},{6,7},{7,6},{8,9},{9,8},{10,11... | collective-permute-start | bytes 393224 | tf_op jit(solution)/shard_map/ppermute | solution.py:230
  12.6 1.5 %collective-permute-done.1.refs_2_ = bf16[16,4096]{1,0:T(8,128)(2,1)S(1)} collective-permute-done((bf16[16,4096]{1,0:T(8,128)(2,1)S(1)}, bf16[16,4096]{1,0:T(8,128)(2,1)S(1)}, u32[]{:S(2)}, u32[]{:S(2)}) %collective-permute-start.1) | collective-permute-done | bytes 131104 | tf_op jit(solution)/shard_map/ppermute | solution.py:230
  14.1 1.8 %shard_map.123 = (bf16[32,4096]{1,0:T(8,128)(2,1)S(1)}, bf16[32,4096]{1,0:T(8,128)(2,1)S(1)}, f32[64,256]{1,0:T(8,128)S(1)}, f32[64,256]{1,0:T(8,128)S(1)}, bf16...) custom-call(bf16[16,4096]{1,0:T(8,128)(2,1)S(1)} %get-tuple-element.29.refs_0_, ...), custom_call_target="tpu_custom_call" | custom-call | flops 4026531840 | bytes 7514112 | tf_op jit(solution)/shard_map/pallas_call | solution.py:35
  15.9 1.5 %collective-permute-start.3 = (bf16[32,4096]{1,0:T(8,128)(2,1)S(1)}, bf16[32,4096]{1,0:T(8,128)(2,1)S(1)}, u32[]{:S(2)}, u32[]{:S(2)}) collective-permute-start(bf16[32,4096]{1,0:T(8,128)(2,1)S(1)} %get-tuple-element.32), channel_id=1, source_target_pairs={{0,1},{1,0},{2,3},{3,2},{4,5},{5,4},{6,7},{7,6},{8,9},{9,8},{10,11... | collective-permute-start | bytes 786440 | tf_op jit(solution)/shard_map/ppermute | solution.py:230
  17.4 0.8 %collective-permute-done.7.refs_2_.refs_5_ = bf16[16,4096]{1,0:T(8,128)(2,1)S(1)} collective-permute-done((bf16[16,4096]{1,0:T(8,128)(2,1)S(1)}, bf16[16,4096]{1,0:T(8,128)(2,1)S(1)}, u32[]{:S(2)}, u32[]{:S(2)}) %collective-permute-start.7) | collective-permute-done | bytes 131104 | tf_op jit(solution)/shard_map/ppermute | solution.py:230
  18.2 0.2 collective-permute-done.6.refs_1_.refs_4_
  18.4 2.5 %shard_map.126 = (bf16[16,4096]{1,0:T(8,128)(2,1)S(1)}, bf16[16,4224]{1,0:T(8,128)(2,1)S(1)}, bf16[16,4224]{1,0:T(8,128)(2,1)S(1)}, bf16[16,4224]{1,0:T(8,128)(2,1)S(1)}) custom-call(bf16[16,4096]{1,0:T(8,128)(2,1)S(1)} %shard_map.121._.refs_0_.refs_3_, bf16[16,4096]{1,0:T(8,128)(2,1)S(1)} %collective-permute-done.6.refs_1_.refs_4_, ...), custom_call_target="tpu_custom_call" | custom-call | flops 4026531840 | bytes 7485440 | tf_op jit(solution)/shard_map/pallas_call | solution.py:35
  20.9 1.7 %collective-permute-start.9 = (bf16[16,4224]{1,0:T(8,128)(2,1)S(1)}, bf16[16,4224]{1,0:T(8,128)(2,1)S(1)}, u32[]{:S(2)}, u32[]{:S(2)}) collective-permute-start(bf16[16,4224]{1,0:T(8,128)(2,1)S(1)} %get-tuple-element.39), channel_id=1, source_target_pairs={{0,3},{1,2},{2,1},{3,0},{4,7},{5,6},{6,5},{7,4},{8,11},{9,10},{10,... | collective-permute-start | bytes 405512 | tf_op jit(solution)/shard_map/ppermute | solution.py:230
  22.7 1.4 %collective-permute-start.11 = (bf16[16,4224]{1,0:T(8,128)(2,1)S(1)}, bf16[16,4224]{1,0:T(8,128)(2,1)S(1)}, u32[]{:S(2)}, u32[]{:S(2)}) collective-permute-start(bf16[16,4224]{1,0:T(8,128)(2,1)S(1)} %get-tuple-element.41), channel_id=1, source_target_pairs={{0,2},{1,3},{2,0},{3,1},{4,6},{5,7},{6,4},{7,5},{8,10},{9,11},{10,... | collective-permute-start | bytes 405512 | tf_op jit(solution)/shard_map/ppermute | solution.py:230
  24.1 0.4 %collective-permute-start.10 = (bf16[16,4224]{1,0:T(8,128)(2,1)S(1)}, bf16[16,4224]{1,0:T(8,128)(2,1)S(1)}, u32[]{:S(2)}, u32[]{:S(2)}) collective-permute-start(bf16[16,4224]{1,0:T(8,128)(2,1)S(1)} %get-tuple-element.40), channel_id=1, source_target_pairs={{0,1},{1,0},{2,3},{3,2},{4,5},{5,4},{6,7},{7,6},{8,9},{9,8},{10,11... | collective-permute-start | bytes 405512 | tf_op jit(solution)/shard_map/ppermute | solution.py:230
  24.5 0.1 shard_map.124
  24.6 0.1 collective-permute-start.4
  24.6 2.7 %collective-permute-start.5 = (bf16[16,4352]{1,0:T(8,128)(2,1)S(1)}, bf16[16,4352]{1,0:T(8,128)(2,1)S(1)}, u32[]{:S(2)}, u32[]{:S(2)}) collective-permute-start(bf16[16,4352]{1,0:T(8,128)(2,1)S(1)} %get-tuple-element.34), channel_id=1, source_target_pairs={{0,6},{1,7},{2,4},{3,5},{4,10},{5,11},{6,8},{7,9},{8,14},{9,15},{1... | collective-permute-start | bytes 417800 | tf_op jit(solution)/shard_map/ppermute | solution.py:230
  27.4 1.0 %shard_map.127 = f32[16,256]{1,0:T(8,128)} custom-call(bf16[16,4096]{1,0:T(8,128)(2,1)S(1)} %shard_map.121._.refs_0_.refs_3_, bf16[16,4096]{1,0:T(8,128)(2,1)S(1)} %collective-permute-done.6.refs_1_.refs_4_, bf16[16,4096]{1,0:T(8,128)(2,1)S(1)} %collective-permute-done.7.refs_2_.refs_5_, bf16[16,4096]{1,0:T(8,128)(2,1)S(1)} %collective-permute-done.8.refs_3_.refs_6_, ...), custom_call_target="tpu_custom_call" | custom-call | flops 838860800 | bytes 704512 | tf_op jit(solution)/shard_map/pallas_call | solution.py:35
  28.4 0.0 collective-permute-done.9.refs_0_.refs_1_
  28.4 1.8 %collective-permute-done.11.refs_2_.refs_3_ = bf16[16,4224]{1,0:T(8,128)(2,1)S(1)} collective-permute-done((bf16[16,4224]{1,0:T(8,128)(2,1)S(1)}, bf16[16,4224]{1,0:T(8,128)(2,1)S(1)}, u32[]{:S(2)}, u32[]{:S(2)}) %collective-permute-start.11) | collective-permute-done | bytes 135200 | tf_op jit(solution)/shard_map/ppermute | solution.py:230
  30.2 0.1 collective-permute-done.10.refs_1_.refs_2_
  30.3 0.1 shard_map.129
  30.4 3.7 %collective-permute-start.12 = (bf16[16,4224]{1,0:T(8,128)(2,1)S(1)}, bf16[16,4224]{1,0:T(8,128)(2,1)S(1)}, u32[]{:S(2)}, u32[]{:S(2)}) collective-permute-start(bf16[16,4224]{1,0:T(8,128)(2,1)S(1)} %shard_map.129), channel_id=1, source_target_pairs={{0,28},{1,29},{2,30},{3,31},{4,0},{5,1},{6,2},{7,3},{8,4},{9,5},{1... | collective-permute-start | bytes 405512 | tf_op jit(solution)/shard_map/ppermute | solution.py:230
  34.1 0.8 %shard_map.128 = f32[1,1,16,1024]{3,2,1,0:T(8,128)} custom-call(bf16[16,64]{1,0:T(8,128)(2,1)S(1)} %get-tuple-element.35.refs_4_.latent_ref, bf16[16,4224]{1,0:T(8,128)(2,1)S(1)} %collective-permute-done.9.refs_0_.refs_1_, bf16[16,4224]{1,0:T(8,128)(2,1)S(1)} %collective-permute-done.10.refs_1_.refs_2_, ...), custom_call_target="tpu_custom_call" | custom-call | flops 838860800 | bytes 997376 | tf_op jit(solution)/shard_map/pallas_call | solution.py:35
  35.0 1.3 %shard_map.125 = bf16[1,128,4096]{2,1,0:T(8,128)(2,1)} custom-call(bf16[16,4352]{1,0:T(8,128)(2,1)S(1)} %collective-permute-done.4.refs_0_, bf16[16,4352]{1,0:T(8,128)(2,1)S(1)} %collective-permute-done.5.refs_1_), custom_call_target="tpu_custom_call" | custom-call | flops 16777216 | bytes 1327104 | tf_op jit(solution)/shard_map/pallas_call | solution.py:35
  36.3 0.4 %collective-permute-done.12.refs_0_ = bf16[16,4224]{1,0:T(8,128)(2,1)S(1)} collective-permute-done((bf16[16,4224]{1,0:T(8,128)(2,1)S(1)}, bf16[16,4224]{1,0:T(8,128)(2,1)S(1)}, u32[]{:S(2)}, u32[]{:S(2)}) %collective-permute-start.12) | collective-permute-done | bytes 135200 | tf_op jit(solution)/shard_map/ppermute | solution.py:230
  36.7 1.3 %shard_map.130 = bf16[1,128,4096]{2,1,0:T(8,128)(2,1)} custom-call(bf16[16,4224]{1,0:T(8,128)(2,1)S(1)} %collective-permute-done.12.refs_0_), custom_call_target="tpu_custom_call" | custom-call | flops 16777216 | bytes 1183744 | tf_op jit(solution)/shard_map/pallas_call | solution.py:35
  (15 shorter events, 0.0 us)
Async XLA Ops:
  2.3 9.0 %collective-permute-start.2 = (bf16[16,4096]{1,0:T(8,128)(2,1)S(1)}, bf16[16,4096]{1,0:T(8,128)(2,1)S(1)}, u32[]{:S(2)}, u32[]{:S(2)}) collective-permute-start(bf16[16,4096]{1,0:T(8,128)(2,1)S(1)} %get-tuple-element.29.refs_0_), channel_id=1, source_target_pairs={{0,3},{1,2},{2,1},{3,0},{4,7},{5,6},{6,5},{7,4},{8,11},{9,10},{10,... | collective-permute-start | bytes 393224 | tf_op jit(solution)/shard_map/ppermute | solution.py:230
  6.3 7.8 %collective-permute-start.1 = (bf16[16,4096]{1,0:T(8,128)(2,1)S(1)}, bf16[16,4096]{1,0:T(8,128)(2,1)S(1)}, u32[]{:S(2)}, u32[]{:S(2)}) collective-permute-start(bf16[16,4096]{1,0:T(8,128)(2,1)S(1)} %get-tuple-element.29.refs_0_), channel_id=1, source_target_pairs={{0,2},{1,3},{2,0},{3,1},{4,6},{5,7},{6,4},{7,5},{8,10},{9,11},{10,... | collective-permute-start | bytes 393224 | tf_op jit(solution)/shard_map/ppermute | solution.py:230
  6.8 7.3 %collective-permute-start = (bf16[16,4096]{1,0:T(8,128)(2,1)S(1)}, bf16[16,4096]{1,0:T(8,128)(2,1)S(1)}, u32[]{:S(2)}, u32[]{:S(2)}) collective-permute-start(bf16[16,4096]{1,0:T(8,128)(2,1)S(1)} %get-tuple-element.29.refs_0_), channel_id=1, source_target_pairs={{0,1},{1,0},{2,3},{3,2},{4,5},{5,4},{6,7},{7,6},{8,9},{9,8},{10,11... | collective-permute-start | bytes 393224 | tf_op jit(solution)/shard_map/ppermute | solution.py:230
  6.9 3.7 %copy-start = (bf16[1,256,4096]{2,1,0:T(8,128)(2,1)S(1)}, bf16[1,256,4096]{2,1,0:T(8,128)(2,1)}, u32[]{:S(2)}) copy-start(bf16[1,256,4096]{2,1,0:T(8,128)(2,1)} %param.14) | copy-start | bytes 6291460
  6.9 3.7 %copy-start.1 = (bf16[1,1,16,4096]{3,2,1,0:T(8,128)(2,1)S(1)}, bf16[1,1,16,4096]{3,2,1,0:T(8,128)(2,1)}, u32[]{:S(2)}) copy-start(bf16[1,1,16,4096]{3,2,1,0:T(8,128)(2,1)} %param.16) | copy-start | bytes 393220
  6.9 3.7 %copy-start.2 = (bf16[1,256,16]{1,2,0:T(8,128)(2,1)S(1)}, bf16[1,256,16]{1,2,0:T(8,128)(2,1)}, u32[]{:S(2)}) copy-start(bf16[1,256,16]{1,2,0:T(8,128)(2,1)} %param.15) | copy-start | bytes 24580
  7.2 10.3 %collective-permute-start.8 = (bf16[16,4096]{1,0:T(8,128)(2,1)S(1)}, bf16[16,4096]{1,0:T(8,128)(2,1)S(1)}, u32[]{:S(2)}, u32[]{:S(2)}) collective-permute-start(bf16[16,4096]{1,0:T(8,128)(2,1)S(1)} %shard_map.121._.refs_0_.refs_3_), channel_id=1, source_target_pairs={{0,3},{1,2},{2,1},{3,0},{4,7},{5,6},{6,5},{7,4},{8,11},{9,10},{10,... | collective-permute-start | bytes 393224 | tf_op jit(solution)/shard_map/ppermute | solution.py:230
  10.1 8.1 %collective-permute-start.7 = (bf16[16,4096]{1,0:T(8,128)(2,1)S(1)}, bf16[16,4096]{1,0:T(8,128)(2,1)S(1)}, u32[]{:S(2)}, u32[]{:S(2)}) collective-permute-start(bf16[16,4096]{1,0:T(8,128)(2,1)S(1)} %shard_map.121._.refs_0_.refs_3_), channel_id=1, source_target_pairs={{0,2},{1,3},{2,0},{3,1},{4,6},{5,7},{6,4},{7,5},{8,10},{9,11},{10,... | collective-permute-start | bytes 393224 | tf_op jit(solution)/shard_map/ppermute | solution.py:230
  10.6 3.5 %copy-start.3 = (bf16[1,256,4096]{2,1,0:T(8,128)(2,1)S(1)}, bf16[1,256,4096]{2,1,0:T(8,128)(2,1)}, u32[]{:S(2)}) copy-start(bf16[1,256,4096]{2,1,0:T(8,128)(2,1)} %param.12) | copy-start | bytes 6291460
  10.6 3.5 %copy-start.4 = (bf16[1,256,4096]{2,1,0:T(8,128)(2,1)S(1)}, bf16[1,256,4096]{2,1,0:T(8,128)(2,1)}, u32[]{:S(2)}) copy-start(bf16[1,256,4096]{2,1,0:T(8,128)(2,1)} %param.13) | copy-start | bytes 6291460
  11.3 7.1 %collective-permute-start.6 = (bf16[16,4096]{1,0:T(8,128)(2,1)S(1)}, bf16[16,4096]{1,0:T(8,128)(2,1)S(1)}, u32[]{:S(2)}, u32[]{:S(2)}) collective-permute-start(bf16[16,4096]{1,0:T(8,128)(2,1)S(1)} %shard_map.121._.refs_0_.refs_3_), channel_id=1, source_target_pairs={{0,1},{1,0},{2,3},{3,2},{4,5},{5,4},{6,7},{7,6},{8,9},{9,8},{10,11... | collective-permute-start | bytes 393224 | tf_op jit(solution)/shard_map/ppermute | solution.py:230
  15.9 8.6 %collective-permute-start.3 = (bf16[32,4096]{1,0:T(8,128)(2,1)S(1)}, bf16[32,4096]{1,0:T(8,128)(2,1)S(1)}, u32[]{:S(2)}, u32[]{:S(2)}) collective-permute-start(bf16[32,4096]{1,0:T(8,128)(2,1)S(1)} %get-tuple-element.32), channel_id=1, source_target_pairs={{0,1},{1,0},{2,3},{3,2},{4,5},{5,4},{6,7},{7,6},{8,9},{9,8},{10,11... | collective-permute-start | bytes 786440 | tf_op jit(solution)/shard_map/ppermute | solution.py:230
  20.9 7.5 %collective-permute-start.9 = (bf16[16,4224]{1,0:T(8,128)(2,1)S(1)}, bf16[16,4224]{1,0:T(8,128)(2,1)S(1)}, u32[]{:S(2)}, u32[]{:S(2)}) collective-permute-start(bf16[16,4224]{1,0:T(8,128)(2,1)S(1)} %get-tuple-element.39), channel_id=1, source_target_pairs={{0,3},{1,2},{2,1},{3,0},{4,7},{5,6},{6,5},{7,4},{8,11},{9,10},{10,... | collective-permute-start | bytes 405512 | tf_op jit(solution)/shard_map/ppermute | solution.py:230
  22.7 7.5 %collective-permute-start.11 = (bf16[16,4224]{1,0:T(8,128)(2,1)S(1)}, bf16[16,4224]{1,0:T(8,128)(2,1)S(1)}, u32[]{:S(2)}, u32[]{:S(2)}) collective-permute-start(bf16[16,4224]{1,0:T(8,128)(2,1)S(1)} %get-tuple-element.41), channel_id=1, source_target_pairs={{0,2},{1,3},{2,0},{3,1},{4,6},{5,7},{6,4},{7,5},{8,10},{9,11},{10,... | collective-permute-start | bytes 405512 | tf_op jit(solution)/shard_map/ppermute | solution.py:230
  24.1 6.3 %collective-permute-start.10 = (bf16[16,4224]{1,0:T(8,128)(2,1)S(1)}, bf16[16,4224]{1,0:T(8,128)(2,1)S(1)}, u32[]{:S(2)}, u32[]{:S(2)}) collective-permute-start(bf16[16,4224]{1,0:T(8,128)(2,1)S(1)} %get-tuple-element.40), channel_id=1, source_target_pairs={{0,1},{1,0},{2,3},{3,2},{4,5},{5,4},{6,7},{7,6},{8,9},{9,8},{10,11... | collective-permute-start | bytes 405512 | tf_op jit(solution)/shard_map/ppermute | solution.py:230
  24.6 10.4 %collective-permute-start.4 = (bf16[16,4352]{1,0:T(8,128)(2,1)S(1)}, bf16[16,4352]{1,0:T(8,128)(2,1)S(1)}, u32[]{:S(2)}, u32[]{:S(2)}) collective-permute-start(bf16[16,4352]{1,0:T(8,128)(2,1)S(1)} %get-tuple-element.33), channel_id=1, source_target_pairs={{0,4},{1,5},{2,6},{3,7},{4,8},{5,9},{6,10},{7,11},{8,12},{9,13},{1... | collective-permute-start | bytes 417800 | tf_op jit(solution)/shard_map/ppermute | solution.py:230
  24.6 10.4 %collective-permute-start.5 = (bf16[16,4352]{1,0:T(8,128)(2,1)S(1)}, bf16[16,4352]{1,0:T(8,128)(2,1)S(1)}, u32[]{:S(2)}, u32[]{:S(2)}) collective-permute-start(bf16[16,4352]{1,0:T(8,128)(2,1)S(1)} %get-tuple-element.34), channel_id=1, source_target_pairs={{0,6},{1,7},{2,4},{3,5},{4,10},{5,11},{6,8},{7,9},{8,14},{9,15},{1... | collective-permute-start | bytes 417800 | tf_op jit(solution)/shard_map/ppermute | solution.py:230
  30.4 6.3 %collective-permute-start.12 = (bf16[16,4224]{1,0:T(8,128)(2,1)S(1)}, bf16[16,4224]{1,0:T(8,128)(2,1)S(1)}, u32[]{:S(2)}, u32[]{:S(2)}) collective-permute-start(bf16[16,4224]{1,0:T(8,128)(2,1)S(1)} %shard_map.129), channel_id=1, source_target_pairs={{0,28},{1,29},{2,30},{3,31},{4,0},{5,1},{6,2},{7,3},{8,4},{9,5},{1... | collective-permute-start | bytes 405512 | tf_op jit(solution)/shard_map/ppermute | solution.py:230

commit v13 on v10

--- a/solution.py
+++ b/solution.py
@@ -92,7 +92,7 @@
     cot_copy.wait()
 
 
-def gather_grads(place_ref, cot_ref, rows_ref):
+def gather_grads(place_ref, cot_ref, _, rows_ref):
     place = place_ref[...]
     gate = jnp.sum(place, axis=1, keepdims=True)
     rows_ref[...] = (f32dot(picks(place), cot_ref[...]) * gate).astype(jnp.bfloat16)
@@ -273,24 +273,23 @@
     x_blocks = [x_rows] + [shifted(x_rows, 0, k) for k in flips[1:]]
 
     near = functools.partial(pltpu.with_memory_space_constraint, memory_space=pltpu.VMEM)
+    gate_near, up_near, down_near, a_near, b_near = map(
+        near, (gate_weight[0], up_weight[0], down_weight[0], down_map, up_map)
+    )
+    (down_near,) = call(
+        add_adapter,
+        [sds(units, width)],
+        (down_near, a_near, b_near, place),
+        moved=1,
+    )
     (g_rows,) = call(
         gather_grads,
         [sds(slots, width)],
-        (place, cot_near),
+        (place, cot_near, down_near),
         flops=200 * units * rank * width,
     )
     g_rows = between_groups(g_rows, flight)
     g_blocks = [g_rows] + [shifted(g_rows, 0, k) for k in flips[1:]]
-
-    gate_near, up_near, down_near, a_near, b_near = map(
-        near, (gate_weight[0], up_weight[0], down_weight[0], down_map, up_map)
-    )
-    (down_near,) = call(
-        add_adapter,
-        [sds(units, width)],
-        (down_near, a_near, b_near, g_rows),
-        moved=1,
-    )
 
     wide = width + tokens
     *out_blocks, pre_gate, pre_up, hidden, latent = call(

time: 37.2 us -> 36.2 us (0.973)
  starting transfers between devices: 18.8 us -> 17 us
  local copies, waits for them, and re-layouts: 0.02 us -> 0.93 us
    ppermute x14, starting transfers between devices: 18.8 us -> 17 us  [shifted(): return lax.ppermute(block, ('section', 'expert'), route)]
    unnamed x10 -> x12, local copies, waits for them, and re-layouts: 0.02 us -> 0.93 us
  transfers between devices with their start and end apart: 14 -> 14, of which waited for: 5 -> 5; matrix products, arithmetic and copies ran while one was open for 0% -> 0% of each run, Pallas kernels for 23% -> 24%
where the time goes in v13:
time: 36.2 us; the launch traced here: 36 us
  starting transfers between devices  17 us (47%)
  Pallas kernels  11.7 us (32%)
  waiting for transfers between devices  5.72 us (16%)
  local copies, waits for them, and re-layouts  0.93 us (3%)
  between operations  0.74 us (2%)
    ppermute x14, starting transfers between devices, shifted(): return lax.ppermute(block, ('section', 'expert'), route)  17 us
    pallas_call x11, Pallas kernels, call(): pl.pallas_call(body, out_shape=outs, in_specs=[NEAR] * len(args) + [FAR]...  11.7 us
    ppermute x14, waiting for transfers between devices, shifted(): return lax.ppermute(block, ('section', 'expert'), route)  5.72 us
    unnamed x12, local copies, waits for them, and re-layouts  0.93 us
  transfers between devices with their start and end apart: 14, of which 5 were waited for; matrix products, arithmetic and copies ran while one was open for 0% of the time, Pallas kernels for 24%

profile of v13, /device:TPU:0, one launch (start us, length us, event | category | flops | bytes accessed | tf_op | source)
XLA Modules:
  0.0 36.0 jit_solution(548146328427858766)
XLA Ops:
  0.7 1.8 %shard_map.120 = (bf16[16,4096]{1,0:T(8,128)(2,1)S(1)}, f32[16,128]{1,0:T(8,128)S(1)}, bf16[128,4096]{1,0:T(8,128)(2,1)S(1)}) custom-call(s32[8,128]{1,0:T(8,128)} %bitcast.25, s32[8,128]{1,0:T(8,128)} %bitcast.26, bf16[1,128,4096]{2,1,0:T(8,128)(2,1)} %x_hbm.1, bf16[1,128,4096]{2,1,0:T(8,128)(2,1)} %cot_hbm.1), custom_call_target="tpu_custom_call" | custom-call | flops 16777216 | bytes 3293184 | tf_op jit(solution)/shard_map/pallas_call | solution.py:35
  2.5 4.0 %collective-permute-start.2 = (bf16[16,4096]{1,0:T(8,128)(2,1)S(1)}, bf16[16,4096]{1,0:T(8,128)(2,1)S(1)}, u32[]{:S(2)}, u32[]{:S(2)}) collective-permute-start(bf16[16,4096]{1,0:T(8,128)(2,1)S(1)} %get-tuple-element.30.refs_0_), channel_id=1, source_target_pairs={{0,3},{1,2},{2,1},{3,0},{4,7},{5,6},{6,5},{7,4},{8,11},{9,10},{10,... | collective-permute-start | bytes 393224 | tf_op jit(solution)/shard_map/ppermute | solution.py:211
  6.4 0.5 %collective-permute-start.1 = (bf16[16,4096]{1,0:T(8,128)(2,1)S(1)}, bf16[16,4096]{1,0:T(8,128)(2,1)S(1)}, u32[]{:S(2)}, u32[]{:S(2)}) collective-permute-start(bf16[16,4096]{1,0:T(8,128)(2,1)S(1)} %get-tuple-element.30.refs_0_), channel_id=1, source_target_pairs={{0,2},{1,3},{2,0},{3,1},{4,6},{5,7},{6,4},{7,5},{8,10},{9,11},{10,... | collective-permute-start | bytes 393224 | tf_op jit(solution)/shard_map/ppermute | solution.py:211
  6.9 0.1 collective-permute-start
  7.1 0.9 %copy-done.1 = bf16[1,1,16,4096]{3,2,1,0:T(8,128)(2,1)S(1)} copy-done((bf16[1,1,16,4096]{3,2,1,0:T(8,128)(2,1)S(1)}, bf16[1,1,16,4096]{3,2,1,0:T(8,128)(2,1)}, u32[]{:S(2)}) %copy-start.1) | copy-done | bytes 131096
  8.0 0.7 %shard_map.121.refs_6_._.refs_8_ = bf16[256,4096]{1,0:T(8,128)(2,1)S(1)} custom-call(bf16[256,4096]{1,0:T(8,128)(2,1)S(1)} %bitcast.16, bf16[16,256]{1,0:T(8,128)(2,1)S(1)} %bitcast.19, bf16[16,4096]{1,0:T(8,128)(2,1)S(1)} %bitcast.17, f32[16,128]{1,0:T(8,128)S(1)} %get-tuple-element.29._.place_ref), custom_call_target="tpu_custom_call" | custom-call | bytes 1 | tf_op jit(solution)/shard_map/pallas_call | solution.py:35
  8.7 0.0 copy-start.4
  8.7 0.3 shard_map.125.refs_0_.refs_3_
  9.0 2.9 %collective-permute-start.9 = (bf16[16,4096]{1,0:T(8,128)(2,1)S(1)}, bf16[16,4096]{1,0:T(8,128)(2,1)S(1)}, u32[]{:S(2)}, u32[]{:S(2)}) collective-permute-start(bf16[16,4096]{1,0:T(8,128)(2,1)S(1)} %shard_map.125.refs_0_.refs_3_), channel_id=1, source_target_pairs={{0,3},{1,2},{2,1},{3,0},{4,7},{5,6},{6,5},{7,4},{8,11},{9,10},{10,... | collective-permute-start | bytes 393224 | tf_op jit(solution)/shard_map/ppermute | solution.py:211
  11.9 0.5 %collective-permute-start.8 = (bf16[16,4096]{1,0:T(8,128)(2,1)S(1)}, bf16[16,4096]{1,0:T(8,128)(2,1)S(1)}, u32[]{:S(2)}, u32[]{:S(2)}) collective-permute-start(bf16[16,4096]{1,0:T(8,128)(2,1)S(1)} %shard_map.125.refs_0_.refs_3_), channel_id=1, source_target_pairs={{0,2},{1,3},{2,0},{3,1},{4,6},{5,7},{6,4},{7,5},{8,10},{9,11},{10,... | collective-permute-start | bytes 393224 | tf_op jit(solution)/shard_map/ppermute | solution.py:211
  12.4 0.4 %collective-permute-start.7 = (bf16[16,4096]{1,0:T(8,128)(2,1)S(1)}, bf16[16,4096]{1,0:T(8,128)(2,1)S(1)}, u32[]{:S(2)}, u32[]{:S(2)}) collective-permute-start(bf16[16,4096]{1,0:T(8,128)(2,1)S(1)} %shard_map.125.refs_0_.refs_3_), channel_id=1, source_target_pairs={{0,1},{1,0},{2,3},{3,2},{4,5},{5,4},{6,7},{7,6},{8,9},{9,8},{10,11... | collective-permute-start | bytes 393224 | tf_op jit(solution)/shard_map/ppermute | solution.py:211
  12.8 1.2 %collective-permute-done.1.refs_2_ = bf16[16,4096]{1,0:T(8,128)(2,1)S(1)} collective-permute-done((bf16[16,4096]{1,0:T(8,128)(2,1)S(1)}, bf16[16,4096]{1,0:T(8,128)(2,1)S(1)}, u32[]{:S(2)}, u32[]{:S(2)}) %collective-permute-start.1) | collective-permute-done | bytes 131104 | tf_op jit(solution)/shard_map/ppermute | solution.py:211
  14.0 1.8 %shard_map.122 = (bf16[16,4096]{1,0:T(8,128)(2,1)S(1)}, bf16[16,4224]{1,0:T(8,128)(2,1)S(1)}, bf16[16,4224]{1,0:T(8,128)(2,1)S(1)}, bf16[16,4224]{1,0:T(8,128)(2...) custom-call(bf16[16,4096]{1,0:T(8,128)(2,1)S(1)} %get-tuple-element., ...), custom_call_target="tpu_custom_call" | custom-call | flops 4026531840 | bytes 7526400 | tf_op jit(solution)/shard_map/pallas_call | solution.py:35
  15.8 2.5 %collective-permute-start.3 = (bf16[16,4224]{1,0:T(8,128)(2,1)S(1)}, bf16[16,4224]{1,0:T(8,128)(2,1)S(1)}, u32[]{:S(2)}, u32[]{:S(2)}) collective-permute-start(bf16[16,4224]{1,0:T(8,128)(2,1)S(1)} %get-tuple-element.32), channel_id=1, source_target_pairs={{0,3},{1,2},{2,1},{3,0},{4,7},{5,6},{6,5},{7,4},{8,11},{9,10},{10,... | collective-permute-start | bytes 405512 | tf_op jit(solution)/shard_map/ppermute | solution.py:211
  18.3 0.6 %collective-permute-start.4 = (bf16[16,4224]{1,0:T(8,128)(2,1)S(1)}, bf16[16,4224]{1,0:T(8,128)(2,1)S(1)}, u32[]{:S(2)}, u32[]{:S(2)}) collective-permute-start(bf16[16,4224]{1,0:T(8,128)(2,1)S(1)} %get-tuple-element.33), channel_id=1, source_target_pairs={{0,1},{1,0},{2,3},{3,2},{4,5},{5,4},{6,7},{7,6},{8,9},{9,8},{10,11... | collective-permute-start | bytes 405512 | tf_op jit(solution)/shard_map/ppermute | solution.py:211
  18.9 0.5 %collective-permute-start.5 = (bf16[16,4224]{1,0:T(8,128)(2,1)S(1)}, bf16[16,4224]{1,0:T(8,128)(2,1)S(1)}, u32[]{:S(2)}, u32[]{:S(2)}) collective-permute-start(bf16[16,4224]{1,0:T(8,128)(2,1)S(1)} %get-tuple-element.34), channel_id=1, source_target_pairs={{0,2},{1,3},{2,0},{3,1},{4,6},{5,7},{6,4},{7,5},{8,10},{9,11},{10,... | collective-permute-start | bytes 405512 | tf_op jit(solution)/shard_map/ppermute | solution.py:211
  19.4 2.5 %shard_map.126 = (bf16[16,4096]{1,0:T(8,128)(2,1)S(1)}, bf16[16,4096]{1,0:T(8,128)(2,1)S(1)}, bf16[16,4096]{1,0:T(8,128)(2,1)S(1)}, bf16[16,4096]{1,0:T(8,128)(2,1)S(1)}) custom-call(bf16[16,4096]{1,0:T(8,128)(2,1)S(1)} %shard_map.125.refs_0_.refs_3_, bf16[16,4096]{1,0:T(8,128)(2,1)S(1)} %collective-permute-done.7.refs_1_.refs_4_, ...), custom_call_target="tpu_custom_call" | custom-call | flops 4026531840 | bytes 7471104 | tf_op jit(solution)/shard_map/pallas_call | solution.py:35
  21.9 2.5 %collective-permute-start.10 = (bf16[16,4096]{1,0:T(8,128)(2,1)S(1)}, bf16[16,4096]{1,0:T(8,128)(2,1)S(1)}, u32[]{:S(2)}, u32[]{:S(2)}) collective-permute-start(bf16[16,4096]{1,0:T(8,128)(2,1)S(1)} %get-tuple-element.39), channel_id=1, source_target_pairs={{0,3},{1,2},{2,1},{3,0},{4,7},{5,6},{6,5},{7,4},{8,11},{9,10},{10,... | collective-permute-start | bytes 393224 | tf_op jit(solution)/shard_map/ppermute | solution.py:211
  24.4 0.6 %collective-permute-start.11 = (bf16[16,4096]{1,0:T(8,128)(2,1)S(1)}, bf16[16,4096]{1,0:T(8,128)(2,1)S(1)}, u32[]{:S(2)}, u32[]{:S(2)}) collective-permute-start(bf16[16,4096]{1,0:T(8,128)(2,1)S(1)} %get-tuple-element.40), channel_id=1, source_target_pairs={{0,1},{1,0},{2,3},{3,2},{4,5},{5,4},{6,7},{7,6},{8,9},{9,8},{10,11... | collective-permute-start | bytes 393224 | tf_op jit(solution)/shard_map/ppermute | solution.py:211
  24.9 0.5 %collective-permute-start.12 = (bf16[16,4096]{1,0:T(8,128)(2,1)S(1)}, bf16[16,4096]{1,0:T(8,128)(2,1)S(1)}, u32[]{:S(2)}, u32[]{:S(2)}) collective-permute-start(bf16[16,4096]{1,0:T(8,128)(2,1)S(1)} %get-tuple-element.41), channel_id=1, source_target_pairs={{0,2},{1,3},{2,0},{3,1},{4,6},{5,7},{6,4},{7,5},{8,10},{9,11},{10,... | collective-permute-start | bytes 393224 | tf_op jit(solution)/shard_map/ppermute | solution.py:211
  25.4 1.0 %shard_map.127 = f32[16,256]{1,0:T(8,128)} custom-call(bf16[16,4096]{1,0:T(8,128)(2,1)S(1)} %shard_map.125.refs_0_.refs_3_, bf16[16,4096]{1,0:T(8,128)(2,1)S(1)} %collective-permute-done.7.refs_1_.refs_4_, bf16[16,4096]{1,0:T(8,128)(2,1)S(1)} %collective-permute-done.8.refs_2_.refs_5_, bf16[16,4096]{1,0:T(8,128)(2,1)S(1)} %collective-permute-done.9.refs_3_.refs_6_, ...), custom_call_target="tpu_custom_call" | custom-call | flops 838860800 | bytes 704512 | tf_op jit(solution)/shard_map/pallas_call | solution.py:35
  26.5 0.1 shard_map.123
  26.6 0.1 collective-permute-start.6
  26.7 0.9 %shard_map.128 = f32[1,1,16,1024]{3,2,1,0:T(8,128)} custom-call(bf16[16,64]{1,0:T(8,128)(2,1)S(1)} %get-tuple-element.45.latent_ref, bf16[16,4224]{1,0:T(8,128)(2,1)S(1)} %collective-permute-done.3.refs_1_.refs_0_, bf16[16,4224]{1,0:T(8,128)(2,1)S(1)} %collective-permute-done.4.refs_2_.refs_1_, bf16[16,4224]{1,0:T(8,128)(2,1)S(1)} %collective-permute-done.5.refs_3_.refs_2_, ...), custom_call_target="tpu_custom_call" | custom-call | flops 838860800 | bytes 997376 | tf_op jit(solution)/shard_map/pallas_call | solution.py:35
  27.5 1.6 %collective-permute-done.10.refs_1_ = bf16[16,4096]{1,0:T(8,128)(2,1)S(1)} collective-permute-done((bf16[16,4096]{1,0:T(8,128)(2,1)S(1)}, bf16[16,4096]{1,0:T(8,128)(2,1)S(1)}, u32[]{:S(2)}, u32[]{:S(2)}) %collective-permute-start.10) | collective-permute-done | bytes 131104 | tf_op jit(solution)/shard_map/ppermute | solution.py:211
  29.1 1.6 %collective-permute-done.11.refs_2_ = bf16[16,4096]{1,0:T(8,128)(2,1)S(1)} collective-permute-done((bf16[16,4096]{1,0:T(8,128)(2,1)S(1)}, bf16[16,4096]{1,0:T(8,128)(2,1)S(1)}, u32[]{:S(2)}, u32[]{:S(2)}) %collective-permute-start.11) | collective-permute-done | bytes 131104 | tf_op jit(solution)/shard_map/ppermute | solution.py:211
  30.7 0.1 shard_map.129
  30.8 1.5 %collective-permute-start.13 = (bf16[16,4224]{1,0:T(8,128)(2,1)S(1)}, bf16[16,4224]{1,0:T(8,128)(2,1)S(1)}, u32[]{:S(2)}, u32[]{:S(2)}) collective-permute-start(bf16[16,4224]{1,0:T(8,128)(2,1)S(1)} %shard_map.129), channel_id=1, source_target_pairs={{0,28},{1,29},{2,30},{3,31},{4,0},{5,1},{6,2},{7,3},{8,4},{9,5},{1... | collective-permute-start | bytes 405512 | tf_op jit(solution)/shard_map/ppermute | solution.py:211
  32.2 0.6 %collective-permute-done.6.message_ref = bf16[16,4224]{1,0:T(8,128)(2,1)S(1)} collective-permute-done((bf16[16,4224]{1,0:T(8,128)(2,1)S(1)}, bf16[16,4224]{1,0:T(8,128)(2,1)S(1)}, u32[]{:S(2)}, u32[]{:S(2)}) %collective-permute-start.6) | collective-permute-done | bytes 135200 | tf_op jit(solution)/shard_map/ppermute | solution.py:211
  32.9 1.2 %shard_map.124 = bf16[1,128,4096]{2,1,0:T(8,128)(2,1)} custom-call(bf16[16,4224]{1,0:T(8,128)(2,1)S(1)} %collective-permute-done.6.message_ref), custom_call_target="tpu_custom_call" | custom-call | flops 16777216 | bytes 1183744 | tf_op jit(solution)/shard_map/pallas_call | solution.py:35
  34.1 0.7 %collective-permute-done.13.message_ref = bf16[16,4224]{1,0:T(8,128)(2,1)S(1)} collective-permute-done((bf16[16,4224]{1,0:T(8,128)(2,1)S(1)}, bf16[16,4224]{1,0:T(8,128)(2,1)S(1)}, u32[]{:S(2)}, u32[]{:S(2)}) %collective-permute-start.13) | collective-permute-done | bytes 135200 | tf_op jit(solution)/shard_map/ppermute | solution.py:211
  34.8 1.2 %shard_map.130 = bf16[1,128,4096]{2,1,0:T(8,128)(2,1)} custom-call(bf16[16,4224]{1,0:T(8,128)(2,1)S(1)} %collective-permute-done.13.message_ref), custom_call_target="tpu_custom_call" | custom-call | flops 16777216 | bytes 1183744 | tf_op jit(solution)/shard_map/pallas_call | solution.py:35
  (19 shorter events, 0.0 us)
Async XLA Ops:
  0.6 6.5 %copy-start.3 = (bf16[1,256,16]{1,2,0:T(8,128)(2,1)S(1)}, bf16[1,256,16]{1,2,0:T(8,128)(2,1)}, u32[]{:S(2)}) copy-start(bf16[1,256,16]{1,2,0:T(8,128)(2,1)} %param.15) | copy-start | bytes 24580
  0.6 6.4 %copy-start = (bf16[1,256,4096]{2,1,0:T(8,128)(2,1)S(1)}, bf16[1,256,4096]{2,1,0:T(8,128)(2,1)}, u32[]{:S(2)}) copy-start(bf16[1,256,4096]{2,1,0:T(8,128)(2,1)} %param.14) | copy-start | bytes 6291460
  2.5 9.9 %collective-permute-start.2 = (bf16[16,4096]{1,0:T(8,128)(2,1)S(1)}, bf16[16,4096]{1,0:T(8,128)(2,1)S(1)}, u32[]{:S(2)}, u32[]{:S(2)}) collective-permute-start(bf16[16,4096]{1,0:T(8,128)(2,1)S(1)} %get-tuple-element.30.refs_0_), channel_id=1, source_target_pairs={{0,3},{1,2},{2,1},{3,0},{4,7},{5,6},{6,5},{7,4},{8,11},{9,10},{10,... | collective-permute-start | bytes 393224 | tf_op jit(solution)/shard_map/ppermute | solution.py:211
  6.4 7.5 %collective-permute-start.1 = (bf16[16,4096]{1,0:T(8,128)(2,1)S(1)}, bf16[16,4096]{1,0:T(8,128)(2,1)S(1)}, u32[]{:S(2)}, u32[]{:S(2)}) collective-permute-start(bf16[16,4096]{1,0:T(8,128)(2,1)S(1)} %get-tuple-element.30.refs_0_), channel_id=1, source_target_pairs={{0,2},{1,3},{2,0},{3,1},{4,6},{5,7},{6,4},{7,5},{8,10},{9,11},{10,... | collective-permute-start | bytes 393224 | tf_op jit(solution)/shard_map/ppermute | solution.py:211
  6.9 7.0 %collective-permute-start = (bf16[16,4096]{1,0:T(8,128)(2,1)S(1)}, bf16[16,4096]{1,0:T(8,128)(2,1)S(1)}, u32[]{:S(2)}, u32[]{:S(2)}) collective-permute-start(bf16[16,4096]{1,0:T(8,128)(2,1)S(1)} %get-tuple-element.30.refs_0_), channel_id=1, source_target_pairs={{0,1},{1,0},{2,3},{3,2},{4,5},{5,4},{6,7},{7,6},{8,9},{9,8},{10,11... | collective-permute-start | bytes 393224 | tf_op jit(solution)/shard_map/ppermute | solution.py:211
  7.1 0.9 %copy-start.1 = (bf16[1,1,16,4096]{3,2,1,0:T(8,128)(2,1)S(1)}, bf16[1,1,16,4096]{3,2,1,0:T(8,128)(2,1)}, u32[]{:S(2)}) copy-start(bf16[1,1,16,4096]{3,2,1,0:T(8,128)(2,1)} %param.16) | copy-start | bytes 393220
  8.7 5.2 %copy-start.4 = (bf16[1,256,4096]{2,1,0:T(8,128)(2,1)S(1)}, bf16[1,256,4096]{2,1,0:T(8,128)(2,1)}, u32[]{:S(2)}) copy-start(bf16[1,256,4096]{2,1,0:T(8,128)(2,1)} %param.12) | copy-start | bytes 6291460
  8.7 5.2 %copy-start.5 = (bf16[1,256,4096]{2,1,0:T(8,128)(2,1)S(1)}, bf16[1,256,4096]{2,1,0:T(8,128)(2,1)}, u32[]{:S(2)}) copy-start(bf16[1,256,4096]{2,1,0:T(8,128)(2,1)} %param.13) | copy-start | bytes 6291460
  9.0 9.9 %collective-permute-start.9 = (bf16[16,4096]{1,0:T(8,128)(2,1)S(1)}, bf16[16,4096]{1,0:T(8,128)(2,1)S(1)}, u32[]{:S(2)}, u32[]{:S(2)}) collective-permute-start(bf16[16,4096]{1,0:T(8,128)(2,1)S(1)} %shard_map.125.refs_0_.refs_3_), channel_id=1, source_target_pairs={{0,3},{1,2},{2,1},{3,0},{4,7},{5,6},{6,5},{7,4},{8,11},{9,10},{10,... | collective-permute-start | bytes 393224 | tf_op jit(solution)/shard_map/ppermute | solution.py:211
  11.9 7.5 %collective-permute-start.8 = (bf16[16,4096]{1,0:T(8,128)(2,1)S(1)}, bf16[16,4096]{1,0:T(8,128)(2,1)S(1)}, u32[]{:S(2)}, u32[]{:S(2)}) collective-permute-start(bf16[16,4096]{1,0:T(8,128)(2,1)S(1)} %shard_map.125.refs_0_.refs_3_), channel_id=1, source_target_pairs={{0,2},{1,3},{2,0},{3,1},{4,6},{5,7},{6,4},{7,5},{8,10},{9,11},{10,... | collective-permute-start | bytes 393224 | tf_op jit(solution)/shard_map/ppermute | solution.py:211
  12.4 7.0 %collective-permute-start.7 = (bf16[16,4096]{1,0:T(8,128)(2,1)S(1)}, bf16[16,4096]{1,0:T(8,128)(2,1)S(1)}, u32[]{:S(2)}, u32[]{:S(2)}) collective-permute-start(bf16[16,4096]{1,0:T(8,128)(2,1)S(1)} %shard_map.125.refs_0_.refs_3_), channel_id=1, source_target_pairs={{0,1},{1,0},{2,3},{3,2},{4,5},{5,4},{6,7},{7,6},{8,9},{9,8},{10,11... | collective-permute-start | bytes 393224 | tf_op jit(solution)/shard_map/ppermute | solution.py:211
  15.8 9.1 %collective-permute-start.3 = (bf16[16,4224]{1,0:T(8,128)(2,1)S(1)}, bf16[16,4224]{1,0:T(8,128)(2,1)S(1)}, u32[]{:S(2)}, u32[]{:S(2)}) collective-permute-start(bf16[16,4224]{1,0:T(8,128)(2,1)S(1)} %get-tuple-element.32), channel_id=1, source_target_pairs={{0,3},{1,2},{2,1},{3,0},{4,7},{5,6},{6,5},{7,4},{8,11},{9,10},{10,... | collective-permute-start | bytes 405512 | tf_op jit(solution)/shard_map/ppermute | solution.py:211
  18.3 8.2 %collective-permute-start.4 = (bf16[16,4224]{1,0:T(8,128)(2,1)S(1)}, bf16[16,4224]{1,0:T(8,128)(2,1)S(1)}, u32[]{:S(2)}, u32[]{:S(2)}) collective-permute-start(bf16[16,4224]{1,0:T(8,128)(2,1)S(1)} %get-tuple-element.33), channel_id=1, source_target_pairs={{0,1},{1,0},{2,3},{3,2},{4,5},{5,4},{6,7},{7,6},{8,9},{9,8},{10,11... | collective-permute-start | bytes 405512 | tf_op jit(solution)/shard_map/ppermute | solution.py:211
  18.9 7.6 %collective-permute-start.5 = (bf16[16,4224]{1,0:T(8,128)(2,1)S(1)}, bf16[16,4224]{1,0:T(8,128)(2,1)S(1)}, u32[]{:S(2)}, u32[]{:S(2)}) collective-permute-start(bf16[16,4224]{1,0:T(8,128)(2,1)S(1)} %get-tuple-element.34), channel_id=1, source_target_pairs={{0,2},{1,3},{2,0},{3,1},{4,6},{5,7},{6,4},{7,5},{8,10},{9,11},{10,... | collective-permute-start | bytes 405512 | tf_op jit(solution)/shard_map/ppermute | solution.py:211
  19.4 6.1 %copy-start.2 = (bf16[1,1,16,4096]{3,2,1,0:T(8,128)(2,1)S(1)}, bf16[1,1,16,4096]{3,2,1,0:T(8,128)(2,1)}, u32[]{:S(2)}) copy-start(bf16[1,1,16,4096]{3,2,1,0:T(8,128)(2,1)} %param.16) | copy-start | bytes 393220
  21.9 7.2 %collective-permute-start.10 = (bf16[16,4096]{1,0:T(8,128)(2,1)S(1)}, bf16[16,4096]{1,0:T(8,128)(2,1)S(1)}, u32[]{:S(2)}, u32[]{:S(2)}) collective-permute-start(bf16[16,4096]{1,0:T(8,128)(2,1)S(1)} %get-tuple-element.39), channel_id=1, source_target_pairs={{0,3},{1,2},{2,1},{3,0},{4,7},{5,6},{6,5},{7,4},{8,11},{9,10},{10,... | collective-permute-start | bytes 393224 | tf_op jit(solution)/shard_map/ppermute | solution.py:211
  24.4 6.3 %collective-permute-start.11 = (bf16[16,4096]{1,0:T(8,128)(2,1)S(1)}, bf16[16,4096]{1,0:T(8,128)(2,1)S(1)}, u32[]{:S(2)}, u32[]{:S(2)}) collective-permute-start(bf16[16,4096]{1,0:T(8,128)(2,1)S(1)} %get-tuple-element.40), channel_id=1, source_target_pairs={{0,1},{1,0},{2,3},{3,2},{4,5},{5,4},{6,7},{7,6},{8,9},{9,8},{10,11... | collective-permute-start | bytes 393224 | tf_op jit(solution)/shard_map/ppermute | solution.py:211
  24.9 5.8 %collective-permute-start.12 = (bf16[16,4096]{1,0:T(8,128)(2,1)S(1)}, bf16[16,4096]{1,0:T(8,128)(2,1)S(1)}, u32[]{:S(2)}, u32[]{:S(2)}) collective-permute-start(bf16[16,4096]{1,0:T(8,128)(2,1)S(1)} %get-tuple-element.41), channel_id=1, source_target_pairs={{0,2},{1,3},{2,0},{3,1},{4,6},{5,7},{6,4},{7,5},{8,10},{9,11},{10,... | collective-permute-start | bytes 393224 | tf_op jit(solution)/shard_map/ppermute | solution.py:211
  26.6 6.3 %collective-permute-start.6 = (bf16[16,4224]{1,0:T(8,128)(2,1)S(1)}, bf16[16,4224]{1,0:T(8,128)(2,1)S(1)}, u32[]{:S(2)}, u32[]{:S(2)}) collective-permute-start(bf16[16,4224]{1,0:T(8,128)(2,1)S(1)} %shard_map.123), channel_id=1, source_target_pairs={{0,4},{1,5},{2,6},{3,7},{4,8},{5,9},{6,10},{7,11},{8,12},{9,13},{1... | collective-permute-start | bytes 405512 | tf_op jit(solution)/shard_map/ppermute | solution.py:211
  30.8 4.0 %collective-permute-start.13 = (bf16[16,4224]{1,0:T(8,128)(2,1)S(1)}, bf16[16,4224]{1,0:T(8,128)(2,1)S(1)}, u32[]{:S(2)}, u32[]{:S(2)}) collective-permute-start(bf16[16,4224]{1,0:T(8,128)(2,1)S(1)} %shard_map.129), channel_id=1, source_target_pairs={{0,28},{1,29},{2,30},{3,31},{4,0},{5,1},{6,2},{7,3},{8,4},{9,5},{1... | collective-permute-start | bytes 405512 | tf_op jit(solution)/shard_map/ppermute | solution.py:211

commit v14 on v13

--- a/solution.py
+++ b/solution.py
@@ -282,6 +282,7 @@
         (down_near, a_near, b_near, place),
         moved=1,
     )
+    down_near, x_blocks[3] = lax.optimization_barrier((down_near, x_blocks[3]))
     (g_rows,) = call(
         gather_grads,
         [sds(slots, width)],

time: 36.2 us -> 37.7 us (1.041)
  waiting for transfers between devices: 5.72 us -> 6.57 us
  starting transfers between devices: 17 us -> 17.6 us
    ppermute x14, waiting for transfers between devices: 5.72 us -> 6.57 us  [shifted(): return lax.ppermute(block, ('section', 'expert'), route)]
    ppermute x14, starting transfers between devices: 17 us -> 17.6 us  [shifted(): return lax.ppermute(block, ('section', 'expert'), route)]
  transfers between devices with their start and end apart: 14 -> 14, of which waited for: 5 -> 6; matrix products, arithmetic and copies ran while one was open for 0% -> 0% of each run, Pallas kernels for 24% -> 23%
where the time goes in v14:
time: 37.7 us; the launch traced here: 37.5 us
  starting transfers between devices  17.6 us (47%)
  Pallas kernels  11.7 us (31%)
  waiting for transfers between devices  6.57 us (17%)
  local copies, waits for them, and re-layouts  0.92 us (2%)
  between operations  0.73 us (2%)
    ppermute x14, starting transfers between devices, shifted(): return lax.ppermute(block, ('section', 'expert'), route)  17.6 us
    pallas_call x11, Pallas kernels, call(): pl.pallas_call(body, out_shape=outs, in_specs=[NEAR] * len(args) + [FAR]...  11.7 us
    ppermute x14, waiting for transfers between devices, shifted(): return lax.ppermute(block, ('section', 'expert'), route)  6.57 us
    unnamed x12, local copies, waits for them, and re-layouts  0.92 us
  transfers between devices with their start and end apart: 14, of which 6 were waited for; matrix products, arithmetic and copies ran while one was open for 0% of the time, Pallas kernels for 23%

profile of v14, /device:TPU:0, one launch (start us, length us, event | category | flops | bytes accessed | tf_op | source)
XLA Modules:
  0.0 37.5 jit_solution(16569570375333656573)
XLA Ops:
  0.7 1.8 %shard_map.120 = (bf16[16,4096]{1,0:T(8,128)(2,1)S(1)}, f32[16,128]{1,0:T(8,128)S(1)}, bf16[128,4096]{1,0:T(8,128)(2,1)S(1)}) custom-call(s32[8,128]{1,0:T(8,128)} %bitcast.25, s32[8,128]{1,0:T(8,128)} %bitcast.26, bf16[1,128,4096]{2,1,0:T(8,128)(2,1)} %x_hbm.1, bf16[1,128,4096]{2,1,0:T(8,128)(2,1)} %cot_hbm.1), custom_call_target="tpu_custom_call" | custom-call | flops 16777216 | bytes 3293184 | tf_op jit(solution)/shard_map/pallas_call | solution.py:35
  2.5 4.0 %collective-permute-start.2 = (bf16[16,4096]{1,0:T(8,128)(2,1)S(1)}, bf16[16,4096]{1,0:T(8,128)(2,1)S(1)}, u32[]{:S(2)}, u32[]{:S(2)}) collective-permute-start(bf16[16,4096]{1,0:T(8,128)(2,1)S(1)} %get-tuple-element.32.refs_0_), channel_id=1, source_target_pairs={{0,3},{1,2},{2,1},{3,0},{4,7},{5,6},{6,5},{7,4},{8,11},{9,10},{10,... | collective-permute-start | bytes 393224 | tf_op jit(solution)/shard_map/ppermute | solution.py:211
  6.4 0.5 %collective-permute-start.1 = (bf16[16,4096]{1,0:T(8,128)(2,1)S(1)}, bf16[16,4096]{1,0:T(8,128)(2,1)S(1)}, u32[]{:S(2)}, u32[]{:S(2)}) collective-permute-start(bf16[16,4096]{1,0:T(8,128)(2,1)S(1)} %get-tuple-element.32.refs_0_), channel_id=1, source_target_pairs={{0,2},{1,3},{2,0},{3,1},{4,6},{5,7},{6,4},{7,5},{8,10},{9,11},{10,... | collective-permute-start | bytes 393224 | tf_op jit(solution)/shard_map/ppermute | solution.py:211
  6.9 0.1 collective-permute-start
  7.1 0.9 %copy-done.1 = bf16[1,1,16,4096]{3,2,1,0:T(8,128)(2,1)S(1)} copy-done((bf16[1,1,16,4096]{3,2,1,0:T(8,128)(2,1)S(1)}, bf16[1,1,16,4096]{3,2,1,0:T(8,128)(2,1)}, u32[]{:S(2)}) %copy-start.1) | copy-done | bytes 131096
  8.0 0.7 %shard_map.121.refs_6_._.refs_8_ = bf16[256,4096]{1,0:T(8,128)(2,1)S(1)} custom-call(bf16[256,4096]{1,0:T(8,128)(2,1)S(1)} %bitcast.16, bf16[16,256]{1,0:T(8,128)(2,1)S(1)} %bitcast.19, bf16[16,4096]{1,0:T(8,128)(2,1)S(1)} %bitcast.17, f32[16,128]{1,0:T(8,128)S(1)} %get-tuple-element.31._.place_ref), custom_call_target="tpu_custom_call" | custom-call | bytes 1 | tf_op jit(solution)/shard_map/pallas_call | solution.py:35
  8.7 1.6 %collective-permute-done.2.refs_3_ = bf16[16,4096]{1,0:T(8,128)(2,1)S(1)} collective-permute-done((bf16[16,4096]{1,0:T(8,128)(2,1)S(1)}, bf16[16,4096]{1,0:T(8,128)(2,1)S(1)}, u32[]{:S(2)}, u32[]{:S(2)}) %collective-permute-start.2) | collective-permute-done | bytes 131104 | tf_op jit(solution)/shard_map/ppermute | solution.py:211
  10.3 0.2 shard_map.125.refs_0_.refs_3_
  10.6 3.4 %collective-permute-start.9 = (bf16[16,4096]{1,0:T(8,128)(2,1)S(1)}, bf16[16,4096]{1,0:T(8,128)(2,1)S(1)}, u32[]{:S(2)}, u32[]{:S(2)}) collective-permute-start(bf16[16,4096]{1,0:T(8,128)(2,1)S(1)} %shard_map.125.refs_0_.refs_3_), channel_id=1, source_target_pairs={{0,3},{1,2},{2,1},{3,0},{4,7},{5,6},{6,5},{7,4},{8,11},{9,10},{10,... | collective-permute-start | bytes 393224 | tf_op jit(solution)/shard_map/ppermute | solution.py:211
  14.0 0.5 %collective-permute-start.8 = (bf16[16,4096]{1,0:T(8,128)(2,1)S(1)}, bf16[16,4096]{1,0:T(8,128)(2,1)S(1)}, u32[]{:S(2)}, u32[]{:S(2)}) collective-permute-start(bf16[16,4096]{1,0:T(8,128)(2,1)S(1)} %shard_map.125.refs_0_.refs_3_), channel_id=1, source_target_pairs={{0,2},{1,3},{2,0},{3,1},{4,6},{5,7},{6,4},{7,5},{8,10},{9,11},{10,... | collective-permute-start | bytes 393224 | tf_op jit(solution)/shard_map/ppermute | solution.py:211
  14.5 0.1 collective-permute-start.7
  14.7 1.9 %shard_map.122 = (bf16[16,4096]{1,0:T(8,128)(2,1)S(1)}, bf16[16,4224]{1,0:T(8,128)(2,1)S(1)}, bf16[16,4224]{1,0:T(8,128)(2,1)S(1)}, bf16[16,4224]{1,0:T(8,128)(2...) custom-call(bf16[16,4096]{1,0:T(8,128)(2,1)S(1)} %get-tuple-element., ...), custom_call_target="tpu_custom_call" | custom-call | flops 4026531840 | bytes 7526400 | tf_op jit(solution)/shard_map/pallas_call | solution.py:35
  16.5 2.9 %collective-permute-start.3 = (bf16[16,4224]{1,0:T(8,128)(2,1)S(1)}, bf16[16,4224]{1,0:T(8,128)(2,1)S(1)}, u32[]{:S(2)}, u32[]{:S(2)}) collective-permute-start(bf16[16,4224]{1,0:T(8,128)(2,1)S(1)} %get-tuple-element.36), channel_id=1, source_target_pairs={{0,3},{1,2},{2,1},{3,0},{4,7},{5,6},{6,5},{7,4},{8,11},{9,10},{10,... | collective-permute-start | bytes 405512 | tf_op jit(solution)/shard_map/ppermute | solution.py:211
  19.4 0.5 %collective-permute-start.4 = (bf16[16,4224]{1,0:T(8,128)(2,1)S(1)}, bf16[16,4224]{1,0:T(8,128)(2,1)S(1)}, u32[]{:S(2)}, u32[]{:S(2)}) collective-permute-start(bf16[16,4224]{1,0:T(8,128)(2,1)S(1)} %get-tuple-element.37), channel_id=1, source_target_pairs={{0,1},{1,0},{2,3},{3,2},{4,5},{5,4},{6,7},{7,6},{8,9},{9,8},{10,11... | collective-permute-start | bytes 405512 | tf_op jit(solution)/shard_map/ppermute | solution.py:211
  20.0 0.1 collective-permute-start.5
  20.1 1.4 %collective-permute-done.8.refs_2_.refs_5_ = bf16[16,4096]{1,0:T(8,128)(2,1)S(1)} collective-permute-done((bf16[16,4096]{1,0:T(8,128)(2,1)S(1)}, bf16[16,4096]{1,0:T(8,128)(2,1)S(1)}, u32[]{:S(2)}, u32[]{:S(2)}) %collective-permute-start.8) | collective-permute-done | bytes 131104 | tf_op jit(solution)/shard_map/ppermute | solution.py:211
  21.5 2.5 %shard_map.126 = (bf16[16,4096]{1,0:T(8,128)(2,1)S(1)}, bf16[16,4096]{1,0:T(8,128)(2,1)S(1)}, bf16[16,4096]{1,0:T(8,128)(2,1)S(1)}, bf16[16,4096]{1,0:T(8,128)(2,1)S(1)}) custom-call(bf16[16,4096]{1,0:T(8,128)(2,1)S(1)} %shard_map.125.refs_0_.refs_3_, bf16[16,4096]{1,0:T(8,128)(2,1)S(1)} %collective-permute-done.7.refs_1_.refs_4_, ...), custom_call_target="tpu_custom_call" | custom-call | flops 4026531840 | bytes 7471104 | tf_op jit(solution)/shard_map/pallas_call | solution.py:35
  24.0 1.5 %collective-permute-start.10 = (bf16[16,4096]{1,0:T(8,128)(2,1)S(1)}, bf16[16,4096]{1,0:T(8,128)(2,1)S(1)}, u32[]{:S(2)}, u32[]{:S(2)}) collective-permute-start(bf16[16,4096]{1,0:T(8,128)(2,1)S(1)} %get-tuple-element.43), channel_id=1, source_target_pairs={{0,3},{1,2},{2,1},{3,0},{4,7},{5,6},{6,5},{7,4},{8,11},{9,10},{10,... | collective-permute-start | bytes 393224 | tf_op jit(solution)/shard_map/ppermute | solution.py:211
  25.5 0.9 %collective-permute-start.11 = (bf16[16,4096]{1,0:T(8,128)(2,1)S(1)}, bf16[16,4096]{1,0:T(8,128)(2,1)S(1)}, u32[]{:S(2)}, u32[]{:S(2)}) collective-permute-start(bf16[16,4096]{1,0:T(8,128)(2,1)S(1)} %get-tuple-element.44), channel_id=1, source_target_pairs={{0,1},{1,0},{2,3},{3,2},{4,5},{5,4},{6,7},{7,6},{8,9},{9,8},{10,11... | collective-permute-start | bytes 393224 | tf_op jit(solution)/shard_map/ppermute | solution.py:211
  26.5 1.1 %collective-permute-start.12 = (bf16[16,4096]{1,0:T(8,128)(2,1)S(1)}, bf16[16,4096]{1,0:T(8,128)(2,1)S(1)}, u32[]{:S(2)}, u32[]{:S(2)}) collective-permute-start(bf16[16,4096]{1,0:T(8,128)(2,1)S(1)} %get-tuple-element.45), channel_id=1, source_target_pairs={{0,2},{1,3},{2,0},{3,1},{4,6},{5,7},{6,4},{7,5},{8,10},{9,11},{10,... | collective-permute-start | bytes 393224 | tf_op jit(solution)/shard_map/ppermute | solution.py:211
  27.5 1.0 %shard_map.127 = f32[16,256]{1,0:T(8,128)} custom-call(bf16[16,4096]{1,0:T(8,128)(2,1)S(1)} %shard_map.125.refs_0_.refs_3_, bf16[16,4096]{1,0:T(8,128)(2,1)S(1)} %collective-permute-done.7.refs_1_.refs_4_, bf16[16,4096]{1,0:T(8,128)(2,1)S(1)} %collective-permute-done.8.refs_2_.refs_5_, bf16[16,4096]{1,0:T(8,128)(2,1)S(1)} %collective-permute-done.9.refs_3_.refs_6_, ...), custom_call_target="tpu_custom_call" | custom-call | flops 838860800 | bytes 704512 | tf_op jit(solution)/shard_map/pallas_call | solution.py:35
  28.6 0.1 shard_map.123
  28.7 0.1 collective-permute-start.6
  28.8 0.9 %shard_map.128 = f32[1,1,16,1024]{3,2,1,0:T(8,128)} custom-call(bf16[16,64]{1,0:T(8,128)(2,1)S(1)} %get-tuple-element.49.latent_ref, bf16[16,4224]{1,0:T(8,128)(2,1)S(1)} %collective-permute-done.3.refs_1_.refs_0_, bf16[16,4224]{1,0:T(8,128)(2,1)S(1)} %collective-permute-done.4.refs_2_.refs_1_, bf16[16,4224]{1,0:T(8,128)(2,1)S(1)} %collective-permute-done.5.refs_3_.refs_2_, ...), custom_call_target="tpu_custom_call" | custom-call | flops 838860800 | bytes 997376 | tf_op jit(solution)/shard_map/pallas_call | solution.py:35
  29.6 0.3 collective-permute-done.10.refs_1_
  29.9 1.0 %collective-permute-done.11.refs_2_ = bf16[16,4096]{1,0:T(8,128)(2,1)S(1)} collective-permute-done((bf16[16,4096]{1,0:T(8,128)(2,1)S(1)}, bf16[16,4096]{1,0:T(8,128)(2,1)S(1)}, u32[]{:S(2)}, u32[]{:S(2)}) %collective-permute-start.11) | collective-permute-done | bytes 131104 | tf_op jit(solution)/shard_map/ppermute | solution.py:211
  30.9 0.5 %collective-permute-done.12.refs_3_ = bf16[16,4096]{1,0:T(8,128)(2,1)S(1)} collective-permute-done((bf16[16,4096]{1,0:T(8,128)(2,1)S(1)}, bf16[16,4096]{1,0:T(8,128)(2,1)S(1)}, u32[]{:S(2)}, u32[]{:S(2)}) %collective-permute-start.12) | collective-permute-done | bytes 131104 | tf_op jit(solution)/shard_map/ppermute | solution.py:211
  31.4 0.1 shard_map.129
  31.5 1.8 %collective-permute-start.13 = (bf16[16,4224]{1,0:T(8,128)(2,1)S(1)}, bf16[16,4224]{1,0:T(8,128)(2,1)S(1)}, u32[]{:S(2)}, u32[]{:S(2)}) collective-permute-start(bf16[16,4224]{1,0:T(8,128)(2,1)S(1)} %shard_map.129), channel_id=1, source_target_pairs={{0,28},{1,29},{2,30},{3,31},{4,0},{5,1},{6,2},{7,3},{8,4},{9,5},{1... | collective-permute-start | bytes 405512 | tf_op jit(solution)/shard_map/ppermute | solution.py:211
  33.3 1.7 %collective-permute-done.6.message_ref = bf16[16,4224]{1,0:T(8,128)(2,1)S(1)} collective-permute-done((bf16[16,4224]{1,0:T(8,128)(2,1)S(1)}, bf16[16,4224]{1,0:T(8,128)(2,1)S(1)}, u32[]{:S(2)}, u32[]{:S(2)}) %collective-permute-start.6) | collective-permute-done | bytes 135200 | tf_op jit(solution)/shard_map/ppermute | solution.py:211
  35.0 1.2 %shard_map.124 = bf16[1,128,4096]{2,1,0:T(8,128)(2,1)} custom-call(bf16[16,4224]{1,0:T(8,128)(2,1)S(1)} %collective-permute-done.6.message_ref), custom_call_target="tpu_custom_call" | custom-call | flops 16777216 | bytes 1183744 | tf_op jit(solution)/shard_map/pallas_call | solution.py:35
  36.3 1.2 %shard_map.130 = bf16[1,128,4096]{2,1,0:T(8,128)(2,1)} custom-call(bf16[16,4224]{1,0:T(8,128)(2,1)S(1)} %collective-permute-done.13.message_ref), custom_call_target="tpu_custom_call" | custom-call | flops 16777216 | bytes 1183744 | tf_op jit(solution)/shard_map/pallas_call | solution.py:35
  (19 shorter events, 0.0 us)
Async XLA Ops:
  0.6 6.5 %copy-start.3 = (bf16[1,256,16]{1,2,0:T(8,128)(2,1)S(1)}, bf16[1,256,16]{1,2,0:T(8,128)(2,1)}, u32[]{:S(2)}) copy-start(bf16[1,256,16]{1,2,0:T(8,128)(2,1)} %param.15) | copy-start | bytes 24580
  0.6 6.4 %copy-start = (bf16[1,256,4096]{2,1,0:T(8,128)(2,1)S(1)}, bf16[1,256,4096]{2,1,0:T(8,128)(2,1)}, u32[]{:S(2)}) copy-start(bf16[1,256,4096]{2,1,0:T(8,128)(2,1)} %param.14) | copy-start | bytes 6291460
  2.5 7.9 %collective-permute-start.2 = (bf16[16,4096]{1,0:T(8,128)(2,1)S(1)}, bf16[16,4096]{1,0:T(8,128)(2,1)S(1)}, u32[]{:S(2)}, u32[]{:S(2)}) collective-permute-start(bf16[16,4096]{1,0:T(8,128)(2,1)S(1)} %get-tuple-element.32.refs_0_), channel_id=1, source_target_pairs={{0,3},{1,2},{2,1},{3,0},{4,7},{5,6},{6,5},{7,4},{8,11},{9,10},{10,... | collective-permute-start | bytes 393224 | tf_op jit(solution)/shard_map/ppermute | solution.py:211
  6.4 8.2 %collective-permute-start.1 = (bf16[16,4096]{1,0:T(8,128)(2,1)S(1)}, bf16[16,4096]{1,0:T(8,128)(2,1)S(1)}, u32[]{:S(2)}, u32[]{:S(2)}) collective-permute-start(bf16[16,4096]{1,0:T(8,128)(2,1)S(1)} %get-tuple-element.32.refs_0_), channel_id=1, source_target_pairs={{0,2},{1,3},{2,0},{3,1},{4,6},{5,7},{6,4},{7,5},{8,10},{9,11},{10,... | collective-permute-start | bytes 393224 | tf_op jit(solution)/shard_map/ppermute | solution.py:211
  6.9 7.7 %collective-permute-start = (bf16[16,4096]{1,0:T(8,128)(2,1)S(1)}, bf16[16,4096]{1,0:T(8,128)(2,1)S(1)}, u32[]{:S(2)}, u32[]{:S(2)}) collective-permute-start(bf16[16,4096]{1,0:T(8,128)(2,1)S(1)} %get-tuple-element.32.refs_0_), channel_id=1, source_target_pairs={{0,1},{1,0},{2,3},{3,2},{4,5},{5,4},{6,7},{7,6},{8,9},{9,8},{10,11... | collective-permute-start | bytes 393224 | tf_op jit(solution)/shard_map/ppermute | solution.py:211
  7.1 0.9 %copy-start.1 = (bf16[1,1,16,4096]{3,2,1,0:T(8,128)(2,1)S(1)}, bf16[1,1,16,4096]{3,2,1,0:T(8,128)(2,1)}, u32[]{:S(2)}) copy-start(bf16[1,1,16,4096]{3,2,1,0:T(8,128)(2,1)} %param.16) | copy-start | bytes 393220
  10.3 4.3 %copy-start.4 = (bf16[1,256,4096]{2,1,0:T(8,128)(2,1)S(1)}, bf16[1,256,4096]{2,1,0:T(8,128)(2,1)}, u32[]{:S(2)}) copy-start(bf16[1,256,4096]{2,1,0:T(8,128)(2,1)} %param.12) | copy-start | bytes 6291460
  10.3 4.3 %copy-start.5 = (bf16[1,256,4096]{2,1,0:T(8,128)(2,1)S(1)}, bf16[1,256,4096]{2,1,0:T(8,128)(2,1)}, u32[]{:S(2)}) copy-start(bf16[1,256,4096]{2,1,0:T(8,128)(2,1)} %param.13) | copy-start | bytes 6291460
  10.6 9.4 %collective-permute-start.9 = (bf16[16,4096]{1,0:T(8,128)(2,1)S(1)}, bf16[16,4096]{1,0:T(8,128)(2,1)S(1)}, u32[]{:S(2)}, u32[]{:S(2)}) collective-permute-start(bf16[16,4096]{1,0:T(8,128)(2,1)S(1)} %shard_map.125.refs_0_.refs_3_), channel_id=1, source_target_pairs={{0,3},{1,2},{2,1},{3,0},{4,7},{5,6},{6,5},{7,4},{8,11},{9,10},{10,... | collective-permute-start | bytes 393224 | tf_op jit(solution)/shard_map/ppermute | solution.py:211
  14.0 7.5 %collective-permute-start.8 = (bf16[16,4096]{1,0:T(8,128)(2,1)S(1)}, bf16[16,4096]{1,0:T(8,128)(2,1)S(1)}, u32[]{:S(2)}, u32[]{:S(2)}) collective-permute-start(bf16[16,4096]{1,0:T(8,128)(2,1)S(1)} %shard_map.125.refs_0_.refs_3_), channel_id=1, source_target_pairs={{0,2},{1,3},{2,0},{3,1},{4,6},{5,7},{6,4},{7,5},{8,10},{9,11},{10,... | collective-permute-start | bytes 393224 | tf_op jit(solution)/shard_map/ppermute | solution.py:211
  14.5 7.0 %collective-permute-start.7 = (bf16[16,4096]{1,0:T(8,128)(2,1)S(1)}, bf16[16,4096]{1,0:T(8,128)(2,1)S(1)}, u32[]{:S(2)}, u32[]{:S(2)}) collective-permute-start(bf16[16,4096]{1,0:T(8,128)(2,1)S(1)} %shard_map.125.refs_0_.refs_3_), channel_id=1, source_target_pairs={{0,1},{1,0},{2,3},{3,2},{4,5},{5,4},{6,7},{7,6},{8,9},{9,8},{10,11... | collective-permute-start | bytes 393224 | tf_op jit(solution)/shard_map/ppermute | solution.py:211
  16.5 9.9 %collective-permute-start.3 = (bf16[16,4224]{1,0:T(8,128)(2,1)S(1)}, bf16[16,4224]{1,0:T(8,128)(2,1)S(1)}, u32[]{:S(2)}, u32[]{:S(2)}) collective-permute-start(bf16[16,4224]{1,0:T(8,128)(2,1)S(1)} %get-tuple-element.36), channel_id=1, source_target_pairs={{0,3},{1,2},{2,1},{3,0},{4,7},{5,6},{6,5},{7,4},{8,11},{9,10},{10,... | collective-permute-start | bytes 405512 | tf_op jit(solution)/shard_map/ppermute | solution.py:211
  19.4 9.1 %collective-permute-start.4 = (bf16[16,4224]{1,0:T(8,128)(2,1)S(1)}, bf16[16,4224]{1,0:T(8,128)(2,1)S(1)}, u32[]{:S(2)}, u32[]{:S(2)}) collective-permute-start(bf16[16,4224]{1,0:T(8,128)(2,1)S(1)} %get-tuple-element.37), channel_id=1, source_target_pairs={{0,1},{1,0},{2,3},{3,2},{4,5},{5,4},{6,7},{7,6},{8,9},{9,8},{10,11... | collective-permute-start | bytes 405512 | tf_op jit(solution)/shard_map/ppermute | solution.py:211
  20.0 8.6 %collective-permute-start.5 = (bf16[16,4224]{1,0:T(8,128)(2,1)S(1)}, bf16[16,4224]{1,0:T(8,128)(2,1)S(1)}, u32[]{:S(2)}, u32[]{:S(2)}) collective-permute-start(bf16[16,4224]{1,0:T(8,128)(2,1)S(1)} %get-tuple-element.38), channel_id=1, source_target_pairs={{0,2},{1,3},{2,0},{3,1},{4,6},{5,7},{6,4},{7,5},{8,10},{9,11},{10,... | collective-permute-start | bytes 405512 | tf_op jit(solution)/shard_map/ppermute | solution.py:211
  21.5 6.1 %copy-start.2 = (bf16[1,1,16,4096]{3,2,1,0:T(8,128)(2,1)S(1)}, bf16[1,1,16,4096]{3,2,1,0:T(8,128)(2,1)}, u32[]{:S(2)}) copy-start(bf16[1,1,16,4096]{3,2,1,0:T(8,128)(2,1)} %param.16) | copy-start | bytes 393220
  24.0 5.9 %collective-permute-start.10 = (bf16[16,4096]{1,0:T(8,128)(2,1)S(1)}, bf16[16,4096]{1,0:T(8,128)(2,1)S(1)}, u32[]{:S(2)}, u32[]{:S(2)}) collective-permute-start(bf16[16,4096]{1,0:T(8,128)(2,1)S(1)} %get-tuple-element.43), channel_id=1, source_target_pairs={{0,3},{1,2},{2,1},{3,0},{4,7},{5,6},{6,5},{7,4},{8,11},{9,10},{10,... | collective-permute-start | bytes 393224 | tf_op jit(solution)/shard_map/ppermute | solution.py:211
  25.5 5.4 %collective-permute-start.11 = (bf16[16,4096]{1,0:T(8,128)(2,1)S(1)}, bf16[16,4096]{1,0:T(8,128)(2,1)S(1)}, u32[]{:S(2)}, u32[]{:S(2)}) collective-permute-start(bf16[16,4096]{1,0:T(8,128)(2,1)S(1)} %get-tuple-element.44), channel_id=1, source_target_pairs={{0,1},{1,0},{2,3},{3,2},{4,5},{5,4},{6,7},{7,6},{8,9},{9,8},{10,11... | collective-permute-start | bytes 393224 | tf_op jit(solution)/shard_map/ppermute | solution.py:211
  26.5 5.0 %collective-permute-start.12 = (bf16[16,4096]{1,0:T(8,128)(2,1)S(1)}, bf16[16,4096]{1,0:T(8,128)(2,1)S(1)}, u32[]{:S(2)}, u32[]{:S(2)}) collective-permute-start(bf16[16,4096]{1,0:T(8,128)(2,1)S(1)} %get-tuple-element.45), channel_id=1, source_target_pairs={{0,2},{1,3},{2,0},{3,1},{4,6},{5,7},{6,4},{7,5},{8,10},{9,11},{10,... | collective-permute-start | bytes 393224 | tf_op jit(solution)/shard_map/ppermute | solution.py:211
  28.7 6.3 %collective-permute-start.6 = (bf16[16,4224]{1,0:T(8,128)(2,1)S(1)}, bf16[16,4224]{1,0:T(8,128)(2,1)S(1)}, u32[]{:S(2)}, u32[]{:S(2)}) collective-permute-start(bf16[16,4224]{1,0:T(8,128)(2,1)S(1)} %shard_map.123), channel_id=1, source_target_pairs={{0,4},{1,5},{2,6},{3,7},{4,8},{5,9},{6,10},{7,11},{8,12},{9,13},{1... | collective-permute-start | bytes 405512 | tf_op jit(solution)/shard_map/ppermute | solution.py:211
  31.5 4.8 %collective-permute-start.13 = (bf16[16,4224]{1,0:T(8,128)(2,1)S(1)}, bf16[16,4224]{1,0:T(8,128)(2,1)S(1)}, u32[]{:S(2)}, u32[]{:S(2)}) collective-permute-start(bf16[16,4224]{1,0:T(8,128)(2,1)S(1)} %shard_map.129), channel_id=1, source_target_pairs={{0,28},{1,29},{2,30},{3,31},{4,0},{5,1},{6,2},{7,3},{8,4},{9,5},{1... | collective-permute-start | bytes 405512 | tf_op jit(solution)/shard_map/ppermute | solution.py:211

commit v15 on v13

--- a/solution.py
+++ b/solution.py
@@ -11,7 +11,7 @@
 MOST = 16
 LOWRANK_SCALE = 2.0
 LEVEL_STEP = 1.0 / 4096.0
-CHUNKS = 4
+CHUNKS = 8
 DIAGONAL_FIRST = (3, 1, 2)
 MIB = 1 << 20
 LAST = (((1,), (1,)), ((), ()))
@@ -98,12 +98,21 @@
     rows_ref[...] = (f32dot(picks(place), cot_ref[...]) * gate).astype(jnp.bfloat16)
 
 
-def add_adapter(down_ref, a_ref, b_ref, _, out_ref):
-    width = down_ref.shape[1]
-    span = width // 8
-    for c in range(8):
+def add_adapter(_, down_hbm, a_hbm, b_hbm, out_ref, down_ref, a_ref, b_ref, sems, small_sems):
+    small = [
+        pltpu.make_async_copy(a_hbm, a_ref, small_sems.at[0]),
+        pltpu.make_async_copy(b_hbm, b_ref, small_sems.at[1]),
+    ]
+    for copy in small:
+        copy.start()
+    copies = fetch(down_hbm, down_ref, sems)
+    for copy in small:
+        copy.wait()
+    span = down_ref.shape[1] // CHUNKS
+    for c in range(CHUNKS):
         part = slice(c * span, (c + 1) * span)
         adapter = LOWRANK_SCALE * f32dot(a_ref[...], b_ref[:, part], FIRST)
+        copies[c].wait()
         out_ref[:, part] = (down_ref[:, part].astype(jnp.float32) + adapter).astype(jnp.bfloat16)
 
 
@@ -273,13 +282,21 @@
     x_blocks = [x_rows] + [shifted(x_rows, 0, k) for k in flips[1:]]
 
     near = functools.partial(pltpu.with_memory_space_constraint, memory_space=pltpu.VMEM)
-    gate_near, up_near, down_near, a_near, b_near = map(
-        near, (gate_weight[0], up_weight[0], down_weight[0], down_map, up_map)
+    gate_near, up_near, a_near, b_near = map(
+        near, (gate_weight[0], up_weight[0], down_map, up_map)
     )
     (down_near,) = call(
         add_adapter,
         [sds(units, width)],
-        (down_near, a_near, b_near, place),
+        (place,),
+        (down_weight, down_map, up_map),
+        scratch=[
+            pltpu.VMEM((units, width), jnp.bfloat16),
+            pltpu.VMEM((rank, units), jnp.bfloat16),
+            pltpu.VMEM((rank, width), jnp.bfloat16),
+            dma((CHUNKS,)),
+            dma((2,)),
+        ],
         moved=1,
     )
     (g_rows,) = call(

time: 36.2 us -> 38.7 us (1.069)
  Pallas kernels: 11.7 us -> 15.5 us
  local copies, waits for them, and re-layouts: 0.93 us -> 0.02 us
  starting transfers between devices: 17 us -> 16.3 us
    pallas_call x11, Pallas kernels: 11.7 us -> 15.5 us  [call(): pl.pallas_call(body, out_shape=outs, in_specs=[NEAR] * len(args) + [FAR]...]
    unnamed x12 -> x8, local copies, waits for them, and re-layouts: 0.93 us -> 0.02 us
    ppermute x14, starting transfers between devices: 17 us -> 16.3 us  [shifted(): return lax.ppermute(block, ('section', 'expert'), route)]
  transfers between devices with their start and end apart: 14 -> 14, of which waited for: 5 -> 5; matrix products, arithmetic and copies ran while one was open for 0% -> 0% of each run, Pallas kernels for 24% -> 31%
where the time goes in v15:
time: 38.7 us; the launch traced here: 38.4 us
  starting transfers between devices  16.3 us (42%)
  Pallas kernels  15.5 us (40%)
  waiting for transfers between devices  5.83 us (15%)
  between operations  0.75 us (2%)
    ppermute x14, starting transfers between devices, shifted(): return lax.ppermute(block, ('section', 'expert'), route)  16.3 us
    pallas_call x11, Pallas kernels, call(): pl.pallas_call(body, out_shape=outs, in_specs=[NEAR] * len(args) + [FAR]...  15.5 us
    ppermute x14, waiting for transfers between devices, shifted(): return lax.ppermute(block, ('section', 'expert'), route)  5.83 us
  transfers between devices with their start and end apart: 14, of which 5 were waited for; matrix products, arithmetic and copies ran while one was open for 0% of the time, Pallas kernels for 31%

profile of v15, /device:TPU:0, one launch (start us, length us, event | category | flops | bytes accessed | tf_op | source)
XLA Modules:
  0.0 38.4 jit_solution(14023465337402143813)
XLA Ops:
  0.6 2.4 %shard_map.120 = (bf16[16,4096]{1,0:T(8,128)(2,1)S(1)}, f32[16,128]{1,0:T(8,128)S(1)}, bf16[128,4096]{1,0:T(8,128)(2,1)S(1)}) custom-call(s32[8,128]{1,0:T(8,128)} %bitcast.23, s32[8,128]{1,0:T(8,128)} %bitcast.24, bf16[1,128,4096]{2,1,0:T(8,128)(2,1)} %x_hbm.1, bf16[1,128,4096]{2,1,0:T(8,128)(2,1)} %cot_hbm.1), custom_call_target="tpu_custom_call" | custom-call | flops 16777216 | bytes 3293184 | tf_op jit(solution)/shard_map/pallas_call | solution.py:35
  3.0 4.0 %collective-permute-start.2 = (bf16[16,4096]{1,0:T(8,128)(2,1)S(1)}, bf16[16,4096]{1,0:T(8,128)(2,1)S(1)}, u32[]{:S(2)}, u32[]{:S(2)}) collective-permute-start(bf16[16,4096]{1,0:T(8,128)(2,1)S(1)} %get-tuple-element.30.refs_0_), channel_id=1, source_target_pairs={{0,3},{1,2},{2,1},{3,0},{4,7},{5,6},{6,5},{7,4},{8,11},{9,10},{10,... | collective-permute-start | bytes 393224 | tf_op jit(solution)/shard_map/ppermute | solution.py:220
  7.0 0.5 %collective-permute-start.1 = (bf16[16,4096]{1,0:T(8,128)(2,1)S(1)}, bf16[16,4096]{1,0:T(8,128)(2,1)S(1)}, u32[]{:S(2)}, u32[]{:S(2)}) collective-permute-start(bf16[16,4096]{1,0:T(8,128)(2,1)S(1)} %get-tuple-element.30.refs_0_), channel_id=1, source_target_pairs={{0,2},{1,3},{2,0},{3,1},{4,6},{5,7},{6,4},{7,5},{8,10},{9,11},{10,... | collective-permute-start | bytes 393224 | tf_op jit(solution)/shard_map/ppermute | solution.py:220
  7.5 0.1 collective-permute-start
  7.6 4.0 %shard_map.121.refs_6_._.refs_8_ = bf16[256,4096]{1,0:T(8,128)(2,1)S(1)} custom-call(f32[16,128]{1,0:T(8,128)S(1)} %get-tuple-element.29._.place_ref, bf16[1,256,4096]{2,1,0:T(8,128)(2,1)} %down_hbm.1, bf16[16,256]{1,0:T(8,128)(2,1)} %bitcast.17, bf16[16,4096]{1,0:T(8,128)(2,1)} %bitcast.15), custom_call_target="tpu_custom_call" | custom-call | bytes 1 | tf_op jit(solution)/shard_map/pallas_call | solution.py:35
  11.6 0.0 copy-start.1
  11.6 0.0 copy-start.2
  11.6 0.0 copy-start.3
  11.6 0.3 shard_map.125.refs_0_.refs_3_
  11.8 2.9 %collective-permute-start.9 = (bf16[16,4096]{1,0:T(8,128)(2,1)S(1)}, bf16[16,4096]{1,0:T(8,128)(2,1)S(1)}, u32[]{:S(2)}, u32[]{:S(2)}) collective-permute-start(bf16[16,4096]{1,0:T(8,128)(2,1)S(1)} %shard_map.125.refs_0_.refs_3_), channel_id=1, source_target_pairs={{0,3},{1,2},{2,1},{3,0},{4,7},{5,6},{6,5},{7,4},{8,11},{9,10},{10,... | collective-permute-start | bytes 393224 | tf_op jit(solution)/shard_map/ppermute | solution.py:220
  14.8 0.5 %collective-permute-start.8 = (bf16[16,4096]{1,0:T(8,128)(2,1)S(1)}, bf16[16,4096]{1,0:T(8,128)(2,1)S(1)}, u32[]{:S(2)}, u32[]{:S(2)}) collective-permute-start(bf16[16,4096]{1,0:T(8,128)(2,1)S(1)} %shard_map.125.refs_0_.refs_3_), channel_id=1, source_target_pairs={{0,2},{1,3},{2,0},{3,1},{4,6},{5,7},{6,4},{7,5},{8,10},{9,11},{10,... | collective-permute-start | bytes 393224 | tf_op jit(solution)/shard_map/ppermute | solution.py:220
  15.3 0.1 collective-permute-start.7
  15.4 1.9 %shard_map.122 = (bf16[16,4096]{1,0:T(8,128)(2,1)S(1)}, bf16[16,4224]{1,0:T(8,128)(2,1)S(1)}, bf16[16,4224]{1,0:T(8,128)(2,1)S(1)}, bf16[16,4224]{1,0:T(8,128)(2...) custom-call(bf16[16,4096]{1,0:T(8,128)(2,1)S(1)} %get-tuple-element., ...), custom_call_target="tpu_custom_call" | custom-call | flops 4026531840 | bytes 7526400 | tf_op jit(solution)/shard_map/pallas_call | solution.py:35
  17.3 2.9 %collective-permute-start.3 = (bf16[16,4224]{1,0:T(8,128)(2,1)S(1)}, bf16[16,4224]{1,0:T(8,128)(2,1)S(1)}, u32[]{:S(2)}, u32[]{:S(2)}) collective-permute-start(bf16[16,4224]{1,0:T(8,128)(2,1)S(1)} %get-tuple-element.32), channel_id=1, source_target_pairs={{0,3},{1,2},{2,1},{3,0},{4,7},{5,6},{6,5},{7,4},{8,11},{9,10},{10,... | collective-permute-start | bytes 405512 | tf_op jit(solution)/shard_map/ppermute | solution.py:220
  20.2 0.5 %collective-permute-start.4 = (bf16[16,4224]{1,0:T(8,128)(2,1)S(1)}, bf16[16,4224]{1,0:T(8,128)(2,1)S(1)}, u32[]{:S(2)}, u32[]{:S(2)}) collective-permute-start(bf16[16,4224]{1,0:T(8,128)(2,1)S(1)} %get-tuple-element.33), channel_id=1, source_target_pairs={{0,1},{1,0},{2,3},{3,2},{4,5},{5,4},{6,7},{7,6},{8,9},{9,8},{10,11... | collective-permute-start | bytes 405512 | tf_op jit(solution)/shard_map/ppermute | solution.py:220
  20.7 0.1 collective-permute-start.5
  20.8 1.2 %collective-permute-done.8.refs_2_.refs_5_ = bf16[16,4096]{1,0:T(8,128)(2,1)S(1)} collective-permute-done((bf16[16,4096]{1,0:T(8,128)(2,1)S(1)}, bf16[16,4096]{1,0:T(8,128)(2,1)S(1)}, u32[]{:S(2)}, u32[]{:S(2)}) %collective-permute-start.8) | collective-permute-done | bytes 131104 | tf_op jit(solution)/shard_map/ppermute | solution.py:220
  22.1 2.5 %shard_map.126 = (bf16[16,4096]{1,0:T(8,128)(2,1)S(1)}, bf16[16,4096]{1,0:T(8,128)(2,1)S(1)}, bf16[16,4096]{1,0:T(8,128)(2,1)S(1)}, bf16[16,4096]{1,0:T(8,128)(2,1)S(1)}) custom-call(bf16[16,4096]{1,0:T(8,128)(2,1)S(1)} %shard_map.125.refs_0_.refs_3_, bf16[16,4096]{1,0:T(8,128)(2,1)S(1)} %collective-permute-done.7.refs_1_.refs_4_, ...), custom_call_target="tpu_custom_call" | custom-call | flops 4026531840 | bytes 7471104 | tf_op jit(solution)/shard_map/pallas_call | solution.py:35
  24.6 1.7 %collective-permute-start.10 = (bf16[16,4096]{1,0:T(8,128)(2,1)S(1)}, bf16[16,4096]{1,0:T(8,128)(2,1)S(1)}, u32[]{:S(2)}, u32[]{:S(2)}) collective-permute-start(bf16[16,4096]{1,0:T(8,128)(2,1)S(1)} %get-tuple-element.39), channel_id=1, source_target_pairs={{0,3},{1,2},{2,1},{3,0},{4,7},{5,6},{6,5},{7,4},{8,11},{9,10},{10,... | collective-permute-start | bytes 393224 | tf_op jit(solution)/shard_map/ppermute | solution.py:220
  26.3 2.2 %collective-permute-start.11 = (bf16[16,4096]{1,0:T(8,128)(2,1)S(1)}, bf16[16,4096]{1,0:T(8,128)(2,1)S(1)}, u32[]{:S(2)}, u32[]{:S(2)}) collective-permute-start(bf16[16,4096]{1,0:T(8,128)(2,1)S(1)} %get-tuple-element.40), channel_id=1, source_target_pairs={{0,1},{1,0},{2,3},{3,2},{4,5},{5,4},{6,7},{7,6},{8,9},{9,8},{10,11... | collective-permute-start | bytes 393224 | tf_op jit(solution)/shard_map/ppermute | solution.py:220
  28.4 1.0 %shard_map.127 = f32[16,256]{1,0:T(8,128)} custom-call(bf16[16,4096]{1,0:T(8,128)(2,1)S(1)} %shard_map.125.refs_0_.refs_3_, bf16[16,4096]{1,0:T(8,128)(2,1)S(1)} %collective-permute-done.7.refs_1_.refs_4_, bf16[16,4096]{1,0:T(8,128)(2,1)S(1)} %collective-permute-done.8.refs_2_.refs_5_, bf16[16,4096]{1,0:T(8,128)(2,1)S(1)} %collective-permute-done.9.refs_3_.refs_6_, ...), custom_call_target="tpu_custom_call" | custom-call | flops 838860800 | bytes 704512 | tf_op jit(solution)/shard_map/pallas_call | solution.py:35
  29.5 0.1 shard_map.123
  29.6 0.1 collective-permute-start.6
  29.7 0.9 %shard_map.128 = f32[1,1,16,1024]{3,2,1,0:T(8,128)} custom-call(bf16[16,64]{1,0:T(8,128)(2,1)S(1)} %get-tuple-element.45.latent_ref, bf16[16,4224]{1,0:T(8,128)(2,1)S(1)} %collective-permute-done.3.refs_1_.refs_0_, bf16[16,4224]{1,0:T(8,128)(2,1)S(1)} %collective-permute-done.4.refs_2_.refs_1_, bf16[16,4224]{1,0:T(8,128)(2,1)S(1)} %collective-permute-done.5.refs_3_.refs_2_, ...), custom_call_target="tpu_custom_call" | custom-call | flops 838860800 | bytes 997376 | tf_op jit(solution)/shard_map/pallas_call | solution.py:35
  30.5 0.2 collective-permute-done.10.refs_1_
  30.7 2.1 %collective-permute-done.11.refs_2_ = bf16[16,4096]{1,0:T(8,128)(2,1)S(1)} collective-permute-done((bf16[16,4096]{1,0:T(8,128)(2,1)S(1)}, bf16[16,4096]{1,0:T(8,128)(2,1)S(1)}, u32[]{:S(2)}, u32[]{:S(2)}) %collective-permute-start.11) | collective-permute-done | bytes 131104 | tf_op jit(solution)/shard_map/ppermute | solution.py:220
  32.8 0.6 %collective-permute-done.12.refs_3_ = bf16[16,4096]{1,0:T(8,128)(2,1)S(1)} collective-permute-done((bf16[16,4096]{1,0:T(8,128)(2,1)S(1)}, bf16[16,4096]{1,0:T(8,128)(2,1)S(1)}, u32[]{:S(2)}, u32[]{:S(2)}) %collective-permute-start.12) | collective-permute-done | bytes 131104 | tf_op jit(solution)/shard_map/ppermute | solution.py:220
  33.4 0.1 shard_map.129
  33.5 0.7 %collective-permute-start.13 = (bf16[16,4224]{1,0:T(8,128)(2,1)S(1)}, bf16[16,4224]{1,0:T(8,128)(2,1)S(1)}, u32[]{:S(2)}, u32[]{:S(2)}) collective-permute-start(bf16[16,4224]{1,0:T(8,128)(2,1)S(1)} %shard_map.129), channel_id=1, source_target_pairs={{0,28},{1,29},{2,30},{3,31},{4,0},{5,1},{6,2},{7,3},{8,4},{9,5},{1... | collective-permute-start | bytes 405512 | tf_op jit(solution)/shard_map/ppermute | solution.py:220
  34.2 1.7 %collective-permute-done.6.message_ref = bf16[16,4224]{1,0:T(8,128)(2,1)S(1)} collective-permute-done((bf16[16,4224]{1,0:T(8,128)(2,1)S(1)}, bf16[16,4224]{1,0:T(8,128)(2,1)S(1)}, u32[]{:S(2)}, u32[]{:S(2)}) %collective-permute-start.6) | collective-permute-done | bytes 135200 | tf_op jit(solution)/shard_map/ppermute | solution.py:220
  35.9 1.2 %shard_map.124 = bf16[1,128,4096]{2,1,0:T(8,128)(2,1)} custom-call(bf16[16,4224]{1,0:T(8,128)(2,1)S(1)} %collective-permute-done.6.message_ref), custom_call_target="tpu_custom_call" | custom-call | flops 16777216 | bytes 1183744 | tf_op jit(solution)/shard_map/pallas_call | solution.py:35
  37.1 1.2 %shard_map.130 = bf16[1,128,4096]{2,1,0:T(8,128)(2,1)} custom-call(bf16[16,4224]{1,0:T(8,128)(2,1)S(1)} %collective-permute-done.13.message_ref), custom_call_target="tpu_custom_call" | custom-call | flops 16777216 | bytes 1183744 | tf_op jit(solution)/shard_map/pallas_call | solution.py:35
  (15 shorter events, 0.0 us)
Async XLA Ops:
  3.0 12.3 %collective-permute-start.2 = (bf16[16,4096]{1,0:T(8,128)(2,1)S(1)}, bf16[16,4096]{1,0:T(8,128)(2,1)S(1)}, u32[]{:S(2)}, u32[]{:S(2)}) collective-permute-start(bf16[16,4096]{1,0:T(8,128)(2,1)S(1)} %get-tuple-element.30.refs_0_), channel_id=1, source_target_pairs={{0,3},{1,2},{2,1},{3,0},{4,7},{5,6},{6,5},{7,4},{8,11},{9,10},{10,... | collective-permute-start | bytes 393224 | tf_op jit(solution)/shard_map/ppermute | solution.py:220
  7.0 8.4 %collective-permute-start.1 = (bf16[16,4096]{1,0:T(8,128)(2,1)S(1)}, bf16[16,4096]{1,0:T(8,128)(2,1)S(1)}, u32[]{:S(2)}, u32[]{:S(2)}) collective-permute-start(bf16[16,4096]{1,0:T(8,128)(2,1)S(1)} %get-tuple-element.30.refs_0_), channel_id=1, source_target_pairs={{0,2},{1,3},{2,0},{3,1},{4,6},{5,7},{6,4},{7,5},{8,10},{9,11},{10,... | collective-permute-start | bytes 393224 | tf_op jit(solution)/shard_map/ppermute | solution.py:220
  7.5 7.9 %collective-permute-start = (bf16[16,4096]{1,0:T(8,128)(2,1)S(1)}, bf16[16,4096]{1,0:T(8,128)(2,1)S(1)}, u32[]{:S(2)}, u32[]{:S(2)}) collective-permute-start(bf16[16,4096]{1,0:T(8,128)(2,1)S(1)} %get-tuple-element.30.refs_0_), channel_id=1, source_target_pairs={{0,1},{1,0},{2,3},{3,2},{4,5},{5,4},{6,7},{7,6},{8,9},{9,8},{10,11... | collective-permute-start | bytes 393224 | tf_op jit(solution)/shard_map/ppermute | solution.py:220
  11.6 3.8 %copy-start.1 = (bf16[1,256,16]{1,2,0:T(8,128)(2,1)S(1)}, bf16[1,256,16]{1,2,0:T(8,128)(2,1)}, u32[]{:S(2)}) copy-start(bf16[1,256,16]{1,2,0:T(8,128)(2,1)} %param.15) | copy-start | bytes 24580
  11.6 3.8 %copy-start.2 = (bf16[1,256,4096]{2,1,0:T(8,128)(2,1)S(1)}, bf16[1,256,4096]{2,1,0:T(8,128)(2,1)}, u32[]{:S(2)}) copy-start(bf16[1,256,4096]{2,1,0:T(8,128)(2,1)} %param.12) | copy-start | bytes 6291460
  11.6 3.8 %copy-start.3 = (bf16[1,256,4096]{2,1,0:T(8,128)(2,1)S(1)}, bf16[1,256,4096]{2,1,0:T(8,128)(2,1)}, u32[]{:S(2)}) copy-start(bf16[1,256,4096]{2,1,0:T(8,128)(2,1)} %param.13) | copy-start | bytes 6291460
  11.8 8.9 %collective-permute-start.9 = (bf16[16,4096]{1,0:T(8,128)(2,1)S(1)}, bf16[16,4096]{1,0:T(8,128)(2,1)S(1)}, u32[]{:S(2)}, u32[]{:S(2)}) collective-permute-start(bf16[16,4096]{1,0:T(8,128)(2,1)S(1)} %shard_map.125.refs_0_.refs_3_), channel_id=1, source_target_pairs={{0,3},{1,2},{2,1},{3,0},{4,7},{5,6},{6,5},{7,4},{8,11},{9,10},{10,... | collective-permute-start | bytes 393224 | tf_op jit(solution)/shard_map/ppermute | solution.py:220
  14.8 7.3 %collective-permute-start.8 = (bf16[16,4096]{1,0:T(8,128)(2,1)S(1)}, bf16[16,4096]{1,0:T(8,128)(2,1)S(1)}, u32[]{:S(2)}, u32[]{:S(2)}) collective-permute-start(bf16[16,4096]{1,0:T(8,128)(2,1)S(1)} %shard_map.125.refs_0_.refs_3_), channel_id=1, source_target_pairs={{0,2},{1,3},{2,0},{3,1},{4,6},{5,7},{6,4},{7,5},{8,10},{9,11},{10,... | collective-permute-start | bytes 393224 | tf_op jit(solution)/shard_map/ppermute | solution.py:220
  15.3 6.8 %collective-permute-start.7 = (bf16[16,4096]{1,0:T(8,128)(2,1)S(1)}, bf16[16,4096]{1,0:T(8,128)(2,1)S(1)}, u32[]{:S(2)}, u32[]{:S(2)}) collective-permute-start(bf16[16,4096]{1,0:T(8,128)(2,1)S(1)} %shard_map.125.refs_0_.refs_3_), channel_id=1, source_target_pairs={{0,1},{1,0},{2,3},{3,2},{4,5},{5,4},{6,7},{7,6},{8,9},{9,8},{10,11... | collective-permute-start | bytes 393224 | tf_op jit(solution)/shard_map/ppermute | solution.py:220
  17.3 11.1 %collective-permute-start.3 = (bf16[16,4224]{1,0:T(8,128)(2,1)S(1)}, bf16[16,4224]{1,0:T(8,128)(2,1)S(1)}, u32[]{:S(2)}, u32[]{:S(2)}) collective-permute-start(bf16[16,4224]{1,0:T(8,128)(2,1)S(1)} %get-tuple-element.32), channel_id=1, source_target_pairs={{0,3},{1,2},{2,1},{3,0},{4,7},{5,6},{6,5},{7,4},{8,11},{9,10},{10,... | collective-permute-start | bytes 405512 | tf_op jit(solution)/shard_map/ppermute | solution.py:220
  20.2 9.3 %collective-permute-start.4 = (bf16[16,4224]{1,0:T(8,128)(2,1)S(1)}, bf16[16,4224]{1,0:T(8,128)(2,1)S(1)}, u32[]{:S(2)}, u32[]{:S(2)}) collective-permute-start(bf16[16,4224]{1,0:T(8,128)(2,1)S(1)} %get-tuple-element.33), channel_id=1, source_target_pairs={{0,1},{1,0},{2,3},{3,2},{4,5},{5,4},{6,7},{7,6},{8,9},{9,8},{10,11... | collective-permute-start | bytes 405512 | tf_op jit(solution)/shard_map/ppermute | solution.py:220
  20.7 8.8 %collective-permute-start.5 = (bf16[16,4224]{1,0:T(8,128)(2,1)S(1)}, bf16[16,4224]{1,0:T(8,128)(2,1)S(1)}, u32[]{:S(2)}, u32[]{:S(2)}) collective-permute-start(bf16[16,4224]{1,0:T(8,128)(2,1)S(1)} %get-tuple-element.34), channel_id=1, source_target_pairs={{0,2},{1,3},{2,0},{3,1},{4,6},{5,7},{6,4},{7,5},{8,10},{9,11},{10,... | collective-permute-start | bytes 405512 | tf_op jit(solution)/shard_map/ppermute | solution.py:220
  22.1 6.4 %copy-start = (bf16[1,1,16,4096]{3,2,1,0:T(8,128)(2,1)S(1)}, bf16[1,1,16,4096]{3,2,1,0:T(8,128)(2,1)}, u32[]{:S(2)}) copy-start(bf16[1,1,16,4096]{3,2,1,0:T(8,128)(2,1)} %param.16) | copy-start | bytes 393220
  24.6 6.1 %collective-permute-start.10 = (bf16[16,4096]{1,0:T(8,128)(2,1)S(1)}, bf16[16,4096]{1,0:T(8,128)(2,1)S(1)}, u32[]{:S(2)}, u32[]{:S(2)}) collective-permute-start(bf16[16,4096]{1,0:T(8,128)(2,1)S(1)} %get-tuple-element.39), channel_id=1, source_target_pairs={{0,3},{1,2},{2,1},{3,0},{4,7},{5,6},{6,5},{7,4},{8,11},{9,10},{10,... | collective-permute-start | bytes 393224 | tf_op jit(solution)/shard_map/ppermute | solution.py:220
  26.3 6.5 %collective-permute-start.11 = (bf16[16,4096]{1,0:T(8,128)(2,1)S(1)}, bf16[16,4096]{1,0:T(8,128)(2,1)S(1)}, u32[]{:S(2)}, u32[]{:S(2)}) collective-permute-start(bf16[16,4096]{1,0:T(8,128)(2,1)S(1)} %get-tuple-element.40), channel_id=1, source_target_pairs={{0,1},{1,0},{2,3},{3,2},{4,5},{5,4},{6,7},{7,6},{8,9},{9,8},{10,11... | collective-permute-start | bytes 393224 | tf_op jit(solution)/shard_map/ppermute | solution.py:220
  28.4 5.0 %collective-permute-start.12 = (bf16[16,4096]{1,0:T(8,128)(2,1)S(1)}, bf16[16,4096]{1,0:T(8,128)(2,1)S(1)}, u32[]{:S(2)}, u32[]{:S(2)}) collective-permute-start(bf16[16,4096]{1,0:T(8,128)(2,1)S(1)} %get-tuple-element.41), channel_id=1, source_target_pairs={{0,2},{1,3},{2,0},{3,1},{4,6},{5,7},{6,4},{7,5},{8,10},{9,11},{10,... | collective-permute-start | bytes 393224 | tf_op jit(solution)/shard_map/ppermute | solution.py:220
  29.6 6.3 %collective-permute-start.6 = (bf16[16,4224]{1,0:T(8,128)(2,1)S(1)}, bf16[16,4224]{1,0:T(8,128)(2,1)S(1)}, u32[]{:S(2)}, u32[]{:S(2)}) collective-permute-start(bf16[16,4224]{1,0:T(8,128)(2,1)S(1)} %shard_map.123), channel_id=1, source_target_pairs={{0,4},{1,5},{2,6},{3,7},{4,8},{5,9},{6,10},{7,11},{8,12},{9,13},{1... | collective-permute-start | bytes 405512 | tf_op jit(solution)/shard_map/ppermute | solution.py:220
  33.5 3.7 %collective-permute-start.13 = (bf16[16,4224]{1,0:T(8,128)(2,1)S(1)}, bf16[16,4224]{1,0:T(8,128)(2,1)S(1)}, u32[]{:S(2)}, u32[]{:S(2)}) collective-permute-start(bf16[16,4224]{1,0:T(8,128)(2,1)S(1)} %shard_map.129), channel_id=1, source_target_pairs={{0,28},{1,29},{2,30},{3,31},{4,0},{5,1},{6,2},{7,3},{8,4},{9,5},{1... | collective-permute-start | bytes 405512 | tf_op jit(solution)/shard_map/ppermute | solution.py:220

commit v16 on v13

--- a/solution.py
+++ b/solution.py
@@ -47,18 +47,8 @@
     return jnp.where(place > 0, 1.0, 0.0).astype(jnp.bfloat16)
 
 
-def fetch(hbm, ref, sems):
-    span = ref.shape[1] // CHUNKS
-    copies = []
-    for c in range(CHUNKS):
-        part = pl.ds(c * span, span)
-        copies.append(pltpu.make_async_copy(hbm.at[0, :, part], ref.at[:, part], sems.at[c]))
-        copies[-1].start()
-    return copies
-
-
-def gather(flight, choice_hbm, steps_hbm, x_hbm, cot_hbm, *refs):
-    rows_ref, place_ref, cot_ref, choice_ref, steps_ref, x_ref, *sems = refs
+def gather(flight, choice_hbm, steps_hbm, x_hbm, cot_hbm, a_hbm, b_hbm, *refs):
+    rows_ref, place_ref, cot_ref, a_ref, b_ref, choice_ref, steps_ref, x_ref, *sems = refs
     tokens, width = x_ref.shape
     span = width // CHUNKS
     small = [
@@ -67,9 +57,20 @@
     ]
     for copy in small:
         copy.start()
-    copies = fetch(x_hbm, x_ref, sems[1])
-    cot_copy = pltpu.make_async_copy(cot_hbm.at[0], cot_ref, sems[0].at[2])
-    cot_copy.start()
+    band = tokens // CHUNKS
+    copies = []
+    for c in range(CHUNKS):
+        bands = pl.ds(c * band, band)
+        copy = pltpu.make_async_copy(x_hbm.at[0, bands, :], x_ref.at[bands, :], sems[1].at[c])
+        copy.start()
+        copies.append(copy)
+    later = [
+        pltpu.make_async_copy(cot_hbm.at[0], cot_ref, sems[0].at[2]),
+        pltpu.make_async_copy(a_hbm, a_ref, sems[0].at[3]),
+        pltpu.make_async_copy(b_hbm, b_ref, sems[0].at[4]),
+    ]
+    for copy in later:
+        copy.start()
     before = lax.broadcasted_iota(jnp.int32, (tokens, tokens), 0) < lax.broadcasted_iota(
         jnp.int32, (tokens, tokens), 1
     )
@@ -85,11 +86,13 @@
         index = f32dot(routed.astype(jnp.bfloat16), before)
         place_ref[f * MOST:(f + 1) * MOST, :] = jnp.where(slot == index, level * LEVEL_STEP, 0.0)
     pick = picks(place_ref[...])
+    for copy in copies:
+        copy.wait()
     for c in range(CHUNKS):
-        copies[c].wait()
         part = slice(c * span, (c + 1) * span)
         rows_ref[:, part] = f32dot(pick, x_ref[:, part]).astype(jnp.bfloat16)
-    cot_copy.wait()
+    for copy in later:
+        copy.wait()
 
 
 def gather_grads(place_ref, cot_ref, _, rows_ref):
@@ -98,13 +101,23 @@
     rows_ref[...] = (f32dot(picks(place), cot_ref[...]) * gate).astype(jnp.bfloat16)
 
 
-def add_adapter(down_ref, a_ref, b_ref, _, out_ref):
-    width = down_ref.shape[1]
-    span = width // 8
-    for c in range(8):
-        part = slice(c * span, (c + 1) * span)
-        adapter = LOWRANK_SCALE * f32dot(a_ref[...], b_ref[:, part], FIRST)
-        out_ref[:, part] = (down_ref[:, part].astype(jnp.float32) + adapter).astype(jnp.bfloat16)
+def add_adapter(a_ref, b_ref, down_hbm, out_ref, down_ref, sems):
+    units, width = down_ref.shape
+    band, span = units // 2, 512
+    copies = []
+    for i in range(2):
+        bands = pl.ds(i * band, band)
+        copy = pltpu.make_async_copy(down_hbm.at[0, bands, :], down_ref.at[bands, :], sems.at[i])
+        copy.start()
+        copies.append(copy)
+    for i in range(2):
+        copies[i].wait()
+        lines = slice(i * band, (i + 1) * band)
+        for c in range(width // span):
+            part = slice(c * span, (c + 1) * span)
+            adapter = LOWRANK_SCALE * f32dot(a_ref[:, lines], b_ref[:, part], FIRST)
+            total = down_ref[lines, part].astype(jnp.float32) + adapter
+            out_ref[lines, part] = total.astype(jnp.bfloat16)
 
 
 def forward(*refs):
@@ -246,12 +259,14 @@
         up_map = lax.dynamic_index_in_dim(adapter_up_maps[0], group, 0, keepdims=False)
     down_map = jnp.swapaxes(adapter_down_maps[0], 0, 1)
 
-    x_rows, place, cot_near = call(
+    x_rows, place, cot_near, a_near, b_near = call(
         functools.partial(gather, flight),
         [
             sds(slots, width),
             sds(slots, tokens, dtype=jnp.float32),
             sds(tokens, width),
+            sds(rank, units),
+            sds(rank, width),
         ],
         (),
         (
@@ -259,12 +274,14 @@
             jnp.swapaxes(route_gate_steps[0], 0, 1),
             section_layer_input,
             cotangent,
+            down_map,
+            up_map,
         ),
         scratch=[
             pltpu.VMEM((top, tokens), jnp.int32),
             pltpu.VMEM((top, tokens), jnp.int32),
             pltpu.VMEM((tokens, width), jnp.bfloat16),
-            dma((3,)),
+            dma((5,)),
             dma((CHUNKS,)),
         ],
         flops=2 * slots * tokens * width,
@@ -273,13 +290,13 @@
     x_blocks = [x_rows] + [shifted(x_rows, 0, k) for k in flips[1:]]
 
     near = functools.partial(pltpu.with_memory_space_constraint, memory_space=pltpu.VMEM)
-    gate_near, up_near, down_near, a_near, b_near = map(
-        near, (gate_weight[0], up_weight[0], down_weight[0], down_map, up_map)
-    )
+    gate_near, up_near = map(near, (gate_weight[0], up_weight[0]))
     (down_near,) = call(
         add_adapter,
         [sds(units, width)],
-        (down_near, a_near, b_near, place),
+        (a_near, b_near),
+        (down_weight,),
+        scratch=[pltpu.VMEM((units, width), jnp.bfloat16), dma((2,))],
         moved=1,
     )
     (g_rows,) = call(

time: 36.2 us -> 36.6 us (1.011)
  Pallas kernels: 11.7 us -> 13.2 us
  waiting for transfers between devices: 5.72 us -> 4.53 us
  starting transfers between devices: 17 us -> 18 us
  local copies, waits for them, and re-layouts: 0.93 us -> 0.01 us
    pallas_call x11, Pallas kernels: 11.7 us -> 13.2 us  [call(): pl.pallas_call(body, out_shape=outs, in_specs=[NEAR] * len(args) + [FAR]...]
    ppermute x14, waiting for transfers between devices: 5.72 us -> 4.53 us  [shifted(): return lax.ppermute(block, ('section', 'expert'), route)]
    ppermute x14, starting transfers between devices: 17 us -> 18 us  [shifted(): return lax.ppermute(block, ('section', 'expert'), route)]
    unnamed x12 -> x4, local copies, waits for them, and re-layouts: 0.93 us -> 0.01 us
  transfers between devices with their start and end apart: 14 -> 14, of which waited for: 5 -> 8; matrix products, arithmetic and copies ran while one was open for 0% -> 0% of each run, Pallas kernels for 24% -> 28%
where the time goes in v16:
time: 36.6 us; the launch traced here: 36.4 us
  starting transfers between devices  18 us (49%)
  Pallas kernels  13.2 us (36%)
  waiting for transfers between devices  4.53 us (12%)
  between operations  0.71 us (2%)
    ppermute x14, starting transfers between devices, shifted(): return lax.ppermute(block, ('section', 'expert'), route)  18 us
    pallas_call x11, Pallas kernels, call(): pl.pallas_call(body, out_shape=outs, in_specs=[NEAR] * len(args) + [FAR]...  13.2 us
    ppermute x14, waiting for transfers between devices, shifted(): return lax.ppermute(block, ('section', 'expert'), route)  4.53 us
  transfers between devices with their start and end apart: 14, of which 8 were waited for; matrix products, arithmetic and copies ran while one was open for 0% of the time, Pallas kernels for 28%

profile of v16, /device:TPU:0, one launch (start us, length us, event | category | flops | bytes accessed | tf_op | source)
XLA Modules:
  0.0 36.4 jit_solution(14836132583116297530)
XLA Ops:
  0.6 1.9 %shard_map.120 = (bf16[16,4096]{1,0:T(8,128)(2,1)S(1)}, f32[16,128]{1,0:T(8,128)S(1)}, bf16[128,4096]{1,0:T(8,128)(2,1)S(1)}, bf16[16,256]{1,0:T(8,128)(2,1)S(1)}, bf16[16,4096]{1,0:T(8,128)(2,1)S(1)}) custom-call(s32[8,128]{1,0:T(8,128)} %bitcast.21, s32[8,128]{1,0:T(8,128)} %bitcast.22, bf16[1,128,4096]{2,1,0:T(8,128)(2,1)} %x_hbm.1, ...), custom_call_target="tpu_custom_call" | custom-call | flops 16777216 | bytes 3571712 | tf_op jit(solution)/shard_map/pallas_call | solution.py:35
  2.5 4.0 %collective-permute-start.2 = (bf16[16,4096]{1,0:T(8,128)(2,1)S(1)}, bf16[16,4096]{1,0:T(8,128)(2,1)S(1)}, u32[]{:S(2)}, u32[]{:S(2)}) collective-permute-start(bf16[16,4096]{1,0:T(8,128)(2,1)S(1)} %get-tuple-element.32.refs_0_), channel_id=1, source_target_pairs={{0,3},{1,2},{2,1},{3,0},{4,7},{5,6},{6,5},{7,4},{8,11},{9,10},{10,... | collective-permute-start | bytes 393224 | tf_op jit(solution)/shard_map/ppermute | solution.py:224
  6.5 0.5 %collective-permute-start.1 = (bf16[16,4096]{1,0:T(8,128)(2,1)S(1)}, bf16[16,4096]{1,0:T(8,128)(2,1)S(1)}, u32[]{:S(2)}, u32[]{:S(2)}) collective-permute-start(bf16[16,4096]{1,0:T(8,128)(2,1)S(1)} %get-tuple-element.32.refs_0_), channel_id=1, source_target_pairs={{0,2},{1,3},{2,0},{3,1},{4,6},{5,7},{6,4},{7,5},{8,10},{9,11},{10,... | collective-permute-start | bytes 393224 | tf_op jit(solution)/shard_map/ppermute | solution.py:224
  7.0 0.1 collective-permute-start
  7.1 2.2 %shard_map.121.refs_6_._.refs_8_ = bf16[256,4096]{1,0:T(8,128)(2,1)S(1)} custom-call(bf16[16,256]{1,0:T(8,128)(2,1)S(1)} %get-tuple-element.33.a_ref.refs_7_, bf16[16,4096]{1,0:T(8,128)(2,1)S(1)} %get-tuple-element.34.b_ref.refs_5_, bf16[1,256,4096]{2,1,0:T(8,128)(2,1)} %down_hbm.1), custom_call_target="tpu_custom_call" | custom-call | bytes 1 | tf_op jit(solution)/shard_map/pallas_call | solution.py:35
  9.3 0.3 shard_map.125.refs_0_.refs_3_
  9.6 2.9 %collective-permute-start.9 = (bf16[16,4096]{1,0:T(8,128)(2,1)S(1)}, bf16[16,4096]{1,0:T(8,128)(2,1)S(1)}, u32[]{:S(2)}, u32[]{:S(2)}) collective-permute-start(bf16[16,4096]{1,0:T(8,128)(2,1)S(1)} %shard_map.125.refs_0_.refs_3_), channel_id=1, source_target_pairs={{0,3},{1,2},{2,1},{3,0},{4,7},{5,6},{6,5},{7,4},{8,11},{9,10},{10,... | collective-permute-start | bytes 393224 | tf_op jit(solution)/shard_map/ppermute | solution.py:224
  12.5 0.5 %collective-permute-start.8 = (bf16[16,4096]{1,0:T(8,128)(2,1)S(1)}, bf16[16,4096]{1,0:T(8,128)(2,1)S(1)}, u32[]{:S(2)}, u32[]{:S(2)}) collective-permute-start(bf16[16,4096]{1,0:T(8,128)(2,1)S(1)} %shard_map.125.refs_0_.refs_3_), channel_id=1, source_target_pairs={{0,2},{1,3},{2,0},{3,1},{4,6},{5,7},{6,4},{7,5},{8,10},{9,11},{10,... | collective-permute-start | bytes 393224 | tf_op jit(solution)/shard_map/ppermute | solution.py:224
  13.0 0.1 collective-permute-start.7
  13.1 0.1 collective-permute-done.1.refs_2_
  13.2 0.2 collective-permute-done.refs_1_
  13.5 1.8 %shard_map.122 = (bf16[16,4096]{1,0:T(8,128)(2,1)S(1)}, bf16[16,4224]{1,0:T(8,128)(2,1)S(1)}, bf16[16,4224]{1,0:T(8,128)(2,1)S(1)}, bf16[16,4224]{1,0:T(8,128)(2...) custom-call(bf16[16,4096]{1,0:T(8,128)(2,1)S(1)} %get-tuple-element., ...), custom_call_target="tpu_custom_call" | custom-call | flops 4026531840 | bytes 7526400 | tf_op jit(solution)/shard_map/pallas_call | solution.py:35
  15.3 2.6 %collective-permute-start.3 = (bf16[16,4224]{1,0:T(8,128)(2,1)S(1)}, bf16[16,4224]{1,0:T(8,128)(2,1)S(1)}, u32[]{:S(2)}, u32[]{:S(2)}) collective-permute-start(bf16[16,4224]{1,0:T(8,128)(2,1)S(1)} %get-tuple-element.36), channel_id=1, source_target_pairs={{0,3},{1,2},{2,1},{3,0},{4,7},{5,6},{6,5},{7,4},{8,11},{9,10},{10,... | collective-permute-start | bytes 405512 | tf_op jit(solution)/shard_map/ppermute | solution.py:224
  17.9 0.5 %collective-permute-start.4 = (bf16[16,4224]{1,0:T(8,128)(2,1)S(1)}, bf16[16,4224]{1,0:T(8,128)(2,1)S(1)}, u32[]{:S(2)}, u32[]{:S(2)}) collective-permute-start(bf16[16,4224]{1,0:T(8,128)(2,1)S(1)} %get-tuple-element.37), channel_id=1, source_target_pairs={{0,1},{1,0},{2,3},{3,2},{4,5},{5,4},{6,7},{7,6},{8,9},{9,8},{10,11... | collective-permute-start | bytes 405512 | tf_op jit(solution)/shard_map/ppermute | solution.py:224
  18.4 0.4 %collective-permute-start.5 = (bf16[16,4224]{1,0:T(8,128)(2,1)S(1)}, bf16[16,4224]{1,0:T(8,128)(2,1)S(1)}, u32[]{:S(2)}, u32[]{:S(2)}) collective-permute-start(bf16[16,4224]{1,0:T(8,128)(2,1)S(1)} %get-tuple-element.38), channel_id=1, source_target_pairs={{0,2},{1,3},{2,0},{3,1},{4,6},{5,7},{6,4},{7,5},{8,10},{9,11},{10,... | collective-permute-start | bytes 405512 | tf_op jit(solution)/shard_map/ppermute | solution.py:224
  18.9 0.4 collective-permute-done.7.refs_1_.refs_4_
  19.2 2.5 %shard_map.126 = (bf16[16,4096]{1,0:T(8,128)(2,1)S(1)}, bf16[16,4096]{1,0:T(8,128)(2,1)S(1)}, bf16[16,4096]{1,0:T(8,128)(2,1)S(1)}, bf16[16,4096]{1,0:T(8,128)(2,1)S(1)}) custom-call(bf16[16,4096]{1,0:T(8,128)(2,1)S(1)} %shard_map.125.refs_0_.refs_3_, bf16[16,4096]{1,0:T(8,128)(2,1)S(1)} %collective-permute-done.7.refs_1_.refs_4_, ...), custom_call_target="tpu_custom_call" | custom-call | flops 4026531840 | bytes 7471104 | tf_op jit(solution)/shard_map/pallas_call | solution.py:35
  21.7 2.2 %collective-permute-start.10 = (bf16[16,4096]{1,0:T(8,128)(2,1)S(1)}, bf16[16,4096]{1,0:T(8,128)(2,1)S(1)}, u32[]{:S(2)}, u32[]{:S(2)}) collective-permute-start(bf16[16,4096]{1,0:T(8,128)(2,1)S(1)} %get-tuple-element.43), channel_id=1, source_target_pairs={{0,3},{1,2},{2,1},{3,0},{4,7},{5,6},{6,5},{7,4},{8,11},{9,10},{10,... | collective-permute-start | bytes 393224 | tf_op jit(solution)/shard_map/ppermute | solution.py:224
  23.9 0.5 %collective-permute-start.11 = (bf16[16,4096]{1,0:T(8,128)(2,1)S(1)}, bf16[16,4096]{1,0:T(8,128)(2,1)S(1)}, u32[]{:S(2)}, u32[]{:S(2)}) collective-permute-start(bf16[16,4096]{1,0:T(8,128)(2,1)S(1)} %get-tuple-element.44), channel_id=1, source_target_pairs={{0,1},{1,0},{2,3},{3,2},{4,5},{5,4},{6,7},{7,6},{8,9},{9,8},{10,11... | collective-permute-start | bytes 393224 | tf_op jit(solution)/shard_map/ppermute | solution.py:224
  24.5 1.2 %collective-permute-start.12 = (bf16[16,4096]{1,0:T(8,128)(2,1)S(1)}, bf16[16,4096]{1,0:T(8,128)(2,1)S(1)}, u32[]{:S(2)}, u32[]{:S(2)}) collective-permute-start(bf16[16,4096]{1,0:T(8,128)(2,1)S(1)} %get-tuple-element.45), channel_id=1, source_target_pairs={{0,2},{1,3},{2,0},{3,1},{4,6},{5,7},{6,4},{7,5},{8,10},{9,11},{10,... | collective-permute-start | bytes 393224 | tf_op jit(solution)/shard_map/ppermute | solution.py:224
  25.7 1.0 %shard_map.127 = f32[16,256]{1,0:T(8,128)} custom-call(bf16[16,4096]{1,0:T(8,128)(2,1)S(1)} %shard_map.125.refs_0_.refs_3_, bf16[16,4096]{1,0:T(8,128)(2,1)S(1)} %collective-permute-done.7.refs_1_.refs_4_, bf16[16,4096]{1,0:T(8,128)(2,1)S(1)} %collective-permute-done.8.refs_2_.refs_5_, bf16[16,4096]{1,0:T(8,128)(2,1)S(1)} %collective-permute-done.9.refs_3_.refs_6_, ...), custom_call_target="tpu_custom_call" | custom-call | flops 838860800 | bytes 704512 | tf_op jit(solution)/shard_map/pallas_call | solution.py:35
  26.8 0.1 shard_map.123
  27.0 0.9 %shard_map.128 = f32[1,1,16,1024]{3,2,1,0:T(8,128)} custom-call(bf16[16,64]{1,0:T(8,128)(2,1)S(1)} %get-tuple-element.49.latent_ref, bf16[16,4224]{1,0:T(8,128)(2,1)S(1)} %collective-permute-done.3.refs_1_.refs_0_, bf16[16,4224]{1,0:T(8,128)(2,1)S(1)} %collective-permute-done.4.refs_2_.refs_1_, bf16[16,4224]{1,0:T(8,128)(2,1)S(1)} %collective-permute-done.5.refs_3_.refs_2_, ...), custom_call_target="tpu_custom_call" | custom-call | flops 838860800 | bytes 997376 | tf_op jit(solution)/shard_map/pallas_call | solution.py:35
  27.8 1.1 %collective-permute-done.10.refs_1_ = bf16[16,4096]{1,0:T(8,128)(2,1)S(1)} collective-permute-done((bf16[16,4096]{1,0:T(8,128)(2,1)S(1)}, bf16[16,4096]{1,0:T(8,128)(2,1)S(1)}, u32[]{:S(2)}, u32[]{:S(2)}) %collective-permute-start.10) | collective-permute-done | bytes 131104 | tf_op jit(solution)/shard_map/ppermute | solution.py:224
  28.9 1.3 %collective-permute-done.11.refs_2_ = bf16[16,4096]{1,0:T(8,128)(2,1)S(1)} collective-permute-done((bf16[16,4096]{1,0:T(8,128)(2,1)S(1)}, bf16[16,4096]{1,0:T(8,128)(2,1)S(1)}, u32[]{:S(2)}, u32[]{:S(2)}) %collective-permute-start.11) | collective-permute-done | bytes 131104 | tf_op jit(solution)/shard_map/ppermute | solution.py:224
  30.2 0.1 collective-permute-done.12.refs_3_
  30.3 0.1 shard_map.129
  30.4 2.2 %collective-permute-start.13 = (bf16[16,4224]{1,0:T(8,128)(2,1)S(1)}, bf16[16,4224]{1,0:T(8,128)(2,1)S(1)}, u32[]{:S(2)}, u32[]{:S(2)}) collective-permute-start(bf16[16,4224]{1,0:T(8,128)(2,1)S(1)} %shard_map.129), channel_id=1, source_target_pairs={{0,28},{1,29},{2,30},{3,31},{4,0},{5,1},{6,2},{7,3},{8,4},{9,5},{1... | collective-permute-start | bytes 405512 | tf_op jit(solution)/shard_map/ppermute | solution.py:224
  32.6 0.6 %collective-permute-done.6.message_ref = bf16[16,4224]{1,0:T(8,128)(2,1)S(1)} collective-permute-done((bf16[16,4224]{1,0:T(8,128)(2,1)S(1)}, bf16[16,4224]{1,0:T(8,128)(2,1)S(1)}, u32[]{:S(2)}, u32[]{:S(2)}) %collective-permute-start.6) | collective-permute-done | bytes 135200 | tf_op jit(solution)/shard_map/ppermute | solution.py:224
  33.2 1.2 %shard_map.124 = bf16[1,128,4096]{2,1,0:T(8,128)(2,1)} custom-call(bf16[16,4224]{1,0:T(8,128)(2,1)S(1)} %collective-permute-done.6.message_ref), custom_call_target="tpu_custom_call" | custom-call | flops 16777216 | bytes 1183744 | tf_op jit(solution)/shard_map/pallas_call | solution.py:35
  34.4 0.7 %collective-permute-done.13.message_ref = bf16[16,4224]{1,0:T(8,128)(2,1)S(1)} collective-permute-done((bf16[16,4224]{1,0:T(8,128)(2,1)S(1)}, bf16[16,4224]{1,0:T(8,128)(2,1)S(1)}, u32[]{:S(2)}, u32[]{:S(2)}) %collective-permute-start.13) | collective-permute-done | bytes 135200 | tf_op jit(solution)/shard_map/ppermute | solution.py:224
  35.2 1.2 %shard_map.130 = bf16[1,128,4096]{2,1,0:T(8,128)(2,1)} custom-call(bf16[16,4224]{1,0:T(8,128)(2,1)S(1)} %collective-permute-done.13.message_ref), custom_call_target="tpu_custom_call" | custom-call | flops 16777216 | bytes 1183744 | tf_op jit(solution)/shard_map/pallas_call | solution.py:35
  (11 shorter events, 0.1 us)
Async XLA Ops:
  2.5 10.4 %collective-permute-start.2 = (bf16[16,4096]{1,0:T(8,128)(2,1)S(1)}, bf16[16,4096]{1,0:T(8,128)(2,1)S(1)}, u32[]{:S(2)}, u32[]{:S(2)}) collective-permute-start(bf16[16,4096]{1,0:T(8,128)(2,1)S(1)} %get-tuple-element.32.refs_0_), channel_id=1, source_target_pairs={{0,3},{1,2},{2,1},{3,0},{4,7},{5,6},{6,5},{7,4},{8,11},{9,10},{10,... | collective-permute-start | bytes 393224 | tf_op jit(solution)/shard_map/ppermute | solution.py:224
  6.5 6.7 %collective-permute-start.1 = (bf16[16,4096]{1,0:T(8,128)(2,1)S(1)}, bf16[16,4096]{1,0:T(8,128)(2,1)S(1)}, u32[]{:S(2)}, u32[]{:S(2)}) collective-permute-start(bf16[16,4096]{1,0:T(8,128)(2,1)S(1)} %get-tuple-element.32.refs_0_), channel_id=1, source_target_pairs={{0,2},{1,3},{2,0},{3,1},{4,6},{5,7},{6,4},{7,5},{8,10},{9,11},{10,... | collective-permute-start | bytes 393224 | tf_op jit(solution)/shard_map/ppermute | solution.py:224
  7.0 6.5 %collective-permute-start = (bf16[16,4096]{1,0:T(8,128)(2,1)S(1)}, bf16[16,4096]{1,0:T(8,128)(2,1)S(1)}, u32[]{:S(2)}, u32[]{:S(2)}) collective-permute-start(bf16[16,4096]{1,0:T(8,128)(2,1)S(1)} %get-tuple-element.32.refs_0_), channel_id=1, source_target_pairs={{0,1},{1,0},{2,3},{3,2},{4,5},{5,4},{6,7},{7,6},{8,9},{9,8},{10,11... | collective-permute-start | bytes 393224 | tf_op jit(solution)/shard_map/ppermute | solution.py:224
  9.3 4.2 %copy-start = (bf16[1,256,4096]{2,1,0:T(8,128)(2,1)S(1)}, bf16[1,256,4096]{2,1,0:T(8,128)(2,1)}, u32[]{:S(2)}) copy-start(bf16[1,256,4096]{2,1,0:T(8,128)(2,1)} %param.12) | copy-start | bytes 6291460
  9.3 4.2 %copy-start.1 = (bf16[1,256,4096]{2,1,0:T(8,128)(2,1)S(1)}, bf16[1,256,4096]{2,1,0:T(8,128)(2,1)}, u32[]{:S(2)}) copy-start(bf16[1,256,4096]{2,1,0:T(8,128)(2,1)} %param.13) | copy-start | bytes 6291460
  9.6 8.9 %collective-permute-start.9 = (bf16[16,4096]{1,0:T(8,128)(2,1)S(1)}, bf16[16,4096]{1,0:T(8,128)(2,1)S(1)}, u32[]{:S(2)}, u32[]{:S(2)}) collective-permute-start(bf16[16,4096]{1,0:T(8,128)(2,1)S(1)} %shard_map.125.refs_0_.refs_3_), channel_id=1, source_target_pairs={{0,3},{1,2},{2,1},{3,0},{4,7},{5,6},{6,5},{7,4},{8,11},{9,10},{10,... | collective-permute-start | bytes 393224 | tf_op jit(solution)/shard_map/ppermute | solution.py:224
  12.5 6.4 %collective-permute-start.8 = (bf16[16,4096]{1,0:T(8,128)(2,1)S(1)}, bf16[16,4096]{1,0:T(8,128)(2,1)S(1)}, u32[]{:S(2)}, u32[]{:S(2)}) collective-permute-start(bf16[16,4096]{1,0:T(8,128)(2,1)S(1)} %shard_map.125.refs_0_.refs_3_), channel_id=1, source_target_pairs={{0,2},{1,3},{2,0},{3,1},{4,6},{5,7},{6,4},{7,5},{8,10},{9,11},{10,... | collective-permute-start | bytes 393224 | tf_op jit(solution)/shard_map/ppermute | solution.py:224
  13.0 6.3 %collective-permute-start.7 = (bf16[16,4096]{1,0:T(8,128)(2,1)S(1)}, bf16[16,4096]{1,0:T(8,128)(2,1)S(1)}, u32[]{:S(2)}, u32[]{:S(2)}) collective-permute-start(bf16[16,4096]{1,0:T(8,128)(2,1)S(1)} %shard_map.125.refs_0_.refs_3_), channel_id=1, source_target_pairs={{0,1},{1,0},{2,3},{3,2},{4,5},{5,4},{6,7},{7,6},{8,9},{9,8},{10,11... | collective-permute-start | bytes 393224 | tf_op jit(solution)/shard_map/ppermute | solution.py:224
  15.3 9.2 %collective-permute-start.3 = (bf16[16,4224]{1,0:T(8,128)(2,1)S(1)}, bf16[16,4224]{1,0:T(8,128)(2,1)S(1)}, u32[]{:S(2)}, u32[]{:S(2)}) collective-permute-start(bf16[16,4224]{1,0:T(8,128)(2,1)S(1)} %get-tuple-element.36), channel_id=1, source_target_pairs={{0,3},{1,2},{2,1},{3,0},{4,7},{5,6},{6,5},{7,4},{8,11},{9,10},{10,... | collective-permute-start | bytes 405512 | tf_op jit(solution)/shard_map/ppermute | solution.py:224
  17.9 8.9 %collective-permute-start.4 = (bf16[16,4224]{1,0:T(8,128)(2,1)S(1)}, bf16[16,4224]{1,0:T(8,128)(2,1)S(1)}, u32[]{:S(2)}, u32[]{:S(2)}) collective-permute-start(bf16[16,4224]{1,0:T(8,128)(2,1)S(1)} %get-tuple-element.37), channel_id=1, source_target_pairs={{0,1},{1,0},{2,3},{3,2},{4,5},{5,4},{6,7},{7,6},{8,9},{9,8},{10,11... | collective-permute-start | bytes 405512 | tf_op jit(solution)/shard_map/ppermute | solution.py:224
  18.4 8.4 %collective-permute-start.5 = (bf16[16,4224]{1,0:T(8,128)(2,1)S(1)}, bf16[16,4224]{1,0:T(8,128)(2,1)S(1)}, u32[]{:S(2)}, u32[]{:S(2)}) collective-permute-start(bf16[16,4224]{1,0:T(8,128)(2,1)S(1)} %get-tuple-element.38), channel_id=1, source_target_pairs={{0,2},{1,3},{2,0},{3,1},{4,6},{5,7},{6,4},{7,5},{8,10},{9,11},{10,... | collective-permute-start | bytes 405512 | tf_op jit(solution)/shard_map/ppermute | solution.py:224
  21.7 7.2 %collective-permute-start.10 = (bf16[16,4096]{1,0:T(8,128)(2,1)S(1)}, bf16[16,4096]{1,0:T(8,128)(2,1)S(1)}, u32[]{:S(2)}, u32[]{:S(2)}) collective-permute-start(bf16[16,4096]{1,0:T(8,128)(2,1)S(1)} %get-tuple-element.43), channel_id=1, source_target_pairs={{0,3},{1,2},{2,1},{3,0},{4,7},{5,6},{6,5},{7,4},{8,11},{9,10},{10,... | collective-permute-start | bytes 393224 | tf_op jit(solution)/shard_map/ppermute | solution.py:224
  23.9 6.3 %collective-permute-start.11 = (bf16[16,4096]{1,0:T(8,128)(2,1)S(1)}, bf16[16,4096]{1,0:T(8,128)(2,1)S(1)}, u32[]{:S(2)}, u32[]{:S(2)}) collective-permute-start(bf16[16,4096]{1,0:T(8,128)(2,1)S(1)} %get-tuple-element.44), channel_id=1, source_target_pairs={{0,1},{1,0},{2,3},{3,2},{4,5},{5,4},{6,7},{7,6},{8,9},{9,8},{10,11... | collective-permute-start | bytes 393224 | tf_op jit(solution)/shard_map/ppermute | solution.py:224
  24.5 5.8 %collective-permute-start.12 = (bf16[16,4096]{1,0:T(8,128)(2,1)S(1)}, bf16[16,4096]{1,0:T(8,128)(2,1)S(1)}, u32[]{:S(2)}, u32[]{:S(2)}) collective-permute-start(bf16[16,4096]{1,0:T(8,128)(2,1)S(1)} %get-tuple-element.45), channel_id=1, source_target_pairs={{0,2},{1,3},{2,0},{3,1},{4,6},{5,7},{6,4},{7,5},{8,10},{9,11},{10,... | collective-permute-start | bytes 393224 | tf_op jit(solution)/shard_map/ppermute | solution.py:224
  26.9 6.3 %collective-permute-start.6 = (bf16[16,4224]{1,0:T(8,128)(2,1)S(1)}, bf16[16,4224]{1,0:T(8,128)(2,1)S(1)}, u32[]{:S(2)}, u32[]{:S(2)}) collective-permute-start(bf16[16,4224]{1,0:T(8,128)(2,1)S(1)} %shard_map.123), channel_id=1, source_target_pairs={{0,4},{1,5},{2,6},{3,7},{4,8},{5,9},{6,10},{7,11},{8,12},{9,13},{1... | collective-permute-start | bytes 405512 | tf_op jit(solution)/shard_map/ppermute | solution.py:224
  30.4 4.8 %collective-permute-start.13 = (bf16[16,4224]{1,0:T(8,128)(2,1)S(1)}, bf16[16,4224]{1,0:T(8,128)(2,1)S(1)}, u32[]{:S(2)}, u32[]{:S(2)}) collective-permute-start(bf16[16,4224]{1,0:T(8,128)(2,1)S(1)} %shard_map.129), channel_id=1, source_target_pairs={{0,28},{1,29},{2,30},{3,31},{4,0},{5,1},{6,2},{7,3},{8,4},{9,5},{1... | collective-permute-start | bytes 405512 | tf_op jit(solution)/shard_map/ppermute | solution.py:224

commit v17 on v16

--- a/solution.py
+++ b/solution.py
@@ -334,6 +334,30 @@
         (*g_blocks, hidden, b_near),
         flops=200 * rows * rank * width,
     )
+
+    def merged(parts, gated, columns):
+        return call(functools.partial(combine, gated), [sds(slots, columns)], (place, *parts))[0]
+
+    def reduced(parts, gated):
+        if flight > 1:
+            parts = [between_groups(merged(parts, False, width), flight)]
+        return merged(parts, gated, wide)
+
+    def expanded(message):
+        return call(
+            expand,
+            [sds(1, tokens, width)],
+            (message,),
+            far_outs=True,
+            scratch=[pltpu.VMEM((tokens, width), jnp.bfloat16), dma((CHUNKS,))],
+            flops=2 * slots * tokens * width,
+        )[0]
+
+    out_message = shifted(reduced(out_parts, True), 1, 0)
+    grad_parts, a_grad = lax.optimization_barrier((grad_parts, a_grad))
+    grad_message = reduced(grad_parts, False)
+    grad_message, latent = lax.optimization_barrier((grad_message, latent))
+    grad_message = shifted(grad_message, -1, 0)
     if flight == 1:
         (b_grad,) = call(
             up_map_grad,
@@ -347,29 +371,8 @@
         spread = jnp.where(mine[:, None, None], part[None], 0.0)
         b_grad = lax.psum_scatter(spread, "expert", scatter_dimension=2, tiled=True)[None]
 
-    def merged(parts, gated, columns):
-        return call(functools.partial(combine, gated), [sds(slots, columns)], (place, *parts))[0]
-
-    def reduced(parts, gated):
-        if flight > 1:
-            parts = [between_groups(merged(parts, False, width), flight)]
-        return merged(parts, gated, wide)
-
-    def expanded(message):
-        return call(
-            expand,
-            [sds(1, tokens, width)],
-            (message,),
-            far_outs=True,
-            scratch=[pltpu.VMEM((tokens, width), jnp.bfloat16), dma((CHUNKS,))],
-            flops=2 * slots * tokens * width,
-        )[0]
-
-    out_message = shifted(reduced(out_parts, True), 1, 0)
-    grad_parts, a_grad, b_grad = lax.optimization_barrier((grad_parts, a_grad, b_grad))
-    grad_message = shifted(reduced(grad_parts, False), -1, 0)
     next_input = expanded(out_message)
-    next_input, grad_message = lax.optimization_barrier((next_input, grad_message))
+    next_input, b_grad, grad_message = lax.optimization_barrier((next_input, b_grad, grad_message))
     prev_grad = expanded(grad_message)
     return next_input, prev_grad, jnp.swapaxes(a_grad, 0, 1)[None], b_grad
 

time: 36.6 us -> 36.6 us (level)
  transfers between devices with their start and end apart: 14 -> 14, of which waited for: 8 -> 7; matrix products, arithmetic and copies ran while one was open for 0% -> 0% of each run, Pallas kernels for 28% -> 28%
where the time goes in v17:
time: 36.6 us; the launch traced here: 36.4 us
  starting transfers between devices  18 us (49%)
  Pallas kernels  13.2 us (36%)
  waiting for transfers between devices  4.53 us (12%)
  between operations  0.71 us (2%)
    ppermute x14, starting transfers between devices, shifted(): return lax.ppermute(block, ('section', 'expert'), route)  18 us
    pallas_call x11, Pallas kernels, call(): pl.pallas_call(body, out_shape=outs, in_specs=[NEAR] * len(args) + [FAR]...  13.2 us
    ppermute x14, waiting for transfers between devices, shifted(): return lax.ppermute(block, ('section', 'expert'), route)  4.53 us
  transfers between devices with their start and end apart: 14, of which 7 were waited for; matrix products, arithmetic and copies ran while one was open for 0% of the time, Pallas kernels for 28%

profile of v17, /device:TPU:0, one launch (start us, length us, event | category | flops | bytes accessed | tf_op | source)
XLA Modules:
  0.0 36.4 jit_solution(8433898121143961220)
XLA Ops:
  0.6 1.9 %shard_map.120 = (bf16[16,4096]{1,0:T(8,128)(2,1)S(1)}, f32[16,128]{1,0:T(8,128)S(1)}, bf16[128,4096]{1,0:T(8,128)(2,1)S(1)}, bf16[16,256]{1,0:T(8,128)(2,1)S(1)}, bf16[16,4096]{1,0:T(8,128)(2,1)S(1)}) custom-call(s32[8,128]{1,0:T(8,128)} %bitcast.21, s32[8,128]{1,0:T(8,128)} %bitcast.22, bf16[1,128,4096]{2,1,0:T(8,128)(2,1)} %x_hbm.1, ...), custom_call_target="tpu_custom_call" | custom-call | flops 16777216 | bytes 3571712 | tf_op jit(solution)/shard_map/pallas_call | solution.py:35
  2.5 4.0 %collective-permute-start.2 = (bf16[16,4096]{1,0:T(8,128)(2,1)S(1)}, bf16[16,4096]{1,0:T(8,128)(2,1)S(1)}, u32[]{:S(2)}, u32[]{:S(2)}) collective-permute-start(bf16[16,4096]{1,0:T(8,128)(2,1)S(1)} %get-tuple-element.34.refs_0_), channel_id=1, source_target_pairs={{0,3},{1,2},{2,1},{3,0},{4,7},{5,6},{6,5},{7,4},{8,11},{9,10},{10,... | collective-permute-start | bytes 393224 | tf_op jit(solution)/shard_map/ppermute | solution.py:224
  6.5 0.5 %collective-permute-start.1 = (bf16[16,4096]{1,0:T(8,128)(2,1)S(1)}, bf16[16,4096]{1,0:T(8,128)(2,1)S(1)}, u32[]{:S(2)}, u32[]{:S(2)}) collective-permute-start(bf16[16,4096]{1,0:T(8,128)(2,1)S(1)} %get-tuple-element.34.refs_0_), channel_id=1, source_target_pairs={{0,2},{1,3},{2,0},{3,1},{4,6},{5,7},{6,4},{7,5},{8,10},{9,11},{10,... | collective-permute-start | bytes 393224 | tf_op jit(solution)/shard_map/ppermute | solution.py:224
  7.0 0.1 collective-permute-start
  7.1 2.1 %shard_map.121.refs_6_._.refs_8_ = bf16[256,4096]{1,0:T(8,128)(2,1)S(1)} custom-call(bf16[16,256]{1,0:T(8,128)(2,1)S(1)} %get-tuple-element.35.a_ref.refs_7_, bf16[16,4096]{1,0:T(8,128)(2,1)S(1)} %get-tuple-element.36.b_ref.refs_5_, bf16[1,256,4096]{2,1,0:T(8,128)(2,1)} %down_hbm.1), custom_call_target="tpu_custom_call" | custom-call | bytes 1 | tf_op jit(solution)/shard_map/pallas_call | solution.py:35
  9.3 0.3 shard_map.125.refs_0_.refs_3_
  9.6 2.9 %collective-permute-start.9 = (bf16[16,4096]{1,0:T(8,128)(2,1)S(1)}, bf16[16,4096]{1,0:T(8,128)(2,1)S(1)}, u32[]{:S(2)}, u32[]{:S(2)}) collective-permute-start(bf16[16,4096]{1,0:T(8,128)(2,1)S(1)} %shard_map.125.refs_0_.refs_3_), channel_id=1, source_target_pairs={{0,3},{1,2},{2,1},{3,0},{4,7},{5,6},{6,5},{7,4},{8,11},{9,10},{10,... | collective-permute-start | bytes 393224 | tf_op jit(solution)/shard_map/ppermute | solution.py:224
  12.5 0.5 %collective-permute-start.8 = (bf16[16,4096]{1,0:T(8,128)(2,1)S(1)}, bf16[16,4096]{1,0:T(8,128)(2,1)S(1)}, u32[]{:S(2)}, u32[]{:S(2)}) collective-permute-start(bf16[16,4096]{1,0:T(8,128)(2,1)S(1)} %shard_map.125.refs_0_.refs_3_), channel_id=1, source_target_pairs={{0,2},{1,3},{2,0},{3,1},{4,6},{5,7},{6,4},{7,5},{8,10},{9,11},{10,... | collective-permute-start | bytes 393224 | tf_op jit(solution)/shard_map/ppermute | solution.py:224
  13.0 0.1 collective-permute-start.7
  13.1 0.1 collective-permute-done.1.refs_2_
  13.2 0.2 collective-permute-done.refs_1_
  13.5 1.8 %shard_map.122 = (bf16[16,4096]{1,0:T(8,128)(2,1)S(1)}, bf16[16,4224]{1,0:T(8,128)(2,1)S(1)}, bf16[16,4224]{1,0:T(8,128)(2,1)S(1)}, bf16[16,4224]{1,0:T(8,128)(2...) custom-call(bf16[16,4096]{1,0:T(8,128)(2,1)S(1)} %get-tuple-element., ...), custom_call_target="tpu_custom_call" | custom-call | flops 4026531840 | bytes 7526400 | tf_op jit(solution)/shard_map/pallas_call | solution.py:35
  15.3 2.6 %collective-permute-start.3 = (bf16[16,4224]{1,0:T(8,128)(2,1)S(1)}, bf16[16,4224]{1,0:T(8,128)(2,1)S(1)}, u32[]{:S(2)}, u32[]{:S(2)}) collective-permute-start(bf16[16,4224]{1,0:T(8,128)(2,1)S(1)} %get-tuple-element.38), channel_id=1, source_target_pairs={{0,3},{1,2},{2,1},{3,0},{4,7},{5,6},{6,5},{7,4},{8,11},{9,10},{10,... | collective-permute-start | bytes 405512 | tf_op jit(solution)/shard_map/ppermute | solution.py:224
  17.9 0.5 %collective-permute-start.4 = (bf16[16,4224]{1,0:T(8,128)(2,1)S(1)}, bf16[16,4224]{1,0:T(8,128)(2,1)S(1)}, u32[]{:S(2)}, u32[]{:S(2)}) collective-permute-start(bf16[16,4224]{1,0:T(8,128)(2,1)S(1)} %get-tuple-element.39), channel_id=1, source_target_pairs={{0,1},{1,0},{2,3},{3,2},{4,5},{5,4},{6,7},{7,6},{8,9},{9,8},{10,11... | collective-permute-start | bytes 405512 | tf_op jit(solution)/shard_map/ppermute | solution.py:224
  18.4 0.4 %collective-permute-start.5 = (bf16[16,4224]{1,0:T(8,128)(2,1)S(1)}, bf16[16,4224]{1,0:T(8,128)(2,1)S(1)}, u32[]{:S(2)}, u32[]{:S(2)}) collective-permute-start(bf16[16,4224]{1,0:T(8,128)(2,1)S(1)} %get-tuple-element.40), channel_id=1, source_target_pairs={{0,2},{1,3},{2,0},{3,1},{4,6},{5,7},{6,4},{7,5},{8,10},{9,11},{10,... | collective-permute-start | bytes 405512 | tf_op jit(solution)/shard_map/ppermute | solution.py:224
  18.9 0.4 collective-permute-done.7.refs_1_.refs_4_
  19.2 2.5 %shard_map.126 = (bf16[16,4096]{1,0:T(8,128)(2,1)S(1)}, bf16[16,4096]{1,0:T(8,128)(2,1)S(1)}, bf16[16,4096]{1,0:T(8,128)(2,1)S(1)}, bf16[16,4096]{1,0:T(8,128)(2,1)S(1)}) custom-call(bf16[16,4096]{1,0:T(8,128)(2,1)S(1)} %shard_map.125.refs_0_.refs_3_, bf16[16,4096]{1,0:T(8,128)(2,1)S(1)} %collective-permute-done.7.refs_1_.refs_4_, ...), custom_call_target="tpu_custom_call" | custom-call | flops 4026531840 | bytes 7471104 | tf_op jit(solution)/shard_map/pallas_call | solution.py:35
  21.7 2.2 %collective-permute-start.10 = (bf16[16,4096]{1,0:T(8,128)(2,1)S(1)}, bf16[16,4096]{1,0:T(8,128)(2,1)S(1)}, u32[]{:S(2)}, u32[]{:S(2)}) collective-permute-start(bf16[16,4096]{1,0:T(8,128)(2,1)S(1)} %get-tuple-element.45), channel_id=1, source_target_pairs={{0,3},{1,2},{2,1},{3,0},{4,7},{5,6},{6,5},{7,4},{8,11},{9,10},{10,... | collective-permute-start | bytes 393224 | tf_op jit(solution)/shard_map/ppermute | solution.py:224
  23.9 0.5 %collective-permute-start.11 = (bf16[16,4096]{1,0:T(8,128)(2,1)S(1)}, bf16[16,4096]{1,0:T(8,128)(2,1)S(1)}, u32[]{:S(2)}, u32[]{:S(2)}) collective-permute-start(bf16[16,4096]{1,0:T(8,128)(2,1)S(1)} %get-tuple-element.46), channel_id=1, source_target_pairs={{0,1},{1,0},{2,3},{3,2},{4,5},{5,4},{6,7},{7,6},{8,9},{9,8},{10,11... | collective-permute-start | bytes 393224 | tf_op jit(solution)/shard_map/ppermute | solution.py:224
  24.5 1.2 %collective-permute-start.12 = (bf16[16,4096]{1,0:T(8,128)(2,1)S(1)}, bf16[16,4096]{1,0:T(8,128)(2,1)S(1)}, u32[]{:S(2)}, u32[]{:S(2)}) collective-permute-start(bf16[16,4096]{1,0:T(8,128)(2,1)S(1)} %get-tuple-element.47), channel_id=1, source_target_pairs={{0,2},{1,3},{2,0},{3,1},{4,6},{5,7},{6,4},{7,5},{8,10},{9,11},{10,... | collective-permute-start | bytes 393224 | tf_op jit(solution)/shard_map/ppermute | solution.py:224
  25.7 0.1 shard_map.123
  25.8 0.1 collective-permute-start.6
  25.9 1.0 %shard_map.127 = f32[16,256]{1,0:T(8,128)} custom-call(bf16[16,4096]{1,0:T(8,128)(2,1)S(1)} %shard_map.125.refs_0_.refs_3_, bf16[16,4096]{1,0:T(8,128)(2,1)S(1)} %collective-permute-done.7.refs_1_.refs_4_, bf16[16,4096]{1,0:T(8,128)(2,1)S(1)} %collective-permute-done.8.refs_2_.refs_5_, bf16[16,4096]{1,0:T(8,128)(2,1)S(1)} %collective-permute-done.9.refs_3_.refs_6_, ...), custom_call_target="tpu_custom_call" | custom-call | flops 838860800 | bytes 704512 | tf_op jit(solution)/shard_map/pallas_call | solution.py:35
  27.0 2.0 %collective-permute-done.10.refs_1_ = bf16[16,4096]{1,0:T(8,128)(2,1)S(1)} collective-permute-done((bf16[16,4096]{1,0:T(8,128)(2,1)S(1)}, bf16[16,4096]{1,0:T(8,128)(2,1)S(1)}, u32[]{:S(2)}, u32[]{:S(2)}) %collective-permute-start.10) | collective-permute-done | bytes 131104 | tf_op jit(solution)/shard_map/ppermute | solution.py:224
  28.9 1.3 %collective-permute-done.11.refs_2_ = bf16[16,4096]{1,0:T(8,128)(2,1)S(1)} collective-permute-done((bf16[16,4096]{1,0:T(8,128)(2,1)S(1)}, bf16[16,4096]{1,0:T(8,128)(2,1)S(1)}, u32[]{:S(2)}, u32[]{:S(2)}) %collective-permute-start.11) | collective-permute-done | bytes 131104 | tf_op jit(solution)/shard_map/ppermute | solution.py:224
  30.2 0.1 collective-permute-done.12.refs_3_
  30.3 0.1 shard_map.128
  30.4 2.2 %collective-permute-start.13 = (bf16[16,4224]{1,0:T(8,128)(2,1)S(1)}, bf16[16,4224]{1,0:T(8,128)(2,1)S(1)}, u32[]{:S(2)}, u32[]{:S(2)}) collective-permute-start(bf16[16,4224]{1,0:T(8,128)(2,1)S(1)} %shard_map.128), channel_id=1, source_target_pairs={{0,28},{1,29},{2,30},{3,31},{4,0},{5,1},{6,2},{7,3},{8,4},{9,5},{1... | collective-permute-start | bytes 405512 | tf_op jit(solution)/shard_map/ppermute | solution.py:224
  32.6 0.8 %shard_map.129 = f32[1,1,16,1024]{3,2,1,0:T(8,128)} custom-call(bf16[16,64]{1,0:T(8,128)(2,1)S(1)} %get-tuple-element.56.latent_ref, bf16[16,4224]{1,0:T(8,128)(2,1)S(1)} %collective-permute-done.3.refs_1_.refs_0_, bf16[16,4224]{1,0:T(8,128)(2,1)S(1)} %collective-permute-done.4.refs_2_.refs_1_, bf16[16,4224]{1,0:T(8,128)(2,1)S(1)} %collective-permute-done.5.refs_3_.refs_2_, ...), custom_call_target="tpu_custom_call" | custom-call | flops 838860800 | bytes 997376 | tf_op jit(solution)/shard_map/pallas_call | solution.py:35
  33.5 1.2 %shard_map.124 = bf16[1,128,4096]{2,1,0:T(8,128)(2,1)} custom-call(bf16[16,4224]{1,0:T(8,128)(2,1)S(1)} %collective-permute-done.6.message_ref), custom_call_target="tpu_custom_call" | custom-call | flops 16777216 | bytes 1183744 | tf_op jit(solution)/shard_map/pallas_call | solution.py:35
  34.7 0.5 %collective-permute-done.13.message_ref = bf16[16,4224]{1,0:T(8,128)(2,1)S(1)} collective-permute-done((bf16[16,4224]{1,0:T(8,128)(2,1)S(1)}, bf16[16,4224]{1,0:T(8,128)(2,1)S(1)}, u32[]{:S(2)}, u32[]{:S(2)}) %collective-permute-start.13) | collective-permute-done | bytes 135200 | tf_op jit(solution)/shard_map/ppermute | solution.py:224
  35.2 1.2 %shard_map.130 = bf16[1,128,4096]{2,1,0:T(8,128)(2,1)} custom-call(bf16[16,4224]{1,0:T(8,128)(2,1)S(1)} %collective-permute-done.13.message_ref), custom_call_target="tpu_custom_call" | custom-call | flops 16777216 | bytes 1183744 | tf_op jit(solution)/shard_map/pallas_call | solution.py:35
  (11 shorter events, 0.0 us)
Async XLA Ops:
  2.5 10.4 %collective-permute-start.2 = (bf16[16,4096]{1,0:T(8,128)(2,1)S(1)}, bf16[16,4096]{1,0:T(8,128)(2,1)S(1)}, u32[]{:S(2)}, u32[]{:S(2)}) collective-permute-start(bf16[16,4096]{1,0:T(8,128)(2,1)S(1)} %get-tuple-element.34.refs_0_), channel_id=1, source_target_pairs={{0,3},{1,2},{2,1},{3,0},{4,7},{5,6},{6,5},{7,4},{8,11},{9,10},{10,... | collective-permute-start | bytes 393224 | tf_op jit(solution)/shard_map/ppermute | solution.py:224
  6.5 6.7 %collective-permute-start.1 = (bf16[16,4096]{1,0:T(8,128)(2,1)S(1)}, bf16[16,4096]{1,0:T(8,128)(2,1)S(1)}, u32[]{:S(2)}, u32[]{:S(2)}) collective-permute-start(bf16[16,4096]{1,0:T(8,128)(2,1)S(1)} %get-tuple-element.34.refs_0_), channel_id=1, source_target_pairs={{0,2},{1,3},{2,0},{3,1},{4,6},{5,7},{6,4},{7,5},{8,10},{9,11},{10,... | collective-permute-start | bytes 393224 | tf_op jit(solution)/shard_map/ppermute | solution.py:224
  7.0 6.5 %collective-permute-start = (bf16[16,4096]{1,0:T(8,128)(2,1)S(1)}, bf16[16,4096]{1,0:T(8,128)(2,1)S(1)}, u32[]{:S(2)}, u32[]{:S(2)}) collective-permute-start(bf16[16,4096]{1,0:T(8,128)(2,1)S(1)} %get-tuple-element.34.refs_0_), channel_id=1, source_target_pairs={{0,1},{1,0},{2,3},{3,2},{4,5},{5,4},{6,7},{7,6},{8,9},{9,8},{10,11... | collective-permute-start | bytes 393224 | tf_op jit(solution)/shard_map/ppermute | solution.py:224
  9.3 4.2 %copy-start = (bf16[1,256,4096]{2,1,0:T(8,128)(2,1)S(1)}, bf16[1,256,4096]{2,1,0:T(8,128)(2,1)}, u32[]{:S(2)}) copy-start(bf16[1,256,4096]{2,1,0:T(8,128)(2,1)} %param.12) | copy-start | bytes 6291460
  9.3 4.2 %copy-start.1 = (bf16[1,256,4096]{2,1,0:T(8,128)(2,1)S(1)}, bf16[1,256,4096]{2,1,0:T(8,128)(2,1)}, u32[]{:S(2)}) copy-start(bf16[1,256,4096]{2,1,0:T(8,128)(2,1)} %param.13) | copy-start | bytes 6291460
  9.6 8.9 %collective-permute-start.9 = (bf16[16,4096]{1,0:T(8,128)(2,1)S(1)}, bf16[16,4096]{1,0:T(8,128)(2,1)S(1)}, u32[]{:S(2)}, u32[]{:S(2)}) collective-permute-start(bf16[16,4096]{1,0:T(8,128)(2,1)S(1)} %shard_map.125.refs_0_.refs_3_), channel_id=1, source_target_pairs={{0,3},{1,2},{2,1},{3,0},{4,7},{5,6},{6,5},{7,4},{8,11},{9,10},{10,... | collective-permute-start | bytes 393224 | tf_op jit(solution)/shard_map/ppermute | solution.py:224
  12.5 6.4 %collective-permute-start.8 = (bf16[16,4096]{1,0:T(8,128)(2,1)S(1)}, bf16[16,4096]{1,0:T(8,128)(2,1)S(1)}, u32[]{:S(2)}, u32[]{:S(2)}) collective-permute-start(bf16[16,4096]{1,0:T(8,128)(2,1)S(1)} %shard_map.125.refs_0_.refs_3_), channel_id=1, source_target_pairs={{0,2},{1,3},{2,0},{3,1},{4,6},{5,7},{6,4},{7,5},{8,10},{9,11},{10,... | collective-permute-start | bytes 393224 | tf_op jit(solution)/shard_map/ppermute | solution.py:224
  13.0 6.2 %collective-permute-start.7 = (bf16[16,4096]{1,0:T(8,128)(2,1)S(1)}, bf16[16,4096]{1,0:T(8,128)(2,1)S(1)}, u32[]{:S(2)}, u32[]{:S(2)}) collective-permute-start(bf16[16,4096]{1,0:T(8,128)(2,1)S(1)} %shard_map.125.refs_0_.refs_3_), channel_id=1, source_target_pairs={{0,1},{1,0},{2,3},{3,2},{4,5},{5,4},{6,7},{7,6},{8,9},{9,8},{10,11... | collective-permute-start | bytes 393224 | tf_op jit(solution)/shard_map/ppermute | solution.py:224
  15.3 9.2 %collective-permute-start.3 = (bf16[16,4224]{1,0:T(8,128)(2,1)S(1)}, bf16[16,4224]{1,0:T(8,128)(2,1)S(1)}, u32[]{:S(2)}, u32[]{:S(2)}) collective-permute-start(bf16[16,4224]{1,0:T(8,128)(2,1)S(1)} %get-tuple-element.38), channel_id=1, source_target_pairs={{0,3},{1,2},{2,1},{3,0},{4,7},{5,6},{6,5},{7,4},{8,11},{9,10},{10,... | collective-permute-start | bytes 405512 | tf_op jit(solution)/shard_map/ppermute | solution.py:224
  17.9 7.8 %collective-permute-start.4 = (bf16[16,4224]{1,0:T(8,128)(2,1)S(1)}, bf16[16,4224]{1,0:T(8,128)(2,1)S(1)}, u32[]{:S(2)}, u32[]{:S(2)}) collective-permute-start(bf16[16,4224]{1,0:T(8,128)(2,1)S(1)} %get-tuple-element.39), channel_id=1, source_target_pairs={{0,1},{1,0},{2,3},{3,2},{4,5},{5,4},{6,7},{7,6},{8,9},{9,8},{10,11... | collective-permute-start | bytes 405512 | tf_op jit(solution)/shard_map/ppermute | solution.py:224
  18.4 7.3 %collective-permute-start.5 = (bf16[16,4224]{1,0:T(8,128)(2,1)S(1)}, bf16[16,4224]{1,0:T(8,128)(2,1)S(1)}, u32[]{:S(2)}, u32[]{:S(2)}) collective-permute-start(bf16[16,4224]{1,0:T(8,128)(2,1)S(1)} %get-tuple-element.40), channel_id=1, source_target_pairs={{0,2},{1,3},{2,0},{3,1},{4,6},{5,7},{6,4},{7,5},{8,10},{9,11},{10,... | collective-permute-start | bytes 405512 | tf_op jit(solution)/shard_map/ppermute | solution.py:224
  21.7 7.2 %collective-permute-start.10 = (bf16[16,4096]{1,0:T(8,128)(2,1)S(1)}, bf16[16,4096]{1,0:T(8,128)(2,1)S(1)}, u32[]{:S(2)}, u32[]{:S(2)}) collective-permute-start(bf16[16,4096]{1,0:T(8,128)(2,1)S(1)} %get-tuple-element.45), channel_id=1, source_target_pairs={{0,3},{1,2},{2,1},{3,0},{4,7},{5,6},{6,5},{7,4},{8,11},{9,10},{10,... | collective-permute-start | bytes 393224 | tf_op jit(solution)/shard_map/ppermute | solution.py:224
  23.9 6.3 %collective-permute-start.11 = (bf16[16,4096]{1,0:T(8,128)(2,1)S(1)}, bf16[16,4096]{1,0:T(8,128)(2,1)S(1)}, u32[]{:S(2)}, u32[]{:S(2)}) collective-permute-start(bf16[16,4096]{1,0:T(8,128)(2,1)S(1)} %get-tuple-element.46), channel_id=1, source_target_pairs={{0,1},{1,0},{2,3},{3,2},{4,5},{5,4},{6,7},{7,6},{8,9},{9,8},{10,11... | collective-permute-start | bytes 393224 | tf_op jit(solution)/shard_map/ppermute | solution.py:224
  24.5 5.8 %collective-permute-start.12 = (bf16[16,4096]{1,0:T(8,128)(2,1)S(1)}, bf16[16,4096]{1,0:T(8,128)(2,1)S(1)}, u32[]{:S(2)}, u32[]{:S(2)}) collective-permute-start(bf16[16,4096]{1,0:T(8,128)(2,1)S(1)} %get-tuple-element.47), channel_id=1, source_target_pairs={{0,2},{1,3},{2,0},{3,1},{4,6},{5,7},{6,4},{7,5},{8,10},{9,11},{10,... | collective-permute-start | bytes 393224 | tf_op jit(solution)/shard_map/ppermute | solution.py:224
  25.8 7.6 %collective-permute-start.6 = (bf16[16,4224]{1,0:T(8,128)(2,1)S(1)}, bf16[16,4224]{1,0:T(8,128)(2,1)S(1)}, u32[]{:S(2)}, u32[]{:S(2)}) collective-permute-start(bf16[16,4224]{1,0:T(8,128)(2,1)S(1)} %shard_map.123), channel_id=1, source_target_pairs={{0,4},{1,5},{2,6},{3,7},{4,8},{5,9},{6,10},{7,11},{8,12},{9,13},{1... | collective-permute-start | bytes 405512 | tf_op jit(solution)/shard_map/ppermute | solution.py:224
  30.4 4.8 %collective-permute-start.13 = (bf16[16,4224]{1,0:T(8,128)(2,1)S(1)}, bf16[16,4224]{1,0:T(8,128)(2,1)S(1)}, u32[]{:S(2)}, u32[]{:S(2)}) collective-permute-start(bf16[16,4224]{1,0:T(8,128)(2,1)S(1)} %shard_map.128), channel_id=1, source_target_pairs={{0,28},{1,29},{2,30},{3,31},{4,0},{5,1},{6,2},{7,3},{8,4},{9,5},{1... | collective-permute-start | bytes 405512 | tf_op jit(solution)/shard_map/ppermute | solution.py:224

commit v18 on v16

--- a/solution.py
+++ b/solution.py
@@ -29,7 +29,7 @@
 
 
 def call(
-    body, outs, args, far_args=(), far_outs=False, scratch=(), flops=0, moved=None, grant=24 * MIB
+    body, outs, args, far_args=(), far_outs=False, scratch=(), flops=0, moved=None, aliases={}
 ):
     moved = moved or sum(a.size * a.dtype.itemsize for a in (*args, *far_args, *outs))
     return pl.pallas_call(
@@ -38,7 +38,8 @@
         in_specs=[NEAR] * len(args) + [FAR] * len(far_args),
         out_specs=[FAR if far_outs else NEAR] * len(outs),
         scratch_shapes=scratch,
-        compiler_params=pltpu.CompilerParams(vmem_limit_bytes=grant),
+        input_output_aliases=aliases,
+        compiler_params=pltpu.CompilerParams(vmem_limit_bytes=24 * MIB),
         cost_estimate=pl.CostEstimate(flops=flops, bytes_accessed=moved, transcendentals=0),
     )(*args, *(pltpu.with_memory_space_constraint(a, pltpu.HBM) for a in far_args))
 
@@ -214,12 +215,19 @@
         copy.wait()
 
 
-def shifted(block, step, flip):
+def expand_end(message_ref, _, out_hbm, out_ref, sems):
+    @pl.when(lax.axis_index("section") == lax.axis_size("section") - 1)
+    def _():
+        expand(message_ref, out_hbm, out_ref, sems)
+
+
+def shifted(block, step, flip, ends=None):
     sections, experts = lax.axis_size("section"), lax.axis_size("expert")
     route = [
         (s * experts + e, (s + step) % sections * experts + (e ^ flip))
         for s in range(sections)
         for e in range(experts)
+        if ends is None or ends != (0 <= s + step < sections)
     ]
     return lax.ppermute(block, ("section", "expert"), route)
 
@@ -367,10 +375,22 @@
 
     out_message = shifted(reduced(out_parts, True), 1, 0)
     grad_parts, a_grad, b_grad = lax.optimization_barrier((grad_parts, a_grad, b_grad))
-    grad_message = shifted(reduced(grad_parts, False), -1, 0)
+    grad_message = reduced(grad_parts, False)
+    end_message = shifted(grad_message, -1, 0, ends=True)
+    grad_message = shifted(grad_message, -1, 0, ends=False)
     next_input = expanded(out_message)
     next_input, grad_message = lax.optimization_barrier((next_input, grad_message))
     prev_grad = expanded(grad_message)
+    prev_grad, end_message = lax.optimization_barrier((prev_grad, end_message))
+    (prev_grad,) = call(
+        expand_end,
+        [sds(1, tokens, width)],
+        (end_message,),
+        (prev_grad,),
+        far_outs=True,
+        scratch=[pltpu.VMEM((tokens, width), jnp.bfloat16), dma((CHUNKS,))],
+        aliases={1: 0},
+    )
     return next_input, prev_grad, jnp.swapaxes(a_grad, 0, 1)[None], b_grad
 
 

time: 36.6 us -> 41.1 us (1.12)
  starting transfers between devices: 18 us -> 23.3 us
  waiting for transfers between devices: 4.53 us -> 3.23 us
    ppermute x14 -> x15, starting transfers between devices: 18 us -> 23.3 us  [shifted(): return lax.ppermute(block, ('section', 'expert'), route)]
    ppermute x14 -> x15, waiting for transfers between devices: 4.53 us -> 3.23 us  [shifted(): return lax.ppermute(block, ('section', 'expert'), route)]
    pallas_call x11 -> x12, Pallas kernels: 13.2 us -> 13.2 us  [call(): pl.pallas_call(body, out_shape=outs, in_specs=[NEAR] * len(args) + [FAR]...]
  transfers between devices with their start and end apart: 14 -> 15, of which waited for: 8 -> 6; matrix products, arithmetic and copies ran while one was open for 0% -> 0% of each run, Pallas kernels for 28% -> 28%
where the time goes in v18:
time: 41.1 us; the launch traced here: 40.5 us
  starting transfers between devices  23.3 us (57%)
  Pallas kernels  13.2 us (32%)
  waiting for transfers between devices  3.23 us (8%)
  between operations  0.75 us (2%)
    ppermute x15, starting transfers between devices, shifted(): return lax.ppermute(block, ('section', 'expert'), route)  23.3 us
    pallas_call x12, Pallas kernels, call(): pl.pallas_call(body, out_shape=outs, in_specs=[NEAR] * len(args) + [FAR]...  13.2 us
    ppermute x15, waiting for transfers between devices, shifted(): return lax.ppermute(block, ('section', 'expert'), route)  3.23 us
  transfers between devices with their start and end apart: 15, of which 6 were waited for; matrix products, arithmetic and copies ran while one was open for 0% of the time, Pallas kernels for 28%

profile of v18, /device:TPU:0, one launch (start us, length us, event | category | flops | bytes accessed | tf_op | source)
XLA Modules:
  0.0 40.5 jit_solution(3541508924221510046)
XLA Ops:
  0.6 1.9 %shard_map.120 = (bf16[16,4096]{1,0:T(8,128)(2,1)S(1)}, f32[16,128]{1,0:T(8,128)S(1)}, bf16[128,4096]{1,0:T(8,128)(2,1)S(1)}, bf16[16,256]{1,0:T(8,128)(2,1)S(1)}, bf16[16,4096]{1,0:T(8,128)(2,1)S(1)}) custom-call(s32[8,128]{1,0:T(8,128)} %bitcast.21, s32[8,128]{1,0:T(8,128)} %bitcast.22, bf16[1,128,4096]{2,1,0:T(8,128)(2,1)} %x_hbm.1, ...), custom_call_target="tpu_custom_call" | custom-call | flops 16777216 | bytes 3571712 | tf_op jit(solution)/shard_map/pallas_call | solution.py:35
  2.5 4.0 %collective-permute-start.2 = (bf16[16,4096]{1,0:T(8,128)(2,1)S(1)}, bf16[16,4096]{1,0:T(8,128)(2,1)S(1)}, u32[]{:S(2)}, u32[]{:S(2)}) collective-permute-start(bf16[16,4096]{1,0:T(8,128)(2,1)S(1)} %get-tuple-element.34.refs_0_), channel_id=1, source_target_pairs={{0,3},{1,2},{2,1},{3,0},{4,7},{5,6},{6,5},{7,4},{8,11},{9,10},{10,... | collective-permute-start | bytes 393224 | tf_op jit(solution)/shard_map/ppermute | solution.py:232
  6.5 0.5 %collective-permute-start.1 = (bf16[16,4096]{1,0:T(8,128)(2,1)S(1)}, bf16[16,4096]{1,0:T(8,128)(2,1)S(1)}, u32[]{:S(2)}, u32[]{:S(2)}) collective-permute-start(bf16[16,4096]{1,0:T(8,128)(2,1)S(1)} %get-tuple-element.34.refs_0_), channel_id=1, source_target_pairs={{0,2},{1,3},{2,0},{3,1},{4,6},{5,7},{6,4},{7,5},{8,10},{9,11},{10,... | collective-permute-start | bytes 393224 | tf_op jit(solution)/shard_map/ppermute | solution.py:232
  7.0 0.1 collective-permute-start
  7.1 2.2 %shard_map.121.refs_6_._.refs_8_ = bf16[256,4096]{1,0:T(8,128)(2,1)S(1)} custom-call(bf16[16,256]{1,0:T(8,128)(2,1)S(1)} %get-tuple-element.35.a_ref.refs_7_, bf16[16,4096]{1,0:T(8,128)(2,1)S(1)} %get-tuple-element.36.b_ref.refs_5_, bf16[1,256,4096]{2,1,0:T(8,128)(2,1)} %down_hbm.1), custom_call_target="tpu_custom_call" | custom-call | bytes 1 | tf_op jit(solution)/shard_map/pallas_call | solution.py:35
  9.3 0.3 shard_map.125.refs_0_.refs_3_
  9.6 2.9 %collective-permute-start.9 = (bf16[16,4096]{1,0:T(8,128)(2,1)S(1)}, bf16[16,4096]{1,0:T(8,128)(2,1)S(1)}, u32[]{:S(2)}, u32[]{:S(2)}) collective-permute-start(bf16[16,4096]{1,0:T(8,128)(2,1)S(1)} %shard_map.125.refs_0_.refs_3_), channel_id=1, source_target_pairs={{0,3},{1,2},{2,1},{3,0},{4,7},{5,6},{6,5},{7,4},{8,11},{9,10},{10,... | collective-permute-start | bytes 393224 | tf_op jit(solution)/shard_map/ppermute | solution.py:232
  12.5 0.5 %collective-permute-start.8 = (bf16[16,4096]{1,0:T(8,128)(2,1)S(1)}, bf16[16,4096]{1,0:T(8,128)(2,1)S(1)}, u32[]{:S(2)}, u32[]{:S(2)}) collective-permute-start(bf16[16,4096]{1,0:T(8,128)(2,1)S(1)} %shard_map.125.refs_0_.refs_3_), channel_id=1, source_target_pairs={{0,2},{1,3},{2,0},{3,1},{4,6},{5,7},{6,4},{7,5},{8,10},{9,11},{10,... | collective-permute-start | bytes 393224 | tf_op jit(solution)/shard_map/ppermute | solution.py:232
  13.0 0.1 collective-permute-start.7
  13.1 0.1 collective-permute-done.1.refs_2_
  13.2 0.2 collective-permute-done.refs_1_
  13.5 1.8 %shard_map.122 = (bf16[16,4096]{1,0:T(8,128)(2,1)S(1)}, bf16[16,4224]{1,0:T(8,128)(2,1)S(1)}, bf16[16,4224]{1,0:T(8,128)(2,1)S(1)}, bf16[16,4224]{1,0:T(8,128)(2...) custom-call(bf16[16,4096]{1,0:T(8,128)(2,1)S(1)} %get-tuple-element., ...), custom_call_target="tpu_custom_call" | custom-call | flops 4026531840 | bytes 7526400 | tf_op jit(solution)/shard_map/pallas_call | solution.py:35
  15.3 2.6 %collective-permute-start.3 = (bf16[16,4224]{1,0:T(8,128)(2,1)S(1)}, bf16[16,4224]{1,0:T(8,128)(2,1)S(1)}, u32[]{:S(2)}, u32[]{:S(2)}) collective-permute-start(bf16[16,4224]{1,0:T(8,128)(2,1)S(1)} %get-tuple-element.38), channel_id=1, source_target_pairs={{0,3},{1,2},{2,1},{3,0},{4,7},{5,6},{6,5},{7,4},{8,11},{9,10},{10,... | collective-permute-start | bytes 405512 | tf_op jit(solution)/shard_map/ppermute | solution.py:232
  17.9 0.5 %collective-permute-start.4 = (bf16[16,4224]{1,0:T(8,128)(2,1)S(1)}, bf16[16,4224]{1,0:T(8,128)(2,1)S(1)}, u32[]{:S(2)}, u32[]{:S(2)}) collective-permute-start(bf16[16,4224]{1,0:T(8,128)(2,1)S(1)} %get-tuple-element.39), channel_id=1, source_target_pairs={{0,1},{1,0},{2,3},{3,2},{4,5},{5,4},{6,7},{7,6},{8,9},{9,8},{10,11... | collective-permute-start | bytes 405512 | tf_op jit(solution)/shard_map/ppermute | solution.py:232
  18.4 0.4 %collective-permute-start.5 = (bf16[16,4224]{1,0:T(8,128)(2,1)S(1)}, bf16[16,4224]{1,0:T(8,128)(2,1)S(1)}, u32[]{:S(2)}, u32[]{:S(2)}) collective-permute-start(bf16[16,4224]{1,0:T(8,128)(2,1)S(1)} %get-tuple-element.40), channel_id=1, source_target_pairs={{0,2},{1,3},{2,0},{3,1},{4,6},{5,7},{6,4},{7,5},{8,10},{9,11},{10,... | collective-permute-start | bytes 405512 | tf_op jit(solution)/shard_map/ppermute | solution.py:232
  18.9 0.4 collective-permute-done.7.refs_1_.refs_4_
  19.2 2.5 %shard_map.126 = (bf16[16,4096]{1,0:T(8,128)(2,1)S(1)}, bf16[16,4096]{1,0:T(8,128)(2,1)S(1)}, bf16[16,4096]{1,0:T(8,128)(2,1)S(1)}, bf16[16,4096]{1,0:T(8,128)(2,1)S(1)}) custom-call(bf16[16,4096]{1,0:T(8,128)(2,1)S(1)} %shard_map.125.refs_0_.refs_3_, bf16[16,4096]{1,0:T(8,128)(2,1)S(1)} %collective-permute-done.7.refs_1_.refs_4_, ...), custom_call_target="tpu_custom_call" | custom-call | flops 4026531840 | bytes 7471104 | tf_op jit(solution)/shard_map/pallas_call | solution.py:35
  21.7 2.2 %collective-permute-start.10 = (bf16[16,4096]{1,0:T(8,128)(2,1)S(1)}, bf16[16,4096]{1,0:T(8,128)(2,1)S(1)}, u32[]{:S(2)}, u32[]{:S(2)}) collective-permute-start(bf16[16,4096]{1,0:T(8,128)(2,1)S(1)} %get-tuple-element.45), channel_id=1, source_target_pairs={{0,3},{1,2},{2,1},{3,0},{4,7},{5,6},{6,5},{7,4},{8,11},{9,10},{10,... | collective-permute-start | bytes 393224 | tf_op jit(solution)/shard_map/ppermute | solution.py:232
  23.9 0.5 %collective-permute-start.11 = (bf16[16,4096]{1,0:T(8,128)(2,1)S(1)}, bf16[16,4096]{1,0:T(8,128)(2,1)S(1)}, u32[]{:S(2)}, u32[]{:S(2)}) collective-permute-start(bf16[16,4096]{1,0:T(8,128)(2,1)S(1)} %get-tuple-element.46), channel_id=1, source_target_pairs={{0,1},{1,0},{2,3},{3,2},{4,5},{5,4},{6,7},{7,6},{8,9},{9,8},{10,11... | collective-permute-start | bytes 393224 | tf_op jit(solution)/shard_map/ppermute | solution.py:232
  24.5 1.2 %collective-permute-start.12 = (bf16[16,4096]{1,0:T(8,128)(2,1)S(1)}, bf16[16,4096]{1,0:T(8,128)(2,1)S(1)}, u32[]{:S(2)}, u32[]{:S(2)}) collective-permute-start(bf16[16,4096]{1,0:T(8,128)(2,1)S(1)} %get-tuple-element.47), channel_id=1, source_target_pairs={{0,2},{1,3},{2,0},{3,1},{4,6},{5,7},{6,4},{7,5},{8,10},{9,11},{10,... | collective-permute-start | bytes 393224 | tf_op jit(solution)/shard_map/ppermute | solution.py:232
  25.7 1.0 %shard_map.127 = f32[16,256]{1,0:T(8,128)} custom-call(bf16[16,4096]{1,0:T(8,128)(2,1)S(1)} %shard_map.125.refs_0_.refs_3_, bf16[16,4096]{1,0:T(8,128)(2,1)S(1)} %collective-permute-done.7.refs_1_.refs_4_, bf16[16,4096]{1,0:T(8,128)(2,1)S(1)} %collective-permute-done.8.refs_2_.refs_5_, bf16[16,4096]{1,0:T(8,128)(2,1)S(1)} %collective-permute-done.9.refs_3_.refs_6_, ...), custom_call_target="tpu_custom_call" | custom-call | flops 838860800 | bytes 704512 | tf_op jit(solution)/shard_map/pallas_call | solution.py:35
  26.8 0.1 shard_map.123
  26.9 0.1 collective-permute-start.6
  27.0 0.9 %shard_map.128 = f32[1,1,16,1024]{3,2,1,0:T(8,128)} custom-call(bf16[16,64]{1,0:T(8,128)(2,1)S(1)} %get-tuple-element.51.latent_ref, bf16[16,4224]{1,0:T(8,128)(2,1)S(1)} %collective-permute-done.3.refs_1_.refs_0_, bf16[16,4224]{1,0:T(8,128)(2,1)S(1)} %collective-permute-done.4.refs_2_.refs_1_, bf16[16,4224]{1,0:T(8,128)(2,1)S(1)} %collective-permute-done.5.refs_3_.refs_2_, ...), custom_call_target="tpu_custom_call" | custom-call | flops 838860800 | bytes 997376 | tf_op jit(solution)/shard_map/pallas_call | solution.py:35
  27.8 1.1 %collective-permute-done.10.refs_1_ = bf16[16,4096]{1,0:T(8,128)(2,1)S(1)} collective-permute-done((bf16[16,4096]{1,0:T(8,128)(2,1)S(1)}, bf16[16,4096]{1,0:T(8,128)(2,1)S(1)}, u32[]{:S(2)}, u32[]{:S(2)}) %collective-permute-start.10) | collective-permute-done | bytes 131104 | tf_op jit(solution)/shard_map/ppermute | solution.py:232
  28.9 1.3 %collective-permute-done.11.refs_2_ = bf16[16,4096]{1,0:T(8,128)(2,1)S(1)} collective-permute-done((bf16[16,4096]{1,0:T(8,128)(2,1)S(1)}, bf16[16,4096]{1,0:T(8,128)(2,1)S(1)}, u32[]{:S(2)}, u32[]{:S(2)}) %collective-permute-start.11) | collective-permute-done | bytes 131104 | tf_op jit(solution)/shard_map/ppermute | solution.py:232
  30.2 0.1 collective-permute-done.12.refs_3_
  30.3 0.1 shard_map.129
  30.4 1.3 %collective-permute-start.13 = (bf16[16,4224]{1,0:T(8,128)(2,1)S(1)}, bf16[16,4224]{1,0:T(8,128)(2,1)S(1)}, u32[]{:S(2)}, u32[]{:S(2)}) collective-permute-start(bf16[16,4224]{1,0:T(8,128)(2,1)S(1)} %shard_map.129), channel_id=1, source_target_pairs={{4,0},{5,1},{6,2},{7,3},{8,4},{9,5},{10,6},{11,7},{12,8},{13,9},{1... | collective-permute-start | bytes 405512 | tf_op jit(solution)/shard_map/ppermute | solution.py:232
  31.7 6.3 %collective-permute-start.14 = (bf16[16,4224]{1,0:T(8,128)(2,1)S(1)}, bf16[16,4224]{1,0:T(8,128)(2,1)S(1)}, u32[]{:S(2)}, u32[]{:S(2)}) collective-permute-start(bf16[16,4224]{1,0:T(8,128)(2,1)S(1)} %shard_map.129), channel_id=1, source_target_pairs={{0,28},{1,29},{2,30},{3,31}} | collective-permute-start | bytes 405512 | tf_op jit(solution)/shard_map/ppermute | solution.py:232
  38.0 1.2 %shard_map.124 = bf16[1,128,4096]{2,1,0:T(8,128)(2,1)} custom-call(bf16[16,4224]{1,0:T(8,128)(2,1)S(1)} %collective-permute-done.6.message_ref), custom_call_target="tpu_custom_call" | custom-call | flops 16777216 | bytes 1183744 | tf_op jit(solution)/shard_map/pallas_call | solution.py:35
  39.2 1.2 %shard_map.130._ = bf16[1,128,4096]{2,1,0:T(8,128)(2,1)} custom-call(bf16[16,4224]{1,0:T(8,128)(2,1)S(1)} %collective-permute-done.13.message_ref), custom_call_target="tpu_custom_call" | custom-call | flops 16777216 | bytes 1183744 | tf_op jit(solution)/shard_map/pallas_call | solution.py:35
  (14 shorter events, 0.1 us)
Async XLA Ops:
  2.5 10.4 %collective-permute-start.2 = (bf16[16,4096]{1,0:T(8,128)(2,1)S(1)}, bf16[16,4096]{1,0:T(8,128)(2,1)S(1)}, u32[]{:S(2)}, u32[]{:S(2)}) collective-permute-start(bf16[16,4096]{1,0:T(8,128)(2,1)S(1)} %get-tuple-element.34.refs_0_), channel_id=1, source_target_pairs={{0,3},{1,2},{2,1},{3,0},{4,7},{5,6},{6,5},{7,4},{8,11},{9,10},{10,... | collective-permute-start | bytes 393224 | tf_op jit(solution)/shard_map/ppermute | solution.py:232
  6.5 6.7 %collective-permute-start.1 = (bf16[16,4096]{1,0:T(8,128)(2,1)S(1)}, bf16[16,4096]{1,0:T(8,128)(2,1)S(1)}, u32[]{:S(2)}, u32[]{:S(2)}) collective-permute-start(bf16[16,4096]{1,0:T(8,128)(2,1)S(1)} %get-tuple-element.34.refs_0_), channel_id=1, source_target_pairs={{0,2},{1,3},{2,0},{3,1},{4,6},{5,7},{6,4},{7,5},{8,10},{9,11},{10,... | collective-permute-start | bytes 393224 | tf_op jit(solution)/shard_map/ppermute | solution.py:232
  7.0 6.5 %collective-permute-start = (bf16[16,4096]{1,0:T(8,128)(2,1)S(1)}, bf16[16,4096]{1,0:T(8,128)(2,1)S(1)}, u32[]{:S(2)}, u32[]{:S(2)}) collective-permute-start(bf16[16,4096]{1,0:T(8,128)(2,1)S(1)} %get-tuple-element.34.refs_0_), channel_id=1, source_target_pairs={{0,1},{1,0},{2,3},{3,2},{4,5},{5,4},{6,7},{7,6},{8,9},{9,8},{10,11... | collective-permute-start | bytes 393224 | tf_op jit(solution)/shard_map/ppermute | solution.py:232
  9.3 4.2 %copy-start = (bf16[1,256,4096]{2,1,0:T(8,128)(2,1)S(1)}, bf16[1,256,4096]{2,1,0:T(8,128)(2,1)}, u32[]{:S(2)}) copy-start(bf16[1,256,4096]{2,1,0:T(8,128)(2,1)} %param.12) | copy-start | bytes 6291460
  9.3 4.2 %copy-start.1 = (bf16[1,256,4096]{2,1,0:T(8,128)(2,1)S(1)}, bf16[1,256,4096]{2,1,0:T(8,128)(2,1)}, u32[]{:S(2)}) copy-start(bf16[1,256,4096]{2,1,0:T(8,128)(2,1)} %param.13) | copy-start | bytes 6291460
  9.6 8.9 %collective-permute-start.9 = (bf16[16,4096]{1,0:T(8,128)(2,1)S(1)}, bf16[16,4096]{1,0:T(8,128)(2,1)S(1)}, u32[]{:S(2)}, u32[]{:S(2)}) collective-permute-start(bf16[16,4096]{1,0:T(8,128)(2,1)S(1)} %shard_map.125.refs_0_.refs_3_), channel_id=1, source_target_pairs={{0,3},{1,2},{2,1},{3,0},{4,7},{5,6},{6,5},{7,4},{8,11},{9,10},{10,... | collective-permute-start | bytes 393224 | tf_op jit(solution)/shard_map/ppermute | solution.py:232
  12.5 6.4 %collective-permute-start.8 = (bf16[16,4096]{1,0:T(8,128)(2,1)S(1)}, bf16[16,4096]{1,0:T(8,128)(2,1)S(1)}, u32[]{:S(2)}, u32[]{:S(2)}) collective-permute-start(bf16[16,4096]{1,0:T(8,128)(2,1)S(1)} %shard_map.125.refs_0_.refs_3_), channel_id=1, source_target_pairs={{0,2},{1,3},{2,0},{3,1},{4,6},{5,7},{6,4},{7,5},{8,10},{9,11},{10,... | collective-permute-start | bytes 393224 | tf_op jit(solution)/shard_map/ppermute | solution.py:232
  13.0 6.3 %collective-permute-start.7 = (bf16[16,4096]{1,0:T(8,128)(2,1)S(1)}, bf16[16,4096]{1,0:T(8,128)(2,1)S(1)}, u32[]{:S(2)}, u32[]{:S(2)}) collective-permute-start(bf16[16,4096]{1,0:T(8,128)(2,1)S(1)} %shard_map.125.refs_0_.refs_3_), channel_id=1, source_target_pairs={{0,1},{1,0},{2,3},{3,2},{4,5},{5,4},{6,7},{7,6},{8,9},{9,8},{10,11... | collective-permute-start | bytes 393224 | tf_op jit(solution)/shard_map/ppermute | solution.py:232
  15.3 9.2 %collective-permute-start.3 = (bf16[16,4224]{1,0:T(8,128)(2,1)S(1)}, bf16[16,4224]{1,0:T(8,128)(2,1)S(1)}, u32[]{:S(2)}, u32[]{:S(2)}) collective-permute-start(bf16[16,4224]{1,0:T(8,128)(2,1)S(1)} %get-tuple-element.38), channel_id=1, source_target_pairs={{0,3},{1,2},{2,1},{3,0},{4,7},{5,6},{6,5},{7,4},{8,11},{9,10},{10,... | collective-permute-start | bytes 405512 | tf_op jit(solution)/shard_map/ppermute | solution.py:232
  17.9 8.9 %collective-permute-start.4 = (bf16[16,4224]{1,0:T(8,128)(2,1)S(1)}, bf16[16,4224]{1,0:T(8,128)(2,1)S(1)}, u32[]{:S(2)}, u32[]{:S(2)}) collective-permute-start(bf16[16,4224]{1,0:T(8,128)(2,1)S(1)} %get-tuple-element.39), channel_id=1, source_target_pairs={{0,1},{1,0},{2,3},{3,2},{4,5},{5,4},{6,7},{7,6},{8,9},{9,8},{10,11... | collective-permute-start | bytes 405512 | tf_op jit(solution)/shard_map/ppermute | solution.py:232
  18.4 8.4 %collective-permute-start.5 = (bf16[16,4224]{1,0:T(8,128)(2,1)S(1)}, bf16[16,4224]{1,0:T(8,128)(2,1)S(1)}, u32[]{:S(2)}, u32[]{:S(2)}) collective-permute-start(bf16[16,4224]{1,0:T(8,128)(2,1)S(1)} %get-tuple-element.40), channel_id=1, source_target_pairs={{0,2},{1,3},{2,0},{3,1},{4,6},{5,7},{6,4},{7,5},{8,10},{9,11},{10,... | collective-permute-start | bytes 405512 | tf_op jit(solution)/shard_map/ppermute | solution.py:232
  21.7 7.2 %collective-permute-start.10 = (bf16[16,4096]{1,0:T(8,128)(2,1)S(1)}, bf16[16,4096]{1,0:T(8,128)(2,1)S(1)}, u32[]{:S(2)}, u32[]{:S(2)}) collective-permute-start(bf16[16,4096]{1,0:T(8,128)(2,1)S(1)} %get-tuple-element.45), channel_id=1, source_target_pairs={{0,3},{1,2},{2,1},{3,0},{4,7},{5,6},{6,5},{7,4},{8,11},{9,10},{10,... | collective-permute-start | bytes 393224 | tf_op jit(solution)/shard_map/ppermute | solution.py:232
  23.9 6.3 %collective-permute-start.11 = (bf16[16,4096]{1,0:T(8,128)(2,1)S(1)}, bf16[16,4096]{1,0:T(8,128)(2,1)S(1)}, u32[]{:S(2)}, u32[]{:S(2)}) collective-permute-start(bf16[16,4096]{1,0:T(8,128)(2,1)S(1)} %get-tuple-element.46), channel_id=1, source_target_pairs={{0,1},{1,0},{2,3},{3,2},{4,5},{5,4},{6,7},{7,6},{8,9},{9,8},{10,11... | collective-permute-start | bytes 393224 | tf_op jit(solution)/shard_map/ppermute | solution.py:232
  24.5 5.8 %collective-permute-start.12 = (bf16[16,4096]{1,0:T(8,128)(2,1)S(1)}, bf16[16,4096]{1,0:T(8,128)(2,1)S(1)}, u32[]{:S(2)}, u32[]{:S(2)}) collective-permute-start(bf16[16,4096]{1,0:T(8,128)(2,1)S(1)} %get-tuple-element.47), channel_id=1, source_target_pairs={{0,2},{1,3},{2,0},{3,1},{4,6},{5,7},{6,4},{7,5},{8,10},{9,11},{10,... | collective-permute-start | bytes 393224 | tf_op jit(solution)/shard_map/ppermute | solution.py:232
  26.9 11.1 %collective-permute-start.6 = (bf16[16,4224]{1,0:T(8,128)(2,1)S(1)}, bf16[16,4224]{1,0:T(8,128)(2,1)S(1)}, u32[]{:S(2)}, u32[]{:S(2)}) collective-permute-start(bf16[16,4224]{1,0:T(8,128)(2,1)S(1)} %shard_map.123), channel_id=1, source_target_pairs={{0,4},{1,5},{2,6},{3,7},{4,8},{5,9},{6,10},{7,11},{8,12},{9,13},{1... | collective-permute-start | bytes 405512 | tf_op jit(solution)/shard_map/ppermute | solution.py:232
  30.4 8.8 %collective-permute-start.13 = (bf16[16,4224]{1,0:T(8,128)(2,1)S(1)}, bf16[16,4224]{1,0:T(8,128)(2,1)S(1)}, u32[]{:S(2)}, u32[]{:S(2)}) collective-permute-start(bf16[16,4224]{1,0:T(8,128)(2,1)S(1)} %shard_map.129), channel_id=1, source_target_pairs={{4,0},{5,1},{6,2},{7,3},{8,4},{9,5},{10,6},{11,7},{12,8},{13,9},{1... | collective-permute-start | bytes 405512 | tf_op jit(solution)/shard_map/ppermute | solution.py:232
  31.7 8.8 %collective-permute-start.14 = (bf16[16,4224]{1,0:T(8,128)(2,1)S(1)}, bf16[16,4224]{1,0:T(8,128)(2,1)S(1)}, u32[]{:S(2)}, u32[]{:S(2)}) collective-permute-start(bf16[16,4224]{1,0:T(8,128)(2,1)S(1)} %shard_map.129), channel_id=1, source_target_pairs={{0,28},{1,29},{2,30},{3,31}} | collective-permute-start | bytes 405512 | tf_op jit(solution)/shard_map/ppermute | solution.py:232

commit v19 on v13

--- a/solution.py
+++ b/solution.py
@@ -317,6 +317,30 @@
         (*g_blocks, hidden, b_near),
         flops=200 * rows * rank * width,
     )
+
+    def merged(parts, gated, columns):
+        return call(functools.partial(combine, gated), [sds(slots, columns)], (place, *parts))[0]
+
+    def reduced(parts, gated):
+        if flight > 1:
+            parts = [between_groups(merged(parts, False, width), flight)]
+        return merged(parts, gated, wide)
+
+    def expanded(message):
+        return call(
+            expand,
+            [sds(1, tokens, width)],
+            (message,),
+            far_outs=True,
+            scratch=[pltpu.VMEM((tokens, width), jnp.bfloat16), dma((CHUNKS,))],
+            flops=2 * slots * tokens * width,
+        )[0]
+
+    out_message = shifted(reduced(out_parts, True), 1, 0)
+    grad_parts, a_grad = lax.optimization_barrier((grad_parts, a_grad))
+    grad_message = reduced(grad_parts, False)
+    grad_message, latent = lax.optimization_barrier((grad_message, latent))
+    grad_message = shifted(grad_message, -1, 0)
     if flight == 1:
         (b_grad,) = call(
             up_map_grad,
@@ -330,29 +354,8 @@
         spread = jnp.where(mine[:, None, None], part[None], 0.0)
         b_grad = lax.psum_scatter(spread, "expert", scatter_dimension=2, tiled=True)[None]
 
-    def merged(parts, gated, columns):
-        return call(functools.partial(combine, gated), [sds(slots, columns)], (place, *parts))[0]
-
-    def reduced(parts, gated):
-        if flight > 1:
-            parts = [between_groups(merged(parts, False, width), flight)]
-        return merged(parts, gated, wide)
-
-    def expanded(message):
-        return call(
-            expand,
-            [sds(1, tokens, width)],
-            (message,),
-            far_outs=True,
-            scratch=[pltpu.VMEM((tokens, width), jnp.bfloat16), dma((CHUNKS,))],
-            flops=2 * slots * tokens * width,
-        )[0]
-
-    out_message = shifted(reduced(out_parts, True), 1, 0)
-    grad_parts, a_grad, b_grad = lax.optimization_barrier((grad_parts, a_grad, b_grad))
-    grad_message = shifted(reduced(grad_parts, False), -1, 0)
     next_input = expanded(out_message)
-    next_input, grad_message = lax.optimization_barrier((next_input, grad_message))
+    next_input, b_grad, grad_message = lax.optimization_barrier((next_input, b_grad, grad_message))
     prev_grad = expanded(grad_message)
     return next_input, prev_grad, jnp.swapaxes(a_grad, 0, 1)[None], b_grad
 

time: 36.2 us -> 36.2 us (level)
  transfers between devices with their start and end apart: 14 -> 14, of which waited for: 5 -> 4; matrix products, arithmetic and copies ran while one was open for 0% -> 0% of each run, Pallas kernels for 24% -> 24%
where the time goes in v19:
time: 36.2 us; the launch traced here: 36 us
  starting transfers between devices  17 us (47%)
  Pallas kernels  11.7 us (32%)
  waiting for transfers between devices  5.71 us (16%)
  local copies, waits for them, and re-layouts  0.93 us (3%)
  between operations  0.74 us (2%)
    ppermute x14, starting transfers between devices, shifted(): return lax.ppermute(block, ('section', 'expert'), route)  17 us
    pallas_call x11, Pallas kernels, call(): pl.pallas_call(body, out_shape=outs, in_specs=[NEAR] * len(args) + [FAR]...  11.7 us
    ppermute x14, waiting for transfers between devices, shifted(): return lax.ppermute(block, ('section', 'expert'), route)  5.71 us
    unnamed x12, local copies, waits for them, and re-layouts  0.93 us
  transfers between devices with their start and end apart: 14, of which 4 were waited for; matrix products, arithmetic and copies ran while one was open for 0% of the time, Pallas kernels for 24%

profile of v19, /device:TPU:0, one launch (start us, length us, event | category | flops | bytes accessed | tf_op | source)
XLA Modules:
  0.0 36.0 jit_solution(703860233044746447)
XLA Ops:
  0.7 1.8 %shard_map.120 = (bf16[16,4096]{1,0:T(8,128)(2,1)S(1)}, f32[16,128]{1,0:T(8,128)S(1)}, bf16[128,4096]{1,0:T(8,128)(2,1)S(1)}) custom-call(s32[8,128]{1,0:T(8,128)} %bitcast.25, s32[8,128]{1,0:T(8,128)} %bitcast.26, bf16[1,128,4096]{2,1,0:T(8,128)(2,1)} %x_hbm.1, bf16[1,128,4096]{2,1,0:T(8,128)(2,1)} %cot_hbm.1), custom_call_target="tpu_custom_call" | custom-call | flops 16777216 | bytes 3293184 | tf_op jit(solution)/shard_map/pallas_call | solution.py:35
  2.5 4.0 %collective-permute-start.2 = (bf16[16,4096]{1,0:T(8,128)(2,1)S(1)}, bf16[16,4096]{1,0:T(8,128)(2,1)S(1)}, u32[]{:S(2)}, u32[]{:S(2)}) collective-permute-start(bf16[16,4096]{1,0:T(8,128)(2,1)S(1)} %get-tuple-element.32.refs_0_), channel_id=1, source_target_pairs={{0,3},{1,2},{2,1},{3,0},{4,7},{5,6},{6,5},{7,4},{8,11},{9,10},{10,... | collective-permute-start | bytes 393224 | tf_op jit(solution)/shard_map/ppermute | solution.py:211
  6.4 0.5 %collective-permute-start.1 = (bf16[16,4096]{1,0:T(8,128)(2,1)S(1)}, bf16[16,4096]{1,0:T(8,128)(2,1)S(1)}, u32[]{:S(2)}, u32[]{:S(2)}) collective-permute-start(bf16[16,4096]{1,0:T(8,128)(2,1)S(1)} %get-tuple-element.32.refs_0_), channel_id=1, source_target_pairs={{0,2},{1,3},{2,0},{3,1},{4,6},{5,7},{6,4},{7,5},{8,10},{9,11},{10,... | collective-permute-start | bytes 393224 | tf_op jit(solution)/shard_map/ppermute | solution.py:211
  6.9 0.1 collective-permute-start
  7.1 0.9 %copy-done.1 = bf16[1,1,16,4096]{3,2,1,0:T(8,128)(2,1)S(1)} copy-done((bf16[1,1,16,4096]{3,2,1,0:T(8,128)(2,1)S(1)}, bf16[1,1,16,4096]{3,2,1,0:T(8,128)(2,1)}, u32[]{:S(2)}) %copy-start.1) | copy-done | bytes 131096
  8.0 0.7 %shard_map.121.refs_6_._.refs_8_ = bf16[256,4096]{1,0:T(8,128)(2,1)S(1)} custom-call(bf16[256,4096]{1,0:T(8,128)(2,1)S(1)} %bitcast.16, bf16[16,256]{1,0:T(8,128)(2,1)S(1)} %bitcast.19, bf16[16,4096]{1,0:T(8,128)(2,1)S(1)} %bitcast.17, f32[16,128]{1,0:T(8,128)S(1)} %get-tuple-element.31._.place_ref), custom_call_target="tpu_custom_call" | custom-call | bytes 1 | tf_op jit(solution)/shard_map/pallas_call | solution.py:35
  8.7 0.0 copy-start.4
  8.7 0.0 copy-start.5
  8.7 0.3 shard_map.125.refs_0_.refs_3_
  9.0 2.9 %collective-permute-start.9 = (bf16[16,4096]{1,0:T(8,128)(2,1)S(1)}, bf16[16,4096]{1,0:T(8,128)(2,1)S(1)}, u32[]{:S(2)}, u32[]{:S(2)}) collective-permute-start(bf16[16,4096]{1,0:T(8,128)(2,1)S(1)} %shard_map.125.refs_0_.refs_3_), channel_id=1, source_target_pairs={{0,3},{1,2},{2,1},{3,0},{4,7},{5,6},{6,5},{7,4},{8,11},{9,10},{10,... | collective-permute-start | bytes 393224 | tf_op jit(solution)/shard_map/ppermute | solution.py:211
  11.9 0.5 %collective-permute-start.8 = (bf16[16,4096]{1,0:T(8,128)(2,1)S(1)}, bf16[16,4096]{1,0:T(8,128)(2,1)S(1)}, u32[]{:S(2)}, u32[]{:S(2)}) collective-permute-start(bf16[16,4096]{1,0:T(8,128)(2,1)S(1)} %shard_map.125.refs_0_.refs_3_), channel_id=1, source_target_pairs={{0,2},{1,3},{2,0},{3,1},{4,6},{5,7},{6,4},{7,5},{8,10},{9,11},{10,... | collective-permute-start | bytes 393224 | tf_op jit(solution)/shard_map/ppermute | solution.py:211
  12.4 0.4 %collective-permute-start.7 = (bf16[16,4096]{1,0:T(8,128)(2,1)S(1)}, bf16[16,4096]{1,0:T(8,128)(2,1)S(1)}, u32[]{:S(2)}, u32[]{:S(2)}) collective-permute-start(bf16[16,4096]{1,0:T(8,128)(2,1)S(1)} %shard_map.125.refs_0_.refs_3_), channel_id=1, source_target_pairs={{0,1},{1,0},{2,3},{3,2},{4,5},{5,4},{6,7},{7,6},{8,9},{9,8},{10,11... | collective-permute-start | bytes 393224 | tf_op jit(solution)/shard_map/ppermute | solution.py:211
  12.8 1.2 %collective-permute-done.1.refs_2_ = bf16[16,4096]{1,0:T(8,128)(2,1)S(1)} collective-permute-done((bf16[16,4096]{1,0:T(8,128)(2,1)S(1)}, bf16[16,4096]{1,0:T(8,128)(2,1)S(1)}, u32[]{:S(2)}, u32[]{:S(2)}) %collective-permute-start.1) | collective-permute-done | bytes 131104 | tf_op jit(solution)/shard_map/ppermute | solution.py:211
  14.0 1.8 %shard_map.122 = (bf16[16,4096]{1,0:T(8,128)(2,1)S(1)}, bf16[16,4224]{1,0:T(8,128)(2,1)S(1)}, bf16[16,4224]{1,0:T(8,128)(2,1)S(1)}, bf16[16,4224]{1,0:T(8,128)(2...) custom-call(bf16[16,4096]{1,0:T(8,128)(2,1)S(1)} %get-tuple-element., ...), custom_call_target="tpu_custom_call" | custom-call | flops 4026531840 | bytes 7526400 | tf_op jit(solution)/shard_map/pallas_call | solution.py:35
  15.8 2.5 %collective-permute-start.3 = (bf16[16,4224]{1,0:T(8,128)(2,1)S(1)}, bf16[16,4224]{1,0:T(8,128)(2,1)S(1)}, u32[]{:S(2)}, u32[]{:S(2)}) collective-permute-start(bf16[16,4224]{1,0:T(8,128)(2,1)S(1)} %get-tuple-element.34), channel_id=1, source_target_pairs={{0,3},{1,2},{2,1},{3,0},{4,7},{5,6},{6,5},{7,4},{8,11},{9,10},{10,... | collective-permute-start | bytes 405512 | tf_op jit(solution)/shard_map/ppermute | solution.py:211
  18.3 0.6 %collective-permute-start.4 = (bf16[16,4224]{1,0:T(8,128)(2,1)S(1)}, bf16[16,4224]{1,0:T(8,128)(2,1)S(1)}, u32[]{:S(2)}, u32[]{:S(2)}) collective-permute-start(bf16[16,4224]{1,0:T(8,128)(2,1)S(1)} %get-tuple-element.35), channel_id=1, source_target_pairs={{0,1},{1,0},{2,3},{3,2},{4,5},{5,4},{6,7},{7,6},{8,9},{9,8},{10,11... | collective-permute-start | bytes 405512 | tf_op jit(solution)/shard_map/ppermute | solution.py:211
  18.9 0.5 %collective-permute-start.5 = (bf16[16,4224]{1,0:T(8,128)(2,1)S(1)}, bf16[16,4224]{1,0:T(8,128)(2,1)S(1)}, u32[]{:S(2)}, u32[]{:S(2)}) collective-permute-start(bf16[16,4224]{1,0:T(8,128)(2,1)S(1)} %get-tuple-element.36), channel_id=1, source_target_pairs={{0,2},{1,3},{2,0},{3,1},{4,6},{5,7},{6,4},{7,5},{8,10},{9,11},{10,... | collective-permute-start | bytes 405512 | tf_op jit(solution)/shard_map/ppermute | solution.py:211
  19.4 2.5 %shard_map.126 = (bf16[16,4096]{1,0:T(8,128)(2,1)S(1)}, bf16[16,4096]{1,0:T(8,128)(2,1)S(1)}, bf16[16,4096]{1,0:T(8,128)(2,1)S(1)}, bf16[16,4096]{1,0:T(8,128)(2,1)S(1)}) custom-call(bf16[16,4096]{1,0:T(8,128)(2,1)S(1)} %shard_map.125.refs_0_.refs_3_, bf16[16,4096]{1,0:T(8,128)(2,1)S(1)} %collective-permute-done.7.refs_1_.refs_4_, ...), custom_call_target="tpu_custom_call" | custom-call | flops 4026531840 | bytes 7471104 | tf_op jit(solution)/shard_map/pallas_call | solution.py:35
  21.9 2.5 %collective-permute-start.10 = (bf16[16,4096]{1,0:T(8,128)(2,1)S(1)}, bf16[16,4096]{1,0:T(8,128)(2,1)S(1)}, u32[]{:S(2)}, u32[]{:S(2)}) collective-permute-start(bf16[16,4096]{1,0:T(8,128)(2,1)S(1)} %get-tuple-element.41), channel_id=1, source_target_pairs={{0,3},{1,2},{2,1},{3,0},{4,7},{5,6},{6,5},{7,4},{8,11},{9,10},{10,... | collective-permute-start | bytes 393224 | tf_op jit(solution)/shard_map/ppermute | solution.py:211
  24.4 0.6 %collective-permute-start.11 = (bf16[16,4096]{1,0:T(8,128)(2,1)S(1)}, bf16[16,4096]{1,0:T(8,128)(2,1)S(1)}, u32[]{:S(2)}, u32[]{:S(2)}) collective-permute-start(bf16[16,4096]{1,0:T(8,128)(2,1)S(1)} %get-tuple-element.42), channel_id=1, source_target_pairs={{0,1},{1,0},{2,3},{3,2},{4,5},{5,4},{6,7},{7,6},{8,9},{9,8},{10,11... | collective-permute-start | bytes 393224 | tf_op jit(solution)/shard_map/ppermute | solution.py:211
  24.9 0.5 %collective-permute-start.12 = (bf16[16,4096]{1,0:T(8,128)(2,1)S(1)}, bf16[16,4096]{1,0:T(8,128)(2,1)S(1)}, u32[]{:S(2)}, u32[]{:S(2)}) collective-permute-start(bf16[16,4096]{1,0:T(8,128)(2,1)S(1)} %get-tuple-element.43), channel_id=1, source_target_pairs={{0,2},{1,3},{2,0},{3,1},{4,6},{5,7},{6,4},{7,5},{8,10},{9,11},{10,... | collective-permute-start | bytes 393224 | tf_op jit(solution)/shard_map/ppermute | solution.py:211
  25.4 0.1 shard_map.123
  25.5 0.1 collective-permute-start.6
  25.6 1.0 %shard_map.127 = f32[16,256]{1,0:T(8,128)} custom-call(bf16[16,4096]{1,0:T(8,128)(2,1)S(1)} %shard_map.125.refs_0_.refs_3_, bf16[16,4096]{1,0:T(8,128)(2,1)S(1)} %collective-permute-done.7.refs_1_.refs_4_, bf16[16,4096]{1,0:T(8,128)(2,1)S(1)} %collective-permute-done.8.refs_2_.refs_5_, bf16[16,4096]{1,0:T(8,128)(2,1)S(1)} %collective-permute-done.9.refs_3_.refs_6_, ...), custom_call_target="tpu_custom_call" | custom-call | flops 838860800 | bytes 704512 | tf_op jit(solution)/shard_map/pallas_call | solution.py:35
  26.7 2.4 %collective-permute-done.10.refs_1_ = bf16[16,4096]{1,0:T(8,128)(2,1)S(1)} collective-permute-done((bf16[16,4096]{1,0:T(8,128)(2,1)S(1)}, bf16[16,4096]{1,0:T(8,128)(2,1)S(1)}, u32[]{:S(2)}, u32[]{:S(2)}) %collective-permute-start.10) | collective-permute-done | bytes 131104 | tf_op jit(solution)/shard_map/ppermute | solution.py:211
  29.1 1.6 %collective-permute-done.11.refs_2_ = bf16[16,4096]{1,0:T(8,128)(2,1)S(1)} collective-permute-done((bf16[16,4096]{1,0:T(8,128)(2,1)S(1)}, bf16[16,4096]{1,0:T(8,128)(2,1)S(1)}, u32[]{:S(2)}, u32[]{:S(2)}) %collective-permute-start.11) | collective-permute-done | bytes 131104 | tf_op jit(solution)/shard_map/ppermute | solution.py:211
  30.7 0.1 shard_map.128
  30.8 1.5 %collective-permute-start.13 = (bf16[16,4224]{1,0:T(8,128)(2,1)S(1)}, bf16[16,4224]{1,0:T(8,128)(2,1)S(1)}, u32[]{:S(2)}, u32[]{:S(2)}) collective-permute-start(bf16[16,4224]{1,0:T(8,128)(2,1)S(1)} %shard_map.128), channel_id=1, source_target_pairs={{0,28},{1,29},{2,30},{3,31},{4,0},{5,1},{6,2},{7,3},{8,4},{9,5},{1... | collective-permute-start | bytes 405512 | tf_op jit(solution)/shard_map/ppermute | solution.py:211
  32.2 0.8 %shard_map.129 = f32[1,1,16,1024]{3,2,1,0:T(8,128)} custom-call(bf16[16,64]{1,0:T(8,128)(2,1)S(1)} %get-tuple-element.52.latent_ref, bf16[16,4224]{1,0:T(8,128)(2,1)S(1)} %collective-permute-done.3.refs_1_.refs_0_, bf16[16,4224]{1,0:T(8,128)(2,1)S(1)} %collective-permute-done.4.refs_2_.refs_1_, bf16[16,4224]{1,0:T(8,128)(2,1)S(1)} %collective-permute-done.5.refs_3_.refs_2_, ...), custom_call_target="tpu_custom_call" | custom-call | flops 838860800 | bytes 997376 | tf_op jit(solution)/shard_map/pallas_call | solution.py:35
  33.1 1.2 %shard_map.124 = bf16[1,128,4096]{2,1,0:T(8,128)(2,1)} custom-call(bf16[16,4224]{1,0:T(8,128)(2,1)S(1)} %collective-permute-done.6.message_ref), custom_call_target="tpu_custom_call" | custom-call | flops 16777216 | bytes 1183744 | tf_op jit(solution)/shard_map/pallas_call | solution.py:35
  34.3 0.5 %collective-permute-done.13.message_ref = bf16[16,4224]{1,0:T(8,128)(2,1)S(1)} collective-permute-done((bf16[16,4224]{1,0:T(8,128)(2,1)S(1)}, bf16[16,4224]{1,0:T(8,128)(2,1)S(1)}, u32[]{:S(2)}, u32[]{:S(2)}) %collective-permute-start.13) | collective-permute-done | bytes 135200 | tf_op jit(solution)/shard_map/ppermute | solution.py:211
  34.8 1.2 %shard_map.130 = bf16[1,128,4096]{2,1,0:T(8,128)(2,1)} custom-call(bf16[16,4224]{1,0:T(8,128)(2,1)S(1)} %collective-permute-done.13.message_ref), custom_call_target="tpu_custom_call" | custom-call | flops 16777216 | bytes 1183744 | tf_op jit(solution)/shard_map/pallas_call | solution.py:35
  (19 shorter events, 0.0 us)
Async XLA Ops:
  0.6 6.5 %copy-start.3 = (bf16[1,256,16]{1,2,0:T(8,128)(2,1)S(1)}, bf16[1,256,16]{1,2,0:T(8,128)(2,1)}, u32[]{:S(2)}) copy-start(bf16[1,256,16]{1,2,0:T(8,128)(2,1)} %param.15) | copy-start | bytes 24580
  0.6 6.4 %copy-start = (bf16[1,256,4096]{2,1,0:T(8,128)(2,1)S(1)}, bf16[1,256,4096]{2,1,0:T(8,128)(2,1)}, u32[]{:S(2)}) copy-start(bf16[1,256,4096]{2,1,0:T(8,128)(2,1)} %param.14) | copy-start | bytes 6291460
  2.5 9.9 %collective-permute-start.2 = (bf16[16,4096]{1,0:T(8,128)(2,1)S(1)}, bf16[16,4096]{1,0:T(8,128)(2,1)S(1)}, u32[]{:S(2)}, u32[]{:S(2)}) collective-permute-start(bf16[16,4096]{1,0:T(8,128)(2,1)S(1)} %get-tuple-element.32.refs_0_), channel_id=1, source_target_pairs={{0,3},{1,2},{2,1},{3,0},{4,7},{5,6},{6,5},{7,4},{8,11},{9,10},{10,... | collective-permute-start | bytes 393224 | tf_op jit(solution)/shard_map/ppermute | solution.py:211
  6.4 7.5 %collective-permute-start.1 = (bf16[16,4096]{1,0:T(8,128)(2,1)S(1)}, bf16[16,4096]{1,0:T(8,128)(2,1)S(1)}, u32[]{:S(2)}, u32[]{:S(2)}) collective-permute-start(bf16[16,4096]{1,0:T(8,128)(2,1)S(1)} %get-tuple-element.32.refs_0_), channel_id=1, source_target_pairs={{0,2},{1,3},{2,0},{3,1},{4,6},{5,7},{6,4},{7,5},{8,10},{9,11},{10,... | collective-permute-start | bytes 393224 | tf_op jit(solution)/shard_map/ppermute | solution.py:211
  6.9 7.0 %collective-permute-start = (bf16[16,4096]{1,0:T(8,128)(2,1)S(1)}, bf16[16,4096]{1,0:T(8,128)(2,1)S(1)}, u32[]{:S(2)}, u32[]{:S(2)}) collective-permute-start(bf16[16,4096]{1,0:T(8,128)(2,1)S(1)} %get-tuple-element.32.refs_0_), channel_id=1, source_target_pairs={{0,1},{1,0},{2,3},{3,2},{4,5},{5,4},{6,7},{7,6},{8,9},{9,8},{10,11... | collective-permute-start | bytes 393224 | tf_op jit(solution)/shard_map/ppermute | solution.py:211
  7.1 0.9 %copy-start.1 = (bf16[1,1,16,4096]{3,2,1,0:T(8,128)(2,1)S(1)}, bf16[1,1,16,4096]{3,2,1,0:T(8,128)(2,1)}, u32[]{:S(2)}) copy-start(bf16[1,1,16,4096]{3,2,1,0:T(8,128)(2,1)} %param.16) | copy-start | bytes 393220
  8.7 5.2 %copy-start.4 = (bf16[1,256,4096]{2,1,0:T(8,128)(2,1)S(1)}, bf16[1,256,4096]{2,1,0:T(8,128)(2,1)}, u32[]{:S(2)}) copy-start(bf16[1,256,4096]{2,1,0:T(8,128)(2,1)} %param.12) | copy-start | bytes 6291460
  8.7 5.2 %copy-start.5 = (bf16[1,256,4096]{2,1,0:T(8,128)(2,1)S(1)}, bf16[1,256,4096]{2,1,0:T(8,128)(2,1)}, u32[]{:S(2)}) copy-start(bf16[1,256,4096]{2,1,0:T(8,128)(2,1)} %param.13) | copy-start | bytes 6291460
  9.0 9.9 %collective-permute-start.9 = (bf16[16,4096]{1,0:T(8,128)(2,1)S(1)}, bf16[16,4096]{1,0:T(8,128)(2,1)S(1)}, u32[]{:S(2)}, u32[]{:S(2)}) collective-permute-start(bf16[16,4096]{1,0:T(8,128)(2,1)S(1)} %shard_map.125.refs_0_.refs_3_), channel_id=1, source_target_pairs={{0,3},{1,2},{2,1},{3,0},{4,7},{5,6},{6,5},{7,4},{8,11},{9,10},{10,... | collective-permute-start | bytes 393224 | tf_op jit(solution)/shard_map/ppermute | solution.py:211
  11.9 7.5 %collective-permute-start.8 = (bf16[16,4096]{1,0:T(8,128)(2,1)S(1)}, bf16[16,4096]{1,0:T(8,128)(2,1)S(1)}, u32[]{:S(2)}, u32[]{:S(2)}) collective-permute-start(bf16[16,4096]{1,0:T(8,128)(2,1)S(1)} %shard_map.125.refs_0_.refs_3_), channel_id=1, source_target_pairs={{0,2},{1,3},{2,0},{3,1},{4,6},{5,7},{6,4},{7,5},{8,10},{9,11},{10,... | collective-permute-start | bytes 393224 | tf_op jit(solution)/shard_map/ppermute | solution.py:211
  12.4 7.0 %collective-permute-start.7 = (bf16[16,4096]{1,0:T(8,128)(2,1)S(1)}, bf16[16,4096]{1,0:T(8,128)(2,1)S(1)}, u32[]{:S(2)}, u32[]{:S(2)}) collective-permute-start(bf16[16,4096]{1,0:T(8,128)(2,1)S(1)} %shard_map.125.refs_0_.refs_3_), channel_id=1, source_target_pairs={{0,1},{1,0},{2,3},{3,2},{4,5},{5,4},{6,7},{7,6},{8,9},{9,8},{10,11... | collective-permute-start | bytes 393224 | tf_op jit(solution)/shard_map/ppermute | solution.py:211
  15.8 9.1 %collective-permute-start.3 = (bf16[16,4224]{1,0:T(8,128)(2,1)S(1)}, bf16[16,4224]{1,0:T(8,128)(2,1)S(1)}, u32[]{:S(2)}, u32[]{:S(2)}) collective-permute-start(bf16[16,4224]{1,0:T(8,128)(2,1)S(1)} %get-tuple-element.34), channel_id=1, source_target_pairs={{0,3},{1,2},{2,1},{3,0},{4,7},{5,6},{6,5},{7,4},{8,11},{9,10},{10,... | collective-permute-start | bytes 405512 | tf_op jit(solution)/shard_map/ppermute | solution.py:211
  18.3 7.1 %collective-permute-start.4 = (bf16[16,4224]{1,0:T(8,128)(2,1)S(1)}, bf16[16,4224]{1,0:T(8,128)(2,1)S(1)}, u32[]{:S(2)}, u32[]{:S(2)}) collective-permute-start(bf16[16,4224]{1,0:T(8,128)(2,1)S(1)} %get-tuple-element.35), channel_id=1, source_target_pairs={{0,1},{1,0},{2,3},{3,2},{4,5},{5,4},{6,7},{7,6},{8,9},{9,8},{10,11... | collective-permute-start | bytes 405512 | tf_op jit(solution)/shard_map/ppermute | solution.py:211
  18.9 6.6 %collective-permute-start.5 = (bf16[16,4224]{1,0:T(8,128)(2,1)S(1)}, bf16[16,4224]{1,0:T(8,128)(2,1)S(1)}, u32[]{:S(2)}, u32[]{:S(2)}) collective-permute-start(bf16[16,4224]{1,0:T(8,128)(2,1)S(1)} %get-tuple-element.36), channel_id=1, source_target_pairs={{0,2},{1,3},{2,0},{3,1},{4,6},{5,7},{6,4},{7,5},{8,10},{9,11},{10,... | collective-permute-start | bytes 405512 | tf_op jit(solution)/shard_map/ppermute | solution.py:211
  19.4 6.2 %copy-start.2 = (bf16[1,1,16,4096]{3,2,1,0:T(8,128)(2,1)S(1)}, bf16[1,1,16,4096]{3,2,1,0:T(8,128)(2,1)}, u32[]{:S(2)}) copy-start(bf16[1,1,16,4096]{3,2,1,0:T(8,128)(2,1)} %param.16) | copy-start | bytes 393220
  21.9 7.2 %collective-permute-start.10 = (bf16[16,4096]{1,0:T(8,128)(2,1)S(1)}, bf16[16,4096]{1,0:T(8,128)(2,1)S(1)}, u32[]{:S(2)}, u32[]{:S(2)}) collective-permute-start(bf16[16,4096]{1,0:T(8,128)(2,1)S(1)} %get-tuple-element.41), channel_id=1, source_target_pairs={{0,3},{1,2},{2,1},{3,0},{4,7},{5,6},{6,5},{7,4},{8,11},{9,10},{10,... | collective-permute-start | bytes 393224 | tf_op jit(solution)/shard_map/ppermute | solution.py:211
  24.4 6.3 %collective-permute-start.11 = (bf16[16,4096]{1,0:T(8,128)(2,1)S(1)}, bf16[16,4096]{1,0:T(8,128)(2,1)S(1)}, u32[]{:S(2)}, u32[]{:S(2)}) collective-permute-start(bf16[16,4096]{1,0:T(8,128)(2,1)S(1)} %get-tuple-element.42), channel_id=1, source_target_pairs={{0,1},{1,0},{2,3},{3,2},{4,5},{5,4},{6,7},{7,6},{8,9},{9,8},{10,11... | collective-permute-start | bytes 393224 | tf_op jit(solution)/shard_map/ppermute | solution.py:211
  24.9 5.8 %collective-permute-start.12 = (bf16[16,4096]{1,0:T(8,128)(2,1)S(1)}, bf16[16,4096]{1,0:T(8,128)(2,1)S(1)}, u32[]{:S(2)}, u32[]{:S(2)}) collective-permute-start(bf16[16,4096]{1,0:T(8,128)(2,1)S(1)} %get-tuple-element.43), channel_id=1, source_target_pairs={{0,2},{1,3},{2,0},{3,1},{4,6},{5,7},{6,4},{7,5},{8,10},{9,11},{10,... | collective-permute-start | bytes 393224 | tf_op jit(solution)/shard_map/ppermute | solution.py:211
  25.5 7.5 %collective-permute-start.6 = (bf16[16,4224]{1,0:T(8,128)(2,1)S(1)}, bf16[16,4224]{1,0:T(8,128)(2,1)S(1)}, u32[]{:S(2)}, u32[]{:S(2)}) collective-permute-start(bf16[16,4224]{1,0:T(8,128)(2,1)S(1)} %shard_map.123), channel_id=1, source_target_pairs={{0,4},{1,5},{2,6},{3,7},{4,8},{5,9},{6,10},{7,11},{8,12},{9,13},{1... | collective-permute-start | bytes 405512 | tf_op jit(solution)/shard_map/ppermute | solution.py:211
  30.8 4.0 %collective-permute-start.13 = (bf16[16,4224]{1,0:T(8,128)(2,1)S(1)}, bf16[16,4224]{1,0:T(8,128)(2,1)S(1)}, u32[]{:S(2)}, u32[]{:S(2)}) collective-permute-start(bf16[16,4224]{1,0:T(8,128)(2,1)S(1)} %shard_map.128), channel_id=1, source_target_pairs={{0,28},{1,29},{2,30},{3,31},{4,0},{5,1},{6,2},{7,3},{8,4},{9,5},{1... | collective-permute-start | bytes 405512 | tf_op jit(solution)/shard_map/ppermute | solution.py:211
